TPU v7x, 32 devices: a whole 2x2x4 slice. The times are simulated.
32 devices in a mesh: parts: 2 (over y), dp: 8 (over z, x), tensor: 2 (over core).
Axes of the slice: x: 2, y: 2, z: 4, core: 2. Of those that a mesh axis runs over, the one named last changes fastest.
Arguments:
- sent_rows: bfloat16 [4096, 8192], P(('parts', 'dp'), 'tensor'), parts along dimension 0, may hold values from -6 to 6
- norm_gain: float32 [8192], P('tensor'), may hold values from 0.5 to 12
- qkv_weight: bfloat16 [8192, 1280], P('tensor', 'dp'), may hold values from -0.0625 to 0.0625
- route_counts: int32 [16, 8], P('parts'), parts along dimension 0, may hold values from 0 to 32, as said below
- response_lengths: int32 [16, 8], P(('parts', 'dp')), parts along dimension 0, may hold values from 1 to 64, 128 in all within a row
- prefix_lengths: int32 [16, 8], P(('parts', 'dp')), parts along dimension 0, may hold values from 0 to 8191
Outputs:
- new_keys: bfloat16 [2048, 128], P(('parts', 'dp')), parts along dimension 0
- new_values: bfloat16 [2048, 128], P(('parts', 'dp')), parts along dimension 0
- attended: bfloat16 [2048, 1024], P(('parts', 'dp'), 'tensor'), parts along dimension 0
There are 2 independent parts, one for each index of `parts`. A program takes and returns all parts, laid end to end along the dimension named above; an argument that names none is the same for every part. Nothing has to cross between parts.
Inputs may be any that keep to these rules, and one draw needn't show every extreme that they name: route_counts[s, d] rows go from group s to group d; every column sums to 128; every column holds at least one entry equal to 32, and its entries pair up into pairs that sum to 32.
All inputs are finite; a program needn't handle non-finite values.
Results may differ from a plain program's by a relative error of at most 0.004.
The roundings to bfloat16 on the way count: a program that leaves them out, or rounds other values in their place, can miss the bound.
Values may be sent and summed in bfloat16 or wider, within the bound.
No kernel may reach another device: no remote copies, remote signals or barrier semaphores. Data moves between devices by JAX's collectives and lax.ppermute only.
A program may use at most 128 MiB of HBM per device.

v0:
```python
import jax
import jax.numpy as jnp
from jax import lax
from jax.sharding import PartitionSpec as P

D = 8192
HD = 128
HQ = 8
TOK_DEV = 128


def rotate(block, positions):
    half = block.shape[-1] // 2
    freq = jnp.exp(-jnp.log(500000.0) * jnp.arange(half, dtype=jnp.float32) * 2.0 / block.shape[-1])
    angle = positions.astype(jnp.float32)[:, None] * freq[None, :]
    if block.ndim == 3:
        angle = angle[:, None, :]
    cosine = jnp.cos(angle)
    sine = jnp.sin(angle)
    first = block[..., :half]
    second = block[..., half:]
    return jnp.concatenate(
        [first * cosine - second * sine, second * cosine + first * sine], axis=-1
    )


def positions_of(lengths, prefix, count):
    ends = jnp.cumsum(lengths)
    starts = ends - lengths
    place = jnp.arange(count, dtype=jnp.int32)
    member = (place[:, None] >= starts[None, :]) & (place[:, None] < ends[None, :])
    which = jnp.arange(lengths.shape[0], dtype=jnp.int32)
    sequence = jnp.sum(jnp.where(member, which[None, :], 0), axis=1)
    position = jnp.sum(
        jnp.where(member, prefix[None, :] + place[:, None] - starts[None, :], 0), axis=1
    )
    return (sequence, position)


def pack_rows(received, column, slot, count):
    ends = jnp.cumsum(column)
    starts = ends - column
    place = jnp.arange(count, dtype=jnp.int32)
    member = (place[:, None] >= starts[None, :]) & (place[:, None] < ends[None, :])
    source = jnp.arange(column.shape[0], dtype=jnp.int32)
    anchor = jnp.sum(jnp.where(member, source[None, :], 0), axis=1)
    within = jnp.sum(jnp.where(member, place[:, None] - starts[None, :], 0), axis=1)
    index = anchor * slot + within
    return jnp.take(received, index, axis=0)


def attend(queries, keys, values, sequence, position):
    scores = jnp.einsum(
        "qhd,kd->hqk", queries, keys, preferred_element_type=jnp.float32
    ) / jnp.sqrt(jnp.float32(keys.shape[-1]))
    allowed = (sequence[:, None] == sequence[None, :]) & (position[None, :] <= position[:, None])
    scores = jnp.where(allowed[None, :, :], scores, jnp.float32(-1e30))
    top = jnp.max(scores, axis=-1, keepdims=True)
    expo = jnp.exp(scores - top)
    weights = (expo / jnp.sum(expo, axis=-1, keepdims=True)).astype(jnp.bfloat16)
    out = jnp.einsum("hqk,kd->qhd", weights, values, preferred_element_type=jnp.float32)
    return out.astype(jnp.bfloat16)


def project(rows, norm_gain, qkv_weight):
    wide = rows.astype(jnp.float32)
    squares = jnp.sum(wide * wide, axis=1)
    total = lax.psum(squares, "tensor")
    normed = (wide * lax.rsqrt(total / D + 1e-05)[:, None] * norm_gain[None, :]).astype(
        jnp.bfloat16
    )
    partial_sums = jnp.dot(
        normed,
        lax.all_gather(qkv_weight, "dp", axis=1, tiled=True),
        preferred_element_type=jnp.float32,
    )
    width = HQ * HD
    share = width // lax.axis_size("tensor")
    summed = lax.psum(partial_sums, "tensor")
    mine = lax.dynamic_slice_in_dim(summed, lax.axis_index("tensor") * share, share, 1)
    paired = summed[:, width:]
    return (mine.astype(jnp.bfloat16), paired.astype(jnp.bfloat16))


def per_device(sent_rows, norm_gain, qkv_weight, route_counts, response_lengths, prefix_lengths):
    groups = lax.axis_size("dp")
    slot = sent_rows.shape[0] // groups
    column = lax.dynamic_slice_in_dim(route_counts, lax.axis_index("dp"), 1, 1)[:, 0]
    arrived = lax.all_to_all(sent_rows, "dp", split_axis=0, concat_axis=0, tiled=True)
    packed = pack_rows(arrived, column, slot, TOK_DEV)
    mine, paired = project(packed, norm_gain, qkv_weight)
    sequence, position = positions_of(response_lengths[0], prefix_lengths[0], TOK_DEV)
    new_keys = rotate(paired[:, :HD].astype(jnp.float32), position).astype(jnp.bfloat16)
    new_values = paired[:, HD:]
    heads = mine.reshape(TOK_DEV, mine.shape[1] // HD, HD)
    queries = rotate(heads.astype(jnp.float32), position).astype(jnp.bfloat16)
    out = attend(queries, new_keys, new_values, sequence, position)
    return (new_keys, new_values, out.reshape(TOK_DEV, mine.shape[1]))


def solution(mesh):
    in_specs = (
        P(("parts", "dp"), "tensor"),
        P("tensor"),
        P("tensor", "dp"),
        P("parts", None),
        P(("parts", "dp"), None),
        P(("parts", "dp"), None),
    )
    out_specs = (P(("parts", "dp"), None), P(("parts", "dp"), None), P(("parts", "dp"), "tensor"))
    return jax.shard_map(
        per_device, mesh=mesh, in_specs=in_specs, out_specs=out_specs, check_vma=False
    )
```

profile of v0, /device:TPU:0, one launch (start us, length us, event | category | flops | bytes accessed | tf_op | source)
XLA Modules:
  0.0 222.1 jit_solution(9661315677644150763)
XLA Ops:
  7.2 0.0 all-gather.2.cloned.1.call-start
  7.2 0.7 all-gather.2.cloned.1.call-update
  7.9 0.0 copy-start.2
  7.9 0.0 copy-start.5
  7.9 0.0 copy-start.3
  7.9 7.4 %all-to-all-start = ((bf16[8,32,4096]{2,1,0:T(8,128)(2,1)}), bf16[8,32,4096]{2,1,0:T(8,128)(2,1)S(1)}, u32[]{:S(2)}, u32[]{:S(2)}) async-start(bf16[8,32,4096]{2,1,0:T(8,128)(2,1)} %bitcast.39), calls=%async_computation | async-start | bytes 4194304 | tf_op jit(solution)/shard_map/all_to_all | solution.py:89
  15.3 0.0 copy-done.2
  15.3 0.2 fusion.33
  15.5 0.1 reduce
  15.7 0.0 copy-done.5
  15.7 0.2 reduce-window.13
  15.9 0.0 copy-done.3
  15.9 0.1 select_reduce_fusion
  16.0 0.1 select_reduce_fusion.3
  16.1 0.1 compare_and_fusion
  16.2 85.9 %all-to-all-done = bf16[8,32,4096]{2,1,0:T(8,128)(2,1)S(1)} async-done(((bf16[8,32,4096]{2,1,0:T(8,128)(2,1)}), bf16[8,32,4096]{2,1,0:T(8,128)(2,1)S(1)}, u32[]{:S(2)}, u32[]{:S(2)}) %all-to-all-start) | async-done | bytes 2097184 | tf_op jit(solution)/shard_map/all_to_all | solution.py:89
  102.1 0.0 copy-start.4
  102.1 1.2 gather_fusion
  103.3 0.4 fusion.1
  103.7 2.5 %psum.14 = f32[128]{0:T(128)S(1)} all-reduce(f32[128]{0:T(128)S(1)} %fusion.1), channel_id=1, replica_groups=mesh['parts'=2,'dp'=8,'tensor'=2] {'tensor'}, use_global_device_ids=true, to_apply=%region_4.5 | all-reduce | flops 128 | bytes 1024 | tf_op jit(solution)/shard_map/psum | solution.py:68
  106.2 93.8 %all-gather.2.cloned.1.call-done = bf16[4096,1280]{0,1:T(8,128)(2,1)} async-done(((bf16[4096,160]{0,1:T(8,128)(2,1)}), bf16[4096,1280]{0,1:T(8,128)(2,1)}) %all-gather.2.cloned.1.call-update) | async-done | bytes 10485776 | tf_op jit(solution)/shard_map/all_gather | solution.py:74
  200.0 0.0 copy-done.4
  200.0 7.6 %fusion.8 = f32[128,1280]{1,0:T(8,128)S(1)} fusion(bf16[4096,1280]{0,1:T(8,128)(2,1)} %all-gather.2.cloned.1.call-done, f32[4096]{0:T(1024)S(1)} %copy-done.4, f32[128]{0:T(128)S(1)} %add_rsqrt_fusion, bf16[128,4096]{1,0:T(8,128)(2,1)S(1)} %gather_fusion, pred[128]{0:T(512)(128)(4,1)S(1)} %compare_and_fusion.1), kind=kOutput, calls=%fused_computation.13 | convolution fusion | flops 1344798720 | bytes 12206720 | tf_op jit(solution)/shard_map/dot_general | solution.py:72
  207.6 5.2 %all-reduce.1 = bf16[128,1280]{1,0:T(8,128)(2,1)S(1)} all-reduce(f32[128,1280]{1,0:T(8,128)S(1)} %fusion.8), channel_id=1, replica_groups=mesh['parts'=2,'dp'=8,'tensor'=2] {'tensor'}, use_global_device_ids=true, to_apply=%region_5.6 | all-reduce | flops 163840 | bytes 983040 | tf_op jit(solution)/shard_map/psum | solution.py:79
  212.8 0.0 copy-start.1
  212.8 0.1 reshape.200
  212.9 0.2 fusion.35
  213.1 0.3 multiply_cosine_fusion
  213.5 0.1 pad_maximum_fusion
  213.6 0.0 copy-start
  213.6 0.1 subtract_convert_fusion
  213.7 0.3 fusion.6
  213.9 0.3 fusion.36
  214.3 0.0 copy-done.1
  214.3 0.2 convolution_convert_fusion
  214.5 0.8 copy.18
  215.3 0.0 copy-done
  (11 shorter events, 0.1 us)
Async XLA Ops:
  7.2 192.8 %all-gather.2.cloned.1.call-start = ((), (), s32[]{:S(2)}) async-start(), calls=%async_computation.1 | async-start | bytes 11796480 | tf_op jit(solution)/shard_map/all_gather | solution.py:74
  7.9 7.4 %copy-start.2 = (s32[8,8]{1,0:T(8,128)S(1)}, s32[8,8]{1,0:T(8,128)}, u32[]{:S(2)}) copy-start(s32[8,8]{1,0:T(8,128)} %param.9) | copy-start | bytes 772
  7.9 7.8 %copy-start.5 = (s32[1,8]{1,0:T(1,128)S(1)}, s32[1,8]{1,0:T(1,128)}, u32[]{:S(2)}) copy-start(s32[1,8]{1,0:T(1,128)} %param.10) | copy-start | bytes 100
  7.9 7.9 %copy-start.3 = (s32[1,8]{1,0:T(1,128)S(1)}, s32[1,8]{1,0:T(1,128)}, u32[]{:S(2)}) copy-start(s32[1,8]{1,0:T(1,128)} %param.11) | copy-start | bytes 100
  7.9 94.1 %all-to-all-start = ((bf16[8,32,4096]{2,1,0:T(8,128)(2,1)}), bf16[8,32,4096]{2,1,0:T(8,128)(2,1)S(1)}, u32[]{:S(2)}, u32[]{:S(2)}) async-start(bf16[8,32,4096]{2,1,0:T(8,128)(2,1)} %bitcast.39), calls=%async_computation | async-start | bytes 4194304 | tf_op jit(solution)/shard_map/all_to_all | solution.py:89
  102.1 97.9 %copy-start.4 = (f32[4096]{0:T(1024)S(1)}, f32[4096]{0:T(1024)}, u32[]{:S(2)}) copy-start(f32[4096]{0:T(1024)} %param.7) | copy-start | bytes 49156
  212.8 1.5 copy-start.1
  213.6 1.7 copy-start
Sparse Core Ops, SparseCore 0:
  10.2 189.7 all-gather.1
where the time goes:
time: 222 us
  waiting for transfers between devices  180 us (81%)
  between operations  14.2 us (6%)
  matrix products  8.41 us (4%)
  blocking collectives  7.63 us (3%)
  starting transfers between devices  7.43 us (3%)
  local copies, waits for them, and re-layouts  2.47 us (1%)
    all_gather x1, waiting for transfers between devices, project(): lax.all_gather(qkv_weight, 'dp', axis=1, tiled=True)  93.8 us
    all_to_all x1, waiting for transfers between devices, per_device(): lax.all_to_all(sent_rows, 'dp', split_axis=0, concat_axis=0, tiled=True)  85.9 us
    dot_general x1, matrix products, project(): jnp.dot(normed, lax.all_gather(qkv_weight, 'dp', axis=1, tiled=True), pre...  7.59 us
    all_to_all x1, starting transfers between devices, per_device(): lax.all_to_all(sent_rows, 'dp', split_axis=0, concat_axis=0, tiled=True)  7.4 us
    psum x1, blocking collectives, project(): summed = lax.psum(partial_sums, 'tensor')  5.17 us
  transfers between devices with their start and end apart: 2, of which 2 were waited for; matrix products, arithmetic and copies ran while one was open for 1% of the time, Pallas kernels for 0%

commit v1 on v0

v1 whole, which is shorter than its diff:
```python
import jax
import jax.numpy as jnp
from jax import lax
from jax.sharding import PartitionSpec as P

D = 8192
HD = 128
HQ = 8
TOK_DEV = 128
BLOCK = 16
AHEAD = 16


def rotary(positions):
    half = HD // 2
    freq = jnp.exp(-jnp.log(500000.0) * jnp.arange(half, dtype=jnp.float32) * 2.0 / HD)
    angle = positions.astype(jnp.float32)[:, None] * freq[None, :]
    return (jnp.cos(angle), jnp.sin(angle))


def rotate(block, cosine, sine):
    half = HD // 2
    if block.ndim == 3:
        cosine = cosine[:, None, :]
        sine = sine[:, None, :]
    first = block[..., :half]
    second = block[..., half:]
    return jnp.concatenate(
        [first * cosine - second * sine, second * cosine + first * sine], axis=-1
    )


def members(lengths, count):
    ends = jnp.cumsum(lengths)
    starts = ends - lengths
    place = jnp.arange(count, dtype=jnp.int32)
    member = (place[:, None] >= starts[None, :]) & (place[:, None] < ends[None, :])
    return (member, place[:, None] - starts[None, :])


def positions_of(lengths, prefix, count):
    member, within = members(lengths, count)
    which = jnp.arange(lengths.shape[0], dtype=jnp.int32)
    sequence = jnp.sum(jnp.where(member, which[None, :], 0), axis=1)
    position = jnp.sum(jnp.where(member, prefix[None, :] + within, 0), axis=1)
    return (sequence, position)


def pick_of(column, slot, count):
    member, within = members(column, count)
    source = jnp.arange(column.shape[0], dtype=jnp.int32)
    index = jnp.sum(jnp.where(member, source[None, :] * slot + within, 0), axis=1)
    slots = jnp.arange(column.shape[0] * slot, dtype=jnp.int32)
    return (index[:, None] == slots[None, :]).astype(jnp.bfloat16)


def attend(queries, keys, values, allowed):
    scores = jnp.einsum(
        "qhd,kd->hqk", queries, keys, preferred_element_type=jnp.float32
    ) / jnp.sqrt(jnp.float32(HD))
    scores = jnp.where(allowed[None, :, :], scores, jnp.float32(-1e30))
    top = jnp.max(scores, axis=-1, keepdims=True)
    expo = jnp.exp(scores - top)
    weights = (expo / jnp.sum(expo, axis=-1, keepdims=True)).astype(jnp.bfloat16)
    out = jnp.einsum("hqk,kd->qhd", weights, values, preferred_element_type=jnp.float32)
    return out.astype(jnp.bfloat16)


def norm(rows, norm_gain):
    wide = rows.astype(jnp.float32)
    total = lax.psum(jnp.sum(wide * wide, axis=1), "tensor")
    return (wide * lax.rsqrt(total / D + 1e-05)[:, None] * norm_gain[None, :]).astype(
        jnp.bfloat16
    )


def product(rows, columns):
    return lax.dot_general(
        rows, columns, (((1,), (1,)), ((), ())), preferred_element_type=jnp.float32
    )


def sum_cores(partial):
    width = HQ * HD * partial.shape[1] // (HQ * HD + 2 * HD)
    share = width // lax.axis_size("tensor")
    core = lax.axis_index("tensor")
    rest = partial[:, width:]

    def half(t):
        return jnp.concatenate(
            [lax.dynamic_slice_in_dim(partial, t * share, share, 1), rest], axis=1
        )

    other = lax.ppermute(half(1 - core), "tensor", [(0, 1), (1, 0)])
    return (half(core) + other).astype(jnp.bfloat16)


def gather_line(mine, groups):
    lines = groups // 2
    group = lax.axis_index("dp")
    z = group // 2
    x = group % 2
    early, late = mine[:AHEAD], mine[AHEAD:]
    depth = mine.shape[1]

    def over(block, low, high):
        pairs = [(i, i ^ 1) for i in range(2 * low, 2 * high)]
        return lax.ppermute(block, "dp", pairs)

    def along(block, low, high, step):
        return lax.ppermute(block, "dp", [(i, i + 2 * step) for i in range(2 * low, 2 * high)])

    early_over = over(early, 0, lines)
    early = jnp.concatenate([early, early_over], axis=0)
    pieces = [(z, early, late, over(late, 0, lines))]
    up_early, up_late, down_early, down_late = early, late, early, late
    for k in range(1, lines):
        up_late = along(up_late, k - 1, lines - 1, 1)
        down_late = along(down_late, 1, lines - k + 1, -1)
        up_early = along(up_early, k - 1, lines - 1, 1)
        down_early = along(down_early, 1, lines - k + 1, -1)
        up_over = over(up_late, k, lines)
        down_over = over(down_late, 0, lines - k)
        pieces.append((jnp.where(z >= k, z - k, lines), up_early, up_late, up_over))
        pieces.append((jnp.where(z < lines - k, z + k, lines), down_early, down_late, down_over))
    whole = jnp.zeros((2 * (lines + 1), mine.shape[0], depth), mine.dtype)
    for place, first, own, other in pieces:
        for at, head, tail in ((x, first[:AHEAD], own), (1 - x, first[AHEAD:], other)):
            whole = lax.dynamic_update_slice(whole, head[None], (2 * place + at, 0, 0))
            whole = lax.dynamic_update_slice(whole, tail[None], (2 * place + at, AHEAD, 0))
    return whole[: 2 * lines].reshape(groups * mine.shape[0], depth)


def paired(sent_rows, norm_gain, qkv_weight, groups):
    part = lax.axis_index("parts")
    normed = norm(sent_rows, norm_gain)
    theirs = lax.ppermute(normed, "parts", [(0, 1), (1, 0)])
    turned = qkv_weight.T
    count = turned.shape[0] // (2 * BLOCK)
    mine = lax.dynamic_index_in_dim(
        turned.reshape(count, 2, BLOCK, turned.shape[1]), part, 1, False
    ).reshape(count * BLOCK, turned.shape[1])
    columns = gather_line(mine, groups)
    own = sum_cores(product(normed, columns))
    other = sum_cores(product(theirs, columns))
    first = jnp.where(part == 0, own, other)
    second = jnp.where(part == 0, other, own)
    ready = jnp.concatenate([first, second], axis=0)
    arrived = lax.all_to_all(ready, ("parts", "dp"), 0, 0, tiled=True)
    return arrived.reshape(2, sent_rows.shape[0], arrived.shape[1])


def single(sent_rows, norm_gain, qkv_weight):
    columns = lax.all_gather(qkv_weight.T, "dp", axis=0, tiled=True)
    ready = sum_cores(product(norm(sent_rows, norm_gain), columns))
    return lax.all_to_all(ready, "dp", 0, 0, tiled=True)[None]


def per_device(sent_rows, norm_gain, qkv_weight, route_counts, response_lengths, prefix_lengths):
    groups = lax.axis_size("dp")
    slot = sent_rows.shape[0] // groups
    column = lax.dynamic_slice_in_dim(route_counts, lax.axis_index("dp"), 1, 1)[:, 0]
    pick = pick_of(column, slot, TOK_DEV)
    sequence, position = positions_of(response_lengths[0], prefix_lengths[0], TOK_DEV)
    allowed = (sequence[:, None] == sequence[None, :]) & (position[None, :] <= position[:, None])
    cosine, sine = rotary(position)
    if lax.axis_size("parts") == 2 and groups == 8 and qkv_weight.shape[1] % (2 * BLOCK) == 0:
        arrived = paired(sent_rows, norm_gain, qkv_weight, groups)
    else:
        arrived = single(sent_rows, norm_gain, qkv_weight)
    planes, _, width = arrived.shape
    heads = width * planes // HD
    packed = jnp.einsum("qs,psc->qpc", pick, arrived, preferred_element_type=jnp.float32)
    if planes == 2:
        packed = packed.reshape(TOK_DEV, 2, width // BLOCK, BLOCK).transpose(0, 2, 1, 3)
    packed = packed.reshape(TOK_DEV, heads, HD)
    queries = rotate(packed[:, :-2], cosine, sine).astype(jnp.bfloat16)
    new_keys = rotate(packed[:, -2], cosine, sine).astype(jnp.bfloat16)
    new_values = packed[:, -1].astype(jnp.bfloat16)
    out = attend(queries, new_keys, new_values, allowed)
    return (new_keys, new_values, out.reshape(TOK_DEV, (heads - 2) * HD))


def solution(mesh):
    in_specs = (
        P(("parts", "dp"), "tensor"),
        P("tensor"),
        P("tensor", "dp"),
        P("parts", None),
        P(("parts", "dp"), None),
        P(("parts", "dp"), None),
    )
    out_specs = (P(("parts", "dp"), None), P(("parts", "dp"), None), P(("parts", "dp"), "tensor"))
    return jax.shard_map(
        per_device, mesh=mesh, in_specs=in_specs, out_specs=out_specs, check_vma=False
    )
```

time: 222 us -> 147 us (0.66)
  waiting for transfers between devices: 180 us -> 57.5 us
  local copies, waits for them, and re-layouts: 2.47 us -> 35.1 us
  starting transfers between devices: 7.43 us -> 38.9 us
  between operations: 14.2 us -> 1.14 us
  blocking collectives: 7.63 us -> 2.46 us
  other arithmetic: 1.62 us -> 6.19 us
  matrix products: 8.41 us -> 4.84 us
    all_gather x1 -> x0, waiting for transfers between devices: 93.8 us -> none  [project(): lax.all_gather(qkv_weight, 'dp', axis=1, tiled=True)]
    all_to_all x1, waiting for transfers between devices: 85.9 us -> 12.5 us  [paired(): arrived = lax.all_to_all(ready, ('parts', 'dp'), 0, 0, tiled=True)]
    ppermute x0 -> x23, waiting for transfers between devices: none -> 45 us  [the longest x12 26.5 us: along(): lax.ppermute(block, 'dp', [(i, i + 2 * step) for i in range(2 * low, 2 *...]
    ppermute x0 -> x23, starting transfers between devices: none -> 35.4 us  [the longest x12 19.3 us: along(): lax.ppermute(block, 'dp', [(i, i + 2 * step) for i in range(2 * low, 2 *...]
    dynamic_update_slice x0 -> x28, local copies, waits for them, and re-layouts: none -> 24.1 us  [the longest x14 13.9 us: gather_line(): lax.dynamic_update_slice(whole, tail[None], (2 * place + at, AHEAD, 0))]
    psum x2 -> x1, blocking collectives: 7.63 us -> 2.46 us  [norm(): total = lax.psum(jnp.sum(wide * wide, axis=1), 'tensor')]
    slice x1 -> x7, local copies, waits for them, and re-layouts: 0.2 us -> 5.03 us  [the longest x1 2.83 us: gather_line(): return whole[:2 * lines].reshape(groups * mine.shape[0], depth)]
    all_to_all x1, starting transfers between devices: 7.4 us -> 3.55 us  [paired(): arrived = lax.all_to_all(ready, ('parts', 'dp'), 0, 0, tiled=True)]
  transfers between devices with their start and end apart: 2 -> 24, of which waited for: 2 -> 10; matrix products, arithmetic and copies ran while one was open for 1% -> 26% of each run, Pallas kernels for 0% -> 0%
where the time goes in v1:
time: 147 us; the launch traced here: 146 us
  waiting for transfers between devices  57.5 us (39%)
  starting transfers between devices  38.9 us (26%)
  local copies, waits for them, and re-layouts  35.1 us (24%)
  other arithmetic  6.19 us (4%)
  matrix products  4.84 us (3%)
  blocking collectives  2.46 us (2%)
    ppermute x12, waiting for transfers between devices, along(): lax.ppermute(block, 'dp', [(i, i + 2 * step) for i in range(2 * low, 2 *...  26.5 us
    ppermute x12, starting transfers between devices, along(): lax.ppermute(block, 'dp', [(i, i + 2 * step) for i in range(2 * low, 2 *...  19.3 us
    ppermute x8, waiting for transfers between devices, over(): return lax.ppermute(block, 'dp', pairs)  17 us
    dynamic_update_slice x14, local copies, waits for them, and re-layouts, gather_line(): lax.dynamic_update_slice(whole, tail[None], (2 * place + at, AHEAD, 0))  13.9 us
    ppermute x8, starting transfers between devices, over(): return lax.ppermute(block, 'dp', pairs)  13.9 us
    all_to_all x1, waiting for transfers between devices, paired(): arrived = lax.all_to_all(ready, ('parts', 'dp'), 0, 0, tiled=True)  12.5 us
    dynamic_update_slice x14, local copies, waits for them, and re-layouts, gather_line(): whole = lax.dynamic_update_slice(whole, head[None], (2 * place + at, 0, 0))  10.2 us
    dot_general x2, matrix products, product(): lax.dot_general(rows, columns, (((1,), (1,)), ((), ())), preferred_elemen...  3.65 us
  transfers between devices with their start and end apart: 24, of which 10 were waited for; matrix products, arithmetic and copies ran while one was open for 26% of the time, Pallas kernels for 0%

profile of v1, /device:TPU:0, one launch (start us, length us, event | category | flops | bytes accessed | tf_op | source)
XLA Modules:
  0.0 146.1 jit_solution(10677382566154224313)
XLA Ops:
  0.7 1.2 constant_dynamic-slice_fusion.4
  1.9 3.0 %collective-permute-start.1 = (bf16[64,4096]{1,0:T(8,128)(2,1)S(1)}, bf16[64,4096]{1,0:T(8,128)(2,1)}, u32[]{:S(2)}, u32[]{:S(2)}) collective-permute-start(bf16[64,4096]{1,0:T(8,128)(2,1)S(1)} %bitcast.139), channel_id=1, source_target_pairs={{0,2},{2,0},{4,6},{6,4},{8,10},{10,8},{12,14},{14,12},{1,3},{3,1},... | collective-permute-start | bytes 1572872 | tf_op jit(solution)/shard_map/ppermute | solution.py:108
  4.9 4.3 %collective-permute-start.3 = (bf16[64,4096]{1,0:T(8,128)(2,1)S(1)}, bf16[64,4096]{1,0:T(8,128)(2,1)}, u32[]{:S(2)}, u32[]{:S(2)}) collective-permute-start(bf16[64,4096]{1,0:T(8,128)(2,1)S(1)} %bitcast.140), channel_id=1, source_target_pairs={{0,4},{2,6},{4,8},{6,10},{8,12},{10,14},{1,5},{3,7},{5,9},{7,11},{... | collective-permute-start | bytes 1572872 | tf_op jit(solution)/shard_map/ppermute | solution.py:111
  9.2 1.3 collective-permute-start.6
  10.5 0.9 dynamic-slice_bitcast_fusion
  12.0 2.1 %fusion.1 = f32[256]{0:T(256)S(1)} fusion(bf16[256,4096]{1,0:T(8,128)(2,1)} %param.6), kind=kLoop, calls=%fused_computation.3 | loop fusion | flops 3145472 | bytes 2098176 | tf_op jit(solution)/shard_map/reduce_sum | solution.py:71
  14.1 2.5 %psum.7 = f32[256]{0:T(256)S(1)} all-reduce(f32[256]{0:T(256)S(1)} %fusion.1), channel_id=1, replica_groups=mesh['parts'=2,'dp'=8,'tensor'=2] {'tensor'}, use_global_device_ids=true, to_apply=%region_3.4 | all-reduce | flops 256 | bytes 2048 | tf_op jit(solution)/shard_map/psum | solution.py:71
  16.6 3.6 %broadcast_in_dim.144 = bf16[10,80,4096]{2,1,0:T(8,128)(2,1)} broadcast(bf16[]{:T(256)} %constant.74.clone.1), dimensions={} | broadcast | bytes 6553602 | tf_op jit(solution)/shard_map/broadcast_in_dim | solution.py:126
  20.2 1.6 %bitcast_dynamic-update-slice_fusion.14 = bf16[10,80,4096]{2,1,0:T(8,128)(2,1)} fusion(bf16[10,80,4096]{2,1,0:T(8,128)(2,1)} %broadcast_in_dim.144, s32[]{:T(128)S(6)} %select_n.134, bf16[5,2,16,4096]{3,2,1,0:T(8,128)(2,1)} %bitcast.152, s32[]{:T(128)S(6)} %select_n.131), kind=kLoop, calls=%fused_computation.70 | loop fusion | bytes 262152 | tf_op jit(solution)/shard_map/dynamic_update_slice | solution.py:129
  21.7 2.0 %fusion.3 = bf16[256,4096]{1,0:T(8,128)(2,1)} fusion(bf16[256,4096]{1,0:T(8,128)(2,1)S(1)} %copy-done, f32[4096]{0:T(1024)S(1)} %copy-done.3, f32[256]{0:T(256)S(1)} %add_rsqrt_fusion), kind=kLoop, calls=%fused_computation.5 | loop fusion | flops 4194304 | bytes 4211712 | tf_op jit(solution)/shard_map/convert_element_type | solution.py:72
  23.7 0.8 constant_dynamic-update-slice_fusion
  24.6 4.5 %collective-permute-start.2 = (bf16[32,4096]{1,0:T(8,128)(2,1)S(1)}, bf16[32,4096]{1,0:T(8,128)(2,1)S(1)}, u32[]{:S(2)}, u32[]{:S(2)}) collective-permute-start(bf16[32,4096]{1,0:T(8,128)(2,1)S(1)} %pad_maximum_fusion.5), channel_id=1, source_target_pairs={{0,4},{2,6},{4,8},{6,10},{8,12},{10,14},{1,5},{3,7},{5,9},{7,11},{... | collective-permute-start | bytes 786440 | tf_op jit(solution)/shard_map/ppermute | solution.py:111
  29.1 1.3 collective-permute-start.5
  30.4 0.7 bitcast_dynamic-update-slice_fusion.13
  31.1 3.9 %collective-permute-done.2 = bf16[32,4096]{1,0:T(8,128)(2,1)S(1)} collective-permute-done((bf16[32,4096]{1,0:T(8,128)(2,1)S(1)}, bf16[32,4096]{1,0:T(8,128)(2,1)S(1)}, u32[]{:S(2)}, u32[]{:S(2)}) %collective-permute-start.2) | collective-permute-done | bytes 262176 | tf_op jit(solution)/shard_map/ppermute | solution.py:111
  35.0 1.5 %collective-permute-start.21 = (bf16[256,4096]{1,0:T(8,128)(2,1)}, bf16[256,4096]{1,0:T(8,128)(2,1)S(1)}, u32[]{:S(2)}, u32[]{:S(2)}) collective-permute-start(bf16[256,4096]{1,0:T(8,128)(2,1)} %fusion.3), channel_id=1, source_target_pairs={{0,16},{16,0},{1,17},{17,1},{2,18},{18,2},{3,19},{19,3},{4,20},{20... | collective-permute-start | bytes 6291464 | tf_op jit(solution)/shard_map/ppermute | solution.py:137
  36.5 2.6 %collective-permute-done.5 = bf16[32,4096]{1,0:T(8,128)(2,1)S(1)} collective-permute-done((bf16[32,4096]{1,0:T(8,128)(2,1)S(1)}, bf16[32,4096]{1,0:T(8,128)(2,1)S(1)}, u32[]{:S(2)}, u32[]{:S(2)}) %collective-permute-start.5) | collective-permute-done | bytes 262176 | tf_op jit(solution)/shard_map/ppermute | solution.py:111
  39.1 0.7 collective-permute-start.8
  39.8 1.3 collective-permute-start.11
  41.1 0.7 collective-permute-start.4
  41.8 1.9 %bitcast_dynamic-update-slice_fusion.12 = bf16[10,80,4096]{2,1,0:T(8,128)(2,1)} fusion(bf16[10,80,4096]{2,1,0:T(8,128)(2,1)} %bitcast_dynamic-update-slice_fusion.13, s32[]{:T(128)S(6)} %select_n.135, bf16[64,4096]{1,0:T(8,128)(2,1)} %collective-permute-done.1), kind=kLoop, calls=%fused_computation.25 | loop fusion | bytes 1048580 | tf_op jit(solution)/shard_map/dynamic_update_slice | solution.py:130
  44.4 1.9 %bitcast_dynamic-update-slice_fusion.11 = bf16[10,80,4096]{2,1,0:T(8,128)(2,1)} fusion(bf16[10,80,4096]{2,1,0:T(8,128)(2,1)} %fusion.24, s32[]{:T(128)S(6)} %select_n.137, bf16[64,4096]{1,0:T(8,128)(2,1)} %collective-permute-done.3), kind=kLoop, calls=%fused_computation.24 | loop fusion | bytes 1048580 | tf_op jit(solution)/shard_map/dynamic_update_slice | solution.py:130
  46.9 0.7 collective-permute-start.9
  47.6 3.4 %collective-permute-start.7 = (bf16[64,4096]{1,0:T(8,128)(2,1)S(1)}, bf16[64,4096]{1,0:T(8,128)(2,1)S(1)}, u32[]{:S(2)}, u32[]{:S(2)}) collective-permute-start(bf16[64,4096]{1,0:T(8,128)(2,1)S(1)} %collective-permute-done.6), channel_id=1, source_target_pairs={{0,2},{2,0},{4,6},{6,4},{8,10},{10,8},{1,3},{3,1},{5,7},{7,5},{9,1... | collective-permute-start | bytes 1572872 | tf_op jit(solution)/shard_map/ppermute | solution.py:108
  51.0 0.8 bitcast_dynamic-update-slice_fusion.10
  51.9 0.7 fusion.22
  52.5 0.8 bitcast_dynamic-update-slice_fusion.9
  53.4 0.7 fusion.21
  54.0 1.3 collective-permute-start.12
  55.3 0.7 collective-permute-start.14
  56.0 6.4 %collective-permute-done.7 = bf16[64,4096]{1,0:T(8,128)(2,1)S(1)} collective-permute-done((bf16[64,4096]{1,0:T(8,128)(2,1)S(1)}, bf16[64,4096]{1,0:T(8,128)(2,1)S(1)}, u32[]{:S(2)}, u32[]{:S(2)}) %collective-permute-start.7) | collective-permute-done | bytes 524320 | tf_op jit(solution)/shard_map/ppermute | solution.py:108
  62.4 1.3 collective-permute-start.17
  63.7 0.7 collective-permute-start.10
  64.4 0.8 bitcast_dynamic-update-slice_fusion.8
  65.9 0.9 bitcast_dynamic-update-slice_fusion.7
  67.4 13.3 %collective-permute-done.12 = bf16[64,4096]{1,0:T(8,128)(2,1)S(1)} collective-permute-done((bf16[64,4096]{1,0:T(8,128)(2,1)S(1)}, bf16[64,4096]{1,0:T(8,128)(2,1)S(1)}, u32[]{:S(2)}, u32[]{:S(2)}) %collective-permute-start.12) | collective-permute-done | bytes 524320 | tf_op jit(solution)/shard_map/ppermute | solution.py:111
  80.7 0.7 collective-permute-start.15
  81.4 2.4 %collective-permute-start.13 = (bf16[64,4096]{1,0:T(8,128)(2,1)S(1)}, bf16[64,4096]{1,0:T(8,128)(2,1)S(1)}, u32[]{:S(2)}, u32[]{:S(2)}) collective-permute-start(bf16[64,4096]{1,0:T(8,128)(2,1)S(1)} %collective-permute-done.12), channel_id=1, source_target_pairs={{0,2},{2,0},{4,6},{6,4},{1,3},{3,1},{5,7},{7,5},{16,18},{18,16},{2... | collective-permute-start | bytes 1572872 | tf_op jit(solution)/shard_map/ppermute | solution.py:108
  83.9 0.8 bitcast_dynamic-update-slice_fusion.6
  84.7 0.7 fusion.18
  85.4 0.8 bitcast_dynamic-update-slice_fusion.5
  86.9 5.6 %collective-permute-done.13 = bf16[64,4096]{1,0:T(8,128)(2,1)S(1)} collective-permute-done((bf16[64,4096]{1,0:T(8,128)(2,1)S(1)}, bf16[64,4096]{1,0:T(8,128)(2,1)S(1)}, u32[]{:S(2)}, u32[]{:S(2)}) %collective-permute-start.13) | collective-permute-done | bytes 524320 | tf_op jit(solution)/shard_map/ppermute | solution.py:108
  92.5 1.3 collective-permute-start.18
  93.8 0.7 collective-permute-start.16
  94.5 0.8 bitcast_dynamic-update-slice_fusion.4
  96.0 0.9 bitcast_dynamic-update-slice_fusion.3
  96.9 6.7 %collective-permute-done.18 = bf16[64,4096]{1,0:T(8,128)(2,1)S(1)} collective-permute-done((bf16[64,4096]{1,0:T(8,128)(2,1)S(1)}, bf16[64,4096]{1,0:T(8,128)(2,1)S(1)}, u32[]{:S(2)}, u32[]{:S(2)}) %collective-permute-start.18) | collective-permute-done | bytes 524320 | tf_op jit(solution)/shard_map/ppermute | solution.py:111
  103.6 2.4 %collective-permute-start.19 = (bf16[64,4096]{1,0:T(8,128)(2,1)S(1)}, bf16[64,4096]{1,0:T(8,128)(2,1)S(1)}, u32[]{:S(2)}, u32[]{:S(2)}) collective-permute-start(bf16[64,4096]{1,0:T(8,128)(2,1)S(1)} %collective-permute-done.18), channel_id=1, source_target_pairs={{0,2},{2,0},{1,3},{3,1},{16,18},{18,16},{17,19},{19,17}} | collective-permute-start | bytes 1572872 | tf_op jit(solution)/shard_map/ppermute | solution.py:108
  106.0 0.7 fusion.15
  106.7 0.8 bitcast_dynamic-update-slice_fusion.2
  107.5 0.7 fusion.14
  108.2 0.8 bitcast_dynamic-update-slice_fusion.1
  109.0 0.7 fusion.13
  109.7 5.0 %collective-permute-done.19 = bf16[64,4096]{1,0:T(8,128)(2,1)S(1)} collective-permute-done((bf16[64,4096]{1,0:T(8,128)(2,1)S(1)}, bf16[64,4096]{1,0:T(8,128)(2,1)S(1)}, u32[]{:S(2)}, u32[]{:S(2)}) %collective-permute-start.19) | collective-permute-done | bytes 524320 | tf_op jit(solution)/shard_map/ppermute | solution.py:108
  114.6 0.8 bitcast_dynamic-update-slice_fusion
  115.5 2.8 %slice.116 = bf16[8,80,4096]{2,1,0:T(8,128)(2,1)S(1)} slice(bf16[10,80,4096]{2,1,0:T(8,128)(2,1)} %bitcast_dynamic-update-slice_fusion), slice={[0:8], [0:80], [0:4096]} | slice | bytes 10485760 | tf_op jit(solution)/shard_map/slice | solution.py:131
  118.3 1.8 %fusion.56 = f32[256,640]{1,0:T(8,128)S(1)} fusion(bf16[256,4096]{1,0:T(8,128)(2,1)S(1)} %copy-done.1, bf16[640,4096]{1,0:T(8,128)(2,1)S(1)} %bitcast.137), kind=kOutput, calls=%fused_computation.114 | convolution fusion | flops 1342177280 | bytes 7995392 | tf_op jit(solution)/shard_map/dot_general | solution.py:78
  120.2 1.8 %fusion.57 = f32[256,640]{1,0:T(8,128)S(1)} fusion(bf16[256,4096]{1,0:T(8,128)(2,1)S(1)} %collective-permute-done.21, bf16[640,4096]{1,0:T(8,128)(2,1)S(1)} %bitcast.138), kind=kOutput, calls=%fused_computation.115 | convolution fusion | flops 1342177280 | bytes 7995392 | tf_op jit(solution)/shard_map/dot_general | solution.py:78
  123.1 0.9 collective-permute-done.22
  124.7 0.8 pad_maximum_fusion.4
  125.5 3.6 %all-to-all-start = ((bf16[16,32,384]{2,1,0:T(8,128)(2,1)}), bf16[16,32,384]{2,1,0:T(8,128)(2,1)S(1)}, u32[]{:S(2)}, u32[]{:S(2)}) async-start(bf16[16,32,384]{2,1,0:T(8,128)(2,1)} %bitcast.35), calls=%async_computation | async-start | bytes 786432 | tf_op jit(solution)/shard_map/all_to_all | solution.py:149
  129.7 12.5 %all-to-all-done = bf16[16,32,384]{2,1,0:T(8,128)(2,1)S(1)} async-done(((bf16[16,32,384]{2,1,0:T(8,128)(2,1)}), bf16[16,32,384]{2,1,0:T(8,128)(2,1)S(1)}, u32[]{:S(2)}, u32[]{:S(2)}) %all-to-all-start) | async-done | bytes 393248 | tf_op jit(solution)/shard_map/all_to_all | solution.py:149
  144.6 0.8 copy.37
  145.4 0.7 copy.36
  (75 shorter events, 9.3 us)
Async XLA Ops:
  0.6 21.1 %copy-start = (bf16[256,4096]{1,0:T(8,128)(2,1)S(1)}, bf16[256,4096]{1,0:T(8,128)(2,1)}, u32[]{:S(2)}) copy-start(bf16[256,4096]{1,0:T(8,128)(2,1)} %param.6) | copy-start | bytes 6291460
  0.6 21.1 %copy-start.3 = (f32[4096]{0:T(1024)S(1)}, f32[4096]{0:T(1024)}, u32[]{:S(2)}) copy-start(f32[4096]{0:T(1024)} %param.7) | copy-start | bytes 49156
  1.9 37.9 %collective-permute-start.1 = (bf16[64,4096]{1,0:T(8,128)(2,1)S(1)}, bf16[64,4096]{1,0:T(8,128)(2,1)}, u32[]{:S(2)}, u32[]{:S(2)}) collective-permute-start(bf16[64,4096]{1,0:T(8,128)(2,1)S(1)} %bitcast.139), channel_id=1, source_target_pairs={{0,2},{2,0},{4,6},{6,4},{8,10},{10,8},{12,14},{14,12},{1,3},{3,1},... | collective-permute-start | bytes 1572872 | tf_op jit(solution)/shard_map/ppermute | solution.py:108
  4.9 36.2 %collective-permute-start.3 = (bf16[64,4096]{1,0:T(8,128)(2,1)S(1)}, bf16[64,4096]{1,0:T(8,128)(2,1)}, u32[]{:S(2)}, u32[]{:S(2)}) collective-permute-start(bf16[64,4096]{1,0:T(8,128)(2,1)S(1)} %bitcast.140), channel_id=1, source_target_pairs={{0,4},{2,6},{4,8},{6,10},{8,12},{10,14},{1,5},{3,7},{5,9},{7,11},{... | collective-permute-start | bytes 1572872 | tf_op jit(solution)/shard_map/ppermute | solution.py:111
  9.2 37.7 %collective-permute-start.6 = (bf16[64,4096]{1,0:T(8,128)(2,1)S(1)}, bf16[64,4096]{1,0:T(8,128)(2,1)S(1)}, u32[]{:S(2)}, u32[]{:S(2)}) collective-permute-start(bf16[64,4096]{1,0:T(8,128)(2,1)S(1)} %bitcast.141), channel_id=1, source_target_pairs={{4,0},{6,2},{8,4},{10,6},{12,8},{14,10},{5,1},{7,3},{9,5},{11,7},{... | collective-permute-start | bytes 1572872 | tf_op jit(solution)/shard_map/ppermute | solution.py:111
  11.4 13.1 %collective-permute-start = (bf16[16,4096]{1,0:T(8,128)(2,1)S(1)}, bf16[16,4096]{1,0:T(8,128)(2,1)S(1)}, u32[]{:S(2)}, u32[]{:S(2)}) collective-permute-start(bf16[16,4096]{1,0:T(8,128)(2,1)S(1)} %dynamic-slice_bitcast_fusion), channel_id=1, source_target_pairs={{0,2},{2,0},{4,6},{6,4},{8,10},{10,8},{12,14},{14,12},{1,3},{3,1},... | collective-permute-start | bytes 393224 | tf_op jit(solution)/shard_map/ppermute | solution.py:108
  24.6 10.4 %collective-permute-start.2 = (bf16[32,4096]{1,0:T(8,128)(2,1)S(1)}, bf16[32,4096]{1,0:T(8,128)(2,1)S(1)}, u32[]{:S(2)}, u32[]{:S(2)}) collective-permute-start(bf16[32,4096]{1,0:T(8,128)(2,1)S(1)} %pad_maximum_fusion.5), channel_id=1, source_target_pairs={{0,4},{2,6},{4,8},{6,10},{8,12},{10,14},{1,5},{3,7},{5,9},{7,11},{... | collective-permute-start | bytes 786440 | tf_op jit(solution)/shard_map/ppermute | solution.py:111
  29.1 10.0 %collective-permute-start.5 = (bf16[32,4096]{1,0:T(8,128)(2,1)S(1)}, bf16[32,4096]{1,0:T(8,128)(2,1)S(1)}, u32[]{:S(2)}, u32[]{:S(2)}) collective-permute-start(bf16[32,4096]{1,0:T(8,128)(2,1)S(1)} %pad_maximum_fusion.5), channel_id=1, source_target_pairs={{4,0},{6,2},{8,4},{10,6},{12,8},{14,10},{5,1},{7,3},{9,5},{11,7},{... | collective-permute-start | bytes 786440 | tf_op jit(solution)/shard_map/ppermute | solution.py:111
  35.0 85.2 %collective-permute-start.21 = (bf16[256,4096]{1,0:T(8,128)(2,1)}, bf16[256,4096]{1,0:T(8,128)(2,1)S(1)}, u32[]{:S(2)}, u32[]{:S(2)}) collective-permute-start(bf16[256,4096]{1,0:T(8,128)(2,1)} %fusion.3), channel_id=1, source_target_pairs={{0,16},{16,0},{1,17},{17,1},{2,18},{18,2},{3,19},{19,3},{4,20},{20... | collective-permute-start | bytes 6291464 | tf_op jit(solution)/shard_map/ppermute | solution.py:137
  39.1 14.9 %collective-permute-start.8 = (bf16[32,4096]{1,0:T(8,128)(2,1)S(1)}, bf16[32,4096]{1,0:T(8,128)(2,1)S(1)}, u32[]{:S(2)}, u32[]{:S(2)}) collective-permute-start(bf16[32,4096]{1,0:T(8,128)(2,1)S(1)} %collective-permute-done.2), channel_id=1, source_target_pairs={{4,8},{6,10},{8,12},{10,14},{5,9},{7,11},{9,13},{11,15},{20,24},{2... | collective-permute-start | bytes 786440 | tf_op jit(solution)/shard_map/ppermute | solution.py:111
  39.8 15.5 %collective-permute-start.11 = (bf16[32,4096]{1,0:T(8,128)(2,1)S(1)}, bf16[32,4096]{1,0:T(8,128)(2,1)S(1)}, u32[]{:S(2)}, u32[]{:S(2)}) collective-permute-start(bf16[32,4096]{1,0:T(8,128)(2,1)S(1)} %collective-permute-done.5), channel_id=1, source_target_pairs={{4,0},{6,2},{8,4},{10,6},{5,1},{7,3},{9,5},{11,7},{20,16},{22,18},... | collective-permute-start | bytes 786440 | tf_op jit(solution)/shard_map/ppermute | solution.py:111
  41.1 6.5 %collective-permute-start.4 = (bf16[64,4096]{1,0:T(8,128)(2,1)}, bf16[64,4096]{1,0:T(8,128)(2,1)S(1)}, u32[]{:S(2)}, u32[]{:S(2)}) collective-permute-start(bf16[64,4096]{1,0:T(8,128)(2,1)} %collective-permute-done.3), channel_id=1, source_target_pairs={{4,6},{6,4},{8,10},{10,8},{12,14},{14,12},{5,7},{7,5},{9,11},{11,9... | collective-permute-start | bytes 1572872 | tf_op jit(solution)/shard_map/ppermute | solution.py:108
  46.9 16.7 %collective-permute-start.9 = (bf16[64,4096]{1,0:T(8,128)(2,1)}, bf16[64,4096]{1,0:T(8,128)(2,1)S(1)}, u32[]{:S(2)}, u32[]{:S(2)}) collective-permute-start(bf16[64,4096]{1,0:T(8,128)(2,1)} %collective-permute-done.3), channel_id=1, source_target_pairs={{4,8},{6,10},{8,12},{10,14},{5,9},{7,11},{9,13},{11,15},{20,24},{2... | collective-permute-start | bytes 1572872 | tf_op jit(solution)/shard_map/ppermute | solution.py:111
  47.6 14.7 %collective-permute-start.7 = (bf16[64,4096]{1,0:T(8,128)(2,1)S(1)}, bf16[64,4096]{1,0:T(8,128)(2,1)S(1)}, u32[]{:S(2)}, u32[]{:S(2)}) collective-permute-start(bf16[64,4096]{1,0:T(8,128)(2,1)S(1)} %collective-permute-done.6), channel_id=1, source_target_pairs={{0,2},{2,0},{4,6},{6,4},{8,10},{10,8},{1,3},{3,1},{5,7},{7,5},{9,1... | collective-permute-start | bytes 1572872 | tf_op jit(solution)/shard_map/ppermute | solution.py:108
  54.0 26.7 %collective-permute-start.12 = (bf16[64,4096]{1,0:T(8,128)(2,1)S(1)}, bf16[64,4096]{1,0:T(8,128)(2,1)S(1)}, u32[]{:S(2)}, u32[]{:S(2)}) collective-permute-start(bf16[64,4096]{1,0:T(8,128)(2,1)S(1)} %collective-permute-done.6), channel_id=1, source_target_pairs={{4,0},{6,2},{8,4},{10,6},{5,1},{7,3},{9,5},{11,7},{20,16},{22,18},... | collective-permute-start | bytes 1572872 | tf_op jit(solution)/shard_map/ppermute | solution.py:111
  55.3 40.0 %collective-permute-start.14 = (bf16[32,4096]{1,0:T(8,128)(2,1)S(1)}, bf16[32,4096]{1,0:T(8,128)(2,1)S(1)}, u32[]{:S(2)}, u32[]{:S(2)}) collective-permute-start(bf16[32,4096]{1,0:T(8,128)(2,1)S(1)} %collective-permute-done.8), channel_id=1, source_target_pairs={{8,12},{10,14},{9,13},{11,15},{24,28},{26,30},{25,29},{27,31}} | collective-permute-start | bytes 786440 | tf_op jit(solution)/shard_map/ppermute | solution.py:111
  62.4 45.1 %collective-permute-start.17 = (bf16[32,4096]{1,0:T(8,128)(2,1)S(1)}, bf16[32,4096]{1,0:T(8,128)(2,1)S(1)}, u32[]{:S(2)}, u32[]{:S(2)}) collective-permute-start(bf16[32,4096]{1,0:T(8,128)(2,1)S(1)} %collective-permute-done.11), channel_id=1, source_target_pairs={{4,0},{6,2},{5,1},{7,3},{20,16},{22,18},{21,17},{23,19}} | collective-permute-start | bytes 786440 | tf_op jit(solution)/shard_map/ppermute | solution.py:111
  63.7 17.8 %collective-permute-start.10 = (bf16[64,4096]{1,0:T(8,128)(2,1)S(1)}, bf16[64,4096]{1,0:T(8,128)(2,1)S(1)}, u32[]{:S(2)}, u32[]{:S(2)}) collective-permute-start(bf16[64,4096]{1,0:T(8,128)(2,1)S(1)} %collective-permute-done.9), channel_id=1, source_target_pairs={{8,10},{10,8},{12,14},{14,12},{9,11},{11,9},{13,15},{15,13},{24,26... | collective-permute-start | bytes 1572872 | tf_op jit(solution)/shard_map/ppermute | solution.py:108
  80.7 13.1 %collective-permute-start.15 = (bf16[64,4096]{1,0:T(8,128)(2,1)S(1)}, bf16[64,4096]{1,0:T(8,128)(2,1)S(1)}, u32[]{:S(2)}, u32[]{:S(2)}) collective-permute-start(bf16[64,4096]{1,0:T(8,128)(2,1)S(1)} %collective-permute-done.9), channel_id=1, source_target_pairs={{8,12},{10,14},{9,13},{11,15},{24,28},{26,30},{25,29},{27,31}} | collective-permute-start | bytes 1572872 | tf_op jit(solution)/shard_map/ppermute | solution.py:111
  81.4 11.1 %collective-permute-start.13 = (bf16[64,4096]{1,0:T(8,128)(2,1)S(1)}, bf16[64,4096]{1,0:T(8,128)(2,1)S(1)}, u32[]{:S(2)}, u32[]{:S(2)}) collective-permute-start(bf16[64,4096]{1,0:T(8,128)(2,1)S(1)} %collective-permute-done.12), channel_id=1, source_target_pairs={{0,2},{2,0},{4,6},{6,4},{1,3},{3,1},{5,7},{7,5},{16,18},{18,16},{2... | collective-permute-start | bytes 1572872 | tf_op jit(solution)/shard_map/ppermute | solution.py:108
  92.5 11.1 %collective-permute-start.18 = (bf16[64,4096]{1,0:T(8,128)(2,1)S(1)}, bf16[64,4096]{1,0:T(8,128)(2,1)S(1)}, u32[]{:S(2)}, u32[]{:S(2)}) collective-permute-start(bf16[64,4096]{1,0:T(8,128)(2,1)S(1)} %collective-permute-done.12), channel_id=1, source_target_pairs={{4,0},{6,2},{5,1},{7,3},{20,16},{22,18},{21,17},{23,19}} | collective-permute-start | bytes 1572872 | tf_op jit(solution)/shard_map/ppermute | solution.py:111
  93.8 12.9 %collective-permute-start.16 = (bf16[64,4096]{1,0:T(8,128)(2,1)S(1)}, bf16[64,4096]{1,0:T(8,128)(2,1)S(1)}, u32[]{:S(2)}, u32[]{:S(2)}) collective-permute-start(bf16[64,4096]{1,0:T(8,128)(2,1)S(1)} %collective-permute-done.15), channel_id=1, source_target_pairs={{12,14},{14,12},{13,15},{15,13},{28,30},{30,28},{29,31},{31,29}} | collective-permute-start | bytes 1572872 | tf_op jit(solution)/shard_map/ppermute | solution.py:108
  103.6 11.1 %collective-permute-start.19 = (bf16[64,4096]{1,0:T(8,128)(2,1)S(1)}, bf16[64,4096]{1,0:T(8,128)(2,1)S(1)}, u32[]{:S(2)}, u32[]{:S(2)}) collective-permute-start(bf16[64,4096]{1,0:T(8,128)(2,1)S(1)} %collective-permute-done.18), channel_id=1, source_target_pairs={{0,2},{2,0},{1,3},{3,1},{16,18},{18,16},{17,19},{19,17}} | collective-permute-start | bytes 1572872 | tf_op jit(solution)/shard_map/ppermute | solution.py:108
  107.5 10.8 %copy-start.1 = (bf16[256,4096]{1,0:T(8,128)(2,1)S(1)}, bf16[256,4096]{1,0:T(8,128)(2,1)}, u32[]{:S(2)}) copy-start(bf16[256,4096]{1,0:T(8,128)(2,1)} %fusion.3) | copy-start | bytes 6291460
  120.2 2.7 %copy-start.6 = (s32[1,8]{1,0:T(1,128)S(1)}, s32[1,8]{1,0:T(1,128)}, u32[]{:S(2)}) copy-start(s32[1,8]{1,0:T(1,128)} %param.10) | copy-start | bytes 100
  122.0 7.0 %copy-start.4 = (s32[8,8]{1,0:T(8,128)S(1)}, s32[8,8]{1,0:T(8,128)}, u32[]{:S(2)}) copy-start(s32[8,8]{1,0:T(8,128)} %param.9) | copy-start | bytes 772
  122.0 7.4 %copy-start.5 = (s32[1,8]{1,0:T(1,128)S(1)}, s32[1,8]{1,0:T(1,128)}, u32[]{:S(2)}) copy-start(s32[1,8]{1,0:T(1,128)} %param.11) | copy-start | bytes 100
  122.2 1.8 %collective-permute-start.22 = (f32[256,384]{1,0:T(8,128)S(1)}, f32[256,384]{1,0:T(8,128)S(1)}, u32[]{:S(2)}, u32[]{:S(2)}) collective-permute-start(f32[256,384]{1,0:T(8,128)S(1)} %pad_maximum_fusion.2), channel_id=1, source_target_pairs={{0,1},{1,0},{2,3},{3,2},{4,5},{5,4},{6,7},{7,6},{8,9},{9,8},{10,11... | collective-permute-start | bytes 1179656 | tf_op jit(solution)/shard_map/ppermute | solution.py:94
  122.3 2.2 %collective-permute-start.20 = (f32[256,384]{1,0:T(8,128)S(1)}, f32[256,384]{1,0:T(8,128)S(1)}, u32[]{:S(2)}, u32[]{:S(2)}) collective-permute-start(f32[256,384]{1,0:T(8,128)S(1)} %pad_maximum_fusion), channel_id=1, source_target_pairs={{0,1},{1,0},{2,3},{3,2},{4,5},{5,4},{6,7},{7,6},{8,9},{9,8},{10,11... | collective-permute-start | bytes 1179656 | tf_op jit(solution)/shard_map/ppermute | solution.py:94
  125.5 16.7 %all-to-all-start = ((bf16[16,32,384]{2,1,0:T(8,128)(2,1)}), bf16[16,32,384]{2,1,0:T(8,128)(2,1)S(1)}, u32[]{:S(2)}, u32[]{:S(2)}) async-start(bf16[16,32,384]{2,1,0:T(8,128)(2,1)} %bitcast.35), calls=%async_computation | async-start | bytes 786432 | tf_op jit(solution)/shard_map/all_to_all | solution.py:149
  143.7 2.4 %copy-start.2 = (bf16[128,128]{1,0:T(8,128)(2,1)}, bf16[128,128]{1,0:T(8,128)(2,1)S(1)}, u32[]{:S(2)}) copy-start(bf16[128,128]{1,0:T(8,128)(2,1)S(1)} %pad_maximum_fusion.6) | copy-start | bytes 98308

commit v2 on v1

--- a/solution.py
+++ b/solution.py
@@ -1,6 +1,8 @@
 import jax
 import jax.numpy as jnp
 from jax import lax
+from jax.experimental import pallas as pl
+from jax.experimental.pallas import tpu as pltpu
 from jax.sharding import PartitionSpec as P
 
 D = 8192
@@ -8,7 +10,6 @@
 HQ = 8
 TOK_DEV = 128
 BLOCK = 16
-AHEAD = 16
 
 
 def rotary(positions):
@@ -66,12 +67,14 @@
     return out.astype(jnp.bfloat16)
 
 
-def norm(rows, norm_gain):
+def scale_of(rows):
     wide = rows.astype(jnp.float32)
     total = lax.psum(jnp.sum(wide * wide, axis=1), "tensor")
-    return (wide * lax.rsqrt(total / D + 1e-05)[:, None] * norm_gain[None, :]).astype(
-        jnp.bfloat16
-    )
+    return lax.rsqrt(total / D + 1e-05)
+
+
+def scaled(rows, scale, norm_gain):
+    return (rows.astype(jnp.float32) * scale[:, None] * norm_gain[None, :]).astype(jnp.bfloat16)
 
 
 def product(rows, columns):
@@ -80,79 +83,219 @@
     )
 
 
+def cut(partial, width, core):
+    share = width // lax.axis_size("tensor")
+    mine = lax.dynamic_slice_in_dim(partial, core * share, share, 1)
+    return jnp.concatenate([mine, partial[:, width:]], axis=1)
+
+
 def sum_cores(partial):
     width = HQ * HD * partial.shape[1] // (HQ * HD + 2 * HD)
-    share = width // lax.axis_size("tensor")
     core = lax.axis_index("tensor")
-    rest = partial[:, width:]
-
-    def half(t):
-        return jnp.concatenate(
-            [lax.dynamic_slice_in_dim(partial, t * share, share, 1), rest], axis=1
-        )
-
-    other = lax.ppermute(half(1 - core), "tensor", [(0, 1), (1, 0)])
-    return (half(core) + other).astype(jnp.bfloat16)
-
-
-def gather_line(mine, groups):
-    lines = groups // 2
-    group = lax.axis_index("dp")
-    z = group // 2
-    x = group % 2
-    early, late = mine[:AHEAD], mine[AHEAD:]
-    depth = mine.shape[1]
-
-    def over(block, low, high):
-        pairs = [(i, i ^ 1) for i in range(2 * low, 2 * high)]
-        return lax.ppermute(block, "dp", pairs)
-
-    def along(block, low, high, step):
-        return lax.ppermute(block, "dp", [(i, i + 2 * step) for i in range(2 * low, 2 * high)])
-
-    early_over = over(early, 0, lines)
-    early = jnp.concatenate([early, early_over], axis=0)
-    pieces = [(z, early, late, over(late, 0, lines))]
-    up_early, up_late, down_early, down_late = early, late, early, late
-    for k in range(1, lines):
-        up_late = along(up_late, k - 1, lines - 1, 1)
-        down_late = along(down_late, 1, lines - k + 1, -1)
-        up_early = along(up_early, k - 1, lines - 1, 1)
-        down_early = along(down_early, 1, lines - k + 1, -1)
-        up_over = over(up_late, k, lines)
-        down_over = over(down_late, 0, lines - k)
-        pieces.append((jnp.where(z >= k, z - k, lines), up_early, up_late, up_over))
-        pieces.append((jnp.where(z < lines - k, z + k, lines), down_early, down_late, down_over))
-    whole = jnp.zeros((2 * (lines + 1), mine.shape[0], depth), mine.dtype)
-    for place, first, own, other in pieces:
-        for at, head, tail in ((x, first[:AHEAD], own), (1 - x, first[AHEAD:], other)):
-            whole = lax.dynamic_update_slice(whole, head[None], (2 * place + at, 0, 0))
-            whole = lax.dynamic_update_slice(whole, tail[None], (2 * place + at, AHEAD, 0))
-    return whole[: 2 * lines].reshape(groups * mine.shape[0], depth)
+    other = lax.ppermute(cut(partial, width, 1 - core), "tensor", [(0, 1), (1, 0)])
+    return (cut(partial, width, core) + other).astype(jnp.bfloat16)
+
+
+def over(block, low, high):
+    return lax.ppermute(block, "dp", [(i, i ^ 1) for i in range(2 * low, 2 * high)])
+
+
+def along(block, low, high, step):
+    return lax.ppermute(block, "dp", [(i, i + 2 * step) for i in range(2 * low, 2 * high)])
+
+
+def gather_line(mine):
+    own = (mine, over(mine, 0, 4))
+    up1 = along(mine, 0, 3, 1)
+    down1 = along(mine, 1, 4, -1)
+    up2 = along(up1, 1, 3, 1)
+    down2 = along(down1, 1, 3, -1)
+    up1 = (up1, over(up1, 1, 4))
+    down1 = (down1, over(down1, 0, 3))
+    up3 = along(up2, 2, 3, 1)
+    down3 = along(down2, 1, 2, -1)
+    up2 = (up2, over(up2, 2, 4))
+    down2 = (down2, over(down2, 0, 2))
+    up3 = (up3, over(up3, 3, 4))
+    down3 = (down3, over(down3, 0, 1))
+    return own + up1 + down1 + up2 + down2, up3 + down3
+
+
+def early_kernel(at, *refs):
+    pieces, rows, out, whole, sems = refs[:10], refs[10:12], refs[12], refs[13], refs[14]
+    z, x, part = at[0], at[1], at[2]
+    size = pieces[0].shape[0]
+
+    def copies(k, place):
+        found = []
+        for side in range(2):
+            where = x if side == 0 else 1 - x
+            start = pl.multiple_of((2 * place + where) * size, BLOCK)
+            found.append(
+                pltpu.make_async_copy(
+                    pieces[2 * k + side], whole.at[pl.ds(start, size)], sems.at[2 * k + side]
+                )
+            )
+        return found
+
+    always = copies(0, z) + copies(1, (z + 3) % 4) + copies(2, (z + 1) % 4)
+    from_low = copies(3, (z + 2) % 4)
+    from_high = copies(4, (z + 2) % 4)
+    for copy in always:
+        copy.start()
+
+    @pl.when(z >= 2)
+    def _():
+        for copy in from_low:
+            copy.start()
+        for copy in from_low:
+            copy.wait()
+
+    @pl.when(z < 2)
+    def _():
+        for copy in from_high:
+            copy.start()
+        for copy in from_high:
+            copy.wait()
+
+    for copy in always:
+        copy.wait()
+    count = rows[0].shape[0]
+    for k in range(2):
+        index = part if k == 0 else 1 - part
+        start = pl.multiple_of(index * count, count)
+        for low in range(0, whole.shape[0], 256):
+            high = min(low + 256, whole.shape[0])
+            out[pl.ds(start, count), low:high] = product(rows[k][...], whole[low:high, :])
+
+
+def late_kernel(at, first, up, up_over, down, down_over, own, theirs, keep, send, last, sums, sems):
+    z, x, part, core = at[0], at[1], at[2], at[3]
+    size = up.shape[0]
+    count = own.shape[0]
+    width = first.shape[1]
+    heads = width * HQ // (HQ + 2)
+    share = heads // 2
+    edge = 2 * size
+    span = 256
+
+    def finish(piece, piece_over, offset, low):
+        found = []
+        for side, ref in ((0, piece), (1, piece_over)):
+            where = x if side == 0 else 1 - x
+            start = pl.multiple_of(offset + where * size, BLOCK)
+            found.append(
+                pltpu.make_async_copy(ref, last.at[pl.ds(start, size)], sems.at[side])
+            )
+        for copy in found:
+            copy.start()
+        for copy in found:
+            copy.wait()
+        column = lax.broadcasted_iota(jnp.int32, (count, span), 1)
+        new = (column >= offset) & (column < offset + edge)
+        for k, rows in ((0, own), (1, theirs)):
+            index = part if k == 0 else 1 - part
+            start = pl.multiple_of(index * count, count)
+            block = product(rows[...], last[...])
+            old = first[pl.ds(start, count), low : low + span]
+            sums[pl.ds(start, count), :] = jnp.where(new, block, old)
+
+    for t in range(2):
+
+        @pl.when(core == t)
+        def _():
+            for ref, c in ((keep, t), (send, 1 - t)):
+                ref[:, :share] = first[:, c * share : (c + 1) * share]
+                ref[:, share:] = first[:, heads:]
+
+    @pl.when(z == 0)
+    def _():
+        low = width - span
+        finish(down, down_over, span - edge, low)
+        for t in range(2):
+
+            @pl.when(core == t)
+            def _():
+                for ref, c in ((keep, t), (send, 1 - t)):
+                    if c == 1:
+                        ref[:, share - (heads - low) : share] = sums[:, : heads - low]
+                    ref[:, share:] = sums[:, heads - low :]
+
+    @pl.when(z == 3)
+    def _():
+        finish(up, up_over, 0, 0)
+        for t in range(2):
+
+            @pl.when(core == t)
+            def _():
+                for ref, c in ((keep, t), (send, 1 - t)):
+                    if c == 0:
+                        ref[:, :share] = sums[...]
 
 
 def paired(sent_rows, norm_gain, qkv_weight, groups):
     part = lax.axis_index("parts")
-    normed = norm(sent_rows, norm_gain)
-    theirs = lax.ppermute(normed, "parts", [(0, 1), (1, 0)])
+    group = lax.axis_index("dp")
+    at = jnp.stack([group // 2, group % 2, part, lax.axis_index("tensor")]).astype(jnp.int32)
     turned = qkv_weight.T
+    depth = turned.shape[1]
     count = turned.shape[0] // (2 * BLOCK)
+    size = count * BLOCK
     mine = lax.dynamic_index_in_dim(
-        turned.reshape(count, 2, BLOCK, turned.shape[1]), part, 1, False
-    ).reshape(count * BLOCK, turned.shape[1])
-    columns = gather_line(mine, groups)
-    own = sum_cores(product(normed, columns))
-    other = sum_cores(product(theirs, columns))
-    first = jnp.where(part == 0, own, other)
-    second = jnp.where(part == 0, other, own)
-    ready = jnp.concatenate([first, second], axis=0)
+        turned.reshape(count, 2, BLOCK, depth), part, 1, False
+    ).reshape(size, depth)
+    swap = [(0, 1), (1, 0)]
+    raw = lax.ppermute(sent_rows, "parts", swap)
+    scale = scale_of(sent_rows)
+    normed = scaled(sent_rows, scale, norm_gain)
+    theirs = scaled(raw, lax.ppermute(scale, "parts", swap), norm_gain)
+    early, late = gather_line(mine)
+    slots = sent_rows.shape[0]
+    width = groups * size
+    whole = pl.BlockSpec(memory_space=pltpu.VMEM)
+    anywhere = pl.BlockSpec(memory_space=pl.ANY)
+    scalars = pl.BlockSpec(memory_space=pltpu.SMEM)
+    first = pl.pallas_call(
+        early_kernel,
+        out_shape=jax.ShapeDtypeStruct((2 * slots, width), jnp.float32),
+        in_specs=[scalars] + [anywhere] * 10 + [whole] * 2,
+        out_specs=whole,
+        scratch_shapes=[
+            pltpu.VMEM((width, depth), jnp.bfloat16),
+            pltpu.SemaphoreType.DMA((10,)),
+        ],
+        compiler_params=pltpu.CompilerParams(vmem_limit_bytes=24 << 20),
+        cost_estimate=pl.CostEstimate(
+            flops=4 * slots * width * depth, bytes_accessed=12 << 20, transcendentals=0
+        ),
+        name="project_early",
+    )(at, *early, normed, theirs)
+    share = width * HQ // (HQ + 2) // 2 + width * 2 // (HQ + 2)
+    half = jax.ShapeDtypeStruct((2 * slots, share), jnp.float32)
+    keep, send = pl.pallas_call(
+        late_kernel,
+        out_shape=(half, half),
+        in_specs=[scalars, whole] + [anywhere] * 4 + [whole] * 2,
+        out_specs=(whole, whole),
+        scratch_shapes=[
+            pltpu.VMEM((256, depth), jnp.bfloat16),
+            pltpu.VMEM((2 * slots, 256), jnp.float32),
+            pltpu.SemaphoreType.DMA((2,)),
+        ],
+        compiler_params=pltpu.CompilerParams(vmem_limit_bytes=24 << 20),
+        cost_estimate=pl.CostEstimate(
+            flops=4 * slots * 256 * depth, bytes_accessed=8 << 20, transcendentals=0
+        ),
+        name="project_late",
+    )(at, first, *late, normed, theirs)
+    ready = (keep + lax.ppermute(send, "tensor", swap)).astype(jnp.bfloat16)
     arrived = lax.all_to_all(ready, ("parts", "dp"), 0, 0, tiled=True)
-    return arrived.reshape(2, sent_rows.shape[0], arrived.shape[1])
+    return arrived.reshape(2, slots, share)
 
 
 def single(sent_rows, norm_gain, qkv_weight):
     columns = lax.all_gather(qkv_weight.T, "dp", axis=0, tiled=True)
-    ready = sum_cores(product(norm(sent_rows, norm_gain), columns))
+    ready = sum_cores(product(scaled(sent_rows, scale_of(sent_rows), norm_gain), columns))
     return lax.all_to_all(ready, "dp", 0, 0, tiled=True)[None]
 
 
@@ -164,7 +307,7 @@
     sequence, position = positions_of(response_lengths[0], prefix_lengths[0], TOK_DEV)
     allowed = (sequence[:, None] == sequence[None, :]) & (position[None, :] <= position[:, None])
     cosine, sine = rotary(position)
-    if lax.axis_size("parts") == 2 and groups == 8 and qkv_weight.shape[1] % (2 * BLOCK) == 0:
+    if lax.axis_size("parts") == 2 and groups == 8 and qkv_weight.shape[1] == 160:
         arrived = paired(sent_rows, norm_gain, qkv_weight, groups)
     else:
         arrived = single(sent_rows, norm_gain, qkv_weight)

time: 147 us -> 130 us (0.88)
  local copies, waits for them, and re-layouts: 35.1 us -> 2.39 us
  waiting for transfers between devices: 57.5 us -> 71.2 us
  Pallas kernels: 0 us -> 9.24 us
  starting transfers between devices: 38.9 us -> 32.9 us
  matrix products: 4.84 us -> 1.19 us
  other arithmetic: 6.19 us -> 9.12 us
    dynamic_update_slice x28 -> x0, local copies, waits for them, and re-layouts: 24.1 us -> none  [the longest x14 13.9 us: gather_line(): lax.dynamic_update_slice(whole, tail[None], (2 * place + at, AHEAD, 0))]
    ppermute x11 -> x10, waiting for transfers between devices: 18.5 us -> 33 us  [the longest x1 15.7 us: paired(): theirs = scaled(raw, lax.ppermute(scale, 'parts', swap), norm_gain)]
    pallas_call x0 -> x2, Pallas kernels: none -> 9.24 us  [the longest x1 6.11 us: paired(): pl.pallas_call(early_kernel, out_shape=jax.ShapeDtypeStruct((2 * slots, w...]
    ppermute x12 -> x6, starting transfers between devices: 19.3 us -> 10.4 us  [along(): lax.ppermute(block, 'dp', [(i, i + 2 * step) for i in range(2 * low, 2 *...]
    slice x5 -> x0, local copies, waits for them, and re-layouts: 5 us -> none  [the longest x1 2.83 us: gather_line(): return whole[:2 * lines].reshape(groups * mine.shape[0], depth)]
    convert_element_type x1 -> x2, other arithmetic: 1.98 us -> 5.83 us  [the longest x1 3.88 us: scaled(): (rows.astype(jnp.float32) * scale[:, None] * norm_gain[None, :]).astype(j...]
    dot_general x2 -> x0, matrix products: 3.65 us -> none  [product(): lax.dot_general(rows, columns, (((1,), (1,)), ((), ())), preferred_elemen...]
    broadcast_in_dim x1 -> x0, local copies, waits for them, and re-layouts: 3.56 us -> none  [gather_line(): whole = jnp.zeros((2 * (lines + 1), mine.shape[0], depth), mine.dtype)]
  transfers between devices with their start and end apart: 24 -> 17, of which waited for: 10 -> 8; matrix products, arithmetic and copies ran while one was open for 26% -> 5% of each run, Pallas kernels for 0% -> 5%
where the time goes in v2:
time: 130 us
  waiting for transfers between devices  71.2 us (55%)
  starting transfers between devices  32.9 us (25%)
  Pallas kernels  9.24 us (7%)
  other arithmetic  9.12 us (7%)
  blocking collectives  2.46 us (2%)
  local copies, waits for them, and re-layouts  2.39 us (2%)
    ppermute x6, waiting for transfers between devices, along(): lax.ppermute(block, 'dp', [(i, i + 2 * step) for i in range(2 * low, 2 *...  25.9 us
    ppermute x1, waiting for transfers between devices, paired(): theirs = scaled(raw, lax.ppermute(scale, 'parts', swap), norm_gain)  15.7 us
    ppermute x7, waiting for transfers between devices, over(): lax.ppermute(block, 'dp', [(i, i ^ 1) for i in range(2 * low, 2 * high)])  15.1 us
    ppermute x7, starting transfers between devices, over(): lax.ppermute(block, 'dp', [(i, i ^ 1) for i in range(2 * low, 2 * high)])  12.8 us
    all_to_all x1, waiting for transfers between devices, paired(): arrived = lax.all_to_all(ready, ('parts', 'dp'), 0, 0, tiled=True)  12.2 us
    ppermute x6, starting transfers between devices, along(): lax.ppermute(block, 'dp', [(i, i + 2 * step) for i in range(2 * low, 2 *...  10.4 us
    pallas_call x1, Pallas kernels, paired(): pl.pallas_call(early_kernel, out_shape=jax.ShapeDtypeStruct((2 * slots, w...  6.11 us
    all_to_all x1, starting transfers between devices, paired(): arrived = lax.all_to_all(ready, ('parts', 'dp'), 0, 0, tiled=True)  5.18 us
  transfers between devices with their start and end apart: 17, of which 8 were waited for; matrix products, arithmetic and copies ran while one was open for 5% of the time, Pallas kernels for 5%

profile of v2, /device:TPU:0, one launch (start us, length us, event | category | flops | bytes accessed | tf_op | source)
XLA Modules:
  0.0 129.5 jit_solution(12224326805480999065)
XLA Ops:
  0.6 0.0 copy-start
  0.7 3.0 %collective-permute-start.9 = (bf16[256,4096]{1,0:T(8,128)(2,1)}, bf16[256,4096]{1,0:T(8,128)(2,1)}, u32[]{:S(2)}, u32[]{:S(2)}) collective-permute-start(bf16[256,4096]{1,0:T(8,128)(2,1)} %param.6), channel_id=1, source_target_pairs={{0,16},{16,0},{1,17},{17,1},{2,18},{18,2},{3,19},{19,3},{4,20},{20... | collective-permute-start | bytes 6291464 | tf_op jit(solution)/shard_map/ppermute | solution.py:248
  3.7 3.5 %collective-permute-start.1 = (bf16[80,4096]{1,0:T(8,128)(2,1)S(1)}, bf16[80,4096]{1,0:T(8,128)(2,1)S(1)}, u32[]{:S(2)}, u32[]{:S(2)}) collective-permute-start(bf16[80,4096]{1,0:T(8,128)(2,1)S(1)} %bitcast.58), channel_id=1, source_target_pairs={{0,4},{2,6},{4,8},{6,10},{8,12},{10,14},{1,5},{3,7},{5,9},{7,11},{... | collective-permute-start | bytes 1966088 | tf_op jit(solution)/shard_map/ppermute | solution.py:104
  7.3 1.3 collective-permute-start.3
  8.6 12.4 %collective-permute-done.1.refs_2_ = bf16[80,4096]{1,0:T(8,128)(2,1)S(1)} collective-permute-done((bf16[80,4096]{1,0:T(8,128)(2,1)S(1)}, bf16[80,4096]{1,0:T(8,128)(2,1)S(1)}, u32[]{:S(2)}, u32[]{:S(2)}) %collective-permute-start.1) | collective-permute-done | bytes 655392 | tf_op jit(solution)/shard_map/ppermute | solution.py:104
  20.9 1.5 %collective-permute-start.5 = (bf16[80,4096]{1,0:T(8,128)(2,1)S(1)}, bf16[80,4096]{1,0:T(8,128)(2,1)}, u32[]{:S(2)}, u32[]{:S(2)}) collective-permute-start(bf16[80,4096]{1,0:T(8,128)(2,1)S(1)} %collective-permute-done.1.refs_2_), channel_id=1, source_target_pairs={{4,8},{6,10},{8,12},{10,14},{5,9},{7,11},{9,13},{11,15},{20,24},{2... | collective-permute-start | bytes 1966088 | tf_op jit(solution)/shard_map/ppermute | solution.py:104
  22.4 2.7 %collective-permute-done.3.refs_4_ = bf16[80,4096]{1,0:T(8,128)(2,1)S(1)} collective-permute-done((bf16[80,4096]{1,0:T(8,128)(2,1)S(1)}, bf16[80,4096]{1,0:T(8,128)(2,1)S(1)}, u32[]{:S(2)}, u32[]{:S(2)}) %collective-permute-start.3) | collective-permute-done | bytes 655392 | tf_op jit(solution)/shard_map/ppermute | solution.py:104
  25.1 1.3 collective-permute-start.7
  26.4 2.1 %fusion.1 = f32[256]{0:T(256)S(1)} fusion(bf16[256,4096]{1,0:T(8,128)(2,1)} %param.6), kind=kLoop, calls=%fused_computation.3 | loop fusion | flops 3145472 | bytes 2098176 | tf_op jit(solution)/shard_map/reduce_sum | solution.py:72
  28.5 2.5 %psum.7 = f32[256]{0:T(256)S(1)} all-reduce(f32[256]{0:T(256)S(1)} %fusion.1), channel_id=1, replica_groups=mesh['parts'=2,'dp'=8,'tensor'=2] {'tensor'}, use_global_device_ids=true, to_apply=%region_3.4 | all-reduce | flops 256 | bytes 2048 | tf_op jit(solution)/shard_map/psum | solution.py:72
  30.9 1.5 %collective-permute-start.10 = (f32[256]{0:T(256)S(1)}, f32[256]{0:T(256)S(1)}, u32[]{:S(2)}, u32[]{:S(2)}) collective-permute-start(f32[256]{0:T(256)S(1)} %add_rsqrt_fusion), channel_id=1, source_target_pairs={{0,16},{16,0},{1,17},{17,1},{2,18},{18,2},{3,19},{19,3},{4,20},{20... | collective-permute-start | bytes 3080 | tf_op jit(solution)/shard_map/ppermute | solution.py:251
  32.4 1.5 %collective-permute-start = (bf16[80,4096]{1,0:T(8,128)(2,1)S(1)}, bf16[80,4096]{1,0:T(8,128)(2,1)}, u32[]{:S(2)}, u32[]{:S(2)}) collective-permute-start(bf16[80,4096]{1,0:T(8,128)(2,1)S(1)} %bitcast.60), channel_id=1, source_target_pairs={{0,2},{2,0},{4,6},{6,4},{8,10},{10,8},{12,14},{14,12},{1,3},{3,1},... | collective-permute-start | bytes 1966088 | tf_op jit(solution)/shard_map/ppermute | solution.py:100
  33.9 15.7 %collective-permute-done.10 = f32[256]{0:T(256)S(1)} collective-permute-done((f32[256]{0:T(256)S(1)}, f32[256]{0:T(256)S(1)}, u32[]{:S(2)}, u32[]{:S(2)}) %collective-permute-start.10) | collective-permute-done | bytes 1056 | tf_op jit(solution)/shard_map/ppermute | solution.py:251
  49.6 1.5 %collective-permute-start.2 = (bf16[80,4096]{1,0:T(8,128)(2,1)S(1)}, bf16[80,4096]{1,0:T(8,128)(2,1)}, u32[]{:S(2)}, u32[]{:S(2)}) collective-permute-start(bf16[80,4096]{1,0:T(8,128)(2,1)S(1)} %collective-permute-done.1.refs_2_), channel_id=1, source_target_pairs={{4,6},{6,4},{8,10},{10,8},{12,14},{14,12},{5,7},{7,5},{9,11},{11,9... | collective-permute-start | bytes 1966088 | tf_op jit(solution)/shard_map/ppermute | solution.py:100
  51.2 0.0 collective-permute-done.5.refs_6_
  51.2 1.5 %collective-permute-start.11 = (bf16[80,4096]{1,0:T(8,128)(2,1)}, bf16[80,4096]{1,0:T(8,128)(2,1)}, u32[]{:S(2)}, u32[]{:S(2)}) collective-permute-start(bf16[80,4096]{1,0:T(8,128)(2,1)} %collective-permute-done.5.refs_6_), channel_id=1, source_target_pairs={{8,12},{10,14},{9,13},{11,15},{24,28},{26,30},{25,29},{27,31}} | collective-permute-start | bytes 1966088 | tf_op jit(solution)/shard_map/ppermute | solution.py:104
  52.7 0.0 collective-permute-done.7.refs_8_
  52.7 1.3 collective-permute-start.13
  54.0 0.1 pad_add_fusion.at
  54.0 0.0 collective-permute-done.refs_1_
  54.1 3.6 %collective-permute-start.4 = (bf16[80,4096]{1,0:T(8,128)(2,1)S(1)}, bf16[80,4096]{1,0:T(8,128)(2,1)S(1)}, u32[]{:S(2)}, u32[]{:S(2)}) collective-permute-start(bf16[80,4096]{1,0:T(8,128)(2,1)S(1)} %collective-permute-done.3.refs_4_), channel_id=1, source_target_pairs={{0,2},{2,0},{4,6},{6,4},{8,10},{10,8},{1,3},{3,1},{5,7},{7,5},{9,1... | collective-permute-start | bytes 1966088 | tf_op jit(solution)/shard_map/ppermute | solution.py:100
  57.7 0.0 collective-permute-done.2.refs_3_
  57.7 0.7 collective-permute-start.6
  58.4 0.0 collective-permute-done.11.up
  58.4 2.2 %collective-permute-start.8 = (bf16[80,4096]{1,0:T(8,128)(2,1)}, bf16[80,4096]{1,0:T(8,128)(2,1)S(1)}, u32[]{:S(2)}, u32[]{:S(2)}) collective-permute-start(bf16[80,4096]{1,0:T(8,128)(2,1)} %collective-permute-done.7.refs_8_), channel_id=1, source_target_pairs={{0,2},{2,0},{4,6},{6,4},{1,3},{3,1},{5,7},{7,5},{16,18},{18,16},{2... | collective-permute-start | bytes 1966088 | tf_op jit(solution)/shard_map/ppermute | solution.py:100
  60.6 10.9 %collective-permute-done.13.down = bf16[80,4096]{1,0:T(8,128)(2,1)} collective-permute-done((bf16[80,4096]{1,0:T(8,128)(2,1)}, bf16[80,4096]{1,0:T(8,128)(2,1)}, u32[]{:S(2)}, u32[]{:S(2)}) %collective-permute-start.13) | collective-permute-done | bytes 655392 | tf_op jit(solution)/shard_map/ppermute | solution.py:104
  71.5 0.7 collective-permute-start.12
  72.2 0.0 collective-permute-done.9
  72.2 2.6 %collective-permute-start.14 = (bf16[80,4096]{1,0:T(8,128)(2,1)}, bf16[80,4096]{1,0:T(8,128)(2,1)S(1)}, u32[]{:S(2)}, u32[]{:S(2)}) collective-permute-start(bf16[80,4096]{1,0:T(8,128)(2,1)} %collective-permute-done.13.down), channel_id=1, source_target_pairs={{0,2},{2,0},{1,3},{3,1},{16,18},{18,16},{17,19},{19,17}} | collective-permute-start | bytes 1966088 | tf_op jit(solution)/shard_map/ppermute | solution.py:100
  74.8 3.9 %multiply_convert_fusion = (bf16[256,4096]{1,0:T(8,128)(2,1)S(1)}, bf16[256,4096]{1,0:T(8,128)(2,1)S(1)}) fusion(bf16[256,4096]{1,0:T(8,128)(2,1)} %collective-permute-done.9, f32[256]{0:T(256)S(1)} %collective-permute-done.10, f32[4096]{0:T(1024)S(1)} %copy-done.2, f32[256]{0:T(256)S(1)} %add_rsqrt_fusion, bf16[256,4096]{1,0:T(8,128)(2,1)} %param.6), kind=kLoop, calls=%fused_computation.6 | loop fusion | flops 8388608 | bytes 8407040 | tf_op jit(solution)/shard_map/convert_element_type | solution.py:77
  78.7 0.0 collective-permute-done.6.refs_7_
  78.7 8.9 %collective-permute-done.8.refs_9_ = bf16[80,4096]{1,0:T(8,128)(2,1)S(1)} collective-permute-done((bf16[80,4096]{1,0:T(8,128)(2,1)}, bf16[80,4096]{1,0:T(8,128)(2,1)S(1)}, u32[]{:S(2)}, u32[]{:S(2)}) %collective-permute-start.8) | collective-permute-done | bytes 655392 | tf_op jit(solution)/shard_map/ppermute | solution.py:100
  87.7 6.1 %project_early.1.first = f32[512,640]{1,0:T(8,128)S(1)} custom-call(s32[4]{0:T(128)S(1)} %pad_add_fusion.at, bf16[80,4096]{1,0:T(8,128)(2,1)S(1)} %bitcast.61, bf16[80,4096]{1,0:T(8,128)(2,1)} %collective-permute-done.refs_1_, bf16[80,4096]{1,0:T(8,128)(2,1)S(1)} %collective-permute-done.1.refs_2_, bf16[80,4096]{1,0:T(8,128)(2,1)} %collective-permute-done.2.refs_3_, ...), custom_call_target="tpu_custom_call" | custom-call | flops 2684354560 | bytes 12582912 | tf_op jit(solution)/shard_map/project_early/pallas_call | solution.py:258
  93.8 0.0 copy-start.5
  93.8 6.2 %collective-permute-done.14.down_over = bf16[80,4096]{1,0:T(8,128)(2,1)S(1)} collective-permute-done((bf16[80,4096]{1,0:T(8,128)(2,1)}, bf16[80,4096]{1,0:T(8,128)(2,1)S(1)}, u32[]{:S(2)}, u32[]{:S(2)}) %collective-permute-start.14) | collective-permute-done | bytes 655392 | tf_op jit(solution)/shard_map/ppermute | solution.py:100
  100.0 3.1 %project_late.1 = (f32[512,384]{1,0:T(8,128)S(1)}, f32[512,384]{1,0:T(8,128)S(1)}) custom-call(s32[4]{0:T(128)S(1)} %pad_add_fusion.at, f32[512,640]{1,0:T(8,128)S(1)} %project_early.1.first, bf16[80,4096]{1,0:T(8,128)(2,1)} %collective-permute-done.11.up, bf16[80,4096]{1,0:T(8,128)(2,1)S(1)} %collective-permute-done.12.up_over, ...), custom_call_target="tpu_custom_call" | custom-call | flops 1073741824 | bytes 8388608 | tf_op jit(solution)/shard_map/project_late/pallas_call | solution.py:275
  103.1 0.0 copy-start.3
  103.1 0.0 copy-start.4
  103.1 0.1 collective-permute-start.15
  103.2 0.2 reduce-window.13
  103.4 2.2 %collective-permute-done.15 = f32[512,384]{1,0:T(8,128)} collective-permute-done((f32[512,384]{1,0:T(8,128)S(1)}, f32[512,384]{1,0:T(8,128)}, u32[]{:S(2)}, u32[]{:S(2)}) %collective-permute-start.15) | collective-permute-done | bytes 786464 | tf_op jit(solution)/shard_map/ppermute | solution.py:291
  105.6 2.0 %add_convert_fusion = bf16[512,384]{1,0:T(8,128)(2,1)} fusion(f32[512,384]{1,0:T(8,128)S(1)} %get-tuple-element.5, f32[512,384]{1,0:T(8,128)} %collective-permute-done.15), kind=kLoop, calls=%fused_computation.14 | loop fusion | flops 393216 | bytes 1966080 | tf_op jit(solution)/shard_map/convert_element_type | solution.py:291
  107.5 5.2 %all-to-all-start = ((bf16[16,32,384]{2,1,0:T(8,128)(2,1)}), bf16[16,32,384]{2,1,0:T(8,128)(2,1)S(1)}, u32[]{:S(2)}, u32[]{:S(2)}) async-start(bf16[16,32,384]{2,1,0:T(8,128)(2,1)} %bitcast.9), calls=%async_computation | async-start | bytes 786432 | tf_op jit(solution)/shard_map/all_to_all | solution.py:292
  112.7 0.2 fusion.31
  113.0 0.1 reduce
  113.1 0.1 select_reduce_fusion
  113.2 0.1 select_reduce_fusion.2
  113.3 0.1 compare_and_fusion
  113.4 12.2 %all-to-all-done = bf16[16,32,384]{2,1,0:T(8,128)(2,1)S(1)} async-done(((bf16[16,32,384]{2,1,0:T(8,128)(2,1)}), bf16[16,32,384]{2,1,0:T(8,128)(2,1)S(1)}, u32[]{:S(2)}, u32[]{:S(2)}) %all-to-all-start) | async-done | bytes 393248 | tf_op jit(solution)/shard_map/all_to_all | solution.py:292
  125.6 0.2 copy.33
  125.8 0.4 convolution_bitcast_fusion
  126.2 0.1 copy.35
  126.3 0.1 copy.46
  126.4 0.1 copy.47
  126.6 0.1 copy.45
  126.7 0.3 multiply_cosine_fusion
  127.0 0.1 pad_maximum_fusion
  127.1 0.0 copy-start.1
  127.1 0.1 subtract_convert_fusion
  127.2 0.3 fusion.6
  127.5 0.3 fusion.33
  127.8 0.2 convolution_convert_fusion
  128.0 0.8 copy.41
  128.8 0.7 copy.40
  (20 shorter events, 0.2 us)
Async XLA Ops:
  0.6 3.1 %copy-start = (bf16[4096,160]{0,1:T(8,128)(2,1)S(1)}, bf16[4096,160]{0,1:T(8,128)(2,1)}, u32[]{:S(2)}) copy-start(bf16[4096,160]{0,1:T(8,128)(2,1)} %param.8) | copy-start | bytes 3932164
  0.6 74.2 %copy-start.2 = (f32[4096]{0:T(1024)S(1)}, f32[4096]{0:T(1024)}, u32[]{:S(2)}) copy-start(f32[4096]{0:T(1024)} %param.7) | copy-start | bytes 49156
  0.7 71.6 %collective-permute-start.9 = (bf16[256,4096]{1,0:T(8,128)(2,1)}, bf16[256,4096]{1,0:T(8,128)(2,1)}, u32[]{:S(2)}, u32[]{:S(2)}) collective-permute-start(bf16[256,4096]{1,0:T(8,128)(2,1)} %param.6), channel_id=1, source_target_pairs={{0,16},{16,0},{1,17},{17,1},{2,18},{18,2},{3,19},{19,3},{4,20},{20... | collective-permute-start | bytes 6291464 | tf_op jit(solution)/shard_map/ppermute | solution.py:248
  3.7 17.2 %collective-permute-start.1 = (bf16[80,4096]{1,0:T(8,128)(2,1)S(1)}, bf16[80,4096]{1,0:T(8,128)(2,1)S(1)}, u32[]{:S(2)}, u32[]{:S(2)}) collective-permute-start(bf16[80,4096]{1,0:T(8,128)(2,1)S(1)} %bitcast.58), channel_id=1, source_target_pairs={{0,4},{2,6},{4,8},{6,10},{8,12},{10,14},{1,5},{3,7},{5,9},{7,11},{... | collective-permute-start | bytes 1966088 | tf_op jit(solution)/shard_map/ppermute | solution.py:104
  7.3 17.8 %collective-permute-start.3 = (bf16[80,4096]{1,0:T(8,128)(2,1)S(1)}, bf16[80,4096]{1,0:T(8,128)(2,1)S(1)}, u32[]{:S(2)}, u32[]{:S(2)}) collective-permute-start(bf16[80,4096]{1,0:T(8,128)(2,1)S(1)} %bitcast.59), channel_id=1, source_target_pairs={{4,0},{6,2},{8,4},{10,6},{12,8},{14,10},{5,1},{7,3},{9,5},{11,7},{... | collective-permute-start | bytes 1966088 | tf_op jit(solution)/shard_map/ppermute | solution.py:104
  20.9 30.2 %collective-permute-start.5 = (bf16[80,4096]{1,0:T(8,128)(2,1)S(1)}, bf16[80,4096]{1,0:T(8,128)(2,1)}, u32[]{:S(2)}, u32[]{:S(2)}) collective-permute-start(bf16[80,4096]{1,0:T(8,128)(2,1)S(1)} %collective-permute-done.1.refs_2_), channel_id=1, source_target_pairs={{4,8},{6,10},{8,12},{10,14},{5,9},{7,11},{9,13},{11,15},{20,24},{2... | collective-permute-start | bytes 1966088 | tf_op jit(solution)/shard_map/ppermute | solution.py:104
  25.1 27.6 %collective-permute-start.7 = (bf16[80,4096]{1,0:T(8,128)(2,1)S(1)}, bf16[80,4096]{1,0:T(8,128)(2,1)}, u32[]{:S(2)}, u32[]{:S(2)}) collective-permute-start(bf16[80,4096]{1,0:T(8,128)(2,1)S(1)} %collective-permute-done.3.refs_4_), channel_id=1, source_target_pairs={{4,0},{6,2},{8,4},{10,6},{5,1},{7,3},{9,5},{11,7},{20,16},{22,18},... | collective-permute-start | bytes 1966088 | tf_op jit(solution)/shard_map/ppermute | solution.py:104
  30.9 18.7 %collective-permute-start.10 = (f32[256]{0:T(256)S(1)}, f32[256]{0:T(256)S(1)}, u32[]{:S(2)}, u32[]{:S(2)}) collective-permute-start(f32[256]{0:T(256)S(1)} %add_rsqrt_fusion), channel_id=1, source_target_pairs={{0,16},{16,0},{1,17},{17,1},{2,18},{18,2},{3,19},{19,3},{4,20},{20... | collective-permute-start | bytes 3080 | tf_op jit(solution)/shard_map/ppermute | solution.py:251
  32.4 21.6 %collective-permute-start = (bf16[80,4096]{1,0:T(8,128)(2,1)S(1)}, bf16[80,4096]{1,0:T(8,128)(2,1)}, u32[]{:S(2)}, u32[]{:S(2)}) collective-permute-start(bf16[80,4096]{1,0:T(8,128)(2,1)S(1)} %bitcast.60), channel_id=1, source_target_pairs={{0,2},{2,0},{4,6},{6,4},{8,10},{10,8},{12,14},{14,12},{1,3},{3,1},... | collective-permute-start | bytes 1966088 | tf_op jit(solution)/shard_map/ppermute | solution.py:100
  49.6 8.0 %collective-permute-start.2 = (bf16[80,4096]{1,0:T(8,128)(2,1)S(1)}, bf16[80,4096]{1,0:T(8,128)(2,1)}, u32[]{:S(2)}, u32[]{:S(2)}) collective-permute-start(bf16[80,4096]{1,0:T(8,128)(2,1)S(1)} %collective-permute-done.1.refs_2_), channel_id=1, source_target_pairs={{4,6},{6,4},{8,10},{10,8},{12,14},{14,12},{5,7},{7,5},{9,11},{11,9... | collective-permute-start | bytes 1966088 | tf_op jit(solution)/shard_map/ppermute | solution.py:100
  51.2 7.2 %collective-permute-start.11 = (bf16[80,4096]{1,0:T(8,128)(2,1)}, bf16[80,4096]{1,0:T(8,128)(2,1)}, u32[]{:S(2)}, u32[]{:S(2)}) collective-permute-start(bf16[80,4096]{1,0:T(8,128)(2,1)} %collective-permute-done.5.refs_6_), channel_id=1, source_target_pairs={{8,12},{10,14},{9,13},{11,15},{24,28},{26,30},{25,29},{27,31}} | collective-permute-start | bytes 1966088 | tf_op jit(solution)/shard_map/ppermute | solution.py:104
  52.7 18.9 %collective-permute-start.13 = (bf16[80,4096]{1,0:T(8,128)(2,1)}, bf16[80,4096]{1,0:T(8,128)(2,1)}, u32[]{:S(2)}, u32[]{:S(2)}) collective-permute-start(bf16[80,4096]{1,0:T(8,128)(2,1)} %collective-permute-done.7.refs_8_), channel_id=1, source_target_pairs={{4,0},{6,2},{5,1},{7,3},{20,16},{22,18},{21,17},{23,19}} | collective-permute-start | bytes 1966088 | tf_op jit(solution)/shard_map/ppermute | solution.py:104
  54.1 24.6 %collective-permute-start.4 = (bf16[80,4096]{1,0:T(8,128)(2,1)S(1)}, bf16[80,4096]{1,0:T(8,128)(2,1)S(1)}, u32[]{:S(2)}, u32[]{:S(2)}) collective-permute-start(bf16[80,4096]{1,0:T(8,128)(2,1)S(1)} %collective-permute-done.3.refs_4_), channel_id=1, source_target_pairs={{0,2},{2,0},{4,6},{6,4},{8,10},{10,8},{1,3},{3,1},{5,7},{7,5},{9,1... | collective-permute-start | bytes 1966088 | tf_op jit(solution)/shard_map/ppermute | solution.py:100
  57.7 21.0 %collective-permute-start.6 = (bf16[80,4096]{1,0:T(8,128)(2,1)}, bf16[80,4096]{1,0:T(8,128)(2,1)S(1)}, u32[]{:S(2)}, u32[]{:S(2)}) collective-permute-start(bf16[80,4096]{1,0:T(8,128)(2,1)} %collective-permute-done.5.refs_6_), channel_id=1, source_target_pairs={{8,10},{10,8},{12,14},{14,12},{9,11},{11,9},{13,15},{15,13},{24,26... | collective-permute-start | bytes 1966088 | tf_op jit(solution)/shard_map/ppermute | solution.py:100
  58.4 29.3 %collective-permute-start.8 = (bf16[80,4096]{1,0:T(8,128)(2,1)}, bf16[80,4096]{1,0:T(8,128)(2,1)S(1)}, u32[]{:S(2)}, u32[]{:S(2)}) collective-permute-start(bf16[80,4096]{1,0:T(8,128)(2,1)} %collective-permute-done.7.refs_8_), channel_id=1, source_target_pairs={{0,2},{2,0},{4,6},{6,4},{1,3},{3,1},{5,7},{7,5},{16,18},{18,16},{2... | collective-permute-start | bytes 1966088 | tf_op jit(solution)/shard_map/ppermute | solution.py:100
  71.5 22.3 %collective-permute-start.12 = (bf16[80,4096]{1,0:T(8,128)(2,1)}, bf16[80,4096]{1,0:T(8,128)(2,1)S(1)}, u32[]{:S(2)}, u32[]{:S(2)}) collective-permute-start(bf16[80,4096]{1,0:T(8,128)(2,1)} %collective-permute-done.11.up), channel_id=1, source_target_pairs={{12,14},{14,12},{13,15},{15,13},{28,30},{30,28},{29,31},{31,29}} | collective-permute-start | bytes 1966088 | tf_op jit(solution)/shard_map/ppermute | solution.py:100
  72.2 27.7 %collective-permute-start.14 = (bf16[80,4096]{1,0:T(8,128)(2,1)}, bf16[80,4096]{1,0:T(8,128)(2,1)S(1)}, u32[]{:S(2)}, u32[]{:S(2)}) collective-permute-start(bf16[80,4096]{1,0:T(8,128)(2,1)} %collective-permute-done.13.down), channel_id=1, source_target_pairs={{0,2},{2,0},{1,3},{3,1},{16,18},{18,16},{17,19},{19,17}} | collective-permute-start | bytes 1966088 | tf_op jit(solution)/shard_map/ppermute | solution.py:100
  93.8 9.4 %copy-start.5 = (s32[1,8]{1,0:T(1,128)S(1)}, s32[1,8]{1,0:T(1,128)}, u32[]{:S(2)}) copy-start(s32[1,8]{1,0:T(1,128)} %param.10) | copy-start | bytes 100
  103.1 9.6 %copy-start.3 = (s32[8,8]{1,0:T(8,128)S(1)}, s32[8,8]{1,0:T(8,128)}, u32[]{:S(2)}) copy-start(s32[8,8]{1,0:T(8,128)} %param.9) | copy-start | bytes 772
  103.1 10.0 %copy-start.4 = (s32[1,8]{1,0:T(1,128)S(1)}, s32[1,8]{1,0:T(1,128)}, u32[]{:S(2)}) copy-start(s32[1,8]{1,0:T(1,128)} %param.11) | copy-start | bytes 100
  103.1 2.5 %collective-permute-start.15 = (f32[512,384]{1,0:T(8,128)S(1)}, f32[512,384]{1,0:T(8,128)}, u32[]{:S(2)}, u32[]{:S(2)}) collective-permute-start(f32[512,384]{1,0:T(8,128)S(1)} %get-tuple-element.6), channel_id=1, source_target_pairs={{0,1},{1,0},{2,3},{3,2},{4,5},{5,4},{6,7},{7,6},{8,9},{9,8},{10,11... | collective-permute-start | bytes 2359304 | tf_op jit(solution)/shard_map/ppermute | solution.py:291
  107.5 18.1 %all-to-all-start = ((bf16[16,32,384]{2,1,0:T(8,128)(2,1)}), bf16[16,32,384]{2,1,0:T(8,128)(2,1)S(1)}, u32[]{:S(2)}, u32[]{:S(2)}) async-start(bf16[16,32,384]{2,1,0:T(8,128)(2,1)} %bitcast.9), calls=%async_computation | async-start | bytes 786432 | tf_op jit(solution)/shard_map/all_to_all | solution.py:292
  127.1 2.4 %copy-start.1 = (bf16[128,128]{1,0:T(8,128)(2,1)}, bf16[128,128]{1,0:T(8,128)(2,1)S(1)}, u32[]{:S(2)}) copy-start(bf16[128,128]{1,0:T(8,128)(2,1)S(1)} %pad_maximum_fusion) | copy-start | bytes 98308

commit v3 on v2

--- a/solution.py
+++ b/solution.py
@@ -1,3 +1,5 @@
+import math
+
 import jax
 import jax.numpy as jnp
 from jax import lax
@@ -105,9 +107,10 @@
 
 
 def gather_line(mine):
-    own = (mine, over(mine, 0, 4))
     up1 = along(mine, 0, 3, 1)
     down1 = along(mine, 1, 4, -1)
+    mine, side, up1, down1 = lax.optimization_barrier((mine, over(mine, 0, 4), up1, down1))
+    own = (mine, side)
     up2 = along(up1, 1, 3, 1)
     down2 = along(down1, 1, 3, -1)
     up1 = (up1, over(up1, 1, 4))
@@ -233,6 +236,72 @@
                         ref[:, :share] = sums[...]
 
 
+def sum_kernel(keep, other, out):
+    out[...] = (keep[...] + other[...]).astype(out.dtype)
+
+
+def finish_kernel(pick, arrived, cosine, sine, allowed, keys, values, out):
+    width = arrived.shape[2]
+    count = 2 * width // HD
+    chosen = pick[...]
+    planes = [
+        jnp.dot(chosen, arrived[y], preferred_element_type=jnp.float32).astype(jnp.bfloat16)
+        for y in range(2)
+    ]
+    source = lax.broadcasted_iota(jnp.int32, (HD, 2 * HD), 0)
+    target = lax.broadcasted_iota(jnp.int32, (HD, 2 * HD), 1)
+    heads = []
+    for pair in range(count // 2):
+        total = None
+        for y in range(2):
+            place = source // BLOCK * (2 * BLOCK) + y * BLOCK + source % BLOCK
+            order = (place == target).astype(jnp.float32).astype(jnp.bfloat16)
+            part = jnp.dot(
+                planes[y][:, pair * HD : (pair + 1) * HD],
+                order,
+                preferred_element_type=jnp.float32,
+            )
+            total = part if total is None else total + part
+        heads += [total[:, :HD], total[:, HD:]]
+
+    def turn(block):
+        other = pltpu.roll(block, HD // 2, 1)
+        return (block * cosine[...] + other * sine[...]).astype(jnp.bfloat16)
+
+    key = turn(heads[-2])
+    value = heads[-1].astype(jnp.bfloat16)
+    keys[...] = key
+    values[...] = value
+    mask = allowed[...] > 0
+    for h in range(count - 2):
+        scores = product(turn(heads[h]), key) / math.sqrt(HD)
+        scores = jnp.where(mask, scores, jnp.float32(-1e30))
+        expo = jnp.exp(scores - jnp.max(scores, axis=-1, keepdims=True))
+        weights = (expo / jnp.sum(expo, axis=-1, keepdims=True)).astype(jnp.bfloat16)
+        out[:, h * HD : (h + 1) * HD] = jnp.dot(
+            weights, value, preferred_element_type=jnp.float32
+        ).astype(out.dtype)
+
+
+def finish(pick, arrived, cosine, sine, allowed):
+    whole = pl.BlockSpec(memory_space=pltpu.VMEM)
+    heads = 2 * arrived.shape[2] // HD - 2
+    single = jax.ShapeDtypeStruct((TOK_DEV, HD), jnp.bfloat16)
+    return pl.pallas_call(
+        finish_kernel,
+        out_shape=(single, single, jax.ShapeDtypeStruct((TOK_DEV, heads * HD), jnp.bfloat16)),
+        in_specs=[whole] * 5,
+        out_specs=(whole,) * 3,
+        name="attend",
+    )(
+        pick,
+        arrived,
+        jnp.concatenate([cosine, cosine], axis=1),
+        jnp.concatenate([-sine, sine], axis=1),
+        allowed.astype(jnp.float32),
+    )
+
+
 def paired(sent_rows, norm_gain, qkv_weight, groups):
     part = lax.axis_index("parts")
     group = lax.axis_index("dp")
@@ -245,10 +314,8 @@
         turned.reshape(count, 2, BLOCK, depth), part, 1, False
     ).reshape(size, depth)
     swap = [(0, 1), (1, 0)]
-    raw = lax.ppermute(sent_rows, "parts", swap)
-    scale = scale_of(sent_rows)
-    normed = scaled(sent_rows, scale, norm_gain)
-    theirs = scaled(raw, lax.ppermute(scale, "parts", swap), norm_gain)
+    normed = scaled(sent_rows, scale_of(sent_rows), norm_gain)
+    theirs = lax.ppermute(normed, "parts", swap)
     early, late = gather_line(mine)
     slots = sent_rows.shape[0]
     width = groups * size
@@ -288,7 +355,13 @@
         ),
         name="project_late",
     )(at, first, *late, normed, theirs)
-    ready = (keep + lax.ppermute(send, "tensor", swap)).astype(jnp.bfloat16)
+    ready = pl.pallas_call(
+        sum_kernel,
+        out_shape=jax.ShapeDtypeStruct(keep.shape, jnp.bfloat16),
+        in_specs=[whole, whole],
+        out_specs=whole,
+        name="sum_halves",
+    )(keep, lax.ppermute(send, "tensor", swap))
     arrived = lax.all_to_all(ready, ("parts", "dp"), 0, 0, tiled=True)
     return arrived.reshape(2, slots, share)
 
@@ -296,7 +369,7 @@
 def single(sent_rows, norm_gain, qkv_weight):
     columns = lax.all_gather(qkv_weight.T, "dp", axis=0, tiled=True)
     ready = sum_cores(product(scaled(sent_rows, scale_of(sent_rows), norm_gain), columns))
-    return lax.all_to_all(ready, "dp", 0, 0, tiled=True)[None]
+    return lax.all_to_all(ready, "dp", 0, 0, tiled=True)
 
 
 def per_device(sent_rows, norm_gain, qkv_weight, route_counts, response_lengths, prefix_lengths):
@@ -309,13 +382,10 @@
     cosine, sine = rotary(position)
     if lax.axis_size("parts") == 2 and groups == 8 and qkv_weight.shape[1] == 160:
         arrived = paired(sent_rows, norm_gain, qkv_weight, groups)
-    else:
-        arrived = single(sent_rows, norm_gain, qkv_weight)
-    planes, _, width = arrived.shape
-    heads = width * planes // HD
-    packed = jnp.einsum("qs,psc->qpc", pick, arrived, preferred_element_type=jnp.float32)
-    if planes == 2:
-        packed = packed.reshape(TOK_DEV, 2, width // BLOCK, BLOCK).transpose(0, 2, 1, 3)
+        return finish(pick, arrived, cosine, sine, allowed)
+    arrived = single(sent_rows, norm_gain, qkv_weight)
+    heads = arrived.shape[1] // HD
+    packed = jnp.dot(pick, arrived, preferred_element_type=jnp.float32)
     packed = packed.reshape(TOK_DEV, heads, HD)
     queries = rotate(packed[:, :-2], cosine, sine).astype(jnp.bfloat16)
     new_keys = rotate(packed[:, -2], cosine, sine).astype(jnp.bfloat16)

time: 130 us -> 121 us (0.931)
  waiting for transfers between devices: 71.2 us -> 47.4 us
  Pallas kernels: 9.24 us -> 17.2 us
  local copies, waits for them, and re-layouts: 2.39 us -> 8.78 us
  starting transfers between devices: 32.9 us -> 35.7 us
  other arithmetic: 9.12 us -> 7.41 us
    ppermute x3 -> x2, waiting for transfers between devices: 17.9 us -> 1.66 us  [the longest x1 1.66 us: paired(): lax.ppermute(send, 'tensor', swap)]
    ppermute x7, waiting for transfers between devices: 15.1 us -> 7.39 us  [over(): lax.ppermute(block, 'dp', [(i, i ^ 1) for i in range(2 * low, 2 * high)])]
    unnamed x17 -> x24, local copies, waits for them, and re-layouts: 1.88 us -> 7.69 us
    pallas_call x0 -> x2, Pallas kernels: none -> 5.54 us  [the longest x1 3.34 us: finish(): pl.pallas_call(finish_kernel, out_shape=(single, single, jax.ShapeDtypeSt...]
    all_to_all x1, starting transfers between devices: 5.18 us -> 8.9 us  [paired(): arrived = lax.all_to_all(ready, ('parts', 'dp'), 0, 0, tiled=True)]
    ppermute x3 -> x2, starting transfers between devices: 4.62 us -> 1.59 us  [the longest x1 1.58 us: paired(): theirs = lax.ppermute(normed, 'parts', swap)]
    ppermute x6, waiting for transfers between devices: 25.9 us -> 27.9 us  [along(): lax.ppermute(block, 'dp', [(i, i + 2 * step) for i in range(2 * low, 2 *...]
    all_to_all x1, waiting for transfers between devices: 12.2 us -> 10.5 us  [paired(): arrived = lax.all_to_all(ready, ('parts', 'dp'), 0, 0, tiled=True)]
  transfers between devices with their start and end apart: 17 -> 16, of which waited for: 8 -> 9; matrix products, arithmetic and copies ran while one was open for 5% -> 6% of each run, Pallas kernels for 5% -> 6%
where the time goes in v3:
time: 121 us; the launch traced here: 120 us
  waiting for transfers between devices  47.4 us (39%)
  starting transfers between devices  35.7 us (30%)
  Pallas kernels  17.2 us (14%)
  local copies, waits for them, and re-layouts  8.78 us (7%)
  other arithmetic  7.41 us (6%)
  blocking collectives  2.46 us (2%)
    ppermute x6, waiting for transfers between devices, along(): lax.ppermute(block, 'dp', [(i, i + 2 * step) for i in range(2 * low, 2 *...  27.9 us
    ppermute x7, starting transfers between devices, over(): lax.ppermute(block, 'dp', [(i, i ^ 1) for i in range(2 * low, 2 * high)])  14 us
    ppermute x6, starting transfers between devices, along(): lax.ppermute(block, 'dp', [(i, i + 2 * step) for i in range(2 * low, 2 *...  11.2 us
    all_to_all x1, waiting for transfers between devices, paired(): arrived = lax.all_to_all(ready, ('parts', 'dp'), 0, 0, tiled=True)  10.5 us
    all_to_all x1, starting transfers between devices, paired(): arrived = lax.all_to_all(ready, ('parts', 'dp'), 0, 0, tiled=True)  8.9 us
    unnamed x24, local copies, waits for them, and re-layouts  7.69 us
    ppermute x7, waiting for transfers between devices, over(): lax.ppermute(block, 'dp', [(i, i ^ 1) for i in range(2 * low, 2 * high)])  7.39 us
    pallas_call x1, Pallas kernels, paired(): pl.pallas_call(early_kernel, out_shape=jax.ShapeDtypeStruct((2 * slots, w...  7.32 us
  transfers between devices with their start and end apart: 16, of which 9 were waited for; matrix products, arithmetic and copies ran while one was open for 6% of the time, Pallas kernels for 6%

profile of v3, /device:TPU:0, one launch (start us, length us, event | category | flops | bytes accessed | tf_op | source)
XLA Modules:
  0.0 119.9 jit_solution(9996505663628799800)
XLA Ops:
  0.6 0.0 copy-start
  0.6 0.0 copy-start.8
  0.7 1.3 %copy-done = bf16[4096,160]{0,1:T(8,128)(2,1)S(1)} copy-done((bf16[4096,160]{0,1:T(8,128)(2,1)S(1)}, bf16[4096,160]{0,1:T(8,128)(2,1)}, u32[]{:S(2)}) %copy-start) | copy-done | bytes 1310744
  2.0 0.9 constant_dynamic-slice_fusion
  2.9 2.9 %collective-permute-start = (bf16[80,4096]{1,0:T(8,128)(2,1)}, bf16[80,4096]{1,0:T(8,128)(2,1)}, u32[]{:S(2)}, u32[]{:S(2)}) collective-permute-start(bf16[80,4096]{1,0:T(8,128)(2,1)} %bitcast.6.refs_0_), channel_id=1, source_target_pairs={{0,2},{2,0},{4,6},{6,4},{8,10},{10,8},{12,14},{14,12},{1,3},{3,1},... | collective-permute-start | bytes 1966088 | tf_op jit(solution)/shard_map/ppermute | solution.py:102
  5.8 4.3 %collective-permute-start.1 = (bf16[80,4096]{1,0:T(8,128)(2,1)}, bf16[80,4096]{1,0:T(8,128)(2,1)}, u32[]{:S(2)}, u32[]{:S(2)}) collective-permute-start(bf16[80,4096]{1,0:T(8,128)(2,1)} %bitcast.6.refs_0_), channel_id=1, source_target_pairs={{0,4},{2,6},{4,8},{6,10},{8,12},{10,14},{1,5},{3,7},{5,9},{7,11},{... | collective-permute-start | bytes 1966088 | tf_op jit(solution)/shard_map/ppermute | solution.py:106
  10.1 1.3 %collective-permute-start.2 = (bf16[80,4096]{1,0:T(8,128)(2,1)}, bf16[80,4096]{1,0:T(8,128)(2,1)}, u32[]{:S(2)}, u32[]{:S(2)}) collective-permute-start(bf16[80,4096]{1,0:T(8,128)(2,1)} %bitcast.6.refs_0_), channel_id=1, source_target_pairs={{4,0},{6,2},{8,4},{10,6},{12,8},{14,10},{5,1},{7,3},{9,5},{11,7},{... | collective-permute-start | bytes 1966088 | tf_op jit(solution)/shard_map/ppermute | solution.py:106
  11.4 2.1 %fusion = f32[256]{0:T(256)S(1)} fusion(bf16[256,4096]{1,0:T(8,128)(2,1)} %param.6), kind=kLoop, calls=%fused_computation.2 | loop fusion | flops 3145472 | bytes 2098176 | tf_op jit(solution)/shard_map/reduce_sum | solution.py:74
  13.5 2.5 %psum.7 = f32[256]{0:T(256)S(1)} all-reduce(f32[256]{0:T(256)S(1)} %fusion), channel_id=1, replica_groups=mesh['parts'=2,'dp'=8,'tensor'=2] {'tensor'}, use_global_device_ids=true, to_apply=%region_3.4 | all-reduce | flops 256 | bytes 2048 | tf_op jit(solution)/shard_map/psum | solution.py:74
  16.0 2.2 %fusion.2.refs_10_.own = bf16[256,4096]{1,0:T(8,128)(2,1)S(1)} fusion(bf16[256,4096]{1,0:T(8,128)(2,1)} %param.6, f32[4096]{0:T(1024)S(1)} %copy-done.8, f32[256]{0:T(256)S(1)} %add_rsqrt_fusion), kind=kLoop, calls=%fused_computation.4 | loop fusion | flops 4194304 | bytes 4211712 | tf_op jit(solution)/shard_map/convert_element_type | solution.py:79
  18.2 1.6 %collective-permute-start.9 = (bf16[256,4096]{1,0:T(8,128)(2,1)S(1)}, bf16[256,4096]{1,0:T(8,128)(2,1)}, u32[]{:S(2)}, u32[]{:S(2)}) collective-permute-start(bf16[256,4096]{1,0:T(8,128)(2,1)S(1)} %fusion.2.refs_10_.own), channel_id=1, source_target_pairs={{0,16},{16,0},{1,17},{17,1},{2,18},{18,2},{3,19},{19,3},{4,20},{20... | collective-permute-start | bytes 6291464 | tf_op jit(solution)/shard_map/ppermute | solution.py:318
  19.8 1.0 collective-permute-done.refs_1_
  20.8 2.4 %collective-permute-done.1.refs_2_ = bf16[80,4096]{1,0:T(8,128)(2,1)} collective-permute-done((bf16[80,4096]{1,0:T(8,128)(2,1)}, bf16[80,4096]{1,0:T(8,128)(2,1)}, u32[]{:S(2)}, u32[]{:S(2)}) %collective-permute-start.1) | collective-permute-done | bytes 655392 | tf_op jit(solution)/shard_map/ppermute | solution.py:106
  23.3 5.0 %collective-permute-done.2.refs_4_ = bf16[80,4096]{1,0:T(8,128)(2,1)} collective-permute-done((bf16[80,4096]{1,0:T(8,128)(2,1)}, bf16[80,4096]{1,0:T(8,128)(2,1)}, u32[]{:S(2)}, u32[]{:S(2)}) %collective-permute-start.2) | collective-permute-done | bytes 655392 | tf_op jit(solution)/shard_map/ppermute | solution.py:106
  28.2 1.5 %collective-permute-start.5 = (bf16[80,4096]{1,0:T(8,128)(2,1)}, bf16[80,4096]{1,0:T(8,128)(2,1)}, u32[]{:S(2)}, u32[]{:S(2)}) collective-permute-start(bf16[80,4096]{1,0:T(8,128)(2,1)} %collective-permute-done.1.refs_2_), channel_id=1, source_target_pairs={{4,8},{6,10},{8,12},{10,14},{5,9},{7,11},{9,13},{11,15},{20,24},{2... | collective-permute-start | bytes 1966088 | tf_op jit(solution)/shard_map/ppermute | solution.py:106
  29.7 1.3 %collective-permute-start.7 = (bf16[80,4096]{1,0:T(8,128)(2,1)}, bf16[80,4096]{1,0:T(8,128)(2,1)}, u32[]{:S(2)}, u32[]{:S(2)}) collective-permute-start(bf16[80,4096]{1,0:T(8,128)(2,1)} %collective-permute-done.2.refs_4_), channel_id=1, source_target_pairs={{4,0},{6,2},{8,4},{10,6},{5,1},{7,3},{9,5},{11,7},{20,16},{22,18},... | collective-permute-start | bytes 1966088 | tf_op jit(solution)/shard_map/ppermute | solution.py:106
  31.0 0.7 collective-permute-start.3
  31.7 2.4 %collective-permute-start.4 = (bf16[80,4096]{1,0:T(8,128)(2,1)}, bf16[80,4096]{1,0:T(8,128)(2,1)S(1)}, u32[]{:S(2)}, u32[]{:S(2)}) collective-permute-start(bf16[80,4096]{1,0:T(8,128)(2,1)} %collective-permute-done.2.refs_4_), channel_id=1, source_target_pairs={{0,2},{2,0},{4,6},{6,4},{8,10},{10,8},{1,3},{3,1},{5,7},{7,5},{9,1... | collective-permute-start | bytes 1966088 | tf_op jit(solution)/shard_map/ppermute | solution.py:102
  34.2 0.0 collective-permute-done.5.refs_6_
  34.2 1.5 %collective-permute-start.10 = (bf16[80,4096]{1,0:T(8,128)(2,1)}, bf16[80,4096]{1,0:T(8,128)(2,1)}, u32[]{:S(2)}, u32[]{:S(2)}) collective-permute-start(bf16[80,4096]{1,0:T(8,128)(2,1)} %collective-permute-done.5.refs_6_), channel_id=1, source_target_pairs={{8,12},{10,14},{9,13},{11,15},{24,28},{26,30},{25,29},{27,31}} | collective-permute-start | bytes 1966088 | tf_op jit(solution)/shard_map/ppermute | solution.py:106
  35.7 12.8 %collective-permute-done.7.refs_8_ = bf16[80,4096]{1,0:T(8,128)(2,1)} collective-permute-done((bf16[80,4096]{1,0:T(8,128)(2,1)}, bf16[80,4096]{1,0:T(8,128)(2,1)}, u32[]{:S(2)}, u32[]{:S(2)}) %collective-permute-start.7) | collective-permute-done | bytes 655392 | tf_op jit(solution)/shard_map/ppermute | solution.py:106
  48.5 1.3 %collective-permute-start.12 = (bf16[80,4096]{1,0:T(8,128)(2,1)}, bf16[80,4096]{1,0:T(8,128)(2,1)}, u32[]{:S(2)}, u32[]{:S(2)}) collective-permute-start(bf16[80,4096]{1,0:T(8,128)(2,1)} %collective-permute-done.7.refs_8_), channel_id=1, source_target_pairs={{4,0},{6,2},{5,1},{7,3},{20,16},{22,18},{21,17},{23,19}} | collective-permute-start | bytes 1966088 | tf_op jit(solution)/shard_map/ppermute | solution.py:106
  49.8 0.0 collective-permute-done.3.refs_3_
  49.8 0.8 copy-done.2
  50.6 1.6 %collective-permute-start.6 = (bf16[80,4096]{1,0:T(8,128)(2,1)}, bf16[80,4096]{1,0:T(8,128)(2,1)}, u32[]{:S(2)}, u32[]{:S(2)}) collective-permute-start(bf16[80,4096]{1,0:T(8,128)(2,1)} %collective-permute-done.5.refs_6_), channel_id=1, source_target_pairs={{8,10},{10,8},{12,14},{14,12},{9,11},{11,9},{13,15},{15,13},{24,26... | collective-permute-start | bytes 1966088 | tf_op jit(solution)/shard_map/ppermute | solution.py:102
  52.2 0.0 collective-permute-done.4.refs_5_
  52.2 0.8 copy-done.4
  53.0 2.4 %collective-permute-start.8 = (bf16[80,4096]{1,0:T(8,128)(2,1)}, bf16[80,4096]{1,0:T(8,128)(2,1)}, u32[]{:S(2)}, u32[]{:S(2)}) collective-permute-start(bf16[80,4096]{1,0:T(8,128)(2,1)} %collective-permute-done.7.refs_8_), channel_id=1, source_target_pairs={{0,2},{2,0},{4,6},{6,4},{1,3},{3,1},{5,7},{7,5},{16,18},{18,16},{2... | collective-permute-start | bytes 1966088 | tf_op jit(solution)/shard_map/ppermute | solution.py:102
  55.5 0.0 collective-permute-done.10.up
  55.5 1.5 %collective-permute-start.11 = (bf16[80,4096]{1,0:T(8,128)(2,1)}, bf16[80,4096]{1,0:T(8,128)(2,1)}, u32[]{:S(2)}, u32[]{:S(2)}) collective-permute-start(bf16[80,4096]{1,0:T(8,128)(2,1)} %collective-permute-done.10.up), channel_id=1, source_target_pairs={{12,14},{14,12},{13,15},{15,13},{28,30},{30,28},{29,31},{31,29}} | collective-permute-start | bytes 1966088 | tf_op jit(solution)/shard_map/ppermute | solution.py:102
  57.0 7.7 %collective-permute-done.12.down = bf16[80,4096]{1,0:T(8,128)(2,1)} collective-permute-done((bf16[80,4096]{1,0:T(8,128)(2,1)}, bf16[80,4096]{1,0:T(8,128)(2,1)}, u32[]{:S(2)}, u32[]{:S(2)}) %collective-permute-start.12) | collective-permute-done | bytes 655392 | tf_op jit(solution)/shard_map/ppermute | solution.py:106
  64.7 2.4 %collective-permute-start.13 = (bf16[80,4096]{1,0:T(8,128)(2,1)}, bf16[80,4096]{1,0:T(8,128)(2,1)}, u32[]{:S(2)}, u32[]{:S(2)}) collective-permute-start(bf16[80,4096]{1,0:T(8,128)(2,1)} %collective-permute-done.12.down), channel_id=1, source_target_pairs={{0,2},{2,0},{1,3},{3,1},{16,18},{18,16},{17,19},{19,17}} | collective-permute-start | bytes 1966088 | tf_op jit(solution)/shard_map/ppermute | solution.py:102
  67.2 0.0 copy-done.11
  67.2 0.2 reduce-window.13
  67.4 0.1 pad_add_fusion.at
  67.5 0.0 collective-permute-done.6.refs_7_
  67.5 5.1 %collective-permute-done.8.refs_9_ = bf16[80,4096]{1,0:T(8,128)(2,1)} collective-permute-done((bf16[80,4096]{1,0:T(8,128)(2,1)}, bf16[80,4096]{1,0:T(8,128)(2,1)}, u32[]{:S(2)}, u32[]{:S(2)}) %collective-permute-start.8) | collective-permute-done | bytes 655392 | tf_op jit(solution)/shard_map/ppermute | solution.py:102
  72.5 0.0 collective-permute-done.9.refs_11_.theirs
  72.5 1.1 copy-done.3
  73.6 1.1 copy-done.5
  74.7 7.3 %project_early.1.first = f32[512,640]{1,0:T(8,128)S(1)} custom-call(s32[4]{0:T(128)S(1)} %pad_add_fusion.at, bf16[80,4096]{1,0:T(8,128)(2,1)} %bitcast.6.refs_0_, bf16[80,4096]{1,0:T(8,128)(2,1)} %collective-permute-done.refs_1_, bf16[80,4096]{1,0:T(8,128)(2,1)} %collective-permute-done.1.refs_2_, bf16[80,4096]{1,0:T(8,128)(2,1)S(1)} %copy-done.3, ...), custom_call_target="tpu_custom_call" | custom-call | flops 2684354560 | bytes 12582912 | tf_op jit(solution)/shard_map/project_early/pallas_call | solution.py:325
  82.0 0.0 copy-start.10
  82.0 0.0 copy-start.9
  82.1 0.0 collective-permute-done.11.up_over
  82.1 1.3 %collective-permute-done.13.down_over = bf16[80,4096]{1,0:T(8,128)(2,1)} collective-permute-done((bf16[80,4096]{1,0:T(8,128)(2,1)}, bf16[80,4096]{1,0:T(8,128)(2,1)}, u32[]{:S(2)}, u32[]{:S(2)}) %collective-permute-start.13) | collective-permute-done | bytes 655392 | tf_op jit(solution)/shard_map/ppermute | solution.py:102
  83.4 4.4 %project_late.1 = (f32[512,384]{1,0:T(8,128)S(1)}, f32[512,384]{1,0:T(8,128)S(1)}) custom-call(s32[4]{0:T(128)S(1)} %pad_add_fusion.at, f32[512,640]{1,0:T(8,128)S(1)} %project_early.1.first, bf16[80,4096]{1,0:T(8,128)(2,1)} %collective-permute-done.10.up, bf16[80,4096]{1,0:T(8,128)(2,1)} %collective-permute-done.11.up_over, ...), custom_call_target="tpu_custom_call" | custom-call | flops 1073741824 | bytes 8388608 | tf_op jit(solution)/shard_map/project_late/pallas_call | solution.py:342
  87.7 0.0 copy-start.1
  87.8 0.9 copy-done.1
  88.6 0.0 collective-permute-start.14
  88.6 0.1 select_reduce_fusion
  88.7 0.2 fusion.8
  88.9 0.3 fusion.4
  89.2 1.7 %collective-permute-done.14.other = f32[512,384]{1,0:T(8,128)S(1)} collective-permute-done((f32[512,384]{1,0:T(8,128)S(1)}, f32[512,384]{1,0:T(8,128)S(1)}, u32[]{:S(2)}, u32[]{:S(2)}) %collective-permute-start.14) | collective-permute-done | bytes 786464 | tf_op jit(solution)/shard_map/ppermute | solution.py:364
  90.9 0.9 copy-done.7
  91.8 2.2 %sum_halves.1 = bf16[512,384]{1,0:T(8,128)(2,1)} custom-call(f32[512,384]{1,0:T(8,128)} %copy-done.1, f32[512,384]{1,0:T(8,128)} %copy-done.7), custom_call_target="tpu_custom_call" | custom-call | tf_op jit(solution)/shard_map/sum_halves/pallas_call | solution.py:358
  94.0 8.9 %all-to-all-start = ((bf16[16,32,384]{2,1,0:T(8,128)(2,1)}), bf16[16,32,384]{2,1,0:T(8,128)(2,1)S(1)}, u32[]{:S(2)}, u32[]{:S(2)}) async-start(bf16[16,32,384]{2,1,0:T(8,128)(2,1)} %bitcast.23), calls=%async_computation | async-start | bytes 786432 | tf_op jit(solution)/shard_map/all_to_all | solution.py:365
  103.0 0.1 reduce
  103.1 0.7 pad_maximum_fusion
  103.8 0.1 select_reduce_fusion.2
  103.9 0.7 fusion.3.pick
  104.6 0.7 and_convert_fusion.allowed
  105.3 10.5 %all-to-all-done = bf16[16,32,384]{2,1,0:T(8,128)(2,1)S(1)} async-done(((bf16[16,32,384]{2,1,0:T(8,128)(2,1)}), bf16[16,32,384]{2,1,0:T(8,128)(2,1)S(1)}, u32[]{:S(2)}, u32[]{:S(2)}) %all-to-all-start) | async-done | bytes 393248 | tf_op jit(solution)/shard_map/all_to_all | solution.py:365
  115.8 0.7 copy-done.6
  116.6 3.3 %attend.1 = (bf16[128,128]{1,0:T(8,128)(2,1)}, bf16[128,128]{1,0:T(8,128)(2,1)}, bf16[128,512]{1,0:T(8,128)(2,1)}) custom-call(bf16[128,256]{1,0:T(8,128)(2,1)} %fusion.3.pick, bf16[2,256,384]{2,1,0:T(8,128)(2,1)} %bitcast.22, f32[128,128]{1,0:T(8,128)} %get-tuple-element.22.cosine, f32[128,128]{1,0:T(8,128)} %get-tuple-element.23.sine, ...), custom_call_target="tpu_custom_call" | custom-call | tf_op jit(solution)/shard_map/attend/pallas_call | solution.py:290
  (17 shorter events, 0.1 us)
Async XLA Ops:
  0.6 1.3 %copy-start = (bf16[4096,160]{0,1:T(8,128)(2,1)S(1)}, bf16[4096,160]{0,1:T(8,128)(2,1)}, u32[]{:S(2)}) copy-start(bf16[4096,160]{0,1:T(8,128)(2,1)} %param.8) | copy-start | bytes 3932164
  0.6 15.3 %copy-start.8 = (f32[4096]{0:T(1024)S(1)}, f32[4096]{0:T(1024)}, u32[]{:S(2)}) copy-start(f32[4096]{0:T(1024)} %param.7) | copy-start | bytes 49156
  2.9 18.0 %collective-permute-start = (bf16[80,4096]{1,0:T(8,128)(2,1)}, bf16[80,4096]{1,0:T(8,128)(2,1)}, u32[]{:S(2)}, u32[]{:S(2)}) collective-permute-start(bf16[80,4096]{1,0:T(8,128)(2,1)} %bitcast.6.refs_0_), channel_id=1, source_target_pairs={{0,2},{2,0},{4,6},{6,4},{8,10},{10,8},{12,14},{14,12},{1,3},{3,1},... | collective-permute-start | bytes 1966088 | tf_op jit(solution)/shard_map/ppermute | solution.py:102
  5.8 17.5 %collective-permute-start.1 = (bf16[80,4096]{1,0:T(8,128)(2,1)}, bf16[80,4096]{1,0:T(8,128)(2,1)}, u32[]{:S(2)}, u32[]{:S(2)}) collective-permute-start(bf16[80,4096]{1,0:T(8,128)(2,1)} %bitcast.6.refs_0_), channel_id=1, source_target_pairs={{0,4},{2,6},{4,8},{6,10},{8,12},{10,14},{1,5},{3,7},{5,9},{7,11},{... | collective-permute-start | bytes 1966088 | tf_op jit(solution)/shard_map/ppermute | solution.py:106
  10.1 18.1 %collective-permute-start.2 = (bf16[80,4096]{1,0:T(8,128)(2,1)}, bf16[80,4096]{1,0:T(8,128)(2,1)}, u32[]{:S(2)}, u32[]{:S(2)}) collective-permute-start(bf16[80,4096]{1,0:T(8,128)(2,1)} %bitcast.6.refs_0_), channel_id=1, source_target_pairs={{4,0},{6,2},{8,4},{10,6},{12,8},{14,10},{5,1},{7,3},{9,5},{11,7},{... | collective-permute-start | bytes 1966088 | tf_op jit(solution)/shard_map/ppermute | solution.py:106
  16.0 51.2 %copy-start.11 = (s32[1,8]{1,0:T(1,128)S(1)}, s32[1,8]{1,0:T(1,128)}, u32[]{:S(2)}) copy-start(s32[1,8]{1,0:T(1,128)} %param.10) | copy-start | bytes 100
  18.2 54.3 %collective-permute-start.9 = (bf16[256,4096]{1,0:T(8,128)(2,1)S(1)}, bf16[256,4096]{1,0:T(8,128)(2,1)}, u32[]{:S(2)}, u32[]{:S(2)}) collective-permute-start(bf16[256,4096]{1,0:T(8,128)(2,1)S(1)} %fusion.2.refs_10_.own), channel_id=1, source_target_pairs={{0,16},{16,0},{1,17},{17,1},{2,18},{18,2},{3,19},{19,3},{4,20},{20... | collective-permute-start | bytes 6291464 | tf_op jit(solution)/shard_map/ppermute | solution.py:318
  28.2 6.0 %collective-permute-start.5 = (bf16[80,4096]{1,0:T(8,128)(2,1)}, bf16[80,4096]{1,0:T(8,128)(2,1)}, u32[]{:S(2)}, u32[]{:S(2)}) collective-permute-start(bf16[80,4096]{1,0:T(8,128)(2,1)} %collective-permute-done.1.refs_2_), channel_id=1, source_target_pairs={{4,8},{6,10},{8,12},{10,14},{5,9},{7,11},{9,13},{11,15},{20,24},{2... | collective-permute-start | bytes 1966088 | tf_op jit(solution)/shard_map/ppermute | solution.py:106
  29.7 18.7 %collective-permute-start.7 = (bf16[80,4096]{1,0:T(8,128)(2,1)}, bf16[80,4096]{1,0:T(8,128)(2,1)}, u32[]{:S(2)}, u32[]{:S(2)}) collective-permute-start(bf16[80,4096]{1,0:T(8,128)(2,1)} %collective-permute-done.2.refs_4_), channel_id=1, source_target_pairs={{4,0},{6,2},{8,4},{10,6},{5,1},{7,3},{9,5},{11,7},{20,16},{22,18},... | collective-permute-start | bytes 1966088 | tf_op jit(solution)/shard_map/ppermute | solution.py:106
  31.0 18.7 %collective-permute-start.3 = (bf16[80,4096]{1,0:T(8,128)(2,1)}, bf16[80,4096]{1,0:T(8,128)(2,1)S(1)}, u32[]{:S(2)}, u32[]{:S(2)}) collective-permute-start(bf16[80,4096]{1,0:T(8,128)(2,1)} %collective-permute-done.1.refs_2_), channel_id=1, source_target_pairs={{4,6},{6,4},{8,10},{10,8},{12,14},{14,12},{5,7},{7,5},{9,11},{11,9... | collective-permute-start | bytes 1966088 | tf_op jit(solution)/shard_map/ppermute | solution.py:102
  31.7 20.5 %collective-permute-start.4 = (bf16[80,4096]{1,0:T(8,128)(2,1)}, bf16[80,4096]{1,0:T(8,128)(2,1)S(1)}, u32[]{:S(2)}, u32[]{:S(2)}) collective-permute-start(bf16[80,4096]{1,0:T(8,128)(2,1)} %collective-permute-done.2.refs_4_), channel_id=1, source_target_pairs={{0,2},{2,0},{4,6},{6,4},{8,10},{10,8},{1,3},{3,1},{5,7},{7,5},{9,1... | collective-permute-start | bytes 1966088 | tf_op jit(solution)/shard_map/ppermute | solution.py:102
  34.2 21.3 %collective-permute-start.10 = (bf16[80,4096]{1,0:T(8,128)(2,1)}, bf16[80,4096]{1,0:T(8,128)(2,1)}, u32[]{:S(2)}, u32[]{:S(2)}) collective-permute-start(bf16[80,4096]{1,0:T(8,128)(2,1)} %collective-permute-done.5.refs_6_), channel_id=1, source_target_pairs={{8,12},{10,14},{9,13},{11,15},{24,28},{26,30},{25,29},{27,31}} | collective-permute-start | bytes 1966088 | tf_op jit(solution)/shard_map/ppermute | solution.py:106
  48.5 16.3 %collective-permute-start.12 = (bf16[80,4096]{1,0:T(8,128)(2,1)}, bf16[80,4096]{1,0:T(8,128)(2,1)}, u32[]{:S(2)}, u32[]{:S(2)}) collective-permute-start(bf16[80,4096]{1,0:T(8,128)(2,1)} %collective-permute-done.7.refs_8_), channel_id=1, source_target_pairs={{4,0},{6,2},{5,1},{7,3},{20,16},{22,18},{21,17},{23,19}} | collective-permute-start | bytes 1966088 | tf_op jit(solution)/shard_map/ppermute | solution.py:106
  49.8 0.9 copy-start.2
  50.6 16.8 %collective-permute-start.6 = (bf16[80,4096]{1,0:T(8,128)(2,1)}, bf16[80,4096]{1,0:T(8,128)(2,1)}, u32[]{:S(2)}, u32[]{:S(2)}) collective-permute-start(bf16[80,4096]{1,0:T(8,128)(2,1)} %collective-permute-done.5.refs_6_), channel_id=1, source_target_pairs={{8,10},{10,8},{12,14},{14,12},{9,11},{11,9},{13,15},{15,13},{24,26... | collective-permute-start | bytes 1966088 | tf_op jit(solution)/shard_map/ppermute | solution.py:102
  52.2 0.8 copy-start.4
  53.0 19.5 %collective-permute-start.8 = (bf16[80,4096]{1,0:T(8,128)(2,1)}, bf16[80,4096]{1,0:T(8,128)(2,1)}, u32[]{:S(2)}, u32[]{:S(2)}) collective-permute-start(bf16[80,4096]{1,0:T(8,128)(2,1)} %collective-permute-done.7.refs_8_), channel_id=1, source_target_pairs={{0,2},{2,0},{4,6},{6,4},{1,3},{3,1},{5,7},{7,5},{16,18},{18,16},{2... | collective-permute-start | bytes 1966088 | tf_op jit(solution)/shard_map/ppermute | solution.py:102
  55.5 26.6 %collective-permute-start.11 = (bf16[80,4096]{1,0:T(8,128)(2,1)}, bf16[80,4096]{1,0:T(8,128)(2,1)}, u32[]{:S(2)}, u32[]{:S(2)}) collective-permute-start(bf16[80,4096]{1,0:T(8,128)(2,1)} %collective-permute-done.10.up), channel_id=1, source_target_pairs={{12,14},{14,12},{13,15},{15,13},{28,30},{30,28},{29,31},{31,29}} | collective-permute-start | bytes 1966088 | tf_op jit(solution)/shard_map/ppermute | solution.py:102
  64.7 18.6 %collective-permute-start.13 = (bf16[80,4096]{1,0:T(8,128)(2,1)}, bf16[80,4096]{1,0:T(8,128)(2,1)}, u32[]{:S(2)}, u32[]{:S(2)}) collective-permute-start(bf16[80,4096]{1,0:T(8,128)(2,1)} %collective-permute-done.12.down), channel_id=1, source_target_pairs={{0,2},{2,0},{1,3},{3,1},{16,18},{18,16},{17,19},{19,17}} | collective-permute-start | bytes 1966088 | tf_op jit(solution)/shard_map/ppermute | solution.py:102
  72.5 1.1 copy-start.3
  73.6 1.1 copy-start.5
  82.0 6.6 %copy-start.10 = (s32[1,8]{1,0:T(1,128)S(1)}, s32[1,8]{1,0:T(1,128)}, u32[]{:S(2)}) copy-start(s32[1,8]{1,0:T(1,128)} %param.11) | copy-start | bytes 100
  82.0 6.7 %copy-start.9 = (s32[8,8]{1,0:T(8,128)S(1)}, s32[8,8]{1,0:T(8,128)}, u32[]{:S(2)}) copy-start(s32[8,8]{1,0:T(8,128)} %param.9) | copy-start | bytes 772
  87.7 0.9 copy-start.1
  88.6 2.3 %collective-permute-start.14 = (f32[512,384]{1,0:T(8,128)S(1)}, f32[512,384]{1,0:T(8,128)S(1)}, u32[]{:S(2)}, u32[]{:S(2)}) collective-permute-start(f32[512,384]{1,0:T(8,128)S(1)} %get-tuple-element.14), channel_id=1, source_target_pairs={{0,1},{1,0},{2,3},{3,2},{4,5},{5,4},{6,7},{7,6},{8,9},{9,8},{10,11... | collective-permute-start | bytes 2359304 | tf_op jit(solution)/shard_map/ppermute | solution.py:364
  90.9 0.9 copy-start.7
  94.0 21.8 %all-to-all-start = ((bf16[16,32,384]{2,1,0:T(8,128)(2,1)}), bf16[16,32,384]{2,1,0:T(8,128)(2,1)S(1)}, u32[]{:S(2)}, u32[]{:S(2)}) async-start(bf16[16,32,384]{2,1,0:T(8,128)(2,1)} %bitcast.23), calls=%async_computation | async-start | bytes 786432 | tf_op jit(solution)/shard_map/all_to_all | solution.py:365
  115.8 0.7 copy-start.6

commit v4 on v3

--- a/solution.py
+++ b/solution.py
@@ -98,83 +98,95 @@
     return (cut(partial, width, core) + other).astype(jnp.bfloat16)
 
 
-def over(block, low, high):
-    return lax.ppermute(block, "dp", [(i, i ^ 1) for i in range(2 * low, 2 * high)])
-
-
-def along(block, low, high, step):
-    return lax.ppermute(block, "dp", [(i, i + 2 * step) for i in range(2 * low, 2 * high)])
-
-
-def gather_line(mine):
-    up1 = along(mine, 0, 3, 1)
-    down1 = along(mine, 1, 4, -1)
-    mine, side, up1, down1 = lax.optimization_barrier((mine, over(mine, 0, 4), up1, down1))
-    own = (mine, side)
-    up2 = along(up1, 1, 3, 1)
-    down2 = along(down1, 1, 3, -1)
-    up1 = (up1, over(up1, 1, 4))
-    down1 = (down1, over(down1, 0, 3))
-    up3 = along(up2, 2, 3, 1)
-    down3 = along(down2, 1, 2, -1)
-    up2 = (up2, over(up2, 2, 4))
-    down2 = (down2, over(down2, 0, 2))
-    up3 = (up3, over(up3, 3, 4))
-    down3 = (down3, over(down3, 0, 1))
-    return own + up1 + down1 + up2 + down2, up3 + down3
-
-
-def early_kernel(at, *refs):
-    pieces, rows, out, whole, sems = refs[:10], refs[10:12], refs[12], refs[13], refs[14]
+def over(block, places):
+    return lax.ppermute(block, "dp", [(2 * z + x, 2 * z + 1 - x) for z in places for x in range(2)])
+
+
+def along(block, moves):
+    return lax.ppermute(block, "dp", [(2 * a + x, 2 * b + x) for a, b in moves for x in range(2)])
+
+
+PAIRS = ((0, 1), (1, 0), (2, 3), (3, 2))
+ACROSS = ((1, 2), (2, 1))
+OUTWARD = ((1, 0), (2, 3))
+
+
+def gather_line(mine, at_end, normed):
+    everywhere = range(4)
+    near = along(mine, PAIRS)
+    middle = along(mine, ACROSS)
+    side, near, middle, _ = lax.optimization_barrier(
+        (over(mine, everywhere), near, middle, normed)
+    )
+    far = along(near, ACROSS)
+    second = along(jnp.where(at_end, side, middle), PAIRS)
+    first_over = over(jnp.where(at_end, near, middle), everywhere)
+    last = along(far, OUTWARD)
+    second_over = over(jnp.where(at_end, second, far), everywhere)
+    last_over = over(last, (0, 3))
+    early = (mine, side, near, middle, far, second, first_over, second_over)
+    return early, (last, last_over)
+
+
+def early_kernel(
+    at, mine, side, near, middle, far, second, first_over, second_over, own, theirs, out, whole, sems
+):
     z, x, part = at[0], at[1], at[2]
-    size = pieces[0].shape[0]
-
-    def copies(k, place):
+    size = mine.shape[0]
+
+    def place(pairs):
         found = []
-        for side in range(2):
-            where = x if side == 0 else 1 - x
-            start = pl.multiple_of((2 * place + where) * size, BLOCK)
-            found.append(
-                pltpu.make_async_copy(
-                    pieces[2 * k + side], whole.at[pl.ds(start, size)], sems.at[2 * k + side]
+        for k, (where, pieces) in enumerate(pairs):
+            for j, piece in enumerate(pieces):
+                column = x if j == 0 else 1 - x
+                start = pl.multiple_of((2 * where + column) * size, BLOCK)
+                found.append(
+                    pltpu.make_async_copy(
+                        piece, whole.at[pl.ds(start, size)], sems.at[2 * k + j]
+                    )
                 )
+        for copy in found:
+            copy.start()
+        for copy in found:
+            copy.wait()
+
+    at_end = (z == 0) | (z == 3)
+    pair = z + 1 - 2 * (z % 2)
+
+    @pl.when(at_end)
+    def _():
+        place(
+            (
+                (z, (mine, side)),
+                (pair, (near, first_over)),
+                ((z + 2) % 4, (second, second_over)),
+                (3 - z, (mine, side)),
             )
-        return found
-
-    always = copies(0, z) + copies(1, (z + 3) % 4) + copies(2, (z + 1) % 4)
-    from_low = copies(3, (z + 2) % 4)
-    from_high = copies(4, (z + 2) % 4)
-    for copy in always:
-        copy.start()
-
-    @pl.when(z >= 2)
+        )
+
+    @pl.when(jnp.logical_not(at_end))
     def _():
-        for copy in from_low:
-            copy.start()
-        for copy in from_low:
-            copy.wait()
-
-    @pl.when(z < 2)
-    def _():
-        for copy in from_high:
-            copy.start()
-        for copy in from_high:
-            copy.wait()
-
-    for copy in always:
-        copy.wait()
-    count = rows[0].shape[0]
-    for k in range(2):
+        place(
+            (
+                (z, (mine, side)),
+                (pair, (near, second)),
+                ((z + 2) % 4, (far, second_over)),
+                (3 - z, (middle, first_over)),
+            )
+        )
+
+    count = own.shape[0]
+    for k, rows in ((0, own), (1, theirs)):
         index = part if k == 0 else 1 - part
         start = pl.multiple_of(index * count, count)
         for low in range(0, whole.shape[0], 256):
             high = min(low + 256, whole.shape[0])
-            out[pl.ds(start, count), low:high] = product(rows[k][...], whole[low:high, :])
-
-
-def late_kernel(at, first, up, up_over, down, down_over, own, theirs, keep, send, last, sums, sems):
+            out[pl.ds(start, count), low:high] = product(rows[...], whole[low:high, :])
+
+
+def late_kernel(at, first, piece, piece_over, own, theirs, keep, send, last, sums, sems):
     z, x, part, core = at[0], at[1], at[2], at[3]
-    size = up.shape[0]
+    size = piece.shape[0]
     count = own.shape[0]
     width = first.shape[1]
     heads = width * HQ // (HQ + 2)
@@ -182,7 +194,7 @@
     edge = 2 * size
     span = 256
 
-    def finish(piece, piece_over, offset, low):
+    def complete(offset, low):
         found = []
         for side, ref in ((0, piece), (1, piece_over)):
             where = x if side == 0 else 1 - x
@@ -214,7 +226,7 @@
     @pl.when(z == 0)
     def _():
         low = width - span
-        finish(down, down_over, span - edge, low)
+        complete(span - edge, low)
         for t in range(2):
 
             @pl.when(core == t)
@@ -226,7 +238,7 @@
 
     @pl.when(z == 3)
     def _():
-        finish(up, up_over, 0, 0)
+        complete(0, 0)
         for t in range(2):
 
             @pl.when(core == t)
@@ -292,6 +304,7 @@
         out_shape=(single, single, jax.ShapeDtypeStruct((TOK_DEV, heads * HD), jnp.bfloat16)),
         in_specs=[whole] * 5,
         out_specs=(whole,) * 3,
+        compiler_params=pltpu.CompilerParams(vmem_limit_bytes=6 << 20),
         name="attend",
     )(
         pick,
@@ -316,7 +329,8 @@
     swap = [(0, 1), (1, 0)]
     normed = scaled(sent_rows, scale_of(sent_rows), norm_gain)
     theirs = lax.ppermute(normed, "parts", swap)
-    early, late = gather_line(mine)
+    at_end = (group < 2) | (group >= groups - 2)
+    early, late = gather_line(mine, at_end, normed)
     slots = sent_rows.shape[0]
     width = groups * size
     whole = pl.BlockSpec(memory_space=pltpu.VMEM)
@@ -325,11 +339,11 @@
     first = pl.pallas_call(
         early_kernel,
         out_shape=jax.ShapeDtypeStruct((2 * slots, width), jnp.float32),
-        in_specs=[scalars] + [anywhere] * 10 + [whole] * 2,
+        in_specs=[scalars] + [anywhere] * 8 + [whole] * 2,
         out_specs=whole,
         scratch_shapes=[
             pltpu.VMEM((width, depth), jnp.bfloat16),
-            pltpu.SemaphoreType.DMA((10,)),
+            pltpu.SemaphoreType.DMA((8,)),
         ],
         compiler_params=pltpu.CompilerParams(vmem_limit_bytes=24 << 20),
         cost_estimate=pl.CostEstimate(
@@ -342,7 +356,7 @@
     keep, send = pl.pallas_call(
         late_kernel,
         out_shape=(half, half),
-        in_specs=[scalars, whole] + [anywhere] * 4 + [whole] * 2,
+        in_specs=[scalars, whole] + [anywhere] * 2 + [whole] * 2,
         out_specs=(whole, whole),
         scratch_shapes=[
             pltpu.VMEM((256, depth), jnp.bfloat16),
@@ -360,6 +374,7 @@
         out_shape=jax.ShapeDtypeStruct(keep.shape, jnp.bfloat16),
         in_specs=[whole, whole],
         out_specs=whole,
+        compiler_params=pltpu.CompilerParams(vmem_limit_bytes=6 << 20),
         name="sum_halves",
     )(keep, lax.ppermute(send, "tensor", swap))
     arrived = lax.all_to_all(ready, ("parts", "dp"), 0, 0, tiled=True)

time: 121 us -> 115 us (0.950)
  starting transfers between devices: 35.7 us -> 24 us
  waiting for transfers between devices: 47.4 us -> 57.5 us
  local copies, waits for them, and re-layouts: 8.78 us -> 5.48 us
  Pallas kernels: 17.2 us -> 15 us
  other arithmetic: 7.41 us -> 8.96 us
    ppermute x1, waiting for transfers between devices: 0.01 us -> 15.4 us  [paired(): theirs = lax.ppermute(normed, 'parts', swap)]
    ppermute x13 -> x9, waiting for transfers between devices: 35.3 us -> 28.1 us  [the longest x5 22.8 us: along(): lax.ppermute(block, 'dp', [(2 * a + x, 2 * b + x) for a, b in moves for x...]
    ppermute x13 -> x9, starting transfers between devices: 25.2 us -> 18.6 us  [the longest x5 12.2 us: along(): lax.ppermute(block, 'dp', [(2 * a + x, 2 * b + x) for a, b in moves for x...]
    all_to_all x1, starting transfers between devices: 8.9 us -> 3.8 us  [paired(): arrived = lax.all_to_all(ready, ('parts', 'dp'), 0, 0, tiled=True)]
    select_n x0 -> x2, other arithmetic: none -> 3.45 us  [the longest x1 2.43 us: gather_line(): first_over = over(jnp.where(at_end, near, middle), everywhere)]
    unnamed x24 -> x18, local copies, waits for them, and re-layouts: 7.69 us -> 4.41 us
    all_to_all x1, waiting for transfers between devices: 10.5 us -> 12.3 us  [paired(): arrived = lax.all_to_all(ready, ('parts', 'dp'), 0, 0, tiled=True)]
    pallas_call x1, Pallas kernels: 2.2 us -> 0.88 us  [paired(): pl.pallas_call(sum_kernel, out_shape=jax.ShapeDtypeStruct(keep.shape, jnp...]
  transfers between devices with their start and end apart: 16 -> 12, of which waited for: 9 -> 8; matrix products, arithmetic and copies ran while one was open for 6% -> 8% of each run, Pallas kernels for 6% -> 7%
where the time goes in v4:
time: 115 us; the launch traced here: 114 us
  waiting for transfers between devices  57.5 us (50%)
  starting transfers between devices  24 us (21%)
  Pallas kernels  15 us (13%)
  other arithmetic  8.96 us (8%)
  local copies, waits for them, and re-layouts  5.48 us (5%)
  blocking collectives  2.46 us (2%)
    ppermute x5, waiting for transfers between devices, along(): lax.ppermute(block, 'dp', [(2 * a + x, 2 * b + x) for a, b in moves for x...  22.8 us
    ppermute x1, waiting for transfers between devices, paired(): theirs = lax.ppermute(normed, 'parts', swap)  15.4 us
    all_to_all x1, waiting for transfers between devices, paired(): arrived = lax.all_to_all(ready, ('parts', 'dp'), 0, 0, tiled=True)  12.3 us
    ppermute x5, starting transfers between devices, along(): lax.ppermute(block, 'dp', [(2 * a + x, 2 * b + x) for a, b in moves for x...  12.2 us
    pallas_call x1, Pallas kernels, paired(): pl.pallas_call(early_kernel, out_shape=jax.ShapeDtypeStruct((2 * slots, w...  7.44 us
    ppermute x4, starting transfers between devices, over(): lax.ppermute(block, 'dp', [(2 * z + x, 2 * z + 1 - x) for z in places for...  6.44 us
    ppermute x4, waiting for transfers between devices, over(): lax.ppermute(block, 'dp', [(2 * z + x, 2 * z + 1 - x) for z in places for...  5.36 us
    unnamed x18, local copies, waits for them, and re-layouts  4.41 us
  transfers between devices with their start and end apart: 12, of which 8 were waited for; matrix products, arithmetic and copies ran while one was open for 8% of the time, Pallas kernels for 7%

profile of v4, /device:TPU:0, one launch (start us, length us, event | category | flops | bytes accessed | tf_op | source)
XLA Modules:
  0.0 114.3 jit_solution(12952785261328523171)
XLA Ops:
  0.6 0.0 copy-start
  0.6 0.0 copy-start.5
  0.7 1.3 %copy-done = bf16[4096,160]{0,1:T(8,128)(2,1)S(1)} copy-done((bf16[4096,160]{0,1:T(8,128)(2,1)S(1)}, bf16[4096,160]{0,1:T(8,128)(2,1)}, u32[]{:S(2)}) %copy-start) | copy-done | bytes 1310744
  2.0 0.9 constant_dynamic-slice_fusion
  2.8 2.9 %collective-permute-start = (bf16[80,4096]{1,0:T(8,128)(2,1)}, bf16[80,4096]{1,0:T(8,128)(2,1)}, u32[]{:S(2)}, u32[]{:S(2)}) collective-permute-start(bf16[80,4096]{1,0:T(8,128)(2,1)} %bitcast.6.mine), channel_id=1, source_target_pairs={{0,2},{2,0},{4,6},{6,4},{8,10},{10,8},{12,14},{14,12},{1,3},{3,1},... | collective-permute-start | bytes 1966088 | tf_op jit(solution)/shard_map/ppermute | solution.py:102
  5.8 1.6 %collective-permute-start.1 = (bf16[80,4096]{1,0:T(8,128)(2,1)}, bf16[80,4096]{1,0:T(8,128)(2,1)}, u32[]{:S(2)}, u32[]{:S(2)}) collective-permute-start(bf16[80,4096]{1,0:T(8,128)(2,1)} %bitcast.6.mine), channel_id=1, source_target_pairs={{0,4},{2,6},{4,0},{6,2},{8,12},{10,14},{12,8},{14,10},{1,5},{3,7},... | collective-permute-start | bytes 1966088 | tf_op jit(solution)/shard_map/ppermute | solution.py:106
  7.4 1.5 %collective-permute-start.2 = (bf16[80,4096]{1,0:T(8,128)(2,1)}, bf16[80,4096]{1,0:T(8,128)(2,1)}, u32[]{:S(2)}, u32[]{:S(2)}) collective-permute-start(bf16[80,4096]{1,0:T(8,128)(2,1)} %bitcast.6.mine), channel_id=1, source_target_pairs={{4,8},{6,10},{8,4},{10,6},{5,9},{7,11},{9,5},{11,7},{20,24},{22,26... | collective-permute-start | bytes 1966088 | tf_op jit(solution)/shard_map/ppermute | solution.py:106
  8.9 2.1 %fusion = f32[256]{0:T(256)S(1)} fusion(bf16[256,4096]{1,0:T(8,128)(2,1)} %param.6), kind=kLoop, calls=%fused_computation.2 | loop fusion | flops 3145472 | bytes 2098176 | tf_op jit(solution)/shard_map/reduce_sum | solution.py:74
  10.9 2.5 %psum.7 = f32[256]{0:T(256)S(1)} all-reduce(f32[256]{0:T(256)S(1)} %fusion), channel_id=1, replica_groups=mesh['parts'=2,'dp'=8,'tensor'=2] {'tensor'}, use_global_device_ids=true, to_apply=%region_3.4 | all-reduce | flops 256 | bytes 2048 | tf_op jit(solution)/shard_map/psum | solution.py:74
  13.4 0.0 copy-done.5
  13.4 2.2 %fusion.2.own = bf16[256,4096]{1,0:T(8,128)(2,1)S(1)} fusion(bf16[256,4096]{1,0:T(8,128)(2,1)} %param.6, f32[4096]{0:T(1024)S(1)} %copy-done.5, f32[256]{0:T(256)S(1)} %add_rsqrt_fusion), kind=kLoop, calls=%fused_computation.4 | loop fusion | flops 4194304 | bytes 4211712 | tf_op jit(solution)/shard_map/convert_element_type | solution.py:79
  15.6 0.0 copy-start.8
  15.7 5.2 %collective-permute-done.side = bf16[80,4096]{1,0:T(8,128)(2,1)} collective-permute-done((bf16[80,4096]{1,0:T(8,128)(2,1)}, bf16[80,4096]{1,0:T(8,128)(2,1)}, u32[]{:S(2)}, u32[]{:S(2)}) %collective-permute-start) | collective-permute-done | bytes 655392 | tf_op jit(solution)/shard_map/ppermute | solution.py:102
  20.8 1.5 %collective-permute-done.1.near = bf16[80,4096]{1,0:T(8,128)(2,1)} collective-permute-done((bf16[80,4096]{1,0:T(8,128)(2,1)}, bf16[80,4096]{1,0:T(8,128)(2,1)}, u32[]{:S(2)}, u32[]{:S(2)}) %collective-permute-start.1) | collective-permute-done | bytes 655392 | tf_op jit(solution)/shard_map/ppermute | solution.py:106
  22.3 0.0 collective-permute-done.2.middle
  22.3 0.7 collective-permute-start.3
  23.0 2.4 %broadcast_select_fusion.1 = (bf16[80,4096]{1,0:T(8,128)(2,1)}, bf16[80,4096]{1,0:T(8,128)(2,1)S(1)}) fusion(bf16[80,4096]{1,0:T(8,128)(2,1)} %collective-permute-done.1.near, bf16[80,4096]{1,0:T(8,128)(2,1)} %collective-permute-done.2.middle, pred[]{:T(512)S(6)} %or.3, bf16[80,4096]{1,0:T(8,128)(2,1)} %collective-permute-done.side), kind=kLoop, calls=%fused_computation.6 | loop fusion | flops 655360 | bytes 3276801 | tf_op jit(solution)/shard_map/jit(_where)/select_n | solution.py:123
  25.4 7.1 %collective-permute-start.4 = (bf16[80,4096]{1,0:T(8,128)(2,1)S(1)}, bf16[80,4096]{1,0:T(8,128)(2,1)S(1)}, u32[]{:S(2)}, u32[]{:S(2)}) collective-permute-start(bf16[80,4096]{1,0:T(8,128)(2,1)S(1)} %get-tuple-element.18), channel_id=1, source_target_pairs={{0,4},{2,6},{4,0},{6,2},{8,12},{10,14},{12,8},{14,10},{1,5},{3,7},... | collective-permute-start | bytes 1966088 | tf_op jit(solution)/shard_map/ppermute | solution.py:106
  32.6 1.5 %collective-permute-start.7 = (bf16[256,4096]{1,0:T(8,128)(2,1)S(1)}, bf16[256,4096]{1,0:T(8,128)(2,1)}, u32[]{:S(2)}, u32[]{:S(2)}) collective-permute-start(bf16[256,4096]{1,0:T(8,128)(2,1)S(1)} %fusion.2.own), channel_id=1, source_target_pairs={{0,16},{16,0},{1,17},{17,1},{2,18},{18,2},{3,19},{19,3},{4,20},{20... | collective-permute-start | bytes 6291464 | tf_op jit(solution)/shard_map/ppermute | solution.py:331
  34.1 0.5 collective-permute-start.5
  34.6 0.0 collective-permute-done.3.far
  34.6 1.3 %collective-permute-start.8 = (bf16[80,4096]{1,0:T(8,128)(2,1)S(1)}, bf16[80,4096]{1,0:T(8,128)(2,1)}, u32[]{:S(2)}, u32[]{:S(2)}) collective-permute-start(bf16[80,4096]{1,0:T(8,128)(2,1)S(1)} %collective-permute-done.3.far), channel_id=1, source_target_pairs={{4,0},{6,2},{8,12},{10,14},{5,1},{7,3},{9,13},{11,15},{20,16},{22,... | collective-permute-start | bytes 1966088 | tf_op jit(solution)/shard_map/ppermute | solution.py:106
  35.9 10.9 %collective-permute-done.4.second = bf16[80,4096]{1,0:T(8,128)(2,1)S(1)} collective-permute-done((bf16[80,4096]{1,0:T(8,128)(2,1)S(1)}, bf16[80,4096]{1,0:T(8,128)(2,1)S(1)}, u32[]{:S(2)}, u32[]{:S(2)}) %collective-permute-start.4) | collective-permute-done | bytes 655392 | tf_op jit(solution)/shard_map/ppermute | solution.py:106
  46.8 0.0 copy-start.3
  46.8 1.0 broadcast_select_fusion
  47.8 0.0 copy-start.1
  47.8 0.9 copy-done.1
  48.7 0.5 collective-permute-start.6
  49.2 10.4 %collective-permute-done.8.piece = bf16[80,4096]{1,0:T(8,128)(2,1)} collective-permute-done((bf16[80,4096]{1,0:T(8,128)(2,1)S(1)}, bf16[80,4096]{1,0:T(8,128)(2,1)}, u32[]{:S(2)}, u32[]{:S(2)}) %collective-permute-start.8) | collective-permute-done | bytes 655392 | tf_op jit(solution)/shard_map/ppermute | solution.py:106
  59.7 0.0 copy-done.3
  59.7 2.4 %collective-permute-start.9 = (bf16[80,4096]{1,0:T(8,128)(2,1)}, bf16[80,4096]{1,0:T(8,128)(2,1)}, u32[]{:S(2)}, u32[]{:S(2)}) collective-permute-start(bf16[80,4096]{1,0:T(8,128)(2,1)} %collective-permute-done.8.piece), channel_id=1, source_target_pairs={{0,2},{2,0},{12,14},{14,12},{1,3},{3,1},{13,15},{15,13},{16,18},{1... | collective-permute-start | bytes 1966088 | tf_op jit(solution)/shard_map/ppermute | solution.py:102
  62.1 0.0 copy-done.8
  62.1 0.2 reduce-window.13
  62.3 0.1 pad_add_fusion.at
  62.4 0.0 collective-permute-done.5.first_over
  62.4 0.2 collective-permute-done.6.second_over
  62.6 15.4 %collective-permute-done.7.theirs = bf16[256,4096]{1,0:T(8,128)(2,1)} collective-permute-done((bf16[256,4096]{1,0:T(8,128)(2,1)S(1)}, bf16[256,4096]{1,0:T(8,128)(2,1)}, u32[]{:S(2)}, u32[]{:S(2)}) %collective-permute-start.7) | collective-permute-done | bytes 2097184 | tf_op jit(solution)/shard_map/ppermute | solution.py:331
  78.0 0.0 copy-start.2
  78.0 1.1 copy-done.2
  79.1 0.0 copy-start.4
  79.1 1.1 copy-done.4
  80.2 7.4 %project_early.1.first = f32[512,640]{1,0:T(8,128)S(1)} custom-call(s32[4]{0:T(128)S(1)} %pad_add_fusion.at, bf16[80,4096]{1,0:T(8,128)(2,1)} %bitcast.6.mine, bf16[80,4096]{1,0:T(8,128)(2,1)} %collective-permute-done.side, bf16[80,4096]{1,0:T(8,128)(2,1)} %collective-permute-done.1.near, bf16[80,4096]{1,0:T(8,128)(2,1)} %collective-permute-done.2.middle, ...), custom_call_target="tpu_custom_call" | custom-call | flops 2684354560 | bytes 12582912 | tf_op jit(solution)/shard_map/project_early/pallas_call | solution.py:339
  87.6 0.0 copy-start.7
  87.6 0.0 copy-start.6
  87.6 0.0 collective-permute-done.9.piece_over
  87.7 4.4 %project_late.1 = (f32[512,384]{1,0:T(8,128)S(1)}, f32[512,384]{1,0:T(8,128)S(1)}) custom-call(s32[4]{0:T(128)S(1)} %pad_add_fusion.at, f32[512,640]{1,0:T(8,128)S(1)} %project_early.1.first, bf16[80,4096]{1,0:T(8,128)(2,1)} %collective-permute-done.8.piece, bf16[80,4096]{1,0:T(8,128)(2,1)} %collective-permute-done.9.piece_over, ...), custom_call_target="tpu_custom_call" | custom-call | flops 1073741824 | bytes 8388608 | tf_op jit(solution)/shard_map/project_late/pallas_call | solution.py:356
  92.1 0.1 collective-permute-start.10
  92.1 0.0 copy-done.7
  92.2 0.1 select_reduce_fusion
  92.3 0.0 copy-done.6
  92.3 0.2 fusion.8
  92.5 0.3 fusion.4
  92.8 1.6 %collective-permute-done.10.other = f32[512,384]{1,0:T(8,128)S(1)} collective-permute-done((f32[512,384]{1,0:T(8,128)S(1)}, f32[512,384]{1,0:T(8,128)S(1)}, u32[]{:S(2)}, u32[]{:S(2)}) %collective-permute-start.10) | collective-permute-done | bytes 786464 | tf_op jit(solution)/shard_map/ppermute | solution.py:379
  94.4 0.9 sum_halves.1
  95.3 3.8 %all-to-all-start = ((bf16[16,32,384]{2,1,0:T(8,128)(2,1)}), bf16[16,32,384]{2,1,0:T(8,128)(2,1)S(1)}, u32[]{:S(2)}, u32[]{:S(2)}) async-start(bf16[16,32,384]{2,1,0:T(8,128)(2,1)} %bitcast.7), calls=%async_computation | async-start | bytes 786432 | tf_op jit(solution)/shard_map/all_to_all | solution.py:380
  99.1 0.1 reduce
  99.2 0.1 pad_maximum_fusion
  99.4 0.1 select_reduce_fusion.2
  99.4 0.1 fusion.3.pick
  99.5 0.1 and_convert_fusion.allowed
  99.6 12.3 %all-to-all-done = bf16[16,32,384]{2,1,0:T(8,128)(2,1)S(1)} async-done(((bf16[16,32,384]{2,1,0:T(8,128)(2,1)}), bf16[16,32,384]{2,1,0:T(8,128)(2,1)S(1)}, u32[]{:S(2)}, u32[]{:S(2)}) %all-to-all-start) | async-done | bytes 393248 | tf_op jit(solution)/shard_map/all_to_all | solution.py:380
  112.0 2.3 %attend.1 = (bf16[128,128]{1,0:T(8,128)(2,1)}, bf16[128,128]{1,0:T(8,128)(2,1)}, bf16[128,512]{1,0:T(8,128)(2,1)}) custom-call(bf16[128,256]{1,0:T(8,128)(2,1)S(1)} %fusion.3.pick, bf16[2,256,384]{2,1,0:T(8,128)(2,1)S(1)} %bitcast.22, f32[128,128]{1,0:T(8,128)S(1)} %get-tuple-element.22.cosine, f32[128,128]{1,0:T(8,128)S(1)} %get-tuple-element.23.sine, ...), custom_call_target="tpu_custom_call" | custom-call | tf_op jit(solution)/shard_map/attend/pallas_call | solution.py:302
  (7 shorter events, 0.1 us)
Async XLA Ops:
  0.6 1.3 %copy-start = (bf16[4096,160]{0,1:T(8,128)(2,1)S(1)}, bf16[4096,160]{0,1:T(8,128)(2,1)}, u32[]{:S(2)}) copy-start(bf16[4096,160]{0,1:T(8,128)(2,1)} %param.8) | copy-start | bytes 3932164
  0.6 12.8 %copy-start.5 = (f32[4096]{0:T(1024)S(1)}, f32[4096]{0:T(1024)}, u32[]{:S(2)}) copy-start(f32[4096]{0:T(1024)} %param.7) | copy-start | bytes 49156
  2.8 18.0 %collective-permute-start = (bf16[80,4096]{1,0:T(8,128)(2,1)}, bf16[80,4096]{1,0:T(8,128)(2,1)}, u32[]{:S(2)}, u32[]{:S(2)}) collective-permute-start(bf16[80,4096]{1,0:T(8,128)(2,1)} %bitcast.6.mine), channel_id=1, source_target_pairs={{0,2},{2,0},{4,6},{6,4},{8,10},{10,8},{12,14},{14,12},{1,3},{3,1},... | collective-permute-start | bytes 1966088 | tf_op jit(solution)/shard_map/ppermute | solution.py:102
  5.8 16.5 %collective-permute-start.1 = (bf16[80,4096]{1,0:T(8,128)(2,1)}, bf16[80,4096]{1,0:T(8,128)(2,1)}, u32[]{:S(2)}, u32[]{:S(2)}) collective-permute-start(bf16[80,4096]{1,0:T(8,128)(2,1)} %bitcast.6.mine), channel_id=1, source_target_pairs={{0,4},{2,6},{4,0},{6,2},{8,12},{10,14},{12,8},{14,10},{1,5},{3,7},... | collective-permute-start | bytes 1966088 | tf_op jit(solution)/shard_map/ppermute | solution.py:106
  7.4 14.9 %collective-permute-start.2 = (bf16[80,4096]{1,0:T(8,128)(2,1)}, bf16[80,4096]{1,0:T(8,128)(2,1)}, u32[]{:S(2)}, u32[]{:S(2)}) collective-permute-start(bf16[80,4096]{1,0:T(8,128)(2,1)} %bitcast.6.mine), channel_id=1, source_target_pairs={{4,8},{6,10},{8,4},{10,6},{5,9},{7,11},{9,5},{11,7},{20,24},{22,26... | collective-permute-start | bytes 1966088 | tf_op jit(solution)/shard_map/ppermute | solution.py:106
  15.6 46.5 %copy-start.8 = (s32[1,8]{1,0:T(1,128)S(1)}, s32[1,8]{1,0:T(1,128)}, u32[]{:S(2)}) copy-start(s32[1,8]{1,0:T(1,128)} %param.10) | copy-start | bytes 100
  22.3 12.3 %collective-permute-start.3 = (bf16[80,4096]{1,0:T(8,128)(2,1)}, bf16[80,4096]{1,0:T(8,128)(2,1)S(1)}, u32[]{:S(2)}, u32[]{:S(2)}) collective-permute-start(bf16[80,4096]{1,0:T(8,128)(2,1)} %collective-permute-done.1.near), channel_id=1, source_target_pairs={{4,8},{6,10},{8,4},{10,6},{5,9},{7,11},{9,5},{11,7},{20,24},{22,26... | collective-permute-start | bytes 1966088 | tf_op jit(solution)/shard_map/ppermute | solution.py:106
  25.4 21.3 %collective-permute-start.4 = (bf16[80,4096]{1,0:T(8,128)(2,1)S(1)}, bf16[80,4096]{1,0:T(8,128)(2,1)S(1)}, u32[]{:S(2)}, u32[]{:S(2)}) collective-permute-start(bf16[80,4096]{1,0:T(8,128)(2,1)S(1)} %get-tuple-element.18), channel_id=1, source_target_pairs={{0,4},{2,6},{4,0},{6,2},{8,12},{10,14},{12,8},{14,10},{1,5},{3,7},... | collective-permute-start | bytes 1966088 | tf_op jit(solution)/shard_map/ppermute | solution.py:106
  32.6 45.4 %collective-permute-start.7 = (bf16[256,4096]{1,0:T(8,128)(2,1)S(1)}, bf16[256,4096]{1,0:T(8,128)(2,1)}, u32[]{:S(2)}, u32[]{:S(2)}) collective-permute-start(bf16[256,4096]{1,0:T(8,128)(2,1)S(1)} %fusion.2.own), channel_id=1, source_target_pairs={{0,16},{16,0},{1,17},{17,1},{2,18},{18,2},{3,19},{19,3},{4,20},{20... | collective-permute-start | bytes 6291464 | tf_op jit(solution)/shard_map/ppermute | solution.py:331
  34.1 28.3 %collective-permute-start.5 = (bf16[80,4096]{1,0:T(8,128)(2,1)}, bf16[80,4096]{1,0:T(8,128)(2,1)}, u32[]{:S(2)}, u32[]{:S(2)}) collective-permute-start(bf16[80,4096]{1,0:T(8,128)(2,1)} %get-tuple-element.17), channel_id=1, source_target_pairs={{0,2},{2,0},{4,6},{6,4},{8,10},{10,8},{12,14},{14,12},{1,3},{3,1},... | collective-permute-start | bytes 1966088 | tf_op jit(solution)/shard_map/ppermute | solution.py:102
  34.6 25.1 %collective-permute-start.8 = (bf16[80,4096]{1,0:T(8,128)(2,1)S(1)}, bf16[80,4096]{1,0:T(8,128)(2,1)}, u32[]{:S(2)}, u32[]{:S(2)}) collective-permute-start(bf16[80,4096]{1,0:T(8,128)(2,1)S(1)} %collective-permute-done.3.far), channel_id=1, source_target_pairs={{4,0},{6,2},{8,12},{10,14},{5,1},{7,3},{9,13},{11,15},{20,16},{22,... | collective-permute-start | bytes 1966088 | tf_op jit(solution)/shard_map/ppermute | solution.py:106
  46.8 12.9 %copy-start.3 = (bf16[80,4096]{1,0:T(8,128)(2,1)}, bf16[80,4096]{1,0:T(8,128)(2,1)S(1)}, u32[]{:S(2)}) copy-start(bf16[80,4096]{1,0:T(8,128)(2,1)S(1)} %collective-permute-done.4.second) | copy-start | bytes 1966084
  47.8 0.9 copy-start.1
  48.7 13.9 %collective-permute-start.6 = (bf16[80,4096]{1,0:T(8,128)(2,1)}, bf16[80,4096]{1,0:T(8,128)(2,1)}, u32[]{:S(2)}, u32[]{:S(2)}) collective-permute-start(bf16[80,4096]{1,0:T(8,128)(2,1)} %broadcast_select_fusion), channel_id=1, source_target_pairs={{0,2},{2,0},{4,6},{6,4},{8,10},{10,8},{12,14},{14,12},{1,3},{3,1},... | collective-permute-start | bytes 1966088 | tf_op jit(solution)/shard_map/ppermute | solution.py:102
  59.7 28.0 %collective-permute-start.9 = (bf16[80,4096]{1,0:T(8,128)(2,1)}, bf16[80,4096]{1,0:T(8,128)(2,1)}, u32[]{:S(2)}, u32[]{:S(2)}) collective-permute-start(bf16[80,4096]{1,0:T(8,128)(2,1)} %collective-permute-done.8.piece), channel_id=1, source_target_pairs={{0,2},{2,0},{12,14},{14,12},{1,3},{3,1},{13,15},{15,13},{16,18},{1... | collective-permute-start | bytes 1966088 | tf_op jit(solution)/shard_map/ppermute | solution.py:102
  78.0 1.1 copy-start.2
  79.1 1.1 copy-start.4
  87.6 4.5 %copy-start.7 = (s32[1,8]{1,0:T(1,128)S(1)}, s32[1,8]{1,0:T(1,128)}, u32[]{:S(2)}) copy-start(s32[1,8]{1,0:T(1,128)} %param.11) | copy-start | bytes 100
  87.6 4.6 %copy-start.6 = (s32[8,8]{1,0:T(8,128)S(1)}, s32[8,8]{1,0:T(8,128)}, u32[]{:S(2)}) copy-start(s32[8,8]{1,0:T(8,128)} %param.9) | copy-start | bytes 772
  92.1 2.4 %collective-permute-start.10 = (f32[512,384]{1,0:T(8,128)S(1)}, f32[512,384]{1,0:T(8,128)S(1)}, u32[]{:S(2)}, u32[]{:S(2)}) collective-permute-start(f32[512,384]{1,0:T(8,128)S(1)} %get-tuple-element.12), channel_id=1, source_target_pairs={{0,1},{1,0},{2,3},{3,2},{4,5},{5,4},{6,7},{7,6},{8,9},{9,8},{10,11... | collective-permute-start | bytes 2359304 | tf_op jit(solution)/shard_map/ppermute | solution.py:379
  95.3 16.7 %all-to-all-start = ((bf16[16,32,384]{2,1,0:T(8,128)(2,1)}), bf16[16,32,384]{2,1,0:T(8,128)(2,1)S(1)}, u32[]{:S(2)}, u32[]{:S(2)}) async-start(bf16[16,32,384]{2,1,0:T(8,128)(2,1)} %bitcast.7), calls=%async_computation | async-start | bytes 786432 | tf_op jit(solution)/shard_map/all_to_all | solution.py:380

commit v5 on v4

--- a/solution.py
+++ b/solution.py
@@ -109,29 +109,42 @@
 PAIRS = ((0, 1), (1, 0), (2, 3), (3, 2))
 ACROSS = ((1, 2), (2, 1))
 OUTWARD = ((1, 0), (2, 3))
+ENDS = (0, 3)
+MIDDLE = (1, 2)
+
+
+def overs(places):
+    return [(2 * z + x, 2 * z + 1 - x) for z in places for x in range(2)]
+
+
+def alongs(moves):
+    return [(2 * a + x, 2 * b + x) for a, b in moves for x in range(2)]
 
 
 def gather_line(mine, at_end, normed):
-    everywhere = range(4)
-    near = along(mine, PAIRS)
-    middle = along(mine, ACROSS)
-    side, near, middle, _ = lax.optimization_barrier(
-        (over(mine, everywhere), near, middle, normed)
-    )
-    far = along(near, ACROSS)
-    second = along(jnp.where(at_end, side, middle), PAIRS)
-    first_over = over(jnp.where(at_end, near, middle), everywhere)
-    last = along(far, OUTWARD)
-    second_over = over(jnp.where(at_end, second, far), everywhere)
-    last_over = over(last, (0, 3))
-    early = (mine, side, near, middle, far, second, first_over, second_over)
-    return early, (last, last_over)
+    def send(block, pairs):
+        return lax.ppermute(block, "dp", pairs)
+
+    near = send(mine, alongs(PAIRS))
+    cross = send(mine, alongs(ACROSS) + overs(ENDS))
+    side = send(mine, overs(MIDDLE))
+    near, cross, side, normed = lax.optimization_barrier((near, cross, side, normed))
+    second = send(cross, alongs(PAIRS))
+    far = send(near, alongs(ACROSS))
+    near_over = send(near, overs(ENDS))
+    cross_over = send(cross, overs(MIDDLE))
+    last = send(far, alongs(OUTWARD))
+    second_over = send(jnp.where(at_end, second, far), overs(range(4)))
+    last_over = send(last, overs(ENDS))
+    early = (mine, near, cross, side, second, far, near_over, cross_over, second_over)
+    return early, (last, last_over), normed
 
 
 def early_kernel(
-    at, mine, side, near, middle, far, second, first_over, second_over, own, theirs, out, whole, sems
+    at, mine, near, cross, side, second, far, near_over, cross_over, second_over,
+    own, theirs, keep, send, whole, sems,
 ):
-    z, x, part = at[0], at[1], at[2]
+    z, x, part, core = at[0], at[1], at[2], at[3]
     size = mine.shape[0]
 
     def place(pairs):
@@ -157,10 +170,10 @@
     def _():
         place(
             (
-                (z, (mine, side)),
-                (pair, (near, first_over)),
+                (z, (mine, cross)),
+                (pair, (near, near_over)),
                 ((z + 2) % 4, (second, second_over)),
-                (3 - z, (mine, side)),
+                (3 - z, (mine, cross)),
             )
         )
 
@@ -171,30 +184,40 @@
                 (z, (mine, side)),
                 (pair, (near, second)),
                 ((z + 2) % 4, (far, second_over)),
-                (3 - z, (middle, first_over)),
+                (3 - z, (cross, cross_over)),
             )
         )
 
     count = own.shape[0]
+    share = whole.shape[0] * HQ // (HQ + 2) // 2
     for k, rows in ((0, own), (1, theirs)):
         index = part if k == 0 else 1 - part
         start = pl.multiple_of(index * count, count)
-        for low in range(0, whole.shape[0], 256):
-            high = min(low + 256, whole.shape[0])
-            out[pl.ds(start, count), low:high] = product(rows[...], whole[low:high, :])
-
-
-def late_kernel(at, first, piece, piece_over, own, theirs, keep, send, last, sums, sems):
+        halves = [
+            product(rows[...], whole[c * share : (c + 1) * share, :]) for c in range(2)
+        ]
+        rest = product(rows[...], whole[2 * share :, :])
+        for ref in (keep, send):
+            ref[pl.ds(start, count), share:] = rest
+        for t in range(2):
+
+            @pl.when(core == t)
+            def _():
+                keep[pl.ds(start, count), :share] = halves[t]
+                send[pl.ds(start, count), :share] = halves[1 - t]
+
+
+def late_kernel(
+    at, first_keep, first_send, piece, piece_over, own, theirs, keep, send, last, sems
+):
     z, x, part, core = at[0], at[1], at[2], at[3]
     size = piece.shape[0]
     count = own.shape[0]
-    width = first.shape[1]
-    heads = width * HQ // (HQ + 2)
-    share = heads // 2
+    share = last.shape[0]
     edge = 2 * size
-    span = 256
-
-    def complete(offset, low):
+    gap = share - edge
+
+    def fetch(offset):
         found = []
         for side, ref in ((0, piece), (1, piece_over)):
             where = x if side == 0 else 1 - x
@@ -206,46 +229,51 @@
             copy.start()
         for copy in found:
             copy.wait()
-        column = lax.broadcasted_iota(jnp.int32, (count, span), 1)
-        new = (column >= offset) & (column < offset + edge)
+
+    def blocks():
         for k, rows in ((0, own), (1, theirs)):
             index = part if k == 0 else 1 - part
             start = pl.multiple_of(index * count, count)
-            block = product(rows[...], last[...])
-            old = first[pl.ds(start, count), low : low + span]
-            sums[pl.ds(start, count), :] = jnp.where(new, block, old)
-
-    for t in range(2):
-
-        @pl.when(core == t)
-        def _():
-            for ref, c in ((keep, t), (send, 1 - t)):
-                ref[:, :share] = first[:, c * share : (c + 1) * share]
-                ref[:, share:] = first[:, heads:]
+            yield pl.ds(start, count), product(rows[...], last[...])
+
+    def merge(ref, source, place, lanes, block, new):
+        ref[place, lanes] = jnp.where(new, block, source[place, lanes])
+
+    keep[...] = first_keep[...]
+    send[...] = first_send[...]
+    lane = lax.broadcasted_iota(jnp.int32, (count, share), 1)
 
     @pl.when(z == 0)
     def _():
-        low = width - span
-        complete(span - edge, low)
-        for t in range(2):
-
-            @pl.when(core == t)
+        fetch(gap)
+        for place, block in blocks():
+            for ref in (keep, send):
+                ref[place, share:] = block[:, share // 2 :]
+            head = block[:, : share // 2]
+            new = lane[:, : share // 2] >= gap
+            lanes = slice(share // 2, share)
+
+            @pl.when(core == 1)
             def _():
-                for ref, c in ((keep, t), (send, 1 - t)):
-                    if c == 1:
-                        ref[:, share - (heads - low) : share] = sums[:, : heads - low]
-                    ref[:, share:] = sums[:, heads - low :]
+                merge(keep, first_keep, place, lanes, head, new)
+
+            @pl.when(core == 0)
+            def _():
+                merge(send, first_send, place, lanes, head, new)
 
     @pl.when(z == 3)
     def _():
-        complete(0, 0)
-        for t in range(2):
-
-            @pl.when(core == t)
+        fetch(0)
+        for place, block in blocks():
+            lanes = slice(0, share)
+
+            @pl.when(core == 0)
             def _():
-                for ref, c in ((keep, t), (send, 1 - t)):
-                    if c == 0:
-                        ref[:, :share] = sums[...]
+                merge(keep, first_keep, place, lanes, block, lane < edge)
+
+            @pl.when(core == 1)
+            def _():
+                merge(send, first_send, place, lanes, block, lane < edge)
 
 
 def sum_kernel(keep, other, out):
@@ -327,20 +355,23 @@
         turned.reshape(count, 2, BLOCK, depth), part, 1, False
     ).reshape(size, depth)
     swap = [(0, 1), (1, 0)]
+    raw = lax.ppermute(sent_rows, "parts", swap)
     normed = scaled(sent_rows, scale_of(sent_rows), norm_gain)
-    theirs = lax.ppermute(normed, "parts", swap)
+    theirs = scaled(raw, scale_of(raw), norm_gain)
     at_end = (group < 2) | (group >= groups - 2)
-    early, late = gather_line(mine, at_end, normed)
+    early, late, normed = gather_line(mine, at_end, normed)
     slots = sent_rows.shape[0]
     width = groups * size
     whole = pl.BlockSpec(memory_space=pltpu.VMEM)
     anywhere = pl.BlockSpec(memory_space=pl.ANY)
     scalars = pl.BlockSpec(memory_space=pltpu.SMEM)
+    heads = width * HQ // (HQ + 2)
+    half = jax.ShapeDtypeStruct((2 * slots, heads // 2 + width - heads), jnp.float32)
     first = pl.pallas_call(
         early_kernel,
-        out_shape=jax.ShapeDtypeStruct((2 * slots, width), jnp.float32),
-        in_specs=[scalars] + [anywhere] * 8 + [whole] * 2,
-        out_specs=whole,
+        out_shape=(half, half),
+        in_specs=[scalars] + [anywhere] * 9 + [whole] * 2,
+        out_specs=(whole, whole),
         scratch_shapes=[
             pltpu.VMEM((width, depth), jnp.bfloat16),
             pltpu.SemaphoreType.DMA((8,)),
@@ -351,24 +382,22 @@
         ),
         name="project_early",
     )(at, *early, normed, theirs)
-    share = width * HQ // (HQ + 2) // 2 + width * 2 // (HQ + 2)
-    half = jax.ShapeDtypeStruct((2 * slots, share), jnp.float32)
     keep, send = pl.pallas_call(
         late_kernel,
         out_shape=(half, half),
-        in_specs=[scalars, whole] + [anywhere] * 2 + [whole] * 2,
+        in_specs=[scalars] + [whole] * 2 + [anywhere] * 2 + [whole] * 2,
         out_specs=(whole, whole),
         scratch_shapes=[
-            pltpu.VMEM((256, depth), jnp.bfloat16),
-            pltpu.VMEM((2 * slots, 256), jnp.float32),
+            pltpu.VMEM((heads // 2, depth), jnp.bfloat16),
             pltpu.SemaphoreType.DMA((2,)),
         ],
-        compiler_params=pltpu.CompilerParams(vmem_limit_bytes=24 << 20),
+        input_output_aliases={1: 0, 2: 1},
+        compiler_params=pltpu.CompilerParams(vmem_limit_bytes=16 << 20),
         cost_estimate=pl.CostEstimate(
-            flops=4 * slots * 256 * depth, bytes_accessed=8 << 20, transcendentals=0
+            flops=2 * slots * heads * depth, bytes_accessed=6 << 20, transcendentals=0
         ),
         name="project_late",
-    )(at, first, *late, normed, theirs)
+    )(at, *first, *late, normed, theirs)
     ready = pl.pallas_call(
         sum_kernel,
         out_shape=jax.ShapeDtypeStruct(keep.shape, jnp.bfloat16),
@@ -378,7 +407,7 @@
         name="sum_halves",
     )(keep, lax.ppermute(send, "tensor", swap))
     arrived = lax.all_to_all(ready, ("parts", "dp"), 0, 0, tiled=True)
-    return arrived.reshape(2, slots, share)
+    return arrived.reshape(2, slots, half.shape[1])
 
 
 def single(sent_rows, norm_gain, qkv_weight):

time: 115 us -> 141 us (1.23)
  waiting for transfers between devices: 57.5 us -> 78.3 us
  starting transfers between devices: 24 us -> 29.9 us
  local copies, waits for them, and re-layouts: 5.48 us -> 2.7 us
  other arithmetic: 8.96 us -> 10.9 us
    ppermute x10 -> x11, waiting for transfers between devices: 43.5 us -> 64.3 us  [the longest x1 38.3 us: paired(): raw = lax.ppermute(sent_rows, 'parts', swap)]
    ppermute x10 -> x11, starting transfers between devices: 20.1 us -> 24 us  [the longest x10 21 us: send(): return lax.ppermute(block, 'dp', pairs)]
    convert_element_type x1, other arithmetic: 2.22 us -> 5.08 us  [scaled(): (rows.astype(jnp.float32) * scale[:, None] * norm_gain[None, :]).astype(j...]
    unnamed x18 -> x14, local copies, waits for them, and re-layouts: 4.41 us -> 1.61 us
    all_to_all x1, starting transfers between devices: 3.8 us -> 5.76 us  [paired(): arrived = lax.all_to_all(ready, ('parts', 'dp'), 0, 0, tiled=True)]
    select_n x2 -> x1, other arithmetic: 3.45 us -> 2 us  [gather_line(): second_over = send(jnp.where(at_end, second, far), overs(range(4)))]
  transfers between devices with their start and end apart: 12 -> 13, of which waited for: 8 -> 6; matrix products, arithmetic and copies ran while one was open for 8% -> 9% of each run, Pallas kernels for 7% -> 6%
where the time goes in v5:
time: 141 us
  waiting for transfers between devices  78.3 us (56%)
  starting transfers between devices  29.9 us (21%)
  Pallas kernels  15.6 us (11%)
  other arithmetic  10.9 us (8%)
  local copies, waits for them, and re-layouts  2.7 us (2%)
  blocking collectives  2.46 us (2%)
    ppermute x1, waiting for transfers between devices, paired(): raw = lax.ppermute(sent_rows, 'parts', swap)  38.3 us
    ppermute x10, waiting for transfers between devices, send(): return lax.ppermute(block, 'dp', pairs)  26 us
    ppermute x10, starting transfers between devices, send(): return lax.ppermute(block, 'dp', pairs)  21 us
    all_to_all x1, waiting for transfers between devices, paired(): arrived = lax.all_to_all(ready, ('parts', 'dp'), 0, 0, tiled=True)  12.3 us
    pallas_call x1, Pallas kernels, paired(): pl.pallas_call(early_kernel, out_shape=(half, half), in_specs=[scalars] +...  7.83 us
    all_to_all x1, starting transfers between devices, paired(): arrived = lax.all_to_all(ready, ('parts', 'dp'), 0, 0, tiled=True)  5.76 us
    convert_element_type x1, other arithmetic, scaled(): (rows.astype(jnp.float32) * scale[:, None] * norm_gain[None, :]).astype(j...  5.08 us
    pallas_call x1, Pallas kernels, paired(): pl.pallas_call(late_kernel, out_shape=(half, half), in_specs=[scalars] +...  4.59 us
  transfers between devices with their start and end apart: 13, of which 6 were waited for; matrix products, arithmetic and copies ran while one was open for 9% of the time, Pallas kernels for 6%

profile of v5, /device:TPU:0, one launch (start us, length us, event | category | flops | bytes accessed | tf_op | source)
XLA Modules:
  0.0 140.6 jit_solution(226117420368741054)
XLA Ops:
  0.6 0.0 copy-start
  0.6 3.0 %collective-permute-start.8 = (bf16[256,4096]{1,0:T(8,128)(2,1)}, bf16[256,4096]{1,0:T(8,128)(2,1)S(1)}, u32[]{:S(2)}, u32[]{:S(2)}) collective-permute-start(bf16[256,4096]{1,0:T(8,128)(2,1)} %param.6), channel_id=1, source_target_pairs={{0,16},{16,0},{1,17},{17,1},{2,18},{18,2},{3,19},{19,3},{4,20},{20... | collective-permute-start | bytes 6291464 | tf_op jit(solution)/shard_map/ppermute | solution.py:358
  3.7 0.0 copy-done
  3.7 0.9 constant_dynamic-slice_fusion
  4.6 0.0 copy-start.3
  4.6 1.6 %collective-permute-start = (bf16[80,4096]{1,0:T(8,128)(2,1)}, bf16[80,4096]{1,0:T(8,128)(2,1)}, u32[]{:S(2)}, u32[]{:S(2)}) collective-permute-start(bf16[80,4096]{1,0:T(8,128)(2,1)} %bitcast.6.mine), channel_id=1, source_target_pairs={{0,4},{2,6},{4,0},{6,2},{8,12},{10,14},{12,8},{14,10},{1,5},{3,7},... | collective-permute-start | bytes 1966088 | tf_op jit(solution)/shard_map/ppermute | solution.py:126
  6.2 1.5 %collective-permute-start.1 = (bf16[80,4096]{1,0:T(8,128)(2,1)}, bf16[80,4096]{1,0:T(8,128)(2,1)}, u32[]{:S(2)}, u32[]{:S(2)}) collective-permute-start(bf16[80,4096]{1,0:T(8,128)(2,1)} %bitcast.6.mine), channel_id=1, source_target_pairs={{4,8},{6,10},{8,4},{10,6},{0,2},{2,0},{12,14},{14,12},{5,9},{7,11}... | collective-permute-start | bytes 1966088 | tf_op jit(solution)/shard_map/ppermute | solution.py:126
  7.6 1.5 %collective-permute-start.2 = (bf16[80,4096]{1,0:T(8,128)(2,1)}, bf16[80,4096]{1,0:T(8,128)(2,1)}, u32[]{:S(2)}, u32[]{:S(2)}) collective-permute-start(bf16[80,4096]{1,0:T(8,128)(2,1)} %bitcast.6.mine), channel_id=1, source_target_pairs={{4,6},{6,4},{8,10},{10,8},{5,7},{7,5},{9,11},{11,9},{20,22},{22,20... | collective-permute-start | bytes 1966088 | tf_op jit(solution)/shard_map/ppermute | solution.py:126
  9.1 2.1 %fusion = f32[256]{0:T(256)S(1)} fusion(bf16[256,4096]{1,0:T(8,128)(2,1)} %param.6), kind=kLoop, calls=%fused_computation.4 | loop fusion | flops 3145472 | bytes 2098176 | tf_op jit(solution)/shard_map/reduce_sum | solution.py:74
  11.2 38.3 %collective-permute-done.8 = bf16[256,4096]{1,0:T(8,128)(2,1)S(1)} collective-permute-done((bf16[256,4096]{1,0:T(8,128)(2,1)}, bf16[256,4096]{1,0:T(8,128)(2,1)S(1)}, u32[]{:S(2)}, u32[]{:S(2)}) %collective-permute-start.8) | collective-permute-done | bytes 2097184 | tf_op jit(solution)/shard_map/ppermute | solution.py:358
  49.5 0.0 copy-start.2
  49.5 0.5 fusion.3
  50.0 2.5 %all-reduce = (f32[256]{0:T(256)S(1)}, f32[256]{0:T(256)S(1)}) all-reduce(f32[256]{0:T(256)S(1)} %fusion, f32[256]{0:T(256)S(1)} %fusion.3), channel_id=1, replica_groups=mesh['parts'=2,'dp'=8,'tensor'=2] {'tensor'}, use_global_device_ids=true, to_apply=%region_3.4 | all-reduce | flops 512 | bytes 4096 | tf_op jit(solution)/shard_map/psum | solution.py:74
  52.5 0.0 copy-done.2
  52.5 0.0 copy-done.3
  52.5 0.0 copy-start.6
  52.5 5.1 %fusion.5 = (bf16[256,4096]{1,0:T(8,128)(2,1)S(1)}, bf16[256,4096]{1,0:T(8,128)(2,1)}) fusion(bf16[256,4096]{1,0:T(8,128)(2,1)} %copy-done.2, f32[256]{0:T(256)S(1)} %get-tuple-element.30, f32[4096]{0:T(1024)S(1)} %copy-done.3, f32[256]{0:T(256)S(1)} %get-tuple-element.31, bf16[256,4096]{1,0:T(8,128)(2,1)} %param.6), kind=kLoop, calls=%fused_computation.9 | loop fusion | flops 8388608 | bytes 8407040 | tf_op jit(solution)/shard_map/convert_element_type | solution.py:79
  57.6 0.0 collective-permute-done.near
  57.6 0.0 collective-permute-done.1.cross
  57.6 0.0 collective-permute-done.2.side
  57.6 1.5 %collective-permute-start.4 = (bf16[80,4096]{1,0:T(8,128)(2,1)}, bf16[80,4096]{1,0:T(8,128)(2,1)}, u32[]{:S(2)}, u32[]{:S(2)}) collective-permute-start(bf16[80,4096]{1,0:T(8,128)(2,1)} %collective-permute-done.near), channel_id=1, source_target_pairs={{4,8},{6,10},{8,4},{10,6},{5,9},{7,11},{9,5},{11,7},{20,24},{22,26... | collective-permute-start | bytes 1966088 | tf_op jit(solution)/shard_map/ppermute | solution.py:126
  59.1 3.9 %collective-permute-start.3 = (bf16[80,4096]{1,0:T(8,128)(2,1)}, bf16[80,4096]{1,0:T(8,128)(2,1)}, u32[]{:S(2)}, u32[]{:S(2)}) collective-permute-start(bf16[80,4096]{1,0:T(8,128)(2,1)} %collective-permute-done.1.cross), channel_id=1, source_target_pairs={{0,4},{2,6},{4,0},{6,2},{8,12},{10,14},{12,8},{14,10},{1,5},{3,7},... | collective-permute-start | bytes 1966088 | tf_op jit(solution)/shard_map/ppermute | solution.py:126
  63.0 3.4 %collective-permute-start.5 = (bf16[80,4096]{1,0:T(8,128)(2,1)}, bf16[80,4096]{1,0:T(8,128)(2,1)}, u32[]{:S(2)}, u32[]{:S(2)}) collective-permute-start(bf16[80,4096]{1,0:T(8,128)(2,1)} %collective-permute-done.near), channel_id=1, source_target_pairs={{0,2},{2,0},{12,14},{14,12},{1,3},{3,1},{13,15},{15,13},{16,18},{1... | collective-permute-start | bytes 1966088 | tf_op jit(solution)/shard_map/ppermute | solution.py:126
  66.4 1.5 %collective-permute-start.6 = (bf16[80,4096]{1,0:T(8,128)(2,1)}, bf16[80,4096]{1,0:T(8,128)(2,1)}, u32[]{:S(2)}, u32[]{:S(2)}) collective-permute-start(bf16[80,4096]{1,0:T(8,128)(2,1)} %collective-permute-done.1.cross), channel_id=1, source_target_pairs={{4,6},{6,4},{8,10},{10,8},{5,7},{7,5},{9,11},{11,9},{20,22},{22,20... | collective-permute-start | bytes 1966088 | tf_op jit(solution)/shard_map/ppermute | solution.py:126
  67.9 0.0 collective-permute-done.4.far
  67.9 1.3 collective-permute-start.9
  69.2 8.9 %collective-permute-done.3.second = bf16[80,4096]{1,0:T(8,128)(2,1)} collective-permute-done((bf16[80,4096]{1,0:T(8,128)(2,1)}, bf16[80,4096]{1,0:T(8,128)(2,1)}, u32[]{:S(2)}, u32[]{:S(2)}) %collective-permute-start.3) | collective-permute-done | bytes 655392 | tf_op jit(solution)/shard_map/ppermute | solution.py:126
  78.1 2.0 %broadcast_select_fusion = bf16[80,4096]{1,0:T(8,128)(2,1)} fusion(bf16[80,4096]{1,0:T(8,128)(2,1)} %collective-permute-done.3.second, bf16[80,4096]{1,0:T(8,128)(2,1)} %collective-permute-done.4.far, pred[]{:T(512)S(6)} %or.3), kind=kLoop, calls=%fused_computation.10 | loop fusion | flops 327680 | bytes 1966081 | tf_op jit(solution)/shard_map/jit(_where)/select_n | solution.py:137
  80.1 1.5 %collective-permute-start.7 = (bf16[80,4096]{1,0:T(8,128)(2,1)}, bf16[80,4096]{1,0:T(8,128)(2,1)}, u32[]{:S(2)}, u32[]{:S(2)}) collective-permute-start(bf16[80,4096]{1,0:T(8,128)(2,1)} %broadcast_select_fusion), channel_id=1, source_target_pairs={{0,2},{2,0},{4,6},{6,4},{8,10},{10,8},{12,14},{14,12},{1,3},{3,1},... | collective-permute-start | bytes 1966088 | tf_op jit(solution)/shard_map/ppermute | solution.py:126
  81.6 12.7 %collective-permute-done.9.piece = bf16[80,4096]{1,0:T(8,128)(2,1)} collective-permute-done((bf16[80,4096]{1,0:T(8,128)(2,1)}, bf16[80,4096]{1,0:T(8,128)(2,1)}, u32[]{:S(2)}, u32[]{:S(2)}) %collective-permute-start.9) | collective-permute-done | bytes 655392 | tf_op jit(solution)/shard_map/ppermute | solution.py:126
  94.2 3.4 %collective-permute-start.10 = (bf16[80,4096]{1,0:T(8,128)(2,1)}, bf16[80,4096]{1,0:T(8,128)(2,1)}, u32[]{:S(2)}, u32[]{:S(2)}) collective-permute-start(bf16[80,4096]{1,0:T(8,128)(2,1)} %collective-permute-done.9.piece), channel_id=1, source_target_pairs={{0,2},{2,0},{12,14},{14,12},{1,3},{3,1},{13,15},{15,13},{16,18},{1... | collective-permute-start | bytes 1966088 | tf_op jit(solution)/shard_map/ppermute | solution.py:126
  97.6 0.0 copy-done.6
  97.7 0.2 reduce-window.13
  97.8 0.1 pad_add_fusion.at
  97.9 0.0 collective-permute-done.5.near_over
  97.9 0.0 collective-permute-done.6.cross_over
  97.9 0.0 collective-permute-done.7.second_over
  97.9 0.0 copy-start.1
  97.9 1.6 %copy-done.1 = bf16[256,4096]{1,0:T(8,128)(2,1)S(1)} copy-done((bf16[256,4096]{1,0:T(8,128)(2,1)S(1)}, bf16[256,4096]{1,0:T(8,128)(2,1)}, u32[]{:S(2)}) %copy-start.1) | copy-done | bytes 2097176
  99.5 7.8 %project_early.1 = (f32[512,384]{1,0:T(8,128)S(1)}, f32[512,384]{1,0:T(8,128)S(1)}) custom-call(s32[4]{0:T(128)S(1)} %pad_add_fusion.at, bf16[80,4096]{1,0:T(8,128)(2,1)} %bitcast.6.mine, bf16[80,4096]{1,0:T(8,128)(2,1)} %collective-permute-done.near, bf16[80,4096]{1,0:T(8,128)(2,1)} %collective-permute-done.1.cross, ...), custom_call_target="tpu_custom_call" | custom-call | flops 2684354560 | bytes 12582912 | tf_op jit(solution)/shard_map/project_early/pallas_call | solution.py:370
  107.4 4.4 %collective-permute-done.10.piece_over = bf16[80,4096]{1,0:T(8,128)(2,1)} collective-permute-done((bf16[80,4096]{1,0:T(8,128)(2,1)}, bf16[80,4096]{1,0:T(8,128)(2,1)}, u32[]{:S(2)}, u32[]{:S(2)}) %collective-permute-start.10) | collective-permute-done | bytes 655392 | tf_op jit(solution)/shard_map/ppermute | solution.py:126
  111.8 0.0 copy-start.5
  111.8 0.0 copy-start.4
  111.8 4.6 %project_late.1 = (f32[512,384]{1,0:T(8,128)S(1)}, f32[512,384]{1,0:T(8,128)S(1)}) custom-call(s32[4]{0:T(128)S(1)} %pad_add_fusion.at, f32[512,384]{1,0:T(8,128)S(1)} %get-tuple-element.15.first_keep, f32[512,384]{1,0:T(8,128)S(1)} %get-tuple-element.16.first_send, ...), custom_call_target="tpu_custom_call", output_to_operand_aliasing={{0}: (1, {}), {1}: (2, {})} | custom-call | flops 1073741824 | bytes 6291456 | tf_op jit(solution)/shard_map/project_late/pallas_call | solution.py:385
  116.4 0.1 collective-permute-start.11
  116.5 0.0 copy-done.5
  116.5 0.1 select_reduce_fusion
  116.6 0.0 copy-done.4
  116.6 0.2 fusion.11
  116.8 0.3 fusion.7
  117.1 1.6 %collective-permute-done.11.other = f32[512,384]{1,0:T(8,128)S(1)} collective-permute-done((f32[512,384]{1,0:T(8,128)S(1)}, f32[512,384]{1,0:T(8,128)S(1)}, u32[]{:S(2)}, u32[]{:S(2)}) %collective-permute-start.11) | collective-permute-done | bytes 786464 | tf_op jit(solution)/shard_map/ppermute | solution.py:408
  118.7 0.9 sum_halves.1
  119.6 5.8 %all-to-all-start = ((bf16[16,32,384]{2,1,0:T(8,128)(2,1)}), bf16[16,32,384]{2,1,0:T(8,128)(2,1)S(1)}, u32[]{:S(2)}, u32[]{:S(2)}) async-start(bf16[16,32,384]{2,1,0:T(8,128)(2,1)} %bitcast.7), calls=%async_computation | async-start | bytes 786432 | tf_op jit(solution)/shard_map/all_to_all | solution.py:409
  125.4 0.1 reduce
  125.5 0.1 pad_maximum_fusion
  125.6 0.1 select_reduce_fusion.2
  125.7 0.1 fusion.6.pick
  125.8 0.1 and_convert_fusion.allowed
  125.9 12.3 %all-to-all-done = bf16[16,32,384]{2,1,0:T(8,128)(2,1)S(1)} async-done(((bf16[16,32,384]{2,1,0:T(8,128)(2,1)}), bf16[16,32,384]{2,1,0:T(8,128)(2,1)S(1)}, u32[]{:S(2)}, u32[]{:S(2)}) %all-to-all-start) | async-done | bytes 393248 | tf_op jit(solution)/shard_map/all_to_all | solution.py:409
  138.3 2.3 %attend.1 = (bf16[128,128]{1,0:T(8,128)(2,1)}, bf16[128,128]{1,0:T(8,128)(2,1)}, bf16[128,512]{1,0:T(8,128)(2,1)}) custom-call(bf16[128,256]{1,0:T(8,128)(2,1)S(1)} %fusion.6.pick, bf16[2,256,384]{2,1,0:T(8,128)(2,1)S(1)} %bitcast.22, f32[128,128]{1,0:T(8,128)S(1)} %get-tuple-element.32.cosine, f32[128,128]{1,0:T(8,128)S(1)} %get-tuple-element.33.sine, ...), custom_call_target="tpu_custom_call" | custom-call | tf_op jit(solution)/shard_map/attend/pallas_call | solution.py:330
  (7 shorter events, 0.1 us)
Async XLA Ops:
  0.6 3.0 %copy-start = (bf16[4096,160]{0,1:T(8,128)(2,1)S(1)}, bf16[4096,160]{0,1:T(8,128)(2,1)}, u32[]{:S(2)}) copy-start(bf16[4096,160]{0,1:T(8,128)(2,1)} %param.8) | copy-start | bytes 3932164
  0.6 48.9 %collective-permute-start.8 = (bf16[256,4096]{1,0:T(8,128)(2,1)}, bf16[256,4096]{1,0:T(8,128)(2,1)S(1)}, u32[]{:S(2)}, u32[]{:S(2)}) collective-permute-start(bf16[256,4096]{1,0:T(8,128)(2,1)} %param.6), channel_id=1, source_target_pairs={{0,16},{16,0},{1,17},{17,1},{2,18},{18,2},{3,19},{19,3},{4,20},{20... | collective-permute-start | bytes 6291464 | tf_op jit(solution)/shard_map/ppermute | solution.py:358
  4.6 47.9 %copy-start.3 = (f32[4096]{0:T(1024)S(1)}, f32[4096]{0:T(1024)}, u32[]{:S(2)}) copy-start(f32[4096]{0:T(1024)} %param.7) | copy-start | bytes 49156
  4.6 53.0 %collective-permute-start = (bf16[80,4096]{1,0:T(8,128)(2,1)}, bf16[80,4096]{1,0:T(8,128)(2,1)}, u32[]{:S(2)}, u32[]{:S(2)}) collective-permute-start(bf16[80,4096]{1,0:T(8,128)(2,1)} %bitcast.6.mine), channel_id=1, source_target_pairs={{0,4},{2,6},{4,0},{6,2},{8,12},{10,14},{12,8},{14,10},{1,5},{3,7},... | collective-permute-start | bytes 1966088 | tf_op jit(solution)/shard_map/ppermute | solution.py:126
  6.2 51.5 %collective-permute-start.1 = (bf16[80,4096]{1,0:T(8,128)(2,1)}, bf16[80,4096]{1,0:T(8,128)(2,1)}, u32[]{:S(2)}, u32[]{:S(2)}) collective-permute-start(bf16[80,4096]{1,0:T(8,128)(2,1)} %bitcast.6.mine), channel_id=1, source_target_pairs={{4,8},{6,10},{8,4},{10,6},{0,2},{2,0},{12,14},{14,12},{5,9},{7,11}... | collective-permute-start | bytes 1966088 | tf_op jit(solution)/shard_map/ppermute | solution.py:126
  7.6 50.0 %collective-permute-start.2 = (bf16[80,4096]{1,0:T(8,128)(2,1)}, bf16[80,4096]{1,0:T(8,128)(2,1)}, u32[]{:S(2)}, u32[]{:S(2)}) collective-permute-start(bf16[80,4096]{1,0:T(8,128)(2,1)} %bitcast.6.mine), channel_id=1, source_target_pairs={{4,6},{6,4},{8,10},{10,8},{5,7},{7,5},{9,11},{11,9},{20,22},{22,20... | collective-permute-start | bytes 1966088 | tf_op jit(solution)/shard_map/ppermute | solution.py:126
  49.5 3.0 %copy-start.2 = (bf16[256,4096]{1,0:T(8,128)(2,1)}, bf16[256,4096]{1,0:T(8,128)(2,1)S(1)}, u32[]{:S(2)}) copy-start(bf16[256,4096]{1,0:T(8,128)(2,1)S(1)} %collective-permute-done.8) | copy-start | bytes 6291460
  52.5 45.1 %copy-start.6 = (s32[1,8]{1,0:T(1,128)S(1)}, s32[1,8]{1,0:T(1,128)}, u32[]{:S(2)}) copy-start(s32[1,8]{1,0:T(1,128)} %param.10) | copy-start | bytes 100
  57.6 10.3 %collective-permute-start.4 = (bf16[80,4096]{1,0:T(8,128)(2,1)}, bf16[80,4096]{1,0:T(8,128)(2,1)}, u32[]{:S(2)}, u32[]{:S(2)}) collective-permute-start(bf16[80,4096]{1,0:T(8,128)(2,1)} %collective-permute-done.near), channel_id=1, source_target_pairs={{4,8},{6,10},{8,4},{10,6},{5,9},{7,11},{9,5},{11,7},{20,24},{22,26... | collective-permute-start | bytes 1966088 | tf_op jit(solution)/shard_map/ppermute | solution.py:126
  59.1 19.0 %collective-permute-start.3 = (bf16[80,4096]{1,0:T(8,128)(2,1)}, bf16[80,4096]{1,0:T(8,128)(2,1)}, u32[]{:S(2)}, u32[]{:S(2)}) collective-permute-start(bf16[80,4096]{1,0:T(8,128)(2,1)} %collective-permute-done.1.cross), channel_id=1, source_target_pairs={{0,4},{2,6},{4,0},{6,2},{8,12},{10,14},{12,8},{14,10},{1,5},{3,7},... | collective-permute-start | bytes 1966088 | tf_op jit(solution)/shard_map/ppermute | solution.py:126
  63.0 35.0 %collective-permute-start.5 = (bf16[80,4096]{1,0:T(8,128)(2,1)}, bf16[80,4096]{1,0:T(8,128)(2,1)}, u32[]{:S(2)}, u32[]{:S(2)}) collective-permute-start(bf16[80,4096]{1,0:T(8,128)(2,1)} %collective-permute-done.near), channel_id=1, source_target_pairs={{0,2},{2,0},{12,14},{14,12},{1,3},{3,1},{13,15},{15,13},{16,18},{1... | collective-permute-start | bytes 1966088 | tf_op jit(solution)/shard_map/ppermute | solution.py:126
  66.4 31.6 %collective-permute-start.6 = (bf16[80,4096]{1,0:T(8,128)(2,1)}, bf16[80,4096]{1,0:T(8,128)(2,1)}, u32[]{:S(2)}, u32[]{:S(2)}) collective-permute-start(bf16[80,4096]{1,0:T(8,128)(2,1)} %collective-permute-done.1.cross), channel_id=1, source_target_pairs={{4,6},{6,4},{8,10},{10,8},{5,7},{7,5},{9,11},{11,9},{20,22},{22,20... | collective-permute-start | bytes 1966088 | tf_op jit(solution)/shard_map/ppermute | solution.py:126
  67.9 26.3 %collective-permute-start.9 = (bf16[80,4096]{1,0:T(8,128)(2,1)}, bf16[80,4096]{1,0:T(8,128)(2,1)}, u32[]{:S(2)}, u32[]{:S(2)}) collective-permute-start(bf16[80,4096]{1,0:T(8,128)(2,1)} %collective-permute-done.4.far), channel_id=1, source_target_pairs={{4,0},{6,2},{8,12},{10,14},{5,1},{7,3},{9,13},{11,15},{20,16},{22,... | collective-permute-start | bytes 1966088 | tf_op jit(solution)/shard_map/ppermute | solution.py:126
  80.1 17.9 %collective-permute-start.7 = (bf16[80,4096]{1,0:T(8,128)(2,1)}, bf16[80,4096]{1,0:T(8,128)(2,1)}, u32[]{:S(2)}, u32[]{:S(2)}) collective-permute-start(bf16[80,4096]{1,0:T(8,128)(2,1)} %broadcast_select_fusion), channel_id=1, source_target_pairs={{0,2},{2,0},{4,6},{6,4},{8,10},{10,8},{12,14},{14,12},{1,3},{3,1},... | collective-permute-start | bytes 1966088 | tf_op jit(solution)/shard_map/ppermute | solution.py:126
  94.2 17.5 %collective-permute-start.10 = (bf16[80,4096]{1,0:T(8,128)(2,1)}, bf16[80,4096]{1,0:T(8,128)(2,1)}, u32[]{:S(2)}, u32[]{:S(2)}) collective-permute-start(bf16[80,4096]{1,0:T(8,128)(2,1)} %collective-permute-done.9.piece), channel_id=1, source_target_pairs={{0,2},{2,0},{12,14},{14,12},{1,3},{3,1},{13,15},{15,13},{16,18},{1... | collective-permute-start | bytes 1966088 | tf_op jit(solution)/shard_map/ppermute | solution.py:126
  97.9 1.6 %copy-start.1 = (bf16[256,4096]{1,0:T(8,128)(2,1)S(1)}, bf16[256,4096]{1,0:T(8,128)(2,1)}, u32[]{:S(2)}) copy-start(bf16[256,4096]{1,0:T(8,128)(2,1)} %get-tuple-element.14.own) | copy-start | bytes 6291460
  111.8 4.7 %copy-start.5 = (s32[1,8]{1,0:T(1,128)S(1)}, s32[1,8]{1,0:T(1,128)}, u32[]{:S(2)}) copy-start(s32[1,8]{1,0:T(1,128)} %param.11) | copy-start | bytes 100
  111.8 4.8 %copy-start.4 = (s32[8,8]{1,0:T(8,128)S(1)}, s32[8,8]{1,0:T(8,128)}, u32[]{:S(2)}) copy-start(s32[8,8]{1,0:T(8,128)} %param.9) | copy-start | bytes 772
  116.4 2.4 %collective-permute-start.11 = (f32[512,384]{1,0:T(8,128)S(1)}, f32[512,384]{1,0:T(8,128)S(1)}, u32[]{:S(2)}, u32[]{:S(2)}) collective-permute-start(f32[512,384]{1,0:T(8,128)S(1)} %get-tuple-element.18), channel_id=1, source_target_pairs={{0,1},{1,0},{2,3},{3,2},{4,5},{5,4},{6,7},{7,6},{8,9},{9,8},{10,11... | collective-permute-start | bytes 2359304 | tf_op jit(solution)/shard_map/ppermute | solution.py:408
  119.6 18.7 %all-to-all-start = ((bf16[16,32,384]{2,1,0:T(8,128)(2,1)}), bf16[16,32,384]{2,1,0:T(8,128)(2,1)S(1)}, u32[]{:S(2)}, u32[]{:S(2)}) async-start(bf16[16,32,384]{2,1,0:T(8,128)(2,1)} %bitcast.7), calls=%async_computation | async-start | bytes 786432 | tf_op jit(solution)/shard_map/all_to_all | solution.py:409

commit v6 on v5

--- a/solution.py
+++ b/solution.py
@@ -69,14 +69,17 @@
     return out.astype(jnp.bfloat16)
 
 
-def scale_of(rows):
+def squares(rows):
     wide = rows.astype(jnp.float32)
-    total = lax.psum(jnp.sum(wide * wide, axis=1), "tensor")
+    return jnp.sum(wide * wide, axis=1)
+
+
+def scale_of(total):
     return lax.rsqrt(total / D + 1e-05)
 
 
 def scaled(rows, scale, norm_gain):
-    return (rows.astype(jnp.float32) * scale[:, None] * norm_gain[None, :]).astype(jnp.bfloat16)
+    return (rows.astype(jnp.float32) * scale * norm_gain).astype(jnp.bfloat16)
 
 
 def product(rows, columns):
@@ -121,14 +124,14 @@
     return [(2 * a + x, 2 * b + x) for a, b in moves for x in range(2)]
 
 
-def gather_line(mine, at_end, normed):
+def gather_line(mine, at_end, total):
     def send(block, pairs):
         return lax.ppermute(block, "dp", pairs)
 
     near = send(mine, alongs(PAIRS))
     cross = send(mine, alongs(ACROSS) + overs(ENDS))
     side = send(mine, overs(MIDDLE))
-    near, cross, side, normed = lax.optimization_barrier((near, cross, side, normed))
+    near, cross, side, total = lax.optimization_barrier((near, cross, side, total))
     second = send(cross, alongs(PAIRS))
     far = send(near, alongs(ACROSS))
     near_over = send(near, overs(ENDS))
@@ -137,12 +140,12 @@
     second_over = send(jnp.where(at_end, second, far), overs(range(4)))
     last_over = send(last, overs(ENDS))
     early = (mine, near, cross, side, second, far, near_over, cross_over, second_over)
-    return early, (last, last_over), normed
+    return early, (last, last_over), total
 
 
 def early_kernel(
     at, mine, near, cross, side, second, far, near_over, cross_over, second_over,
-    own, theirs, keep, send, whole, sems,
+    own, theirs, own_scale, their_scale, gain, keep, send, rows, whole, sems,
 ):
     z, x, part, core = at[0], at[1], at[2], at[3]
     size = mine.shape[0]
@@ -163,6 +166,16 @@
         for copy in found:
             copy.wait()
 
+    count = own.shape[0]
+    step = 2 * BLOCK
+    for k, (source, scale) in enumerate(((own, own_scale), (theirs, their_scale))):
+        index = part if k == 0 else 1 - part
+        for low in range(0, count, step):
+            start = pl.multiple_of(index * count + low, step)
+            rows[pl.ds(start, step), :] = scaled(
+                source[low : low + step, :], scale[low : low + step, :], gain[...]
+            )
+
     at_end = (z == 0) | (z == 3)
     pair = z + 1 - 2 * (z % 2)
 
@@ -188,31 +201,22 @@
             )
         )
 
-    count = own.shape[0]
     share = whole.shape[0] * HQ // (HQ + 2) // 2
-    for k, rows in ((0, own), (1, theirs)):
-        index = part if k == 0 else 1 - part
-        start = pl.multiple_of(index * count, count)
-        halves = [
-            product(rows[...], whole[c * share : (c + 1) * share, :]) for c in range(2)
-        ]
-        rest = product(rows[...], whole[2 * share :, :])
-        for ref in (keep, send):
-            ref[pl.ds(start, count), share:] = rest
-        for t in range(2):
-
-            @pl.when(core == t)
-            def _():
-                keep[pl.ds(start, count), :share] = halves[t]
-                send[pl.ds(start, count), :share] = halves[1 - t]
-
-
-def late_kernel(
-    at, first_keep, first_send, piece, piece_over, own, theirs, keep, send, last, sems
-):
-    z, x, part, core = at[0], at[1], at[2], at[3]
+    halves = [product(rows[...], whole[c * share : (c + 1) * share, :]) for c in range(2)]
+    rest = product(rows[...], whole[2 * share :, :])
+    for ref in (keep, send):
+        ref[:, share:] = rest
+    for t in range(2):
+
+        @pl.when(core == t)
+        def _():
+            keep[:, :share] = halves[t]
+            send[:, :share] = halves[1 - t]
+
+
+def late_kernel(at, first_keep, first_send, piece, piece_over, rows, keep, send, last, sems):
+    z, x, core = at[0], at[1], at[3]
     size = piece.shape[0]
-    count = own.shape[0]
     share = last.shape[0]
     edge = 2 * size
     gap = share - edge
@@ -229,51 +233,44 @@
             copy.start()
         for copy in found:
             copy.wait()
-
-    def blocks():
-        for k, rows in ((0, own), (1, theirs)):
-            index = part if k == 0 else 1 - part
-            start = pl.multiple_of(index * count, count)
-            yield pl.ds(start, count), product(rows[...], last[...])
-
-    def merge(ref, source, place, lanes, block, new):
-        ref[place, lanes] = jnp.where(new, block, source[place, lanes])
+        return product(rows[...], last[...])
+
+    def merge(ref, source, lanes, block, new):
+        ref[:, lanes] = jnp.where(new, block, source[:, lanes])
 
     keep[...] = first_keep[...]
     send[...] = first_send[...]
-    lane = lax.broadcasted_iota(jnp.int32, (count, share), 1)
+    lane = lax.broadcasted_iota(jnp.int32, (rows.shape[0], share), 1)
 
     @pl.when(z == 0)
     def _():
-        fetch(gap)
-        for place, block in blocks():
-            for ref in (keep, send):
-                ref[place, share:] = block[:, share // 2 :]
-            head = block[:, : share // 2]
-            new = lane[:, : share // 2] >= gap
-            lanes = slice(share // 2, share)
-
-            @pl.when(core == 1)
-            def _():
-                merge(keep, first_keep, place, lanes, head, new)
-
-            @pl.when(core == 0)
-            def _():
-                merge(send, first_send, place, lanes, head, new)
+        block = fetch(gap)
+        for ref in (keep, send):
+            ref[:, share:] = block[:, share // 2 :]
+        head = block[:, : share // 2]
+        new = lane[:, : share // 2] >= gap
+        lanes = slice(share // 2, share)
+
+        @pl.when(core == 1)
+        def _():
+            merge(keep, first_keep, lanes, head, new)
+
+        @pl.when(core == 0)
+        def _():
+            merge(send, first_send, lanes, head, new)
 
     @pl.when(z == 3)
     def _():
-        fetch(0)
-        for place, block in blocks():
-            lanes = slice(0, share)
-
-            @pl.when(core == 0)
-            def _():
-                merge(keep, first_keep, place, lanes, block, lane < edge)
-
-            @pl.when(core == 1)
-            def _():
-                merge(send, first_send, place, lanes, block, lane < edge)
+        block = fetch(0)
+        lanes = slice(0, share)
+
+        @pl.when(core == 0)
+        def _():
+            merge(keep, first_keep, lanes, block, lane < edge)
+
+        @pl.when(core == 1)
+        def _():
+            merge(send, first_send, lanes, block, lane < edge)
 
 
 def sum_kernel(keep, other, out):
@@ -356,10 +353,11 @@
     ).reshape(size, depth)
     swap = [(0, 1), (1, 0)]
     raw = lax.ppermute(sent_rows, "parts", swap)
-    normed = scaled(sent_rows, scale_of(sent_rows), norm_gain)
-    theirs = scaled(raw, scale_of(raw), norm_gain)
+    total = lax.psum(squares(sent_rows), "tensor")
     at_end = (group < 2) | (group >= groups - 2)
-    early, late, normed = gather_line(mine, at_end, normed)
+    early, late, total = gather_line(mine, at_end, total)
+    share = squares(raw)
+    their_total = share + lax.ppermute(share, "tensor", swap)
     slots = sent_rows.shape[0]
     width = groups * size
     whole = pl.BlockSpec(memory_space=pltpu.VMEM)
@@ -367,25 +365,33 @@
     scalars = pl.BlockSpec(memory_space=pltpu.SMEM)
     heads = width * HQ // (HQ + 2)
     half = jax.ShapeDtypeStruct((2 * slots, heads // 2 + width - heads), jnp.float32)
-    first = pl.pallas_call(
+    keep, send, rows = pl.pallas_call(
         early_kernel,
-        out_shape=(half, half),
-        in_specs=[scalars] + [anywhere] * 9 + [whole] * 2,
-        out_specs=(whole, whole),
+        out_shape=(half, half, jax.ShapeDtypeStruct((2 * slots, depth), jnp.bfloat16)),
+        in_specs=[scalars] + [anywhere] * 9 + [whole] * 5,
+        out_specs=(whole,) * 3,
         scratch_shapes=[
             pltpu.VMEM((width, depth), jnp.bfloat16),
             pltpu.SemaphoreType.DMA((8,)),
         ],
-        compiler_params=pltpu.CompilerParams(vmem_limit_bytes=24 << 20),
+        compiler_params=pltpu.CompilerParams(vmem_limit_bytes=28 << 20),
         cost_estimate=pl.CostEstimate(
             flops=4 * slots * width * depth, bytes_accessed=12 << 20, transcendentals=0
         ),
         name="project_early",
-    )(at, *early, normed, theirs)
+    )(
+        at,
+        *early,
+        sent_rows,
+        raw,
+        scale_of(total)[:, None],
+        scale_of(their_total)[:, None],
+        norm_gain[None, :],
+    )
     keep, send = pl.pallas_call(
         late_kernel,
         out_shape=(half, half),
-        in_specs=[scalars] + [whole] * 2 + [anywhere] * 2 + [whole] * 2,
+        in_specs=[scalars] + [whole] * 2 + [anywhere] * 2 + [whole],
         out_specs=(whole, whole),
         scratch_shapes=[
             pltpu.VMEM((heads // 2, depth), jnp.bfloat16),
@@ -397,7 +403,7 @@
             flops=2 * slots * heads * depth, bytes_accessed=6 << 20, transcendentals=0
         ),
         name="project_late",
-    )(at, *first, *late, normed, theirs)
+    )(at, keep, send, *late, rows)
     ready = pl.pallas_call(
         sum_kernel,
         out_shape=jax.ShapeDtypeStruct(keep.shape, jnp.bfloat16),
@@ -412,7 +418,8 @@
 
 def single(sent_rows, norm_gain, qkv_weight):
     columns = lax.all_gather(qkv_weight.T, "dp", axis=0, tiled=True)
-    ready = sum_cores(product(scaled(sent_rows, scale_of(sent_rows), norm_gain), columns))
+    scale = scale_of(lax.psum(squares(sent_rows), "tensor"))
+    ready = sum_cores(product(scaled(sent_rows, scale[:, None], norm_gain[None, :]), columns))
     return lax.all_to_all(ready, "dp", 0, 0, tiled=True)
 
 

time: 141 us -> 108 us (0.77)
  waiting for transfers between devices: 78.3 us -> 39.9 us
  local copies, waits for them, and re-layouts: 2.7 us -> 8.34 us
    ppermute x1, waiting for transfers between devices: 38.3 us -> 0.01 us  [paired(): raw = lax.ppermute(sent_rows, 'parts', swap)]
    convert_element_type x1 -> x0, other arithmetic: 5.08 us -> none  [scaled(): (rows.astype(jnp.float32) * scale[:, None] * norm_gain[None, :]).astype(j...]
    unnamed x14 -> x28, local copies, waits for them, and re-layouts: 1.61 us -> 5.83 us
    ppermute x10, starting transfers between devices: 21 us -> 23.3 us  [send(): return lax.ppermute(block, 'dp', pairs)]
    broadcast_in_dim x0 -> x2, local copies, waits for them, and re-layouts: none -> 2.28 us  [the longest x1 1.47 us: paired(): scale_of(their_total)[:, None]]
    reduce_sum x2, other arithmetic: 2.58 us -> 4.76 us  [squares(): return jnp.sum(wide * wide, axis=1)]
    rsqrt x1 -> x2, other arithmetic: 0.01 us -> 1.82 us  [scale_of(): return lax.rsqrt(total / D + 1e-05)]
    all_to_all x1, starting transfers between devices: 5.76 us -> 4.14 us  [paired(): arrived = lax.all_to_all(ready, ('parts', 'dp'), 0, 0, tiled=True)]
  transfers between devices with their start and end apart: 13 -> 14, of which waited for: 6 -> 7; matrix products, arithmetic and copies ran while one was open for 9% -> 12% of each run, Pallas kernels for 6% -> 9%
where the time goes in v6:
time: 108 us
  waiting for transfers between devices  39.9 us (37%)
  starting transfers between devices  29.6 us (27%)
  Pallas kernels  15.8 us (15%)
  other arithmetic  10.8 us (10%)
  local copies, waits for them, and re-layouts  8.34 us (8%)
  blocking collectives  2.46 us (2%)
    ppermute x10, waiting for transfers between devices, send(): return lax.ppermute(block, 'dp', pairs)  25.9 us
    ppermute x10, starting transfers between devices, send(): return lax.ppermute(block, 'dp', pairs)  23.3 us
    all_to_all x1, waiting for transfers between devices, paired(): arrived = lax.all_to_all(ready, ('parts', 'dp'), 0, 0, tiled=True)  12.6 us
    pallas_call x1, Pallas kernels, paired(): pl.pallas_call(early_kernel, out_shape=(half, half, jax.ShapeDtypeStruct(...  9.26 us
    unnamed x28, local copies, waits for them, and re-layouts  5.83 us
    reduce_sum x2, other arithmetic, squares(): return jnp.sum(wide * wide, axis=1)  4.76 us
    all_to_all x1, starting transfers between devices, paired(): arrived = lax.all_to_all(ready, ('parts', 'dp'), 0, 0, tiled=True)  4.14 us
    pallas_call x1, Pallas kernels, paired(): pl.pallas_call(late_kernel, out_shape=(half, half), in_specs=[scalars] +...  3.36 us
  transfers between devices with their start and end apart: 14, of which 7 were waited for; matrix products, arithmetic and copies ran while one was open for 12% of the time, Pallas kernels for 9%

profile of v6, /device:TPU:0, one launch (start us, length us, event | category | flops | bytes accessed | tf_op | source)
XLA Modules:
  0.0 107.7 jit_solution(11541905883273714277)
XLA Ops:
  0.6 0.0 copy-start
  0.6 0.0 copy-start.12
  0.7 1.3 %copy-done = bf16[4096,160]{0,1:T(8,128)(2,1)S(1)} copy-done((bf16[4096,160]{0,1:T(8,128)(2,1)S(1)}, bf16[4096,160]{0,1:T(8,128)(2,1)}, u32[]{:S(2)}) %copy-start) | copy-done | bytes 1310744
  2.0 0.0 copy-start.2
  2.0 3.1 %collective-permute-start = (bf16[80,4096]{1,0:T(8,128)(2,1)S(1)}, bf16[80,4096]{1,0:T(8,128)(2,1)}, u32[]{:S(2)}, u32[]{:S(2)}) collective-permute-start(bf16[80,4096]{1,0:T(8,128)(2,1)S(1)} %bitcast.25), channel_id=1, source_target_pairs={{0,4},{2,6},{4,0},{6,2},{8,12},{10,14},{12,8},{14,10},{1,5},{3,7},... | collective-permute-start | bytes 1966088 | tf_op jit(solution)/shard_map/ppermute | solution.py:129
  5.1 1.5 %collective-permute-start.1 = (bf16[80,4096]{1,0:T(8,128)(2,1)S(1)}, bf16[80,4096]{1,0:T(8,128)(2,1)}, u32[]{:S(2)}, u32[]{:S(2)}) collective-permute-start(bf16[80,4096]{1,0:T(8,128)(2,1)S(1)} %bitcast.26), channel_id=1, source_target_pairs={{4,8},{6,10},{8,4},{10,6},{0,2},{2,0},{12,14},{14,12},{5,9},{7,11}... | collective-permute-start | bytes 1966088 | tf_op jit(solution)/shard_map/ppermute | solution.py:129
  6.6 0.7 collective-permute-start.2
  7.3 1.6 %collective-permute-start.8 = (bf16[256,4096]{1,0:T(8,128)(2,1)}, bf16[256,4096]{1,0:T(8,128)(2,1)}, u32[]{:S(2)}, u32[]{:S(2)}) collective-permute-start(bf16[256,4096]{1,0:T(8,128)(2,1)} %own.1), channel_id=1, source_target_pairs={{0,16},{16,0},{1,17},{17,1},{2,18},{18,2},{3,19},{19,3},{4,20},{20... | collective-permute-start | bytes 6291464 | tf_op jit(solution)/shard_map/ppermute | solution.py:355
  8.9 2.1 %multiply_reduce_fusion.1 = f32[256]{0:T(256)S(1)} fusion(bf16[256,4096]{1,0:T(8,128)(2,1)} %own.1), kind=kLoop, calls=%fused_computation.1 | loop fusion | flops 3145472 | bytes 2098176 | tf_op jit(solution)/shard_map/reduce_sum | solution.py:74
  11.0 2.5 %psum.7 = f32[256]{0:T(256)S(1)} all-reduce(f32[256]{0:T(256)S(1)} %multiply_reduce_fusion.1), channel_id=1, replica_groups=mesh['parts'=2,'dp'=8,'tensor'=2] {'tensor'}, use_global_device_ids=true, to_apply=%region_3.4 | all-reduce | flops 256 | bytes 2048 | tf_op jit(solution)/shard_map/psum | solution.py:356
  13.5 6.5 %collective-permute-done.near = bf16[80,4096]{1,0:T(8,128)(2,1)} collective-permute-done((bf16[80,4096]{1,0:T(8,128)(2,1)S(1)}, bf16[80,4096]{1,0:T(8,128)(2,1)}, u32[]{:S(2)}, u32[]{:S(2)}) %collective-permute-start) | collective-permute-done | bytes 655392 | tf_op jit(solution)/shard_map/ppermute | solution.py:129
  19.9 1.5 %collective-permute-done.1.cross = bf16[80,4096]{1,0:T(8,128)(2,1)} collective-permute-done((bf16[80,4096]{1,0:T(8,128)(2,1)S(1)}, bf16[80,4096]{1,0:T(8,128)(2,1)}, u32[]{:S(2)}, u32[]{:S(2)}) %collective-permute-start.1) | collective-permute-done | bytes 655392 | tf_op jit(solution)/shard_map/ppermute | solution.py:129
  21.4 0.0 collective-permute-done.2.side
  21.4 0.8 copy-done.4
  22.3 1.5 %collective-permute-start.4 = (bf16[80,4096]{1,0:T(8,128)(2,1)}, bf16[80,4096]{1,0:T(8,128)(2,1)}, u32[]{:S(2)}, u32[]{:S(2)}) collective-permute-start(bf16[80,4096]{1,0:T(8,128)(2,1)} %collective-permute-done.near), channel_id=1, source_target_pairs={{4,8},{6,10},{8,4},{10,6},{5,9},{7,11},{9,5},{11,7},{20,24},{22,26... | collective-permute-start | bytes 1966088 | tf_op jit(solution)/shard_map/ppermute | solution.py:129
  23.8 5.4 %collective-permute-start.3 = (bf16[80,4096]{1,0:T(8,128)(2,1)}, bf16[80,4096]{1,0:T(8,128)(2,1)}, u32[]{:S(2)}, u32[]{:S(2)}) collective-permute-start(bf16[80,4096]{1,0:T(8,128)(2,1)} %collective-permute-done.1.cross), channel_id=1, source_target_pairs={{0,4},{2,6},{4,0},{6,2},{8,12},{10,14},{12,8},{14,10},{1,5},{3,7},... | collective-permute-start | bytes 1966088 | tf_op jit(solution)/shard_map/ppermute | solution.py:129
  29.1 0.0 copy-done.12
  29.2 0.7 reduce-window.13
  29.9 0.6 pad_add_fusion.at
  30.4 3.5 %collective-permute-start.5 = (bf16[80,4096]{1,0:T(8,128)(2,1)}, bf16[80,4096]{1,0:T(8,128)(2,1)}, u32[]{:S(2)}, u32[]{:S(2)}) collective-permute-start(bf16[80,4096]{1,0:T(8,128)(2,1)} %collective-permute-done.near), channel_id=1, source_target_pairs={{0,2},{2,0},{12,14},{14,12},{1,3},{3,1},{13,15},{15,13},{16,18},{1... | collective-permute-start | bytes 1966088 | tf_op jit(solution)/shard_map/ppermute | solution.py:129
  34.0 1.5 %collective-permute-start.6 = (bf16[80,4096]{1,0:T(8,128)(2,1)}, bf16[80,4096]{1,0:T(8,128)(2,1)}, u32[]{:S(2)}, u32[]{:S(2)}) collective-permute-start(bf16[80,4096]{1,0:T(8,128)(2,1)} %collective-permute-done.1.cross), channel_id=1, source_target_pairs={{4,6},{6,4},{8,10},{10,8},{5,7},{7,5},{9,11},{11,9},{20,22},{22,20... | collective-permute-start | bytes 1966088 | tf_op jit(solution)/shard_map/ppermute | solution.py:129
  35.5 0.0 collective-permute-done.4.far
  35.5 1.3 %collective-permute-start.10 = (bf16[80,4096]{1,0:T(8,128)(2,1)}, bf16[80,4096]{1,0:T(8,128)(2,1)}, u32[]{:S(2)}, u32[]{:S(2)}) collective-permute-start(bf16[80,4096]{1,0:T(8,128)(2,1)} %collective-permute-done.4.far), channel_id=1, source_target_pairs={{4,0},{6,2},{8,12},{10,14},{5,1},{7,3},{9,13},{11,15},{20,16},{22,... | collective-permute-start | bytes 1966088 | tf_op jit(solution)/shard_map/ppermute | solution.py:129
  36.7 6.1 %collective-permute-done.3.second = bf16[80,4096]{1,0:T(8,128)(2,1)} collective-permute-done((bf16[80,4096]{1,0:T(8,128)(2,1)}, bf16[80,4096]{1,0:T(8,128)(2,1)}, u32[]{:S(2)}, u32[]{:S(2)}) %collective-permute-start.3) | collective-permute-done | bytes 655392 | tf_op jit(solution)/shard_map/ppermute | solution.py:129
  42.8 2.0 %broadcast_select_fusion = bf16[80,4096]{1,0:T(8,128)(2,1)} fusion(bf16[80,4096]{1,0:T(8,128)(2,1)} %collective-permute-done.3.second, bf16[80,4096]{1,0:T(8,128)(2,1)} %collective-permute-done.4.far, pred[]{:T(512)S(6)} %or.3), kind=kLoop, calls=%fused_computation.2 | loop fusion | flops 327680 | bytes 1966081 | tf_op jit(solution)/shard_map/jit(_where)/select_n | solution.py:140
  44.8 1.5 %collective-permute-start.7 = (bf16[80,4096]{1,0:T(8,128)(2,1)}, bf16[80,4096]{1,0:T(8,128)(2,1)}, u32[]{:S(2)}, u32[]{:S(2)}) collective-permute-start(bf16[80,4096]{1,0:T(8,128)(2,1)} %broadcast_select_fusion), channel_id=1, source_target_pairs={{0,2},{2,0},{4,6},{6,4},{8,10},{10,8},{12,14},{14,12},{1,3},{3,1},... | collective-permute-start | bytes 1966088 | tf_op jit(solution)/shard_map/ppermute | solution.py:129
  46.3 11.9 %collective-permute-done.10.piece = bf16[80,4096]{1,0:T(8,128)(2,1)} collective-permute-done((bf16[80,4096]{1,0:T(8,128)(2,1)}, bf16[80,4096]{1,0:T(8,128)(2,1)}, u32[]{:S(2)}, u32[]{:S(2)}) %collective-permute-start.10) | collective-permute-done | bytes 655392 | tf_op jit(solution)/shard_map/ppermute | solution.py:129
  58.2 3.4 %collective-permute-start.11 = (bf16[80,4096]{1,0:T(8,128)(2,1)}, bf16[80,4096]{1,0:T(8,128)(2,1)}, u32[]{:S(2)}, u32[]{:S(2)}) collective-permute-start(bf16[80,4096]{1,0:T(8,128)(2,1)} %collective-permute-done.10.piece), channel_id=1, source_target_pairs={{0,2},{2,0},{12,14},{14,12},{1,3},{3,1},{13,15},{15,13},{16,18},{1... | collective-permute-start | bytes 1966088 | tf_op jit(solution)/shard_map/ppermute | solution.py:129
  61.6 0.0 collective-permute-done.8.theirs
  61.6 2.6 %multiply_reduce_fusion = f32[256]{0:T(256)} fusion(bf16[256,4096]{1,0:T(8,128)(2,1)} %collective-permute-done.8.theirs), kind=kLoop, calls=%fused_computation | loop fusion | flops 3145472 | bytes 2098176 | tf_op jit(solution)/shard_map/reduce_sum | solution.py:74
  64.2 0.0 collective-permute-start.9
  64.3 0.6 add_rsqrt_fusion.1
  64.8 0.8 copy.16.own_scale
  65.6 0.1 collective-permute-done.9
  65.7 1.3 %add_rsqrt_fusion = f32[256]{0:T(256)} fusion(f32[256]{0:T(256)} %multiply_reduce_fusion, f32[256]{0:T(256)} %collective-permute-done.9), kind=kLoop, calls=%fused_computation.20 | loop fusion | flops 768 | bytes 3072 | tf_op jit(solution)/shard_map/rsqrt | solution.py:78
  67.0 1.5 %copy.17.their_scale = f32[256,1]{1,0:T(8,128)} copy(f32[256,1]{0,1:T(1,128)} %bitcast.31) | data formatting | bytes 2048 | tf_op jit(solution)/shard_map/broadcast_in_dim | solution.py:388
  68.5 0.0 collective-permute-done.5.near_over
  68.5 0.0 collective-permute-done.6.cross_over
  68.5 0.0 collective-permute-done.7.second_over
  68.5 1.1 %copy-done.3 = bf16[5,1,16,4096]{3,2,1,0:T(8,128)(2,1)S(1)} copy-done((bf16[5,1,16,4096]{3,2,1,0:T(8,128)(2,1)S(1)}, bf16[5,1,16,4096]{3,2,1,0:T(8,128)(2,1)}, u32[]{:S(2)}) %copy-start.3) | copy-done | bytes 655384
  69.6 1.1 %copy-done.5 = bf16[80,4096]{1,0:T(8,128)(2,1)S(1)} copy-done((bf16[80,4096]{1,0:T(8,128)(2,1)S(1)}, bf16[80,4096]{1,0:T(8,128)(2,1)}, u32[]{:S(2)}) %copy-start.5) | copy-done | bytes 655384
  70.7 0.9 copy-done.6
  71.6 0.6 copy-done.8
  72.1 9.3 %project_early.1 = (f32[512,384]{1,0:T(8,128)S(1)}, f32[512,384]{1,0:T(8,128)S(1)}, bf16[512,4096]{1,0:T(8,128)(2,1)S(1)}) custom-call(s32[4]{0:T(128)S(1)} %copy-done.8, bf16[80,4096]{1,0:T(8,128)(2,1)S(1)} %bitcast.28, bf16[80,4096]{1,0:T(8,128)(2,1)} %collective-permute-done.near, bf16[80,4096]{1,0:T(8,128)(2,1)} %collective-permute-done.1.cross, ...), custom_call_target="tpu_custom_call" | custom-call | flops 2684354560 | bytes 12582912 | tf_op jit(solution)/shard_map/project_early/pallas_call | solution.py:368
  81.4 0.0 collective-permute-done.11.piece_over
  81.4 0.0 copy-start.13
  81.4 0.0 copy-start.10
  81.5 0.0 copy-start.9
  81.5 3.4 %project_late.1 = (f32[512,384]{1,0:T(8,128)S(1)}, f32[512,384]{1,0:T(8,128)S(1)}) custom-call(s32[4]{0:T(128)S(1)} %copy-done.8, f32[512,384]{1,0:T(8,128)S(1)} %get-tuple-element.16.first_keep, f32[512,384]{1,0:T(8,128)S(1)} %get-tuple-element.17.first_send, ...), custom_call_target="tpu_custom_call", output_to_operand_aliasing={{0}: (1, {}), {1}: (2, {})} | custom-call | flops 1073741824 | bytes 6291456 | tf_op jit(solution)/shard_map/project_late/pallas_call | solution.py:391
  84.8 0.5 collective-permute-start.12
  85.3 0.0 copy-done.11
  85.4 0.1 select_reduce_fusion
  85.5 0.2 fusion.5
  85.7 0.3 fusion.1
  86.0 1.3 %collective-permute-done.12.other = f32[512,384]{1,0:T(8,128)S(1)} collective-permute-done((f32[512,384]{1,0:T(8,128)S(1)}, f32[512,384]{1,0:T(8,128)S(1)}, u32[]{:S(2)}, u32[]{:S(2)}) %collective-permute-start.12) | collective-permute-done | bytes 786464 | tf_op jit(solution)/shard_map/ppermute | solution.py:414
  87.2 0.9 sum_halves.1
  88.1 4.1 %all-to-all-start = ((bf16[16,32,384]{2,1,0:T(8,128)(2,1)}), bf16[16,32,384]{2,1,0:T(8,128)(2,1)S(1)}, u32[]{:S(2)}, u32[]{:S(2)}) async-start(bf16[16,32,384]{2,1,0:T(8,128)(2,1)} %bitcast.10), calls=%async_computation | async-start | bytes 786432 | tf_op jit(solution)/shard_map/all_to_all | solution.py:415
  92.3 0.1 reduce
  92.4 0.1 pad_maximum_fusion
  92.5 0.1 select_reduce_fusion.2
  92.6 0.1 fusion.pick
  92.7 0.1 and_convert_fusion.allowed
  92.8 12.6 %all-to-all-done = bf16[16,32,384]{2,1,0:T(8,128)(2,1)S(1)} async-done(((bf16[16,32,384]{2,1,0:T(8,128)(2,1)}), bf16[16,32,384]{2,1,0:T(8,128)(2,1)S(1)}, u32[]{:S(2)}, u32[]{:S(2)}) %all-to-all-start) | async-done | bytes 393248 | tf_op jit(solution)/shard_map/all_to_all | solution.py:415
  105.4 2.3 %attend.1 = (bf16[128,128]{1,0:T(8,128)(2,1)}, bf16[128,128]{1,0:T(8,128)(2,1)}, bf16[128,512]{1,0:T(8,128)(2,1)}) custom-call(bf16[128,256]{1,0:T(8,128)(2,1)S(1)} %fusion.pick, bf16[2,256,384]{2,1,0:T(8,128)(2,1)S(1)} %bitcast.29, f32[128,128]{1,0:T(8,128)S(1)} %get-tuple-element.28.cosine, f32[128,128]{1,0:T(8,128)S(1)} %get-tuple-element.29.sine, ...), custom_call_target="tpu_custom_call" | custom-call | tf_op jit(solution)/shard_map/attend/pallas_call | solution.py:327
  (21 shorter events, 0.1 us)
Async XLA Ops:
  0.6 1.3 %copy-start = (bf16[4096,160]{0,1:T(8,128)(2,1)S(1)}, bf16[4096,160]{0,1:T(8,128)(2,1)}, u32[]{:S(2)}) copy-start(bf16[4096,160]{0,1:T(8,128)(2,1)} %param.8) | copy-start | bytes 3932164
  0.6 28.5 %copy-start.12 = (s32[1,8]{1,0:T(1,128)S(1)}, s32[1,8]{1,0:T(1,128)}, u32[]{:S(2)}) copy-start(s32[1,8]{1,0:T(1,128)} %param.10) | copy-start | bytes 100
  2.0 27.9 %copy-start.2 = (bf16[5,1,16,4096]{3,2,1,0:T(8,128)(2,1)}, bf16[5,1,16,4096]{3,2,1,0:T(8,128)(2,1)S(1)}, u32[]{:S(2)}) copy-start(bf16[5,1,16,4096]{3,2,1,0:T(8,128)(2,1)S(1)} %constant_dynamic-slice_fusion) | copy-start | bytes 1966084
  2.0 17.9 %collective-permute-start = (bf16[80,4096]{1,0:T(8,128)(2,1)S(1)}, bf16[80,4096]{1,0:T(8,128)(2,1)}, u32[]{:S(2)}, u32[]{:S(2)}) collective-permute-start(bf16[80,4096]{1,0:T(8,128)(2,1)S(1)} %bitcast.25), channel_id=1, source_target_pairs={{0,4},{2,6},{4,0},{6,2},{8,12},{10,14},{12,8},{14,10},{1,5},{3,7},... | collective-permute-start | bytes 1966088 | tf_op jit(solution)/shard_map/ppermute | solution.py:129
  5.1 16.3 %collective-permute-start.1 = (bf16[80,4096]{1,0:T(8,128)(2,1)S(1)}, bf16[80,4096]{1,0:T(8,128)(2,1)}, u32[]{:S(2)}, u32[]{:S(2)}) collective-permute-start(bf16[80,4096]{1,0:T(8,128)(2,1)S(1)} %bitcast.26), channel_id=1, source_target_pairs={{4,8},{6,10},{8,4},{10,6},{0,2},{2,0},{12,14},{14,12},{5,9},{7,11}... | collective-permute-start | bytes 1966088 | tf_op jit(solution)/shard_map/ppermute | solution.py:129
  6.6 14.8 %collective-permute-start.2 = (bf16[80,4096]{1,0:T(8,128)(2,1)S(1)}, bf16[80,4096]{1,0:T(8,128)(2,1)S(1)}, u32[]{:S(2)}, u32[]{:S(2)}) collective-permute-start(bf16[80,4096]{1,0:T(8,128)(2,1)S(1)} %bitcast.27), channel_id=1, source_target_pairs={{4,6},{6,4},{8,10},{10,8},{5,7},{7,5},{9,11},{11,9},{20,22},{22,20... | collective-permute-start | bytes 1966088 | tf_op jit(solution)/shard_map/ppermute | solution.py:129
  7.3 54.3 %collective-permute-start.8 = (bf16[256,4096]{1,0:T(8,128)(2,1)}, bf16[256,4096]{1,0:T(8,128)(2,1)}, u32[]{:S(2)}, u32[]{:S(2)}) collective-permute-start(bf16[256,4096]{1,0:T(8,128)(2,1)} %own.1), channel_id=1, source_target_pairs={{0,16},{16,0},{1,17},{17,1},{2,18},{18,2},{3,19},{19,3},{4,20},{20... | collective-permute-start | bytes 6291464 | tf_op jit(solution)/shard_map/ppermute | solution.py:355
  21.4 0.8 copy-start.4
  22.3 13.2 %collective-permute-start.4 = (bf16[80,4096]{1,0:T(8,128)(2,1)}, bf16[80,4096]{1,0:T(8,128)(2,1)}, u32[]{:S(2)}, u32[]{:S(2)}) collective-permute-start(bf16[80,4096]{1,0:T(8,128)(2,1)} %collective-permute-done.near), channel_id=1, source_target_pairs={{4,8},{6,10},{8,4},{10,6},{5,9},{7,11},{9,5},{11,7},{20,24},{22,26... | collective-permute-start | bytes 1966088 | tf_op jit(solution)/shard_map/ppermute | solution.py:129
  23.8 19.1 %collective-permute-start.3 = (bf16[80,4096]{1,0:T(8,128)(2,1)}, bf16[80,4096]{1,0:T(8,128)(2,1)}, u32[]{:S(2)}, u32[]{:S(2)}) collective-permute-start(bf16[80,4096]{1,0:T(8,128)(2,1)} %collective-permute-done.1.cross), channel_id=1, source_target_pairs={{0,4},{2,6},{4,0},{6,2},{8,12},{10,14},{12,8},{14,10},{1,5},{3,7},... | collective-permute-start | bytes 1966088 | tf_op jit(solution)/shard_map/ppermute | solution.py:129
  30.4 38.0 %copy-start.1 = (bf16[256,4096]{1,0:T(8,128)(2,1)S(1)}, bf16[256,4096]{1,0:T(8,128)(2,1)}, u32[]{:S(2)}) copy-start(bf16[256,4096]{1,0:T(8,128)(2,1)} %own.1) | copy-start | bytes 6291460
  30.4 38.1 %copy-start.7 = (f32[4096]{0:T(1024)S(1)}, f32[4096]{0:T(1024)}, u32[]{:S(2)}) copy-start(f32[4096]{0:T(1024)} %param.7) | copy-start | bytes 49156
  30.4 38.0 %collective-permute-start.5 = (bf16[80,4096]{1,0:T(8,128)(2,1)}, bf16[80,4096]{1,0:T(8,128)(2,1)}, u32[]{:S(2)}, u32[]{:S(2)}) collective-permute-start(bf16[80,4096]{1,0:T(8,128)(2,1)} %collective-permute-done.near), channel_id=1, source_target_pairs={{0,2},{2,0},{12,14},{14,12},{1,3},{3,1},{13,15},{15,13},{16,18},{1... | collective-permute-start | bytes 1966088 | tf_op jit(solution)/shard_map/ppermute | solution.py:129
  34.0 34.5 %collective-permute-start.6 = (bf16[80,4096]{1,0:T(8,128)(2,1)}, bf16[80,4096]{1,0:T(8,128)(2,1)}, u32[]{:S(2)}, u32[]{:S(2)}) collective-permute-start(bf16[80,4096]{1,0:T(8,128)(2,1)} %collective-permute-done.1.cross), channel_id=1, source_target_pairs={{4,6},{6,4},{8,10},{10,8},{5,7},{7,5},{9,11},{11,9},{20,22},{22,20... | collective-permute-start | bytes 1966088 | tf_op jit(solution)/shard_map/ppermute | solution.py:129
  35.5 22.7 %collective-permute-start.10 = (bf16[80,4096]{1,0:T(8,128)(2,1)}, bf16[80,4096]{1,0:T(8,128)(2,1)}, u32[]{:S(2)}, u32[]{:S(2)}) collective-permute-start(bf16[80,4096]{1,0:T(8,128)(2,1)} %collective-permute-done.4.far), channel_id=1, source_target_pairs={{4,0},{6,2},{8,12},{10,14},{5,1},{7,3},{9,13},{11,15},{20,16},{22,... | collective-permute-start | bytes 1966088 | tf_op jit(solution)/shard_map/ppermute | solution.py:129
  44.8 23.7 %collective-permute-start.7 = (bf16[80,4096]{1,0:T(8,128)(2,1)}, bf16[80,4096]{1,0:T(8,128)(2,1)}, u32[]{:S(2)}, u32[]{:S(2)}) collective-permute-start(bf16[80,4096]{1,0:T(8,128)(2,1)} %broadcast_select_fusion), channel_id=1, source_target_pairs={{0,2},{2,0},{4,6},{6,4},{8,10},{10,8},{12,14},{14,12},{1,3},{3,1},... | collective-permute-start | bytes 1966088 | tf_op jit(solution)/shard_map/ppermute | solution.py:129
  58.2 23.2 %collective-permute-start.11 = (bf16[80,4096]{1,0:T(8,128)(2,1)}, bf16[80,4096]{1,0:T(8,128)(2,1)}, u32[]{:S(2)}, u32[]{:S(2)}) collective-permute-start(bf16[80,4096]{1,0:T(8,128)(2,1)} %collective-permute-done.10.piece), channel_id=1, source_target_pairs={{0,2},{2,0},{12,14},{14,12},{1,3},{3,1},{13,15},{15,13},{16,18},{1... | collective-permute-start | bytes 1966088 | tf_op jit(solution)/shard_map/ppermute | solution.py:129
  64.2 1.5 %collective-permute-start.9 = (f32[256]{0:T(256)}, f32[256]{0:T(256)}, u32[]{:S(2)}, u32[]{:S(2)}) collective-permute-start(f32[256]{0:T(256)} %multiply_reduce_fusion), channel_id=1, source_target_pairs={{0,1},{1,0},{2,3},{3,2},{4,5},{5,4},{6,7},{7,6},{8,9},{9,8},{10,11... | collective-permute-start | bytes 3080 | tf_op jit(solution)/shard_map/ppermute | solution.py:360
  68.5 1.1 %copy-start.3 = (bf16[5,1,16,4096]{3,2,1,0:T(8,128)(2,1)S(1)}, bf16[5,1,16,4096]{3,2,1,0:T(8,128)(2,1)}, u32[]{:S(2)}) copy-start(bf16[5,1,16,4096]{3,2,1,0:T(8,128)(2,1)} %copy-done.2) | copy-start | bytes 1966084
  69.6 1.1 %copy-start.5 = (bf16[80,4096]{1,0:T(8,128)(2,1)S(1)}, bf16[80,4096]{1,0:T(8,128)(2,1)}, u32[]{:S(2)}) copy-start(bf16[80,4096]{1,0:T(8,128)(2,1)} %copy-done.4) | copy-start | bytes 1966084
  70.7 0.9 copy-start.6
  71.6 0.6 copy-start.8
  81.4 3.9 %copy-start.11 = (s32[8,1]{0,1:T(1,128)S(1)}, s32[8,1]{0,1:T(1,128)}, u32[]{:S(2)}) copy-start(s32[8,1]{0,1:T(1,128)} %reduce-window.13) | copy-start | bytes 100
  81.4 3.9 %copy-start.13 = (s32[1,8]{1,0:T(1,128)S(1)}, s32[1,8]{1,0:T(1,128)}, u32[]{:S(2)}) copy-start(s32[1,8]{1,0:T(1,128)} %param.10) | copy-start | bytes 100
  81.4 3.9 %copy-start.10 = (s32[1,8]{1,0:T(1,128)S(1)}, s32[1,8]{1,0:T(1,128)}, u32[]{:S(2)}) copy-start(s32[1,8]{1,0:T(1,128)} %param.11) | copy-start | bytes 100
  81.5 4.0 %copy-start.9 = (s32[8,8]{1,0:T(8,128)S(1)}, s32[8,8]{1,0:T(8,128)}, u32[]{:S(2)}) copy-start(s32[8,8]{1,0:T(8,128)} %param.9) | copy-start | bytes 772
  84.8 2.4 %collective-permute-start.12 = (f32[512,384]{1,0:T(8,128)S(1)}, f32[512,384]{1,0:T(8,128)S(1)}, u32[]{:S(2)}, u32[]{:S(2)}) collective-permute-start(f32[512,384]{1,0:T(8,128)S(1)} %get-tuple-element.20), channel_id=1, source_target_pairs={{0,1},{1,0},{2,3},{3,2},{4,5},{5,4},{6,7},{7,6},{8,9},{9,8},{10,11... | collective-permute-start | bytes 2359304 | tf_op jit(solution)/shard_map/ppermute | solution.py:414
  88.1 17.3 %all-to-all-start = ((bf16[16,32,384]{2,1,0:T(8,128)(2,1)}), bf16[16,32,384]{2,1,0:T(8,128)(2,1)S(1)}, u32[]{:S(2)}, u32[]{:S(2)}) async-start(bf16[16,32,384]{2,1,0:T(8,128)(2,1)} %bitcast.10), calls=%async_computation | async-start | bytes 786432 | tf_op jit(solution)/shard_map/all_to_all | solution.py:415

commit v7 on v6

--- a/solution.py
+++ b/solution.py
@@ -124,57 +124,57 @@
     return [(2 * a + x, 2 * b + x) for a, b in moves for x in range(2)]
 
 
-def gather_line(mine, at_end, total):
+def gather_line(mine, at_end, total, ahead):
     def send(block, pairs):
         return lax.ppermute(block, "dp", pairs)
 
     near = send(mine, alongs(PAIRS))
     cross = send(mine, alongs(ACROSS) + overs(ENDS))
     side = send(mine, overs(MIDDLE))
-    near, cross, side, total = lax.optimization_barrier((near, cross, side, total))
+    near, cross, total, ahead = lax.optimization_barrier((near, cross, total, ahead))
     second = send(cross, alongs(PAIRS))
     far = send(near, alongs(ACROSS))
-    near_over = send(near, overs(ENDS))
-    cross_over = send(cross, overs(MIDDLE))
+    near_next, cross_next, side = lax.optimization_barrier((near, cross, side))
+    near_over = send(near_next, overs(ENDS))
+    cross_over = send(cross_next, overs(MIDDLE))
+    far, total = lax.optimization_barrier((far, total))
     last = send(far, alongs(OUTWARD))
     second_over = send(jnp.where(at_end, second, far), overs(range(4)))
     last_over = send(last, overs(ENDS))
     early = (mine, near, cross, side, second, far, near_over, cross_over, second_over)
-    return early, (last, last_over), total
+    return early, (last, last_over), total, ahead
 
 
 def early_kernel(
     at, mine, near, cross, side, second, far, near_over, cross_over, second_over,
-    own, theirs, own_scale, their_scale, gain, keep, send, rows, whole, sems,
+    own, ahead, behind, own_scale, their_scale, gain, keep, send, rows, whole,
 ):
     z, x, part, core = at[0], at[1], at[2], at[3]
     size = mine.shape[0]
 
     def place(pairs):
-        found = []
-        for k, (where, pieces) in enumerate(pairs):
+        for where, pieces in pairs:
             for j, piece in enumerate(pieces):
                 column = x if j == 0 else 1 - x
                 start = pl.multiple_of((2 * where + column) * size, BLOCK)
-                found.append(
-                    pltpu.make_async_copy(
-                        piece, whole.at[pl.ds(start, size)], sems.at[2 * k + j]
-                    )
+                whole[pl.ds(start, size), :] = piece[...]
+
+    count = own.shape[0]
+    for index, sources, scale in (
+        (part, (own,), own_scale),
+        (1 - part, (ahead, behind), their_scale),
+    ):
+        upright = jnp.broadcast_to(scale[...], (HD, count)).T[:, :1]
+        done = 0
+        for source in sources:
+            for low in range(0, source.shape[0], BLOCK):
+                start = pl.multiple_of(index * count + done + low, BLOCK)
+                rows[pl.ds(start, BLOCK), :] = scaled(
+                    source[low : low + BLOCK, :],
+                    upright[done + low : done + low + BLOCK, :],
+                    gain[...],
                 )
-        for copy in found:
-            copy.start()
-        for copy in found:
-            copy.wait()
-
-    count = own.shape[0]
-    step = 2 * BLOCK
-    for k, (source, scale) in enumerate(((own, own_scale), (theirs, their_scale))):
-        index = part if k == 0 else 1 - part
-        for low in range(0, count, step):
-            start = pl.multiple_of(index * count + low, step)
-            rows[pl.ds(start, step), :] = scaled(
-                source[low : low + step, :], scale[low : low + step, :], gain[...]
-            )
+            done += source.shape[0]
 
     at_end = (z == 0) | (z == 3)
     pair = z + 1 - 2 * (z % 2)
@@ -214,7 +214,7 @@
             send[:, :share] = halves[1 - t]
 
 
-def late_kernel(at, first_keep, first_send, piece, piece_over, rows, keep, send, last, sems):
+def late_kernel(at, first_keep, first_send, piece, piece_over, rows, keep, send, last):
     z, x, core = at[0], at[1], at[3]
     size = piece.shape[0]
     share = last.shape[0]
@@ -222,17 +222,10 @@
     gap = share - edge
 
     def fetch(offset):
-        found = []
         for side, ref in ((0, piece), (1, piece_over)):
             where = x if side == 0 else 1 - x
             start = pl.multiple_of(offset + where * size, BLOCK)
-            found.append(
-                pltpu.make_async_copy(ref, last.at[pl.ds(start, size)], sems.at[side])
-            )
-        for copy in found:
-            copy.start()
-        for copy in found:
-            copy.wait()
+            last[pl.ds(start, size), :] = ref[...]
         return product(rows[...], last[...])
 
     def merge(ref, source, lanes, block, new):
@@ -352,28 +345,25 @@
         turned.reshape(count, 2, BLOCK, depth), part, 1, False
     ).reshape(size, depth)
     swap = [(0, 1), (1, 0)]
-    raw = lax.ppermute(sent_rows, "parts", swap)
+    ahead = lax.ppermute(sent_rows[:size], "parts", swap)
+    behind = lax.ppermute(sent_rows[size:], "parts", swap)
     total = lax.psum(squares(sent_rows), "tensor")
     at_end = (group < 2) | (group >= groups - 2)
-    early, late, total = gather_line(mine, at_end, total)
-    share = squares(raw)
-    their_total = share + lax.ppermute(share, "tensor", swap)
+    early, late, total, ahead = gather_line(mine, at_end, total, ahead)
+    scale = scale_of(total)
+    their_scale = lax.ppermute(scale, "parts", swap)
     slots = sent_rows.shape[0]
     width = groups * size
     whole = pl.BlockSpec(memory_space=pltpu.VMEM)
-    anywhere = pl.BlockSpec(memory_space=pl.ANY)
     scalars = pl.BlockSpec(memory_space=pltpu.SMEM)
     heads = width * HQ // (HQ + 2)
     half = jax.ShapeDtypeStruct((2 * slots, heads // 2 + width - heads), jnp.float32)
     keep, send, rows = pl.pallas_call(
         early_kernel,
         out_shape=(half, half, jax.ShapeDtypeStruct((2 * slots, depth), jnp.bfloat16)),
-        in_specs=[scalars] + [anywhere] * 9 + [whole] * 5,
+        in_specs=[scalars] + [whole] * 15,
         out_specs=(whole,) * 3,
-        scratch_shapes=[
-            pltpu.VMEM((width, depth), jnp.bfloat16),
-            pltpu.SemaphoreType.DMA((8,)),
-        ],
+        scratch_shapes=[pltpu.VMEM((width, depth), jnp.bfloat16)],
         compiler_params=pltpu.CompilerParams(vmem_limit_bytes=28 << 20),
         cost_estimate=pl.CostEstimate(
             flops=4 * slots * width * depth, bytes_accessed=12 << 20, transcendentals=0
@@ -383,20 +373,18 @@
         at,
         *early,
         sent_rows,
-        raw,
-        scale_of(total)[:, None],
-        scale_of(their_total)[:, None],
+        ahead,
+        behind,
+        scale[None, :],
+        their_scale[None, :],
         norm_gain[None, :],
     )
     keep, send = pl.pallas_call(
         late_kernel,
         out_shape=(half, half),
-        in_specs=[scalars] + [whole] * 2 + [anywhere] * 2 + [whole],
+        in_specs=[scalars] + [whole] * 5,
         out_specs=(whole, whole),
-        scratch_shapes=[
-            pltpu.VMEM((heads // 2, depth), jnp.bfloat16),
-            pltpu.SemaphoreType.DMA((2,)),
-        ],
+        scratch_shapes=[pltpu.VMEM((heads // 2, depth), jnp.bfloat16)],
         input_output_aliases={1: 0, 2: 1},
         compiler_params=pltpu.CompilerParams(vmem_limit_bytes=16 << 20),
         cost_estimate=pl.CostEstimate(

time: 108 us -> 103 us (0.954)
  other arithmetic: 10.8 us -> 3.7 us
  waiting for transfers between devices: 39.9 us -> 45.6 us
  local copies, waits for them, and re-layouts: 8.34 us -> 5.59 us
  Pallas kernels: 15.8 us -> 14.3 us
    ppermute x2 -> x3, waiting for transfers between devices: 0.1 us -> 4.97 us  [the longest x1 3.18 us: paired(): ahead = lax.ppermute(sent_rows[:size], 'parts', swap)]
    unnamed x28 -> x12, local copies, waits for them, and re-layouts: 5.83 us -> 1.32 us
    reduce_sum x2 -> x1, other arithmetic: 4.76 us -> 0.49 us  [squares(): return jnp.sum(wide * wide, axis=1)]
    slice x0 -> x2, local copies, waits for them, and re-layouts: none -> 3.18 us  [the longest x1 1.97 us: paired(): ahead = lax.ppermute(sent_rows[:size], 'parts', swap)]
    ppermute x2 -> x3, starting transfers between devices: 1.59 us -> 4.62 us  [the longest x1 1.58 us: paired(): their_scale = lax.ppermute(scale, 'parts', swap)]
    broadcast_in_dim x2 -> x0, local copies, waits for them, and re-layouts: 2.28 us -> none  [the longest x1 1.47 us: paired(): scale_of(their_total)[:, None]]
    ppermute x10, starting transfers between devices: 23.3 us -> 21.1 us  [send(): return lax.ppermute(block, 'dp', pairs)]
    rsqrt x2 -> x1, other arithmetic: 1.82 us -> 0.01 us  [scale_of(): return lax.rsqrt(total / D + 1e-05)]
  transfers between devices with their start and end apart: 14 -> 15, of which waited for: 7 -> 10; matrix products, arithmetic and copies ran while one was open for 12% -> 7% of each run, Pallas kernels for 9% -> 8%
where the time goes in v7:
time: 103 us
  waiting for transfers between devices  45.6 us (44%)
  starting transfers between devices  30.4 us (30%)
  Pallas kernels  14.3 us (14%)
  local copies, waits for them, and re-layouts  5.59 us (5%)
  other arithmetic  3.7 us (4%)
  blocking collectives  2.46 us (2%)
    ppermute x10, waiting for transfers between devices, send(): return lax.ppermute(block, 'dp', pairs)  26.6 us
    ppermute x10, starting transfers between devices, send(): return lax.ppermute(block, 'dp', pairs)  21.1 us
    all_to_all x1, waiting for transfers between devices, paired(): arrived = lax.all_to_all(ready, ('parts', 'dp'), 0, 0, tiled=True)  12.3 us
    pallas_call x1, Pallas kernels, paired(): pl.pallas_call(early_kernel, out_shape=(half, half, jax.ShapeDtypeStruct(...  8.3 us
    all_to_all x1, starting transfers between devices, paired(): arrived = lax.all_to_all(ready, ('parts', 'dp'), 0, 0, tiled=True)  4.67 us
    ppermute x1, waiting for transfers between devices, paired(): ahead = lax.ppermute(sent_rows[:size], 'parts', swap)  3.18 us
    pallas_call x1, Pallas kernels, paired(): pl.pallas_call(late_kernel, out_shape=(half, half), in_specs=[scalars] +...  2.93 us
    psum x1, blocking collectives, paired(): total = lax.psum(squares(sent_rows), 'tensor')  2.46 us
  transfers between devices with their start and end apart: 15, of which 10 were waited for; matrix products, arithmetic and copies ran while one was open for 7% of the time, Pallas kernels for 8%

profile of v7, /device:TPU:0, one launch (start us, length us, event | category | flops | bytes accessed | tf_op | source)
XLA Modules:
  0.0 102.9 jit_solution(1598577981306680698)
XLA Ops:
  0.6 0.0 copy-start
  0.6 0.0 copy-start.1
  0.7 1.3 %copy-done = bf16[4096,160]{0,1:T(8,128)(2,1)S(1)} copy-done((bf16[4096,160]{0,1:T(8,128)(2,1)S(1)}, bf16[4096,160]{0,1:T(8,128)(2,1)}, u32[]{:S(2)}) %copy-start) | copy-done | bytes 1310744
  2.0 0.9 constant_dynamic-slice_fusion
  2.9 3.0 %collective-permute-start = (bf16[80,4096]{1,0:T(8,128)(2,1)}, bf16[80,4096]{1,0:T(8,128)(2,1)}, u32[]{:S(2)}, u32[]{:S(2)}) collective-permute-start(bf16[80,4096]{1,0:T(8,128)(2,1)} %bitcast.6.mine), channel_id=1, source_target_pairs={{0,4},{2,6},{4,0},{6,2},{8,12},{10,14},{12,8},{14,10},{1,5},{3,7},... | collective-permute-start | bytes 1966088 | tf_op jit(solution)/shard_map/ppermute | solution.py:129
  5.9 1.5 %collective-permute-start.1 = (bf16[80,4096]{1,0:T(8,128)(2,1)}, bf16[80,4096]{1,0:T(8,128)(2,1)}, u32[]{:S(2)}, u32[]{:S(2)}) collective-permute-start(bf16[80,4096]{1,0:T(8,128)(2,1)} %bitcast.6.mine), channel_id=1, source_target_pairs={{4,8},{6,10},{8,4},{10,6},{0,2},{2,0},{12,14},{14,12},{5,9},{7,11}... | collective-permute-start | bytes 1966088 | tf_op jit(solution)/shard_map/ppermute | solution.py:129
  7.4 2.0 %slice.6 = bf16[80,4096]{1,0:T(8,128)(2,1)} slice(bf16[256,4096]{1,0:T(8,128)(2,1)} %own.1), slice={[0:80], [0:4096]} | slice | bytes 1310720 | tf_op jit(solution)/shard_map/slice | solution.py:348
  9.3 1.5 %collective-permute-start.2 = (bf16[80,4096]{1,0:T(8,128)(2,1)}, bf16[80,4096]{1,0:T(8,128)(2,1)}, u32[]{:S(2)}, u32[]{:S(2)}) collective-permute-start(bf16[80,4096]{1,0:T(8,128)(2,1)} %slice.6), channel_id=1, source_target_pairs={{0,16},{16,0},{1,17},{17,1},{2,18},{18,2},{3,19},{19,3},{4,20},{20... | collective-permute-start | bytes 1966088 | tf_op jit(solution)/shard_map/ppermute | solution.py:348
  10.9 1.5 %collective-permute-start.3 = (bf16[80,4096]{1,0:T(8,128)(2,1)}, bf16[80,4096]{1,0:T(8,128)(2,1)}, u32[]{:S(2)}, u32[]{:S(2)}) collective-permute-start(bf16[80,4096]{1,0:T(8,128)(2,1)} %bitcast.6.mine), channel_id=1, source_target_pairs={{4,6},{6,4},{8,10},{10,8},{5,7},{7,5},{9,11},{11,9},{20,22},{22,20... | collective-permute-start | bytes 1966088 | tf_op jit(solution)/shard_map/ppermute | solution.py:129
  12.4 0.0 copy-done.1
  12.4 0.5 multiply_reduce_fusion
  12.9 2.5 %psum.7 = f32[256]{0:T(256)S(1)} all-reduce(f32[256]{0:T(256)S(1)} %multiply_reduce_fusion), channel_id=1, replica_groups=mesh['parts'=2,'dp'=8,'tensor'=2] {'tensor'}, use_global_device_ids=true, to_apply=%region_3.4 | all-reduce | flops 256 | bytes 2048 | tf_op jit(solution)/shard_map/psum | solution.py:350
  15.3 0.0 copy-start.5
  15.3 0.0 copy-start.2
  15.3 5.6 %collective-permute-done.near = bf16[80,4096]{1,0:T(8,128)(2,1)} collective-permute-done((bf16[80,4096]{1,0:T(8,128)(2,1)}, bf16[80,4096]{1,0:T(8,128)(2,1)}, u32[]{:S(2)}, u32[]{:S(2)}) %collective-permute-start) | collective-permute-done | bytes 655392 | tf_op jit(solution)/shard_map/ppermute | solution.py:129
  20.9 1.5 %collective-permute-done.1.cross = bf16[80,4096]{1,0:T(8,128)(2,1)} collective-permute-done((bf16[80,4096]{1,0:T(8,128)(2,1)}, bf16[80,4096]{1,0:T(8,128)(2,1)}, u32[]{:S(2)}, u32[]{:S(2)}) %collective-permute-start.1) | collective-permute-done | bytes 655392 | tf_op jit(solution)/shard_map/ppermute | solution.py:129
  22.4 3.2 %collective-permute-done.2.ahead = bf16[80,4096]{1,0:T(8,128)(2,1)} collective-permute-done((bf16[80,4096]{1,0:T(8,128)(2,1)}, bf16[80,4096]{1,0:T(8,128)(2,1)}, u32[]{:S(2)}, u32[]{:S(2)}) %collective-permute-start.2) | collective-permute-done | bytes 655392 | tf_op jit(solution)/shard_map/ppermute | solution.py:348
  25.6 1.5 %collective-permute-start.5 = (bf16[80,4096]{1,0:T(8,128)(2,1)}, bf16[80,4096]{1,0:T(8,128)(2,1)}, u32[]{:S(2)}, u32[]{:S(2)}) collective-permute-start(bf16[80,4096]{1,0:T(8,128)(2,1)} %collective-permute-done.near), channel_id=1, source_target_pairs={{4,8},{6,10},{8,4},{10,6},{5,9},{7,11},{9,5},{11,7},{20,24},{22,26... | collective-permute-start | bytes 1966088 | tf_op jit(solution)/shard_map/ppermute | solution.py:129
  27.1 2.4 %collective-permute-start.4 = (bf16[80,4096]{1,0:T(8,128)(2,1)}, bf16[80,4096]{1,0:T(8,128)(2,1)}, u32[]{:S(2)}, u32[]{:S(2)}) collective-permute-start(bf16[80,4096]{1,0:T(8,128)(2,1)} %collective-permute-done.1.cross), channel_id=1, source_target_pairs={{0,4},{2,6},{4,0},{6,2},{8,12},{10,14},{12,8},{14,10},{1,5},{3,7},... | collective-permute-start | bytes 1966088 | tf_op jit(solution)/shard_map/ppermute | solution.py:129
  29.5 1.2 %slice.7 = bf16[176,4096]{1,0:T(8,128)(2,1)} slice(bf16[256,4096]{1,0:T(8,128)(2,1)S(1)} %copy-done.1), slice={[80:256], [0:4096]} | slice | bytes 2883584 | tf_op jit(solution)/shard_map/slice | solution.py:349
  30.7 1.5 %collective-permute-start.9 = (bf16[176,4096]{1,0:T(8,128)(2,1)}, bf16[176,4096]{1,0:T(8,128)(2,1)}, u32[]{:S(2)}, u32[]{:S(2)}) collective-permute-start(bf16[176,4096]{1,0:T(8,128)(2,1)} %slice.7), channel_id=1, source_target_pairs={{0,16},{16,0},{1,17},{17,1},{2,18},{18,2},{3,19},{19,3},{4,20},{20... | collective-permute-start | bytes 4325384 | tf_op jit(solution)/shard_map/ppermute | solution.py:349
  32.2 0.0 collective-permute-done.3.side
  32.2 3.4 %collective-permute-start.6 = (bf16[80,4096]{1,0:T(8,128)(2,1)}, bf16[80,4096]{1,0:T(8,128)(2,1)}, u32[]{:S(2)}, u32[]{:S(2)}) collective-permute-start(bf16[80,4096]{1,0:T(8,128)(2,1)} %collective-permute-done.near), channel_id=1, source_target_pairs={{0,2},{2,0},{12,14},{14,12},{1,3},{3,1},{13,15},{15,13},{16,18},{1... | collective-permute-start | bytes 1966088 | tf_op jit(solution)/shard_map/ppermute | solution.py:129
  35.6 1.6 %collective-permute-start.7 = (bf16[80,4096]{1,0:T(8,128)(2,1)}, bf16[80,4096]{1,0:T(8,128)(2,1)}, u32[]{:S(2)}, u32[]{:S(2)}) collective-permute-start(bf16[80,4096]{1,0:T(8,128)(2,1)} %collective-permute-done.1.cross), channel_id=1, source_target_pairs={{4,6},{6,4},{8,10},{10,8},{5,7},{7,5},{9,11},{11,9},{20,22},{22,20... | collective-permute-start | bytes 1966088 | tf_op jit(solution)/shard_map/ppermute | solution.py:129
  37.2 0.0 collective-permute-done.5.far
  37.2 1.3 %collective-permute-start.11 = (bf16[80,4096]{1,0:T(8,128)(2,1)}, bf16[80,4096]{1,0:T(8,128)(2,1)}, u32[]{:S(2)}, u32[]{:S(2)}) collective-permute-start(bf16[80,4096]{1,0:T(8,128)(2,1)} %collective-permute-done.5.far), channel_id=1, source_target_pairs={{4,0},{6,2},{8,12},{10,14},{5,1},{7,3},{9,13},{11,15},{20,16},{22,... | collective-permute-start | bytes 1966088 | tf_op jit(solution)/shard_map/ppermute | solution.py:129
  38.5 4.6 %collective-permute-done.4.second = bf16[80,4096]{1,0:T(8,128)(2,1)} collective-permute-done((bf16[80,4096]{1,0:T(8,128)(2,1)}, bf16[80,4096]{1,0:T(8,128)(2,1)}, u32[]{:S(2)}, u32[]{:S(2)}) %collective-permute-start.4) | collective-permute-done | bytes 655392 | tf_op jit(solution)/shard_map/ppermute | solution.py:129
  43.1 2.0 %broadcast_select_fusion = bf16[80,4096]{1,0:T(8,128)(2,1)} fusion(bf16[80,4096]{1,0:T(8,128)(2,1)} %collective-permute-done.4.second, bf16[80,4096]{1,0:T(8,128)(2,1)} %collective-permute-done.5.far, pred[]{:T(512)S(6)} %or.3), kind=kLoop, calls=%fused_computation.1 | loop fusion | flops 327680 | bytes 1966081 | tf_op jit(solution)/shard_map/jit(_where)/select_n | solution.py:142
  45.1 1.5 %collective-permute-start.8 = (bf16[80,4096]{1,0:T(8,128)(2,1)}, bf16[80,4096]{1,0:T(8,128)(2,1)}, u32[]{:S(2)}, u32[]{:S(2)}) collective-permute-start(bf16[80,4096]{1,0:T(8,128)(2,1)} %broadcast_select_fusion), channel_id=1, source_target_pairs={{0,2},{2,0},{4,6},{6,4},{8,10},{10,8},{12,14},{14,12},{1,3},{3,1},... | collective-permute-start | bytes 1966088 | tf_op jit(solution)/shard_map/ppermute | solution.py:129
  46.6 11.8 %collective-permute-done.11.piece = bf16[80,4096]{1,0:T(8,128)(2,1)} collective-permute-done((bf16[80,4096]{1,0:T(8,128)(2,1)}, bf16[80,4096]{1,0:T(8,128)(2,1)}, u32[]{:S(2)}, u32[]{:S(2)}) %collective-permute-start.11) | collective-permute-done | bytes 655392 | tf_op jit(solution)/shard_map/ppermute | solution.py:129
  58.3 3.4 %collective-permute-start.12 = (bf16[80,4096]{1,0:T(8,128)(2,1)}, bf16[80,4096]{1,0:T(8,128)(2,1)}, u32[]{:S(2)}, u32[]{:S(2)}) collective-permute-start(bf16[80,4096]{1,0:T(8,128)(2,1)} %collective-permute-done.11.piece), channel_id=1, source_target_pairs={{0,2},{2,0},{12,14},{14,12},{1,3},{3,1},{13,15},{15,13},{16,18},{1... | collective-permute-start | bytes 1966088 | tf_op jit(solution)/shard_map/ppermute | solution.py:129
  61.7 0.0 collective-permute-done.6.near_over
  61.8 1.6 %collective-permute-start.10 = (f32[256]{0:T(256)S(1)}, f32[256]{0:T(256)S(1)}, u32[]{:S(2)}, u32[]{:S(2)}) collective-permute-start(f32[256]{0:T(256)S(1)} %add_rsqrt_fusion), channel_id=1, source_target_pairs={{0,16},{16,0},{1,17},{17,1},{2,18},{18,2},{3,19},{19,3},{4,20},{20... | collective-permute-start | bytes 3080 | tf_op jit(solution)/shard_map/ppermute | solution.py:354
  63.3 0.1 pad_add_fusion.at
  63.4 0.0 copy-done.5
  63.4 0.2 reduce-window.13
  63.6 0.0 collective-permute-done.7.cross_over
  63.6 1.8 %collective-permute-done.10 = f32[256]{0:T(256)S(1)} collective-permute-done((f32[256]{0:T(256)S(1)}, f32[256]{0:T(256)S(1)}, u32[]{:S(2)}, u32[]{:S(2)}) %collective-permute-start.10) | collective-permute-done | bytes 1056 | tf_op jit(solution)/shard_map/ppermute | solution.py:354
  65.4 0.0 collective-permute-done.9.behind
  65.4 0.5 collective-permute-done.8.second_over
  65.8 0.0 copy-done.2
  65.8 8.3 %project_early.1 = (f32[512,384]{1,0:T(8,128)S(1)}, f32[512,384]{1,0:T(8,128)S(1)}, bf16[512,4096]{1,0:T(8,128)(2,1)S(1)}) custom-call(s32[4]{0:T(128)S(1)} %pad_add_fusion.at, bf16[80,4096]{1,0:T(8,128)(2,1)} %bitcast.6.mine, bf16[80,4096]{1,0:T(8,128)(2,1)} %collective-permute-done.near, bf16[80,4096]{1,0:T(8,128)(2,1)} %collective-permute-done.1.cross, ...), custom_call_target="tpu_custom_call" | custom-call | flops 2684354560 | bytes 12582912 | tf_op jit(solution)/shard_map/project_early/pallas_call | solution.py:361
  74.2 2.8 %collective-permute-done.12.piece_over = bf16[80,4096]{1,0:T(8,128)(2,1)} collective-permute-done((bf16[80,4096]{1,0:T(8,128)(2,1)}, bf16[80,4096]{1,0:T(8,128)(2,1)}, u32[]{:S(2)}, u32[]{:S(2)}) %collective-permute-start.12) | collective-permute-done | bytes 655392 | tf_op jit(solution)/shard_map/ppermute | solution.py:129
  77.0 0.0 copy-start.4
  77.0 0.0 copy-start.3
  77.0 2.9 %project_late.1 = (f32[512,384]{1,0:T(8,128)S(1)}, f32[512,384]{1,0:T(8,128)S(1)}) custom-call(s32[4]{0:T(128)S(1)} %pad_add_fusion.at, f32[512,384]{1,0:T(8,128)S(1)} %get-tuple-element.26.first_keep, f32[512,384]{1,0:T(8,128)S(1)} %get-tuple-element.27.first_send, ...), custom_call_target="tpu_custom_call", output_to_operand_aliasing={{0}: (1, {}), {1}: (2, {})} | custom-call | flops 1073741824 | bytes 6291456 | tf_op jit(solution)/shard_map/project_late/pallas_call | solution.py:382
  79.9 0.1 collective-permute-start.13
  80.0 0.0 copy-done.4
  80.0 0.1 select_reduce_fusion
  80.1 0.0 copy-done.3
  80.1 0.2 fusion.5
  80.3 0.3 fusion.1
  80.6 1.6 %collective-permute-done.13.other = f32[512,384]{1,0:T(8,128)S(1)} collective-permute-done((f32[512,384]{1,0:T(8,128)S(1)}, f32[512,384]{1,0:T(8,128)S(1)}, u32[]{:S(2)}, u32[]{:S(2)}) %collective-permute-start.13) | collective-permute-done | bytes 786464 | tf_op jit(solution)/shard_map/ppermute | solution.py:402
  82.2 0.8 sum_halves.1
  83.1 4.7 %all-to-all-start = ((bf16[16,32,384]{2,1,0:T(8,128)(2,1)}), bf16[16,32,384]{2,1,0:T(8,128)(2,1)S(1)}, u32[]{:S(2)}, u32[]{:S(2)}) async-start(bf16[16,32,384]{2,1,0:T(8,128)(2,1)} %bitcast.10), calls=%async_computation | async-start | bytes 786432 | tf_op jit(solution)/shard_map/all_to_all | solution.py:403
  87.8 0.1 reduce
  87.9 0.1 pad_maximum_fusion
  88.0 0.1 select_reduce_fusion.2
  88.1 0.1 fusion.pick
  88.2 0.1 and_convert_fusion.allowed
  88.3 12.3 %all-to-all-done = bf16[16,32,384]{2,1,0:T(8,128)(2,1)S(1)} async-done(((bf16[16,32,384]{2,1,0:T(8,128)(2,1)}), bf16[16,32,384]{2,1,0:T(8,128)(2,1)S(1)}, u32[]{:S(2)}, u32[]{:S(2)}) %all-to-all-start) | async-done | bytes 393248 | tf_op jit(solution)/shard_map/all_to_all | solution.py:403
  100.6 2.3 %attend.1 = (bf16[128,128]{1,0:T(8,128)(2,1)}, bf16[128,128]{1,0:T(8,128)(2,1)}, bf16[128,512]{1,0:T(8,128)(2,1)}) custom-call(bf16[128,256]{1,0:T(8,128)(2,1)S(1)} %fusion.pick, bf16[2,256,384]{2,1,0:T(8,128)(2,1)S(1)} %bitcast.25, f32[128,128]{1,0:T(8,128)S(1)} %get-tuple-element.38.cosine, f32[128,128]{1,0:T(8,128)S(1)} %get-tuple-element.39.sine, ...), custom_call_target="tpu_custom_call" | custom-call | tf_op jit(solution)/shard_map/attend/pallas_call | solution.py:320
  (7 shorter events, 0.1 us)
Async XLA Ops:
  0.6 1.3 %copy-start = (bf16[4096,160]{0,1:T(8,128)(2,1)S(1)}, bf16[4096,160]{0,1:T(8,128)(2,1)}, u32[]{:S(2)}) copy-start(bf16[4096,160]{0,1:T(8,128)(2,1)} %param.8) | copy-start | bytes 3932164
  0.6 11.7 %copy-start.1 = (bf16[256,4096]{1,0:T(8,128)(2,1)S(1)}, bf16[256,4096]{1,0:T(8,128)(2,1)}, u32[]{:S(2)}) copy-start(bf16[256,4096]{1,0:T(8,128)(2,1)} %own.1) | copy-start | bytes 6291460
  2.9 18.1 %collective-permute-start = (bf16[80,4096]{1,0:T(8,128)(2,1)}, bf16[80,4096]{1,0:T(8,128)(2,1)}, u32[]{:S(2)}, u32[]{:S(2)}) collective-permute-start(bf16[80,4096]{1,0:T(8,128)(2,1)} %bitcast.6.mine), channel_id=1, source_target_pairs={{0,4},{2,6},{4,0},{6,2},{8,12},{10,14},{12,8},{14,10},{1,5},{3,7},... | collective-permute-start | bytes 1966088 | tf_op jit(solution)/shard_map/ppermute | solution.py:129
  5.9 16.5 %collective-permute-start.1 = (bf16[80,4096]{1,0:T(8,128)(2,1)}, bf16[80,4096]{1,0:T(8,128)(2,1)}, u32[]{:S(2)}, u32[]{:S(2)}) collective-permute-start(bf16[80,4096]{1,0:T(8,128)(2,1)} %bitcast.6.mine), channel_id=1, source_target_pairs={{4,8},{6,10},{8,4},{10,6},{0,2},{2,0},{12,14},{14,12},{5,9},{7,11}... | collective-permute-start | bytes 1966088 | tf_op jit(solution)/shard_map/ppermute | solution.py:129
  9.3 16.2 %collective-permute-start.2 = (bf16[80,4096]{1,0:T(8,128)(2,1)}, bf16[80,4096]{1,0:T(8,128)(2,1)}, u32[]{:S(2)}, u32[]{:S(2)}) collective-permute-start(bf16[80,4096]{1,0:T(8,128)(2,1)} %slice.6), channel_id=1, source_target_pairs={{0,16},{16,0},{1,17},{17,1},{2,18},{18,2},{3,19},{19,3},{4,20},{20... | collective-permute-start | bytes 1966088 | tf_op jit(solution)/shard_map/ppermute | solution.py:348
  10.9 21.4 %collective-permute-start.3 = (bf16[80,4096]{1,0:T(8,128)(2,1)}, bf16[80,4096]{1,0:T(8,128)(2,1)}, u32[]{:S(2)}, u32[]{:S(2)}) collective-permute-start(bf16[80,4096]{1,0:T(8,128)(2,1)} %bitcast.6.mine), channel_id=1, source_target_pairs={{4,6},{6,4},{8,10},{10,8},{5,7},{7,5},{9,11},{11,9},{20,22},{22,20... | collective-permute-start | bytes 1966088 | tf_op jit(solution)/shard_map/ppermute | solution.py:129
  15.3 48.1 %copy-start.5 = (s32[1,8]{1,0:T(1,128)S(1)}, s32[1,8]{1,0:T(1,128)}, u32[]{:S(2)}) copy-start(s32[1,8]{1,0:T(1,128)} %param.10) | copy-start | bytes 100
  15.3 50.5 %copy-start.2 = (f32[4096]{0:T(1024)S(1)}, f32[4096]{0:T(1024)}, u32[]{:S(2)}) copy-start(f32[4096]{0:T(1024)} %param.7) | copy-start | bytes 49156
  25.6 11.6 %collective-permute-start.5 = (bf16[80,4096]{1,0:T(8,128)(2,1)}, bf16[80,4096]{1,0:T(8,128)(2,1)}, u32[]{:S(2)}, u32[]{:S(2)}) collective-permute-start(bf16[80,4096]{1,0:T(8,128)(2,1)} %collective-permute-done.near), channel_id=1, source_target_pairs={{4,8},{6,10},{8,4},{10,6},{5,9},{7,11},{9,5},{11,7},{20,24},{22,26... | collective-permute-start | bytes 1966088 | tf_op jit(solution)/shard_map/ppermute | solution.py:129
  27.1 16.0 %collective-permute-start.4 = (bf16[80,4096]{1,0:T(8,128)(2,1)}, bf16[80,4096]{1,0:T(8,128)(2,1)}, u32[]{:S(2)}, u32[]{:S(2)}) collective-permute-start(bf16[80,4096]{1,0:T(8,128)(2,1)} %collective-permute-done.1.cross), channel_id=1, source_target_pairs={{0,4},{2,6},{4,0},{6,2},{8,12},{10,14},{12,8},{14,10},{1,5},{3,7},... | collective-permute-start | bytes 1966088 | tf_op jit(solution)/shard_map/ppermute | solution.py:129
  30.7 34.7 %collective-permute-start.9 = (bf16[176,4096]{1,0:T(8,128)(2,1)}, bf16[176,4096]{1,0:T(8,128)(2,1)}, u32[]{:S(2)}, u32[]{:S(2)}) collective-permute-start(bf16[176,4096]{1,0:T(8,128)(2,1)} %slice.7), channel_id=1, source_target_pairs={{0,16},{16,0},{1,17},{17,1},{2,18},{18,2},{3,19},{19,3},{4,20},{20... | collective-permute-start | bytes 4325384 | tf_op jit(solution)/shard_map/ppermute | solution.py:349
  32.2 29.5 %collective-permute-start.6 = (bf16[80,4096]{1,0:T(8,128)(2,1)}, bf16[80,4096]{1,0:T(8,128)(2,1)}, u32[]{:S(2)}, u32[]{:S(2)}) collective-permute-start(bf16[80,4096]{1,0:T(8,128)(2,1)} %collective-permute-done.near), channel_id=1, source_target_pairs={{0,2},{2,0},{12,14},{14,12},{1,3},{3,1},{13,15},{15,13},{16,18},{1... | collective-permute-start | bytes 1966088 | tf_op jit(solution)/shard_map/ppermute | solution.py:129
  35.6 28.0 %collective-permute-start.7 = (bf16[80,4096]{1,0:T(8,128)(2,1)}, bf16[80,4096]{1,0:T(8,128)(2,1)}, u32[]{:S(2)}, u32[]{:S(2)}) collective-permute-start(bf16[80,4096]{1,0:T(8,128)(2,1)} %collective-permute-done.1.cross), channel_id=1, source_target_pairs={{4,6},{6,4},{8,10},{10,8},{5,7},{7,5},{9,11},{11,9},{20,22},{22,20... | collective-permute-start | bytes 1966088 | tf_op jit(solution)/shard_map/ppermute | solution.py:129
  37.2 21.1 %collective-permute-start.11 = (bf16[80,4096]{1,0:T(8,128)(2,1)}, bf16[80,4096]{1,0:T(8,128)(2,1)}, u32[]{:S(2)}, u32[]{:S(2)}) collective-permute-start(bf16[80,4096]{1,0:T(8,128)(2,1)} %collective-permute-done.5.far), channel_id=1, source_target_pairs={{4,0},{6,2},{8,12},{10,14},{5,1},{7,3},{9,13},{11,15},{20,16},{22,... | collective-permute-start | bytes 1966088 | tf_op jit(solution)/shard_map/ppermute | solution.py:129
  45.1 20.8 %collective-permute-start.8 = (bf16[80,4096]{1,0:T(8,128)(2,1)}, bf16[80,4096]{1,0:T(8,128)(2,1)}, u32[]{:S(2)}, u32[]{:S(2)}) collective-permute-start(bf16[80,4096]{1,0:T(8,128)(2,1)} %broadcast_select_fusion), channel_id=1, source_target_pairs={{0,2},{2,0},{4,6},{6,4},{8,10},{10,8},{12,14},{14,12},{1,3},{3,1},... | collective-permute-start | bytes 1966088 | tf_op jit(solution)/shard_map/ppermute | solution.py:129
  58.3 18.6 %collective-permute-start.12 = (bf16[80,4096]{1,0:T(8,128)(2,1)}, bf16[80,4096]{1,0:T(8,128)(2,1)}, u32[]{:S(2)}, u32[]{:S(2)}) collective-permute-start(bf16[80,4096]{1,0:T(8,128)(2,1)} %collective-permute-done.11.piece), channel_id=1, source_target_pairs={{0,2},{2,0},{12,14},{14,12},{1,3},{3,1},{13,15},{15,13},{16,18},{1... | collective-permute-start | bytes 1966088 | tf_op jit(solution)/shard_map/ppermute | solution.py:129
  61.8 3.6 %collective-permute-start.10 = (f32[256]{0:T(256)S(1)}, f32[256]{0:T(256)S(1)}, u32[]{:S(2)}, u32[]{:S(2)}) collective-permute-start(f32[256]{0:T(256)S(1)} %add_rsqrt_fusion), channel_id=1, source_target_pairs={{0,16},{16,0},{1,17},{17,1},{2,18},{18,2},{3,19},{19,3},{4,20},{20... | collective-permute-start | bytes 3080 | tf_op jit(solution)/shard_map/ppermute | solution.py:354
  77.0 3.0 %copy-start.4 = (s32[1,8]{1,0:T(1,128)S(1)}, s32[1,8]{1,0:T(1,128)}, u32[]{:S(2)}) copy-start(s32[1,8]{1,0:T(1,128)} %param.11) | copy-start | bytes 100
  77.0 3.1 %copy-start.3 = (s32[8,8]{1,0:T(8,128)S(1)}, s32[8,8]{1,0:T(8,128)}, u32[]{:S(2)}) copy-start(s32[8,8]{1,0:T(8,128)} %param.9) | copy-start | bytes 772
  79.9 2.4 %collective-permute-start.13 = (f32[512,384]{1,0:T(8,128)S(1)}, f32[512,384]{1,0:T(8,128)S(1)}, u32[]{:S(2)}, u32[]{:S(2)}) collective-permute-start(f32[512,384]{1,0:T(8,128)S(1)} %get-tuple-element.30), channel_id=1, source_target_pairs={{0,1},{1,0},{2,3},{3,2},{4,5},{5,4},{6,7},{7,6},{8,9},{9,8},{10,11... | collective-permute-start | bytes 2359304 | tf_op jit(solution)/shard_map/ppermute | solution.py:402
  83.1 17.6 %all-to-all-start = ((bf16[16,32,384]{2,1,0:T(8,128)(2,1)}), bf16[16,32,384]{2,1,0:T(8,128)(2,1)S(1)}, u32[]{:S(2)}, u32[]{:S(2)}) async-start(bf16[16,32,384]{2,1,0:T(8,128)(2,1)} %bitcast.10), calls=%async_computation | async-start | bytes 786432 | tf_op jit(solution)/shard_map/all_to_all | solution.py:403

commit v8 on v7

--- a/solution.py
+++ b/solution.py
@@ -124,29 +124,28 @@
     return [(2 * a + x, 2 * b + x) for a, b in moves for x in range(2)]
 
 
-def gather_line(mine, at_end, total, ahead):
+def gather_line(mine, first):
     def send(block, pairs):
         return lax.ppermute(block, "dp", pairs)
 
     near = send(mine, alongs(PAIRS))
     cross = send(mine, alongs(ACROSS) + overs(ENDS))
     side = send(mine, overs(MIDDLE))
-    near, cross, total, ahead = lax.optimization_barrier((near, cross, total, ahead))
+    near, cross, side, first = lax.optimization_barrier((near, cross, side, first))
     second = send(cross, alongs(PAIRS))
-    far = send(near, alongs(ACROSS))
-    near_next, cross_next, side = lax.optimization_barrier((near, cross, side))
-    near_over = send(near_next, overs(ENDS))
-    cross_over = send(cross_next, overs(MIDDLE))
-    far, total = lax.optimization_barrier((far, total))
-    last = send(far, alongs(OUTWARD))
-    second_over = send(jnp.where(at_end, second, far), overs(range(4)))
+    onward = send(near, alongs(ACROSS) + overs(ENDS))
+    cross_over = send(cross, overs(MIDDLE))
+    onward, cross_over = lax.optimization_barrier((onward, cross_over))
+    last = send(onward, alongs(OUTWARD))
+    far_over = send(onward, overs(MIDDLE))
+    second_over = send(second, overs(ENDS))
     last_over = send(last, overs(ENDS))
-    early = (mine, near, cross, side, second, far, near_over, cross_over, second_over)
-    return early, (last, last_over), total, ahead
+    early = (mine, near, cross, side, second, onward, cross_over, far_over, second_over)
+    return early, (last, last_over), first
 
 
 def early_kernel(
-    at, mine, near, cross, side, second, far, near_over, cross_over, second_over,
+    at, mine, near, cross, side, second, onward, cross_over, far_over, second_over,
     own, ahead, behind, own_scale, their_scale, gain, keep, send, rows, whole,
 ):
     z, x, part, core = at[0], at[1], at[2], at[3]
@@ -184,7 +183,7 @@
         place(
             (
                 (z, (mine, cross)),
-                (pair, (near, near_over)),
+                (pair, (near, onward)),
                 ((z + 2) % 4, (second, second_over)),
                 (3 - z, (mine, cross)),
             )
@@ -196,7 +195,7 @@
             (
                 (z, (mine, side)),
                 (pair, (near, second)),
-                ((z + 2) % 4, (far, second_over)),
+                ((z + 2) % 4, (onward, far_over)),
                 (3 - z, (cross, cross_over)),
             )
         )
@@ -345,12 +344,11 @@
         turned.reshape(count, 2, BLOCK, depth), part, 1, False
     ).reshape(size, depth)
     swap = [(0, 1), (1, 0)]
-    ahead = lax.ppermute(sent_rows[:size], "parts", swap)
-    behind = lax.ppermute(sent_rows[size:], "parts", swap)
-    total = lax.psum(squares(sent_rows), "tensor")
-    at_end = (group < 2) | (group >= groups - 2)
-    early, late, total, ahead = gather_line(mine, at_end, total, ahead)
-    scale = scale_of(total)
+    cut_at = sent_rows.shape[0] // 4
+    ahead = lax.ppermute(sent_rows[:cut_at], "parts", swap)
+    scale = scale_of(lax.psum(squares(sent_rows), "tensor"))
+    early, late, (ahead, rest, scale) = gather_line(mine, (ahead, sent_rows[cut_at:], scale))
+    behind = lax.ppermute(rest, "parts", swap)
     their_scale = lax.ppermute(scale, "parts", swap)
     slots = sent_rows.shape[0]
     width = groups * size

time: 103 us -> 102 us (level)
  other arithmetic: 3.7 us -> 1.7 us
  local copies, waits for them, and re-layouts: 5.59 us -> 7.52 us
  waiting for transfers between devices: 45.6 us -> 44.5 us
    ppermute x10, waiting for transfers between devices: 26.6 us -> 21.2 us  [send(): return lax.ppermute(block, 'dp', pairs)]
    ppermute x2, waiting for transfers between devices: 3.19 us -> 7.62 us  [the longest x1 7.62 us: paired(): ahead = lax.ppermute(sent_rows[:cut_at], 'parts', swap)]
    select_n x1 -> x0, other arithmetic: 2 us -> none  [gather_line(): second_over = send(jnp.where(at_end, second, far), overs(range(4)))]
    unnamed x12 -> x16, local copies, waits for them, and re-layouts: 1.32 us -> 3.25 us
  transfers between devices with their start and end apart: 15 -> 15, of which waited for: 10 -> 8; matrix products, arithmetic and copies ran while one was open for 7% -> 5% of each run, Pallas kernels for 8% -> 8%
where the time goes in v8:
time: 102 us; the launch traced here: 101 us
  waiting for transfers between devices  44.5 us (44%)
  starting transfers between devices  30.3 us (30%)
  Pallas kernels  14.2 us (14%)
  local copies, waits for them, and re-layouts  7.52 us (7%)
  blocking collectives  2.46 us (2%)
  other arithmetic  1.7 us (2%)
    ppermute x10, waiting for transfers between devices, send(): return lax.ppermute(block, 'dp', pairs)  21.2 us
    ppermute x10, starting transfers between devices, send(): return lax.ppermute(block, 'dp', pairs)  20.9 us
    all_to_all x1, waiting for transfers between devices, paired(): arrived = lax.all_to_all(ready, ('parts', 'dp'), 0, 0, tiled=True)  12.3 us
    pallas_call x1, Pallas kernels, paired(): pl.pallas_call(early_kernel, out_shape=(half, half, jax.ShapeDtypeStruct(...  8.12 us
    ppermute x1, waiting for transfers between devices, paired(): ahead = lax.ppermute(sent_rows[:cut_at], 'parts', swap)  7.62 us
    all_to_all x1, starting transfers between devices, paired(): arrived = lax.all_to_all(ready, ('parts', 'dp'), 0, 0, tiled=True)  4.69 us
    unnamed x16, local copies, waits for them, and re-layouts  3.25 us
    pallas_call x1, Pallas kernels, paired(): pl.pallas_call(late_kernel, out_shape=(half, half), in_specs=[scalars] +...  2.93 us
  transfers between devices with their start and end apart: 15, of which 8 were waited for; matrix products, arithmetic and copies ran while one was open for 5% of the time, Pallas kernels for 8%

profile of v8, /device:TPU:0, one launch (start us, length us, event | category | flops | bytes accessed | tf_op | source)
XLA Modules:
  0.0 101.5 jit_solution(1097421482040560444)
XLA Ops:
  0.6 0.0 copy-start
  0.6 0.0 copy-start.1
  0.7 1.3 %copy-done = bf16[4096,160]{0,1:T(8,128)(2,1)S(1)} copy-done((bf16[4096,160]{0,1:T(8,128)(2,1)S(1)}, bf16[4096,160]{0,1:T(8,128)(2,1)}, u32[]{:S(2)}) %copy-start) | copy-done | bytes 1310744
  2.0 0.9 constant_dynamic-slice_fusion
  2.9 3.0 %collective-permute-start = (bf16[80,4096]{1,0:T(8,128)(2,1)}, bf16[80,4096]{1,0:T(8,128)(2,1)}, u32[]{:S(2)}, u32[]{:S(2)}) collective-permute-start(bf16[80,4096]{1,0:T(8,128)(2,1)} %bitcast.6.mine), channel_id=1, source_target_pairs={{0,4},{2,6},{4,0},{6,2},{8,12},{10,14},{12,8},{14,10},{1,5},{3,7},... | collective-permute-start | bytes 1966088 | tf_op jit(solution)/shard_map/ppermute | solution.py:129
  5.9 1.5 %collective-permute-start.1 = (bf16[80,4096]{1,0:T(8,128)(2,1)}, bf16[80,4096]{1,0:T(8,128)(2,1)}, u32[]{:S(2)}, u32[]{:S(2)}) collective-permute-start(bf16[80,4096]{1,0:T(8,128)(2,1)} %bitcast.6.mine), channel_id=1, source_target_pairs={{4,8},{6,10},{8,4},{10,6},{0,2},{2,0},{12,14},{14,12},{5,9},{7,11}... | collective-permute-start | bytes 1966088 | tf_op jit(solution)/shard_map/ppermute | solution.py:129
  7.4 1.5 %collective-permute-start.2 = (bf16[80,4096]{1,0:T(8,128)(2,1)}, bf16[80,4096]{1,0:T(8,128)(2,1)}, u32[]{:S(2)}, u32[]{:S(2)}) collective-permute-start(bf16[80,4096]{1,0:T(8,128)(2,1)} %bitcast.6.mine), channel_id=1, source_target_pairs={{4,6},{6,4},{8,10},{10,8},{5,7},{7,5},{9,11},{11,9},{20,22},{22,20... | collective-permute-start | bytes 1966088 | tf_op jit(solution)/shard_map/ppermute | solution.py:129
  8.9 1.9 %slice.6 = bf16[64,4096]{1,0:T(8,128)(2,1)} slice(bf16[256,4096]{1,0:T(8,128)(2,1)} %own.1), slice={[0:64], [0:4096]} | slice | bytes 1048576 | tf_op jit(solution)/shard_map/slice | solution.py:348
  10.8 0.0 copy-start.4
  10.8 1.5 %collective-permute-start.3 = (bf16[64,4096]{1,0:T(8,128)(2,1)}, bf16[64,4096]{1,0:T(8,128)(2,1)}, u32[]{:S(2)}, u32[]{:S(2)}) collective-permute-start(bf16[64,4096]{1,0:T(8,128)(2,1)} %slice.6), channel_id=1, source_target_pairs={{0,16},{16,0},{1,17},{17,1},{2,18},{18,2},{3,19},{19,3},{4,20},{20... | collective-permute-start | bytes 1572872 | tf_op jit(solution)/shard_map/ppermute | solution.py:348
  12.3 0.0 copy-done.1
  12.3 1.3 %slice.7 = bf16[192,4096]{1,0:T(8,128)(2,1)} slice(bf16[256,4096]{1,0:T(8,128)(2,1)S(1)} %copy-done.1), slice={[64:256], [0:4096]} | slice | bytes 3145728 | tf_op jit(solution)/shard_map/slice | solution.py:350
  13.6 0.5 multiply_reduce_fusion
  14.1 2.5 %psum.7 = f32[256]{0:T(256)S(1)} all-reduce(f32[256]{0:T(256)S(1)} %multiply_reduce_fusion), channel_id=1, replica_groups=mesh['parts'=2,'dp'=8,'tensor'=2] {'tensor'}, use_global_device_ids=true, to_apply=%region_3.4 | all-reduce | flops 256 | bytes 2048 | tf_op jit(solution)/shard_map/psum | solution.py:349
  16.6 7.6 %collective-permute-done.3.ahead = bf16[64,4096]{1,0:T(8,128)(2,1)} collective-permute-done((bf16[64,4096]{1,0:T(8,128)(2,1)}, bf16[64,4096]{1,0:T(8,128)(2,1)}, u32[]{:S(2)}, u32[]{:S(2)}) %collective-permute-start.3) | collective-permute-done | bytes 524320 | tf_op jit(solution)/shard_map/ppermute | solution.py:348
  24.2 0.0 collective-permute-done.near
  24.2 0.0 collective-permute-done.1.cross
  24.2 0.0 collective-permute-done.2.side
  24.2 0.7 collective-permute-start.6
  24.9 0.6 collective-permute-start.5
  25.5 1.5 %collective-permute-start.9 = (bf16[192,4096]{1,0:T(8,128)(2,1)}, bf16[192,4096]{1,0:T(8,128)(2,1)}, u32[]{:S(2)}, u32[]{:S(2)}) collective-permute-start(bf16[192,4096]{1,0:T(8,128)(2,1)} %slice.7), channel_id=1, source_target_pairs={{0,16},{16,0},{1,17},{17,1},{2,18},{18,2},{3,19},{19,3},{4,20},{20... | collective-permute-start | bytes 4718600 | tf_op jit(solution)/shard_map/ppermute | solution.py:351
  27.0 5.4 %collective-permute-start.4 = (bf16[80,4096]{1,0:T(8,128)(2,1)}, bf16[80,4096]{1,0:T(8,128)(2,1)}, u32[]{:S(2)}, u32[]{:S(2)}) collective-permute-start(bf16[80,4096]{1,0:T(8,128)(2,1)} %collective-permute-done.1.cross), channel_id=1, source_target_pairs={{0,4},{2,6},{4,0},{6,2},{8,12},{10,14},{12,8},{14,10},{1,5},{3,7},... | collective-permute-start | bytes 1966088 | tf_op jit(solution)/shard_map/ppermute | solution.py:129
  32.4 0.0 collective-permute-done.6.cross_over
  32.4 0.0 copy-start.2
  32.4 0.8 copy-done.2
  33.3 7.0 %collective-permute-done.5.onward = bf16[80,4096]{1,0:T(8,128)(2,1)} collective-permute-done((bf16[80,4096]{1,0:T(8,128)(2,1)}, bf16[80,4096]{1,0:T(8,128)(2,1)}, u32[]{:S(2)}, u32[]{:S(2)}) %collective-permute-start.5) | collective-permute-done | bytes 655392 | tf_op jit(solution)/shard_map/ppermute | solution.py:129
  40.3 1.3 %collective-permute-start.11 = (bf16[80,4096]{1,0:T(8,128)(2,1)}, bf16[80,4096]{1,0:T(8,128)(2,1)}, u32[]{:S(2)}, u32[]{:S(2)}) collective-permute-start(bf16[80,4096]{1,0:T(8,128)(2,1)} %collective-permute-done.5.onward), channel_id=1, source_target_pairs={{4,0},{6,2},{8,12},{10,14},{5,1},{7,3},{9,13},{11,15},{20,16},{22,... | collective-permute-start | bytes 1966088 | tf_op jit(solution)/shard_map/ppermute | solution.py:129
  41.6 1.6 %collective-permute-start.7 = (bf16[80,4096]{1,0:T(8,128)(2,1)}, bf16[80,4096]{1,0:T(8,128)(2,1)}, u32[]{:S(2)}, u32[]{:S(2)}) collective-permute-start(bf16[80,4096]{1,0:T(8,128)(2,1)} %collective-permute-done.5.onward), channel_id=1, source_target_pairs={{4,6},{6,4},{8,10},{10,8},{5,7},{7,5},{9,11},{11,9},{20,22},{22,20... | collective-permute-start | bytes 1966088 | tf_op jit(solution)/shard_map/ppermute | solution.py:129
  43.1 2.5 %collective-permute-done.4.second = bf16[80,4096]{1,0:T(8,128)(2,1)} collective-permute-done((bf16[80,4096]{1,0:T(8,128)(2,1)}, bf16[80,4096]{1,0:T(8,128)(2,1)}, u32[]{:S(2)}, u32[]{:S(2)}) %collective-permute-start.4) | collective-permute-done | bytes 655392 | tf_op jit(solution)/shard_map/ppermute | solution.py:129
  45.6 2.3 %collective-permute-start.8 = (bf16[80,4096]{1,0:T(8,128)(2,1)}, bf16[80,4096]{1,0:T(8,128)(2,1)}, u32[]{:S(2)}, u32[]{:S(2)}) collective-permute-start(bf16[80,4096]{1,0:T(8,128)(2,1)} %collective-permute-done.4.second), channel_id=1, source_target_pairs={{0,2},{2,0},{12,14},{14,12},{1,3},{3,1},{13,15},{15,13},{16,18},{1... | collective-permute-start | bytes 1966088 | tf_op jit(solution)/shard_map/ppermute | solution.py:129
  47.9 11.6 %collective-permute-done.11.piece = bf16[80,4096]{1,0:T(8,128)(2,1)} collective-permute-done((bf16[80,4096]{1,0:T(8,128)(2,1)}, bf16[80,4096]{1,0:T(8,128)(2,1)}, u32[]{:S(2)}, u32[]{:S(2)}) %collective-permute-start.11) | collective-permute-done | bytes 655392 | tf_op jit(solution)/shard_map/ppermute | solution.py:129
  59.5 3.0 %collective-permute-start.12 = (bf16[80,4096]{1,0:T(8,128)(2,1)}, bf16[80,4096]{1,0:T(8,128)(2,1)}, u32[]{:S(2)}, u32[]{:S(2)}) collective-permute-start(bf16[80,4096]{1,0:T(8,128)(2,1)} %collective-permute-done.11.piece), channel_id=1, source_target_pairs={{0,2},{2,0},{12,14},{14,12},{1,3},{3,1},{13,15},{15,13},{16,18},{1... | collective-permute-start | bytes 1966088 | tf_op jit(solution)/shard_map/ppermute | solution.py:129
  62.5 1.6 %collective-permute-start.10 = (f32[256]{0:T(256)S(1)}, f32[256]{0:T(256)S(1)}, u32[]{:S(2)}, u32[]{:S(2)}) collective-permute-start(f32[256]{0:T(256)S(1)} %add_rsqrt_fusion), channel_id=1, source_target_pairs={{0,16},{16,0},{1,17},{17,1},{2,18},{18,2},{3,19},{19,3},{4,20},{20... | collective-permute-start | bytes 3080 | tf_op jit(solution)/shard_map/ppermute | solution.py:352
  64.1 0.1 pad_add_fusion.at
  64.2 0.0 copy-done.7
  64.2 0.2 reduce-window.13
  64.4 1.8 %collective-permute-done.10 = f32[256]{0:T(256)S(1)} collective-permute-done((f32[256]{0:T(256)S(1)}, f32[256]{0:T(256)S(1)}, u32[]{:S(2)}, u32[]{:S(2)}) %collective-permute-start.10) | collective-permute-done | bytes 1056 | tf_op jit(solution)/shard_map/ppermute | solution.py:352
  66.1 0.0 collective-permute-done.7.far_over
  66.1 0.0 collective-permute-done.8.second_over
  66.1 0.0 collective-permute-done.9.behind
  66.2 0.0 copy-done.4
  66.2 0.0 copy-start.3
  66.2 1.1 %copy-done.3 = bf16[80,4096]{1,0:T(8,128)(2,1)S(1)} copy-done((bf16[80,4096]{1,0:T(8,128)(2,1)S(1)}, bf16[80,4096]{1,0:T(8,128)(2,1)}, u32[]{:S(2)}) %copy-start.3) | copy-done | bytes 655384
  67.3 8.1 %project_early.1 = (f32[512,384]{1,0:T(8,128)S(1)}, f32[512,384]{1,0:T(8,128)S(1)}, bf16[512,4096]{1,0:T(8,128)(2,1)S(1)}) custom-call(s32[4]{0:T(128)S(1)} %pad_add_fusion.at, bf16[80,4096]{1,0:T(8,128)(2,1)} %bitcast.6.mine, bf16[80,4096]{1,0:T(8,128)(2,1)} %collective-permute-done.near, bf16[80,4096]{1,0:T(8,128)(2,1)} %collective-permute-done.1.cross, ...), custom_call_target="tpu_custom_call" | custom-call | flops 2684354560 | bytes 12582912 | tf_op jit(solution)/shard_map/project_early/pallas_call | solution.py:359
  75.4 0.1 collective-permute-done.12.piece_over
  75.5 0.0 copy-start.6
  75.5 0.0 copy-start.5
  75.5 2.9 %project_late.1 = (f32[512,384]{1,0:T(8,128)S(1)}, f32[512,384]{1,0:T(8,128)S(1)}) custom-call(s32[4]{0:T(128)S(1)} %pad_add_fusion.at, f32[512,384]{1,0:T(8,128)S(1)} %get-tuple-element.24.first_keep, f32[512,384]{1,0:T(8,128)S(1)} %get-tuple-element.25.first_send, ...), custom_call_target="tpu_custom_call", output_to_operand_aliasing={{0}: (1, {}), {1}: (2, {})} | custom-call | flops 1073741824 | bytes 6291456 | tf_op jit(solution)/shard_map/project_late/pallas_call | solution.py:380
  78.4 0.1 collective-permute-start.13
  78.5 0.0 copy-done.6
  78.5 0.1 select_reduce_fusion
  78.6 0.0 copy-done.5
  78.6 0.2 fusion.5
  78.8 0.3 fusion.1
  79.1 1.6 %collective-permute-done.13.other = f32[512,384]{1,0:T(8,128)S(1)} collective-permute-done((f32[512,384]{1,0:T(8,128)S(1)}, f32[512,384]{1,0:T(8,128)S(1)}, u32[]{:S(2)}, u32[]{:S(2)}) %collective-permute-start.13) | collective-permute-done | bytes 786464 | tf_op jit(solution)/shard_map/ppermute | solution.py:400
  80.8 0.8 sum_halves.1
  81.6 4.7 %all-to-all-start = ((bf16[16,32,384]{2,1,0:T(8,128)(2,1)}), bf16[16,32,384]{2,1,0:T(8,128)(2,1)S(1)}, u32[]{:S(2)}, u32[]{:S(2)}) async-start(bf16[16,32,384]{2,1,0:T(8,128)(2,1)} %bitcast.10), calls=%async_computation | async-start | bytes 786432 | tf_op jit(solution)/shard_map/all_to_all | solution.py:401
  86.3 0.1 reduce
  86.4 0.1 pad_maximum_fusion
  86.6 0.1 select_reduce_fusion.2
  86.6 0.1 fusion.pick
  86.7 0.1 and_convert_fusion.allowed
  86.8 12.3 %all-to-all-done = bf16[16,32,384]{2,1,0:T(8,128)(2,1)S(1)} async-done(((bf16[16,32,384]{2,1,0:T(8,128)(2,1)}), bf16[16,32,384]{2,1,0:T(8,128)(2,1)S(1)}, u32[]{:S(2)}, u32[]{:S(2)}) %all-to-all-start) | async-done | bytes 393248 | tf_op jit(solution)/shard_map/all_to_all | solution.py:401
  99.2 2.3 %attend.1 = (bf16[128,128]{1,0:T(8,128)(2,1)}, bf16[128,128]{1,0:T(8,128)(2,1)}, bf16[128,512]{1,0:T(8,128)(2,1)}) custom-call(bf16[128,256]{1,0:T(8,128)(2,1)S(1)} %fusion.pick, bf16[2,256,384]{2,1,0:T(8,128)(2,1)S(1)} %bitcast.25, f32[128,128]{1,0:T(8,128)S(1)} %get-tuple-element.36.cosine, f32[128,128]{1,0:T(8,128)S(1)} %get-tuple-element.37.sine, ...), custom_call_target="tpu_custom_call" | custom-call | tf_op jit(solution)/shard_map/attend/pallas_call | solution.py:319
  (8 shorter events, 0.1 us)
Async XLA Ops:
  0.6 1.3 %copy-start = (bf16[4096,160]{0,1:T(8,128)(2,1)S(1)}, bf16[4096,160]{0,1:T(8,128)(2,1)}, u32[]{:S(2)}) copy-start(bf16[4096,160]{0,1:T(8,128)(2,1)} %param.8) | copy-start | bytes 3932164
  0.6 11.6 %copy-start.1 = (bf16[256,4096]{1,0:T(8,128)(2,1)S(1)}, bf16[256,4096]{1,0:T(8,128)(2,1)}, u32[]{:S(2)}) copy-start(bf16[256,4096]{1,0:T(8,128)(2,1)} %own.1) | copy-start | bytes 6291460
  2.9 21.3 %collective-permute-start = (bf16[80,4096]{1,0:T(8,128)(2,1)}, bf16[80,4096]{1,0:T(8,128)(2,1)}, u32[]{:S(2)}, u32[]{:S(2)}) collective-permute-start(bf16[80,4096]{1,0:T(8,128)(2,1)} %bitcast.6.mine), channel_id=1, source_target_pairs={{0,4},{2,6},{4,0},{6,2},{8,12},{10,14},{12,8},{14,10},{1,5},{3,7},... | collective-permute-start | bytes 1966088 | tf_op jit(solution)/shard_map/ppermute | solution.py:129
  5.9 18.3 %collective-permute-start.1 = (bf16[80,4096]{1,0:T(8,128)(2,1)}, bf16[80,4096]{1,0:T(8,128)(2,1)}, u32[]{:S(2)}, u32[]{:S(2)}) collective-permute-start(bf16[80,4096]{1,0:T(8,128)(2,1)} %bitcast.6.mine), channel_id=1, source_target_pairs={{4,8},{6,10},{8,4},{10,6},{0,2},{2,0},{12,14},{14,12},{5,9},{7,11}... | collective-permute-start | bytes 1966088 | tf_op jit(solution)/shard_map/ppermute | solution.py:129
  7.4 16.8 %collective-permute-start.2 = (bf16[80,4096]{1,0:T(8,128)(2,1)}, bf16[80,4096]{1,0:T(8,128)(2,1)}, u32[]{:S(2)}, u32[]{:S(2)}) collective-permute-start(bf16[80,4096]{1,0:T(8,128)(2,1)} %bitcast.6.mine), channel_id=1, source_target_pairs={{4,6},{6,4},{8,10},{10,8},{5,7},{7,5},{9,11},{11,9},{20,22},{22,20... | collective-permute-start | bytes 1966088 | tf_op jit(solution)/shard_map/ppermute | solution.py:129
  10.8 53.4 %copy-start.7 = (s32[1,8]{1,0:T(1,128)S(1)}, s32[1,8]{1,0:T(1,128)}, u32[]{:S(2)}) copy-start(s32[1,8]{1,0:T(1,128)} %param.10) | copy-start | bytes 100
  10.8 55.4 %copy-start.4 = (f32[4096]{0:T(1024)S(1)}, f32[4096]{0:T(1024)}, u32[]{:S(2)}) copy-start(f32[4096]{0:T(1024)} %param.7) | copy-start | bytes 49156
  10.8 13.4 %collective-permute-start.3 = (bf16[64,4096]{1,0:T(8,128)(2,1)}, bf16[64,4096]{1,0:T(8,128)(2,1)}, u32[]{:S(2)}, u32[]{:S(2)}) collective-permute-start(bf16[64,4096]{1,0:T(8,128)(2,1)} %slice.6), channel_id=1, source_target_pairs={{0,16},{16,0},{1,17},{17,1},{2,18},{18,2},{3,19},{19,3},{4,20},{20... | collective-permute-start | bytes 1572872 | tf_op jit(solution)/shard_map/ppermute | solution.py:348
  24.2 8.2 %collective-permute-start.6 = (bf16[80,4096]{1,0:T(8,128)(2,1)}, bf16[80,4096]{1,0:T(8,128)(2,1)S(1)}, u32[]{:S(2)}, u32[]{:S(2)}) collective-permute-start(bf16[80,4096]{1,0:T(8,128)(2,1)} %collective-permute-done.1.cross), channel_id=1, source_target_pairs={{4,6},{6,4},{8,10},{10,8},{5,7},{7,5},{9,11},{11,9},{20,22},{22,20... | collective-permute-start | bytes 1966088 | tf_op jit(solution)/shard_map/ppermute | solution.py:129
  24.9 15.4 %collective-permute-start.5 = (bf16[80,4096]{1,0:T(8,128)(2,1)}, bf16[80,4096]{1,0:T(8,128)(2,1)}, u32[]{:S(2)}, u32[]{:S(2)}) collective-permute-start(bf16[80,4096]{1,0:T(8,128)(2,1)} %collective-permute-done.near), channel_id=1, source_target_pairs={{4,8},{6,10},{8,4},{10,6},{0,2},{2,0},{12,14},{14,12},{5,9},{7,11}... | collective-permute-start | bytes 1966088 | tf_op jit(solution)/shard_map/ppermute | solution.py:129
  25.5 40.6 %collective-permute-start.9 = (bf16[192,4096]{1,0:T(8,128)(2,1)}, bf16[192,4096]{1,0:T(8,128)(2,1)}, u32[]{:S(2)}, u32[]{:S(2)}) collective-permute-start(bf16[192,4096]{1,0:T(8,128)(2,1)} %slice.7), channel_id=1, source_target_pairs={{0,16},{16,0},{1,17},{17,1},{2,18},{18,2},{3,19},{19,3},{4,20},{20... | collective-permute-start | bytes 4718600 | tf_op jit(solution)/shard_map/ppermute | solution.py:351
  27.0 18.6 %collective-permute-start.4 = (bf16[80,4096]{1,0:T(8,128)(2,1)}, bf16[80,4096]{1,0:T(8,128)(2,1)}, u32[]{:S(2)}, u32[]{:S(2)}) collective-permute-start(bf16[80,4096]{1,0:T(8,128)(2,1)} %collective-permute-done.1.cross), channel_id=1, source_target_pairs={{0,4},{2,6},{4,0},{6,2},{8,12},{10,14},{12,8},{14,10},{1,5},{3,7},... | collective-permute-start | bytes 1966088 | tf_op jit(solution)/shard_map/ppermute | solution.py:129
  32.4 0.8 copy-start.2
  40.3 19.2 %collective-permute-start.11 = (bf16[80,4096]{1,0:T(8,128)(2,1)}, bf16[80,4096]{1,0:T(8,128)(2,1)}, u32[]{:S(2)}, u32[]{:S(2)}) collective-permute-start(bf16[80,4096]{1,0:T(8,128)(2,1)} %collective-permute-done.5.onward), channel_id=1, source_target_pairs={{4,0},{6,2},{8,12},{10,14},{5,1},{7,3},{9,13},{11,15},{20,16},{22,... | collective-permute-start | bytes 1966088 | tf_op jit(solution)/shard_map/ppermute | solution.py:129
  41.6 24.6 %collective-permute-start.7 = (bf16[80,4096]{1,0:T(8,128)(2,1)}, bf16[80,4096]{1,0:T(8,128)(2,1)}, u32[]{:S(2)}, u32[]{:S(2)}) collective-permute-start(bf16[80,4096]{1,0:T(8,128)(2,1)} %collective-permute-done.5.onward), channel_id=1, source_target_pairs={{4,6},{6,4},{8,10},{10,8},{5,7},{7,5},{9,11},{11,9},{20,22},{22,20... | collective-permute-start | bytes 1966088 | tf_op jit(solution)/shard_map/ppermute | solution.py:129
  45.6 20.6 %collective-permute-start.8 = (bf16[80,4096]{1,0:T(8,128)(2,1)}, bf16[80,4096]{1,0:T(8,128)(2,1)}, u32[]{:S(2)}, u32[]{:S(2)}) collective-permute-start(bf16[80,4096]{1,0:T(8,128)(2,1)} %collective-permute-done.4.second), channel_id=1, source_target_pairs={{0,2},{2,0},{12,14},{14,12},{1,3},{3,1},{13,15},{15,13},{16,18},{1... | collective-permute-start | bytes 1966088 | tf_op jit(solution)/shard_map/ppermute | solution.py:129
  59.5 16.0 %collective-permute-start.12 = (bf16[80,4096]{1,0:T(8,128)(2,1)}, bf16[80,4096]{1,0:T(8,128)(2,1)}, u32[]{:S(2)}, u32[]{:S(2)}) collective-permute-start(bf16[80,4096]{1,0:T(8,128)(2,1)} %collective-permute-done.11.piece), channel_id=1, source_target_pairs={{0,2},{2,0},{12,14},{14,12},{1,3},{3,1},{13,15},{15,13},{16,18},{1... | collective-permute-start | bytes 1966088 | tf_op jit(solution)/shard_map/ppermute | solution.py:129
  62.5 3.6 %collective-permute-start.10 = (f32[256]{0:T(256)S(1)}, f32[256]{0:T(256)S(1)}, u32[]{:S(2)}, u32[]{:S(2)}) collective-permute-start(f32[256]{0:T(256)S(1)} %add_rsqrt_fusion), channel_id=1, source_target_pairs={{0,16},{16,0},{1,17},{17,1},{2,18},{18,2},{3,19},{19,3},{4,20},{20... | collective-permute-start | bytes 3080 | tf_op jit(solution)/shard_map/ppermute | solution.py:352
  66.2 1.1 %copy-start.3 = (bf16[80,4096]{1,0:T(8,128)(2,1)S(1)}, bf16[80,4096]{1,0:T(8,128)(2,1)}, u32[]{:S(2)}) copy-start(bf16[80,4096]{1,0:T(8,128)(2,1)} %copy-done.2) | copy-start | bytes 1966084
  75.5 3.0 %copy-start.6 = (s32[1,8]{1,0:T(1,128)S(1)}, s32[1,8]{1,0:T(1,128)}, u32[]{:S(2)}) copy-start(s32[1,8]{1,0:T(1,128)} %param.11) | copy-start | bytes 100
  75.5 3.1 %copy-start.5 = (s32[8,8]{1,0:T(8,128)S(1)}, s32[8,8]{1,0:T(8,128)}, u32[]{:S(2)}) copy-start(s32[8,8]{1,0:T(8,128)} %param.9) | copy-start | bytes 772
  78.4 2.4 %collective-permute-start.13 = (f32[512,384]{1,0:T(8,128)S(1)}, f32[512,384]{1,0:T(8,128)S(1)}, u32[]{:S(2)}, u32[]{:S(2)}) collective-permute-start(f32[512,384]{1,0:T(8,128)S(1)} %get-tuple-element.28), channel_id=1, source_target_pairs={{0,1},{1,0},{2,3},{3,2},{4,5},{5,4},{6,7},{7,6},{8,9},{9,8},{10,11... | collective-permute-start | bytes 2359304 | tf_op jit(solution)/shard_map/ppermute | solution.py:400
  81.6 17.6 %all-to-all-start = ((bf16[16,32,384]{2,1,0:T(8,128)(2,1)}), bf16[16,32,384]{2,1,0:T(8,128)(2,1)S(1)}, u32[]{:S(2)}, u32[]{:S(2)}) async-start(bf16[16,32,384]{2,1,0:T(8,128)(2,1)} %bitcast.10), calls=%async_computation | async-start | bytes 786432 | tf_op jit(solution)/shard_map/all_to_all | solution.py:401

commit v9 on v8

--- a/solution.py
+++ b/solution.py
@@ -135,8 +135,8 @@
     second = send(cross, alongs(PAIRS))
     onward = send(near, alongs(ACROSS) + overs(ENDS))
     cross_over = send(cross, overs(MIDDLE))
+    last = send(onward, alongs(OUTWARD))
     onward, cross_over = lax.optimization_barrier((onward, cross_over))
-    last = send(onward, alongs(OUTWARD))
     far_over = send(onward, overs(MIDDLE))
     second_over = send(second, overs(ENDS))
     last_over = send(last, overs(ENDS))
@@ -146,34 +146,31 @@
 
 def early_kernel(
     at, mine, near, cross, side, second, onward, cross_over, far_over, second_over,
-    own, ahead, behind, own_scale, their_scale, gain, keep, send, rows, whole,
+    own, ahead, behind, own_scale, their_scale, gain, keep, send, rows,
+    raw, whole, row_sems, sems,
 ):
     z, x, part, core = at[0], at[1], at[2], at[3]
     size = mine.shape[0]
+    count = own.shape[0]
+    cut_at = ahead.shape[0]
+    arrivals = (
+        pltpu.make_async_copy(own, raw.at[pl.ds(0, count)], row_sems.at[0]),
+        pltpu.make_async_copy(ahead, raw.at[pl.ds(count, cut_at)], row_sems.at[1]),
+        pltpu.make_async_copy(
+            behind, raw.at[pl.ds(count + cut_at, count - cut_at)], row_sems.at[2]
+        ),
+    )
+    for copy in arrivals:
+        copy.start()
 
     def place(pairs):
         for where, pieces in pairs:
             for j, piece in enumerate(pieces):
-                column = x if j == 0 else 1 - x
-                start = pl.multiple_of((2 * where + column) * size, BLOCK)
-                whole[pl.ds(start, size), :] = piece[...]
-
-    count = own.shape[0]
-    for index, sources, scale in (
-        (part, (own,), own_scale),
-        (1 - part, (ahead, behind), their_scale),
-    ):
-        upright = jnp.broadcast_to(scale[...], (HD, count)).T[:, :1]
-        done = 0
-        for source in sources:
-            for low in range(0, source.shape[0], BLOCK):
-                start = pl.multiple_of(index * count + done + low, BLOCK)
-                rows[pl.ds(start, BLOCK), :] = scaled(
-                    source[low : low + BLOCK, :],
-                    upright[done + low : done + low + BLOCK, :],
-                    gain[...],
-                )
-            done += source.shape[0]
+                index = 2 * where + (x if j == 0 else 1 - x)
+                start = pl.multiple_of(index * size, BLOCK)
+                pltpu.make_async_copy(
+                    piece, whole.at[pl.ds(start, size)], sems.at[index]
+                ).start()
 
     at_end = (z == 0) | (z == 3)
     pair = z + 1 - 2 * (z % 2)
@@ -200,20 +197,44 @@
             )
         )
 
+    for k, (index, scale, waits) in enumerate(
+        ((part, own_scale, arrivals[:1]), (1 - part, their_scale, arrivals[1:]))
+    ):
+        upright = jnp.broadcast_to(scale[...], (HD, count)).T[:, :1]
+        for copy in waits:
+            copy.wait()
+        for low in range(0, count, BLOCK):
+            start = pl.multiple_of(index * count + low, BLOCK)
+            rows[pl.ds(start, BLOCK), :] = scaled(
+                raw[k * count + low : k * count + low + BLOCK, :],
+                upright[low : low + BLOCK, :],
+                gain[...],
+            )
+
     share = whole.shape[0] * HQ // (HQ + 2) // 2
-    halves = [product(rows[...], whole[c * share : (c + 1) * share, :]) for c in range(2)]
-    rest = product(rows[...], whole[2 * share :, :])
-    for ref in (keep, send):
-        ref[:, share:] = rest
-    for t in range(2):
-
-        @pl.when(core == t)
-        def _():
-            keep[:, :share] = halves[t]
-            send[:, :share] = halves[1 - t]
-
-
-def late_kernel(at, first_keep, first_send, piece, piece_over, rows, keep, send, last):
+    held = 0
+    for low, high in ((0, share), (share, 2 * share), (2 * share, whole.shape[0])):
+        while held * size < high:
+            pltpu.make_async_copy(
+                mine, whole.at[pl.ds(held * size, size)], sems.at[held]
+            ).wait()
+            held += 1
+        block = product(rows[...], whole[low:high, :])
+        if low == 2 * share:
+            keep[:, share:] = block
+            send[:, share:] = block
+        else:
+
+            @pl.when(core == low // share)
+            def _():
+                keep[:, :share] = block
+
+            @pl.when(core != low // share)
+            def _():
+                send[:, :share] = block
+
+
+def late_kernel(at, first_keep, first_send, piece, piece_over, rows, keep, send, last, sems):
     z, x, core = at[0], at[1], at[3]
     size = piece.shape[0]
     share = last.shape[0]
@@ -221,10 +242,15 @@
     gap = share - edge
 
     def fetch(offset):
+        found = []
         for side, ref in ((0, piece), (1, piece_over)):
             where = x if side == 0 else 1 - x
             start = pl.multiple_of(offset + where * size, BLOCK)
-            last[pl.ds(start, size), :] = ref[...]
+            copy = pltpu.make_async_copy(ref, last.at[pl.ds(start, size)], sems.at[side])
+            copy.start()
+            found.append(copy)
+        for copy in found:
+            copy.wait()
         return product(rows[...], last[...])
 
     def merge(ref, source, lanes, block, new):
@@ -344,24 +370,32 @@
         turned.reshape(count, 2, BLOCK, depth), part, 1, False
     ).reshape(size, depth)
     swap = [(0, 1), (1, 0)]
-    cut_at = sent_rows.shape[0] // 4
+    cut_at = sent_rows.shape[0] // 8
     ahead = lax.ppermute(sent_rows[:cut_at], "parts", swap)
     scale = scale_of(lax.psum(squares(sent_rows), "tensor"))
-    early, late, (ahead, rest, scale) = gather_line(mine, (ahead, sent_rows[cut_at:], scale))
+    their_scale = lax.ppermute(scale, "parts", swap)
+    early, late, (ahead, rest, their_scale) = gather_line(
+        mine, (ahead, sent_rows[cut_at:], their_scale)
+    )
     behind = lax.ppermute(rest, "parts", swap)
-    their_scale = lax.ppermute(scale, "parts", swap)
     slots = sent_rows.shape[0]
     width = groups * size
     whole = pl.BlockSpec(memory_space=pltpu.VMEM)
+    anywhere = pl.BlockSpec(memory_space=pl.ANY)
     scalars = pl.BlockSpec(memory_space=pltpu.SMEM)
     heads = width * HQ // (HQ + 2)
     half = jax.ShapeDtypeStruct((2 * slots, heads // 2 + width - heads), jnp.float32)
     keep, send, rows = pl.pallas_call(
         early_kernel,
         out_shape=(half, half, jax.ShapeDtypeStruct((2 * slots, depth), jnp.bfloat16)),
-        in_specs=[scalars] + [whole] * 15,
+        in_specs=[scalars] + [anywhere] * 12 + [whole] * 3,
         out_specs=(whole,) * 3,
-        scratch_shapes=[pltpu.VMEM((width, depth), jnp.bfloat16)],
+        scratch_shapes=[
+            pltpu.VMEM((2 * slots, depth), jnp.bfloat16),
+            pltpu.VMEM((width, depth), jnp.bfloat16),
+            pltpu.SemaphoreType.DMA((3,)),
+            pltpu.SemaphoreType.DMA((groups,)),
+        ],
         compiler_params=pltpu.CompilerParams(vmem_limit_bytes=28 << 20),
         cost_estimate=pl.CostEstimate(
             flops=4 * slots * width * depth, bytes_accessed=12 << 20, transcendentals=0
@@ -380,9 +414,12 @@
     keep, send = pl.pallas_call(
         late_kernel,
         out_shape=(half, half),
-        in_specs=[scalars] + [whole] * 5,
+        in_specs=[scalars] + [whole] * 2 + [anywhere] * 2 + [whole],
         out_specs=(whole, whole),
-        scratch_shapes=[pltpu.VMEM((heads // 2, depth), jnp.bfloat16)],
+        scratch_shapes=[
+            pltpu.VMEM((heads // 2, depth), jnp.bfloat16),
+            pltpu.SemaphoreType.DMA((2,)),
+        ],
         input_output_aliases={1: 0, 2: 1},
         compiler_params=pltpu.CompilerParams(vmem_limit_bytes=16 << 20),
         cost_estimate=pl.CostEstimate(

time: 102 us -> 103 us (level)
  waiting for transfers between devices: 44.5 us -> 41.8 us
  Pallas kernels: 14.2 us -> 16.9 us
  other arithmetic: 1.7 us -> 3.29 us
    ppermute x1, waiting for transfers between devices: 7.62 us -> 0.01 us  [paired(): ahead = lax.ppermute(sent_rows[:cut_at], 'parts', swap)]
    ppermute x10, waiting for transfers between devices: 21.2 us -> 25.1 us  [send(): return lax.ppermute(block, 'dp', pairs)]
    pallas_call x1, Pallas kernels: 8.12 us -> 10.5 us  [paired(): pl.pallas_call(early_kernel, out_shape=(half, half, jax.ShapeDtypeStruct(...]
    reduce_sum x1, other arithmetic: 0.49 us -> 2.08 us  [squares(): return jnp.sum(wide * wide, axis=1)]
    ppermute x1, starting transfers between devices: 1.58 us -> 0.51 us  [paired(): their_scale = lax.ppermute(scale, 'parts', swap)]
    ppermute x1, waiting for transfers between devices: 0.01 us -> 1.07 us  [paired(): behind = lax.ppermute(rest, 'parts', swap)]
  transfers between devices with their start and end apart: 15 -> 15, of which waited for: 8 -> 10; matrix products, arithmetic and copies ran while one was open for 5% -> 6% of each run, Pallas kernels for 8% -> 10%
where the time goes in v9:
time: 103 us
  waiting for transfers between devices  41.8 us (41%)
  starting transfers between devices  29.8 us (29%)
  Pallas kernels  16.9 us (16%)
  local copies, waits for them, and re-layouts  7.35 us (7%)
  other arithmetic  3.29 us (3%)
  blocking collectives  2.47 us (2%)
    ppermute x10, waiting for transfers between devices, send(): return lax.ppermute(block, 'dp', pairs)  25.1 us
    ppermute x10, starting transfers between devices, send(): return lax.ppermute(block, 'dp', pairs)  21.7 us
    all_to_all x1, waiting for transfers between devices, paired(): arrived = lax.all_to_all(ready, ('parts', 'dp'), 0, 0, tiled=True)  12.3 us
    pallas_call x1, Pallas kernels, paired(): pl.pallas_call(early_kernel, out_shape=(half, half, jax.ShapeDtypeStruct(...  10.5 us
    all_to_all x1, starting transfers between devices, paired(): arrived = lax.all_to_all(ready, ('parts', 'dp'), 0, 0, tiled=True)  4.46 us
    pallas_call x1, Pallas kernels, paired(): pl.pallas_call(late_kernel, out_shape=(half, half), in_specs=[scalars] +...  3.36 us
    unnamed x16, local copies, waits for them, and re-layouts  3.27 us
    psum x1, blocking collectives, paired(): scale = scale_of(lax.psum(squares(sent_rows), 'tensor'))  2.47 us
  transfers between devices with their start and end apart: 15, of which 10 were waited for; matrix products, arithmetic and copies ran while one was open for 6% of the time, Pallas kernels for 10%

profile of v9, /device:TPU:0, one launch (start us, length us, event | category | flops | bytes accessed | tf_op | source)
XLA Modules:
  0.0 102.5 jit_solution(11292859928921031815)
XLA Ops:
  0.6 0.0 copy-start
  0.6 0.0 copy-start.1
  0.7 1.3 %copy-done = bf16[4096,160]{0,1:T(8,128)(2,1)S(1)} copy-done((bf16[4096,160]{0,1:T(8,128)(2,1)S(1)}, bf16[4096,160]{0,1:T(8,128)(2,1)}, u32[]{:S(2)}) %copy-start) | copy-done | bytes 1310744
  2.0 0.9 constant_dynamic-slice_fusion
  2.8 3.0 %collective-permute-start = (bf16[80,4096]{1,0:T(8,128)(2,1)}, bf16[80,4096]{1,0:T(8,128)(2,1)}, u32[]{:S(2)}, u32[]{:S(2)}) collective-permute-start(bf16[80,4096]{1,0:T(8,128)(2,1)} %bitcast.6.mine), channel_id=1, source_target_pairs={{0,4},{2,6},{4,0},{6,2},{8,12},{10,14},{12,8},{14,10},{1,5},{3,7},... | collective-permute-start | bytes 1966088 | tf_op jit(solution)/shard_map/ppermute | solution.py:129
  5.9 1.5 %collective-permute-start.1 = (bf16[80,4096]{1,0:T(8,128)(2,1)}, bf16[80,4096]{1,0:T(8,128)(2,1)}, u32[]{:S(2)}, u32[]{:S(2)}) collective-permute-start(bf16[80,4096]{1,0:T(8,128)(2,1)} %bitcast.6.mine), channel_id=1, source_target_pairs={{4,8},{6,10},{8,4},{10,6},{0,2},{2,0},{12,14},{14,12},{5,9},{7,11}... | collective-permute-start | bytes 1966088 | tf_op jit(solution)/shard_map/ppermute | solution.py:129
  7.4 1.5 %collective-permute-start.2 = (bf16[80,4096]{1,0:T(8,128)(2,1)}, bf16[80,4096]{1,0:T(8,128)(2,1)}, u32[]{:S(2)}, u32[]{:S(2)}) collective-permute-start(bf16[80,4096]{1,0:T(8,128)(2,1)} %bitcast.6.mine), channel_id=1, source_target_pairs={{4,6},{6,4},{8,10},{10,8},{5,7},{7,5},{9,11},{11,9},{20,22},{22,20... | collective-permute-start | bytes 1966088 | tf_op jit(solution)/shard_map/ppermute | solution.py:129
  8.9 1.7 %slice.6 = bf16[32,4096]{1,0:T(8,128)(2,1)} slice(bf16[256,4096]{1,0:T(8,128)(2,1)} %own.1), slice={[0:32], [0:4096]} | slice | bytes 524288 | tf_op jit(solution)/shard_map/slice | solution.py:374
  10.5 1.5 %collective-permute-start.3 = (bf16[32,4096]{1,0:T(8,128)(2,1)}, bf16[32,4096]{1,0:T(8,128)(2,1)}, u32[]{:S(2)}, u32[]{:S(2)}) collective-permute-start(bf16[32,4096]{1,0:T(8,128)(2,1)} %slice.6), channel_id=1, source_target_pairs={{0,16},{16,0},{1,17},{17,1},{2,18},{18,2},{3,19},{19,3},{4,20},{20... | collective-permute-start | bytes 786440 | tf_op jit(solution)/shard_map/ppermute | solution.py:374
  12.0 2.1 %multiply_reduce_fusion = f32[256]{0:T(256)S(1)} fusion(bf16[256,4096]{1,0:T(8,128)(2,1)} %own.1), kind=kLoop, calls=%fused_computation | loop fusion | flops 3145472 | bytes 2098176 | tf_op jit(solution)/shard_map/reduce_sum | solution.py:74
  14.1 0.0 copy-start.7
  14.1 0.0 copy-start.4
  14.1 2.5 %psum.7 = f32[256]{0:T(256)S(1)} all-reduce(f32[256]{0:T(256)S(1)} %multiply_reduce_fusion), channel_id=1, replica_groups=mesh['parts'=2,'dp'=8,'tensor'=2] {'tensor'}, use_global_device_ids=true, to_apply=%region_3.4 | all-reduce | flops 256 | bytes 2048 | tf_op jit(solution)/shard_map/psum | solution.py:375
  16.6 0.5 collective-permute-start.4
  17.1 0.0 copy-done.1
  17.1 1.3 %slice.7 = bf16[224,4096]{1,0:T(8,128)(2,1)} slice(bf16[256,4096]{1,0:T(8,128)(2,1)S(1)} %copy-done.1), slice={[32:256], [0:4096]} | slice | bytes 3670016 | tf_op jit(solution)/shard_map/slice | solution.py:378
  18.5 1.7 %collective-permute-done.4 = f32[256]{0:T(256)S(1)} collective-permute-done((f32[256]{0:T(256)S(1)}, f32[256]{0:T(256)S(1)}, u32[]{:S(2)}, u32[]{:S(2)}) %collective-permute-start.4) | collective-permute-done | bytes 1056 | tf_op jit(solution)/shard_map/ppermute | solution.py:376
  20.2 0.0 collective-permute-done.3.ahead
  20.2 0.7 collective-permute-done.near
  20.9 1.5 %collective-permute-done.1.cross = bf16[80,4096]{1,0:T(8,128)(2,1)} collective-permute-done((bf16[80,4096]{1,0:T(8,128)(2,1)}, bf16[80,4096]{1,0:T(8,128)(2,1)}, u32[]{:S(2)}, u32[]{:S(2)}) %collective-permute-start.1) | collective-permute-done | bytes 655392 | tf_op jit(solution)/shard_map/ppermute | solution.py:129
  22.4 0.0 collective-permute-done.2.side
  22.4 1.5 %collective-permute-start.10 = (bf16[224,4096]{1,0:T(8,128)(2,1)}, bf16[224,4096]{1,0:T(8,128)(2,1)}, u32[]{:S(2)}, u32[]{:S(2)}) collective-permute-start(bf16[224,4096]{1,0:T(8,128)(2,1)} %slice.7), channel_id=1, source_target_pairs={{0,16},{16,0},{1,17},{17,1},{2,18},{18,2},{3,19},{19,3},{4,20},{20... | collective-permute-start | bytes 5505032 | tf_op jit(solution)/shard_map/ppermute | solution.py:380
  23.9 1.5 %collective-permute-start.6 = (bf16[80,4096]{1,0:T(8,128)(2,1)}, bf16[80,4096]{1,0:T(8,128)(2,1)}, u32[]{:S(2)}, u32[]{:S(2)}) collective-permute-start(bf16[80,4096]{1,0:T(8,128)(2,1)} %collective-permute-done.near), channel_id=1, source_target_pairs={{4,8},{6,10},{8,4},{10,6},{0,2},{2,0},{12,14},{14,12},{5,9},{7,11}... | collective-permute-start | bytes 1966088 | tf_op jit(solution)/shard_map/ppermute | solution.py:129
  25.4 0.7 collective-permute-start.7
  26.1 6.3 %collective-permute-start.5 = (bf16[80,4096]{1,0:T(8,128)(2,1)}, bf16[80,4096]{1,0:T(8,128)(2,1)}, u32[]{:S(2)}, u32[]{:S(2)}) collective-permute-start(bf16[80,4096]{1,0:T(8,128)(2,1)} %collective-permute-done.1.cross), channel_id=1, source_target_pairs={{0,4},{2,6},{4,0},{6,2},{8,12},{10,14},{12,8},{14,10},{1,5},{3,7},... | collective-permute-start | bytes 1966088 | tf_op jit(solution)/shard_map/ppermute | solution.py:129
  32.4 6.8 %collective-permute-done.6.onward = bf16[80,4096]{1,0:T(8,128)(2,1)} collective-permute-done((bf16[80,4096]{1,0:T(8,128)(2,1)}, bf16[80,4096]{1,0:T(8,128)(2,1)}, u32[]{:S(2)}, u32[]{:S(2)}) %collective-permute-start.6) | collective-permute-done | bytes 655392 | tf_op jit(solution)/shard_map/ppermute | solution.py:129
  39.2 1.3 %collective-permute-start.11 = (bf16[80,4096]{1,0:T(8,128)(2,1)}, bf16[80,4096]{1,0:T(8,128)(2,1)}, u32[]{:S(2)}, u32[]{:S(2)}) collective-permute-start(bf16[80,4096]{1,0:T(8,128)(2,1)} %collective-permute-done.6.onward), channel_id=1, source_target_pairs={{4,0},{6,2},{8,12},{10,14},{5,1},{7,3},{9,13},{11,15},{20,16},{22,... | collective-permute-start | bytes 1966088 | tf_op jit(solution)/shard_map/ppermute | solution.py:129
  40.5 0.0 collective-permute-done.7.cross_over
  40.5 0.0 copy-start.2
  40.5 0.9 copy-done.2
  41.4 1.6 %collective-permute-start.8 = (bf16[80,4096]{1,0:T(8,128)(2,1)}, bf16[80,4096]{1,0:T(8,128)(2,1)}, u32[]{:S(2)}, u32[]{:S(2)}) collective-permute-start(bf16[80,4096]{1,0:T(8,128)(2,1)} %collective-permute-done.6.onward), channel_id=1, source_target_pairs={{4,6},{6,4},{8,10},{10,8},{5,7},{7,5},{9,11},{11,9},{20,22},{22,20... | collective-permute-start | bytes 1966088 | tf_op jit(solution)/shard_map/ppermute | solution.py:129
  42.9 4.6 %collective-permute-done.5.second = bf16[80,4096]{1,0:T(8,128)(2,1)} collective-permute-done((bf16[80,4096]{1,0:T(8,128)(2,1)}, bf16[80,4096]{1,0:T(8,128)(2,1)}, u32[]{:S(2)}, u32[]{:S(2)}) %collective-permute-start.5) | collective-permute-done | bytes 655392 | tf_op jit(solution)/shard_map/ppermute | solution.py:129
  47.5 1.9 %collective-permute-start.9 = (bf16[80,4096]{1,0:T(8,128)(2,1)}, bf16[80,4096]{1,0:T(8,128)(2,1)}, u32[]{:S(2)}, u32[]{:S(2)}) collective-permute-start(bf16[80,4096]{1,0:T(8,128)(2,1)} %collective-permute-done.5.second), channel_id=1, source_target_pairs={{0,2},{2,0},{12,14},{14,12},{1,3},{3,1},{13,15},{15,13},{16,18},{1... | collective-permute-start | bytes 1966088 | tf_op jit(solution)/shard_map/ppermute | solution.py:129
  49.4 10.0 %collective-permute-done.11.piece = bf16[80,4096]{1,0:T(8,128)(2,1)} collective-permute-done((bf16[80,4096]{1,0:T(8,128)(2,1)}, bf16[80,4096]{1,0:T(8,128)(2,1)}, u32[]{:S(2)}, u32[]{:S(2)}) %collective-permute-start.11) | collective-permute-done | bytes 655392 | tf_op jit(solution)/shard_map/ppermute | solution.py:129
  59.5 2.4 %collective-permute-start.12 = (bf16[80,4096]{1,0:T(8,128)(2,1)}, bf16[80,4096]{1,0:T(8,128)(2,1)}, u32[]{:S(2)}, u32[]{:S(2)}) collective-permute-start(bf16[80,4096]{1,0:T(8,128)(2,1)} %collective-permute-done.11.piece), channel_id=1, source_target_pairs={{0,2},{2,0},{12,14},{14,12},{1,3},{3,1},{13,15},{15,13},{16,18},{1... | collective-permute-start | bytes 1966088 | tf_op jit(solution)/shard_map/ppermute | solution.py:129
  61.9 0.0 copy-done.7
  61.9 0.2 reduce-window.13
  62.1 0.1 pad_add_fusion.at
  62.2 0.0 collective-permute-done.8.far_over
  62.2 0.0 collective-permute-done.9.second_over
  62.2 1.1 %collective-permute-done.10.behind = bf16[224,4096]{1,0:T(8,128)(2,1)} collective-permute-done((bf16[224,4096]{1,0:T(8,128)(2,1)}, bf16[224,4096]{1,0:T(8,128)(2,1)}, u32[]{:S(2)}, u32[]{:S(2)}) %collective-permute-start.10) | collective-permute-done | bytes 1835040 | tf_op jit(solution)/shard_map/ppermute | solution.py:380
  63.3 0.0 copy-done.4
  63.3 0.0 copy-start.3
  63.3 1.1 %copy-done.3 = bf16[80,4096]{1,0:T(8,128)(2,1)S(1)} copy-done((bf16[80,4096]{1,0:T(8,128)(2,1)S(1)}, bf16[80,4096]{1,0:T(8,128)(2,1)}, u32[]{:S(2)}) %copy-start.3) | copy-done | bytes 655384
  64.3 10.5 %project_early.1 = (f32[512,384]{1,0:T(8,128)S(1)}, f32[512,384]{1,0:T(8,128)S(1)}, bf16[512,4096]{1,0:T(8,128)(2,1)S(1)}) custom-call(s32[4]{0:T(128)S(1)} %pad_add_fusion.at, bf16[80,4096]{1,0:T(8,128)(2,1)} %bitcast.6.mine, bf16[80,4096]{1,0:T(8,128)(2,1)} %collective-permute-done.near, bf16[80,4096]{1,0:T(8,128)(2,1)} %collective-permute-done.1.cross, ...), custom_call_target="tpu_custom_call" | custom-call | flops 2684354560 | bytes 12582912 | tf_op jit(solution)/shard_map/project_early/pallas_call | solution.py:388
  74.8 1.5 %collective-permute-done.12.piece_over = bf16[80,4096]{1,0:T(8,128)(2,1)} collective-permute-done((bf16[80,4096]{1,0:T(8,128)(2,1)}, bf16[80,4096]{1,0:T(8,128)(2,1)}, u32[]{:S(2)}, u32[]{:S(2)}) %collective-permute-start.12) | collective-permute-done | bytes 655392 | tf_op jit(solution)/shard_map/ppermute | solution.py:129
  76.3 0.0 copy-start.6
  76.3 3.4 %project_late.1 = (f32[512,384]{1,0:T(8,128)S(1)}, f32[512,384]{1,0:T(8,128)S(1)}) custom-call(s32[4]{0:T(128)S(1)} %pad_add_fusion.at, f32[512,384]{1,0:T(8,128)S(1)} %get-tuple-element.24.first_keep, f32[512,384]{1,0:T(8,128)S(1)} %get-tuple-element.25.first_send, ...), custom_call_target="tpu_custom_call", output_to_operand_aliasing={{0}: (1, {}), {1}: (2, {})} | custom-call | flops 1073741824 | bytes 6291456 | tf_op jit(solution)/shard_map/project_late/pallas_call | solution.py:414
  79.7 0.1 collective-permute-start.13
  79.8 0.0 copy-done.6
  79.8 0.1 select_reduce_fusion
  79.9 0.0 copy-done.5
  79.9 0.2 fusion.5
  80.1 0.3 fusion.1
  80.4 1.6 %collective-permute-done.13.other = f32[512,384]{1,0:T(8,128)S(1)} collective-permute-done((f32[512,384]{1,0:T(8,128)S(1)}, f32[512,384]{1,0:T(8,128)S(1)}, u32[]{:S(2)}, u32[]{:S(2)}) %collective-permute-start.13) | collective-permute-done | bytes 786464 | tf_op jit(solution)/shard_map/ppermute | solution.py:437
  82.0 0.8 sum_halves.1
  82.9 4.5 %all-to-all-start = ((bf16[16,32,384]{2,1,0:T(8,128)(2,1)}), bf16[16,32,384]{2,1,0:T(8,128)(2,1)S(1)}, u32[]{:S(2)}, u32[]{:S(2)}) async-start(bf16[16,32,384]{2,1,0:T(8,128)(2,1)} %bitcast.10), calls=%async_computation | async-start | bytes 786432 | tf_op jit(solution)/shard_map/all_to_all | solution.py:438
  87.4 0.1 reduce
  87.5 0.1 pad_maximum_fusion
  87.6 0.1 select_reduce_fusion.2
  87.7 0.1 fusion.pick
  87.8 0.1 and_convert_fusion.allowed
  87.9 12.3 %all-to-all-done = bf16[16,32,384]{2,1,0:T(8,128)(2,1)S(1)} async-done(((bf16[16,32,384]{2,1,0:T(8,128)(2,1)}), bf16[16,32,384]{2,1,0:T(8,128)(2,1)S(1)}, u32[]{:S(2)}, u32[]{:S(2)}) %all-to-all-start) | async-done | bytes 393248 | tf_op jit(solution)/shard_map/all_to_all | solution.py:438
  100.2 2.3 %attend.1 = (bf16[128,128]{1,0:T(8,128)(2,1)}, bf16[128,128]{1,0:T(8,128)(2,1)}, bf16[128,512]{1,0:T(8,128)(2,1)}) custom-call(bf16[128,256]{1,0:T(8,128)(2,1)S(1)} %fusion.pick, bf16[2,256,384]{2,1,0:T(8,128)(2,1)S(1)} %bitcast.25, f32[128,128]{1,0:T(8,128)S(1)} %get-tuple-element.36.cosine, f32[128,128]{1,0:T(8,128)S(1)} %get-tuple-element.37.sine, ...), custom_call_target="tpu_custom_call" | custom-call | tf_op jit(solution)/shard_map/attend/pallas_call | solution.py:345
  (8 shorter events, 0.1 us)
Async XLA Ops:
  0.6 1.3 %copy-start = (bf16[4096,160]{0,1:T(8,128)(2,1)S(1)}, bf16[4096,160]{0,1:T(8,128)(2,1)}, u32[]{:S(2)}) copy-start(bf16[4096,160]{0,1:T(8,128)(2,1)} %param.8) | copy-start | bytes 3932164
  0.6 16.5 %copy-start.1 = (bf16[256,4096]{1,0:T(8,128)(2,1)S(1)}, bf16[256,4096]{1,0:T(8,128)(2,1)}, u32[]{:S(2)}) copy-start(bf16[256,4096]{1,0:T(8,128)(2,1)} %own.1) | copy-start | bytes 6291460
  2.8 18.1 %collective-permute-start = (bf16[80,4096]{1,0:T(8,128)(2,1)}, bf16[80,4096]{1,0:T(8,128)(2,1)}, u32[]{:S(2)}, u32[]{:S(2)}) collective-permute-start(bf16[80,4096]{1,0:T(8,128)(2,1)} %bitcast.6.mine), channel_id=1, source_target_pairs={{0,4},{2,6},{4,0},{6,2},{8,12},{10,14},{12,8},{14,10},{1,5},{3,7},... | collective-permute-start | bytes 1966088 | tf_op jit(solution)/shard_map/ppermute | solution.py:129
  5.9 16.5 %collective-permute-start.1 = (bf16[80,4096]{1,0:T(8,128)(2,1)}, bf16[80,4096]{1,0:T(8,128)(2,1)}, u32[]{:S(2)}, u32[]{:S(2)}) collective-permute-start(bf16[80,4096]{1,0:T(8,128)(2,1)} %bitcast.6.mine), channel_id=1, source_target_pairs={{4,8},{6,10},{8,4},{10,6},{0,2},{2,0},{12,14},{14,12},{5,9},{7,11}... | collective-permute-start | bytes 1966088 | tf_op jit(solution)/shard_map/ppermute | solution.py:129
  7.4 15.0 %collective-permute-start.2 = (bf16[80,4096]{1,0:T(8,128)(2,1)}, bf16[80,4096]{1,0:T(8,128)(2,1)}, u32[]{:S(2)}, u32[]{:S(2)}) collective-permute-start(bf16[80,4096]{1,0:T(8,128)(2,1)} %bitcast.6.mine), channel_id=1, source_target_pairs={{4,6},{6,4},{8,10},{10,8},{5,7},{7,5},{9,11},{11,9},{20,22},{22,20... | collective-permute-start | bytes 1966088 | tf_op jit(solution)/shard_map/ppermute | solution.py:129
  10.5 9.7 %collective-permute-start.3 = (bf16[32,4096]{1,0:T(8,128)(2,1)}, bf16[32,4096]{1,0:T(8,128)(2,1)}, u32[]{:S(2)}, u32[]{:S(2)}) collective-permute-start(bf16[32,4096]{1,0:T(8,128)(2,1)} %slice.6), channel_id=1, source_target_pairs={{0,16},{16,0},{1,17},{17,1},{2,18},{18,2},{3,19},{19,3},{4,20},{20... | collective-permute-start | bytes 786440 | tf_op jit(solution)/shard_map/ppermute | solution.py:374
  14.1 47.8 %copy-start.7 = (s32[1,8]{1,0:T(1,128)S(1)}, s32[1,8]{1,0:T(1,128)}, u32[]{:S(2)}) copy-start(s32[1,8]{1,0:T(1,128)} %param.10) | copy-start | bytes 100
  14.1 49.1 %copy-start.4 = (f32[4096]{0:T(1024)S(1)}, f32[4096]{0:T(1024)}, u32[]{:S(2)}) copy-start(f32[4096]{0:T(1024)} %param.7) | copy-start | bytes 49156
  16.6 3.6 %collective-permute-start.4 = (f32[256]{0:T(256)S(1)}, f32[256]{0:T(256)S(1)}, u32[]{:S(2)}, u32[]{:S(2)}) collective-permute-start(f32[256]{0:T(256)S(1)} %add_rsqrt_fusion), channel_id=1, source_target_pairs={{0,16},{16,0},{1,17},{17,1},{2,18},{18,2},{3,19},{19,3},{4,20},{20... | collective-permute-start | bytes 3080 | tf_op jit(solution)/shard_map/ppermute | solution.py:376
  22.4 40.9 %collective-permute-start.10 = (bf16[224,4096]{1,0:T(8,128)(2,1)}, bf16[224,4096]{1,0:T(8,128)(2,1)}, u32[]{:S(2)}, u32[]{:S(2)}) collective-permute-start(bf16[224,4096]{1,0:T(8,128)(2,1)} %slice.7), channel_id=1, source_target_pairs={{0,16},{16,0},{1,17},{17,1},{2,18},{18,2},{3,19},{19,3},{4,20},{20... | collective-permute-start | bytes 5505032 | tf_op jit(solution)/shard_map/ppermute | solution.py:380
  23.9 15.3 %collective-permute-start.6 = (bf16[80,4096]{1,0:T(8,128)(2,1)}, bf16[80,4096]{1,0:T(8,128)(2,1)}, u32[]{:S(2)}, u32[]{:S(2)}) collective-permute-start(bf16[80,4096]{1,0:T(8,128)(2,1)} %collective-permute-done.near), channel_id=1, source_target_pairs={{4,8},{6,10},{8,4},{10,6},{0,2},{2,0},{12,14},{14,12},{5,9},{7,11}... | collective-permute-start | bytes 1966088 | tf_op jit(solution)/shard_map/ppermute | solution.py:129
  25.4 15.1 %collective-permute-start.7 = (bf16[80,4096]{1,0:T(8,128)(2,1)}, bf16[80,4096]{1,0:T(8,128)(2,1)S(1)}, u32[]{:S(2)}, u32[]{:S(2)}) collective-permute-start(bf16[80,4096]{1,0:T(8,128)(2,1)} %collective-permute-done.1.cross), channel_id=1, source_target_pairs={{4,6},{6,4},{8,10},{10,8},{5,7},{7,5},{9,11},{11,9},{20,22},{22,20... | collective-permute-start | bytes 1966088 | tf_op jit(solution)/shard_map/ppermute | solution.py:129
  26.1 21.4 %collective-permute-start.5 = (bf16[80,4096]{1,0:T(8,128)(2,1)}, bf16[80,4096]{1,0:T(8,128)(2,1)}, u32[]{:S(2)}, u32[]{:S(2)}) collective-permute-start(bf16[80,4096]{1,0:T(8,128)(2,1)} %collective-permute-done.1.cross), channel_id=1, source_target_pairs={{0,4},{2,6},{4,0},{6,2},{8,12},{10,14},{12,8},{14,10},{1,5},{3,7},... | collective-permute-start | bytes 1966088 | tf_op jit(solution)/shard_map/ppermute | solution.py:129
  39.2 20.2 %collective-permute-start.11 = (bf16[80,4096]{1,0:T(8,128)(2,1)}, bf16[80,4096]{1,0:T(8,128)(2,1)}, u32[]{:S(2)}, u32[]{:S(2)}) collective-permute-start(bf16[80,4096]{1,0:T(8,128)(2,1)} %collective-permute-done.6.onward), channel_id=1, source_target_pairs={{4,0},{6,2},{8,12},{10,14},{5,1},{7,3},{9,13},{11,15},{20,16},{22,... | collective-permute-start | bytes 1966088 | tf_op jit(solution)/shard_map/ppermute | solution.py:129
  40.5 0.9 copy-start.2
  41.4 20.8 %collective-permute-start.8 = (bf16[80,4096]{1,0:T(8,128)(2,1)}, bf16[80,4096]{1,0:T(8,128)(2,1)}, u32[]{:S(2)}, u32[]{:S(2)}) collective-permute-start(bf16[80,4096]{1,0:T(8,128)(2,1)} %collective-permute-done.6.onward), channel_id=1, source_target_pairs={{4,6},{6,4},{8,10},{10,8},{5,7},{7,5},{9,11},{11,9},{20,22},{22,20... | collective-permute-start | bytes 1966088 | tf_op jit(solution)/shard_map/ppermute | solution.py:129
  47.5 14.7 %collective-permute-start.9 = (bf16[80,4096]{1,0:T(8,128)(2,1)}, bf16[80,4096]{1,0:T(8,128)(2,1)}, u32[]{:S(2)}, u32[]{:S(2)}) collective-permute-start(bf16[80,4096]{1,0:T(8,128)(2,1)} %collective-permute-done.5.second), channel_id=1, source_target_pairs={{0,2},{2,0},{12,14},{14,12},{1,3},{3,1},{13,15},{15,13},{16,18},{1... | collective-permute-start | bytes 1966088 | tf_op jit(solution)/shard_map/ppermute | solution.py:129
  59.5 16.9 %collective-permute-start.12 = (bf16[80,4096]{1,0:T(8,128)(2,1)}, bf16[80,4096]{1,0:T(8,128)(2,1)}, u32[]{:S(2)}, u32[]{:S(2)}) collective-permute-start(bf16[80,4096]{1,0:T(8,128)(2,1)} %collective-permute-done.11.piece), channel_id=1, source_target_pairs={{0,2},{2,0},{12,14},{14,12},{1,3},{3,1},{13,15},{15,13},{16,18},{1... | collective-permute-start | bytes 1966088 | tf_op jit(solution)/shard_map/ppermute | solution.py:129
  63.3 1.1 %copy-start.3 = (bf16[80,4096]{1,0:T(8,128)(2,1)S(1)}, bf16[80,4096]{1,0:T(8,128)(2,1)}, u32[]{:S(2)}) copy-start(bf16[80,4096]{1,0:T(8,128)(2,1)} %copy-done.2) | copy-start | bytes 1966084
  76.3 3.5 %copy-start.6 = (s32[1,8]{1,0:T(1,128)S(1)}, s32[1,8]{1,0:T(1,128)}, u32[]{:S(2)}) copy-start(s32[1,8]{1,0:T(1,128)} %param.11) | copy-start | bytes 100
  76.3 3.6 %copy-start.5 = (s32[8,8]{1,0:T(8,128)S(1)}, s32[8,8]{1,0:T(8,128)}, u32[]{:S(2)}) copy-start(s32[8,8]{1,0:T(8,128)} %param.9) | copy-start | bytes 772
  79.7 2.4 %collective-permute-start.13 = (f32[512,384]{1,0:T(8,128)S(1)}, f32[512,384]{1,0:T(8,128)S(1)}, u32[]{:S(2)}, u32[]{:S(2)}) collective-permute-start(f32[512,384]{1,0:T(8,128)S(1)} %get-tuple-element.28), channel_id=1, source_target_pairs={{0,1},{1,0},{2,3},{3,2},{4,5},{5,4},{6,7},{7,6},{8,9},{9,8},{10,11... | collective-permute-start | bytes 2359304 | tf_op jit(solution)/shard_map/ppermute | solution.py:437
  82.9 17.4 %all-to-all-start = ((bf16[16,32,384]{2,1,0:T(8,128)(2,1)}), bf16[16,32,384]{2,1,0:T(8,128)(2,1)S(1)}, u32[]{:S(2)}, u32[]{:S(2)}) async-start(bf16[16,32,384]{2,1,0:T(8,128)(2,1)} %bitcast.10), calls=%async_computation | async-start | bytes 786432 | tf_op jit(solution)/shard_map/all_to_all | solution.py:438

commit v10 on v8

--- a/solution.py
+++ b/solution.py
@@ -131,14 +131,16 @@
     near = send(mine, alongs(PAIRS))
     cross = send(mine, alongs(ACROSS) + overs(ENDS))
     side = send(mine, overs(MIDDLE))
-    near, cross, side, first = lax.optimization_barrier((near, cross, side, first))
+    near, cross, first = lax.optimization_barrier((near, cross, first))
     second = send(cross, alongs(PAIRS))
     onward = send(near, alongs(ACROSS) + overs(ENDS))
-    cross_over = send(cross, overs(MIDDLE))
-    onward, cross_over = lax.optimization_barrier((onward, cross_over))
-    last = send(onward, alongs(OUTWARD))
-    far_over = send(onward, overs(MIDDLE))
+    cross_next, side = lax.optimization_barrier((cross, side))
+    cross_over = send(cross_next, overs(MIDDLE))
+    onward_next, _ = lax.optimization_barrier((onward, second))
+    last = send(onward_next, alongs(OUTWARD))
     second_over = send(second, overs(ENDS))
+    onward_next, _ = lax.optimization_barrier((onward, cross_over))
+    far_over = send(onward_next, overs(MIDDLE))
     last_over = send(last, overs(ENDS))
     early = (mine, near, cross, side, second, onward, cross_over, far_over, second_over)
     return early, (last, last_over), first
@@ -340,20 +342,24 @@
     depth = turned.shape[1]
     count = turned.shape[0] // (2 * BLOCK)
     size = count * BLOCK
+    swap = [(0, 1), (1, 0)]
+    cut_at = sent_rows.shape[0] * 3 // 16
+    whole = pl.BlockSpec(memory_space=pltpu.VMEM)
+    anywhere = pl.BlockSpec(memory_space=pl.ANY)
+    scalars = pl.BlockSpec(memory_space=pltpu.SMEM)
     mine = lax.dynamic_index_in_dim(
         turned.reshape(count, 2, BLOCK, depth), part, 1, False
     ).reshape(size, depth)
-    swap = [(0, 1), (1, 0)]
-    cut_at = sent_rows.shape[0] // 4
-    ahead = lax.ppermute(sent_rows[:cut_at], "parts", swap)
+    ahead = sent_rows[:cut_at]
+    ahead = lax.ppermute(ahead, "parts", swap)
     scale = scale_of(lax.psum(squares(sent_rows), "tensor"))
-    early, late, (ahead, rest, scale) = gather_line(mine, (ahead, sent_rows[cut_at:], scale))
+    their_scale = lax.ppermute(scale, "parts", swap)
+    early, late, (ahead, rest, their_scale) = gather_line(
+        mine, (ahead, sent_rows[cut_at:], their_scale)
+    )
     behind = lax.ppermute(rest, "parts", swap)
-    their_scale = lax.ppermute(scale, "parts", swap)
     slots = sent_rows.shape[0]
     width = groups * size
-    whole = pl.BlockSpec(memory_space=pltpu.VMEM)
-    scalars = pl.BlockSpec(memory_space=pltpu.SMEM)
     heads = width * HQ // (HQ + 2)
     half = jax.ShapeDtypeStruct((2 * slots, heads // 2 + width - heads), jnp.float32)
     keep, send, rows = pl.pallas_call(

time: 102 us -> 100 us (0.980)
  starting transfers between devices: 30.3 us -> 28.4 us
    ppermute x1, waiting for transfers between devices: 7.62 us -> 0.01 us  [paired(): ahead = lax.ppermute(ahead, 'parts', swap)]
    ppermute x10, waiting for transfers between devices: 21.2 us -> 24.6 us  [send(): return lax.ppermute(block, 'dp', pairs)]
    ppermute x1, waiting for transfers between devices: 1.79 us -> 4.31 us  [paired(): their_scale = lax.ppermute(scale, 'parts', swap)]
    ppermute x1, waiting for transfers between devices: 0.01 us -> 1.78 us  [paired(): behind = lax.ppermute(rest, 'parts', swap)]
    ppermute x10, starting transfers between devices: 20.9 us -> 19.6 us  [send(): return lax.ppermute(block, 'dp', pairs)]
    ppermute x1, starting transfers between devices: 1.58 us -> 0.51 us  [paired(): their_scale = lax.ppermute(scale, 'parts', swap)]
  transfers between devices with their start and end apart: 15 -> 15, of which waited for: 8 -> 10; matrix products, arithmetic and copies ran while one was open for 5% -> 5% of each run, Pallas kernels for 8% -> 8%
where the time goes in v10:
time: 100 us; the launch traced here: 99.6 us
  waiting for transfers between devices  44.7 us (45%)
  starting transfers between devices  28.4 us (28%)
  Pallas kernels  14.2 us (14%)
  local copies, waits for them, and re-layouts  7.37 us (7%)
  blocking collectives  2.47 us (2%)
  other arithmetic  1.7 us (2%)
    ppermute x10, waiting for transfers between devices, send(): return lax.ppermute(block, 'dp', pairs)  24.6 us
    ppermute x10, starting transfers between devices, send(): return lax.ppermute(block, 'dp', pairs)  19.6 us
    all_to_all x1, waiting for transfers between devices, paired(): arrived = lax.all_to_all(ready, ('parts', 'dp'), 0, 0, tiled=True)  12.3 us
    pallas_call x1, Pallas kernels, paired(): pl.pallas_call(early_kernel, out_shape=(half, half, jax.ShapeDtypeStruct(...  8.13 us
    all_to_all x1, starting transfers between devices, paired(): arrived = lax.all_to_all(ready, ('parts', 'dp'), 0, 0, tiled=True)  5.13 us
    ppermute x1, waiting for transfers between devices, paired(): their_scale = lax.ppermute(scale, 'parts', swap)  4.31 us
    unnamed x16, local copies, waits for them, and re-layouts  3.23 us
    pallas_call x1, Pallas kernels, paired(): pl.pallas_call(late_kernel, out_shape=(half, half), in_specs=[scalars] +...  2.92 us
  transfers between devices with their start and end apart: 15, of which 10 were waited for; matrix products, arithmetic and copies ran while one was open for 5% of the time, Pallas kernels for 8%

profile of v10, /device:TPU:0, one launch (start us, length us, event | category | flops | bytes accessed | tf_op | source)
XLA Modules:
  0.0 99.6 jit_solution(8949668068598910641)
XLA Ops:
  0.6 0.0 copy-start
  0.6 0.0 copy-start.1
  0.7 1.3 %copy-done = bf16[4096,160]{0,1:T(8,128)(2,1)S(1)} copy-done((bf16[4096,160]{0,1:T(8,128)(2,1)S(1)}, bf16[4096,160]{0,1:T(8,128)(2,1)}, u32[]{:S(2)}) %copy-start) | copy-done | bytes 1310744
  2.0 0.9 constant_dynamic-slice_fusion
  2.8 3.0 %collective-permute-start = (bf16[80,4096]{1,0:T(8,128)(2,1)}, bf16[80,4096]{1,0:T(8,128)(2,1)}, u32[]{:S(2)}, u32[]{:S(2)}) collective-permute-start(bf16[80,4096]{1,0:T(8,128)(2,1)} %bitcast.6.mine), channel_id=1, source_target_pairs={{0,4},{2,6},{4,0},{6,2},{8,12},{10,14},{12,8},{14,10},{1,5},{3,7},... | collective-permute-start | bytes 1966088 | tf_op jit(solution)/shard_map/ppermute | solution.py:129
  5.9 1.5 %collective-permute-start.1 = (bf16[80,4096]{1,0:T(8,128)(2,1)}, bf16[80,4096]{1,0:T(8,128)(2,1)}, u32[]{:S(2)}, u32[]{:S(2)}) collective-permute-start(bf16[80,4096]{1,0:T(8,128)(2,1)} %bitcast.6.mine), channel_id=1, source_target_pairs={{4,8},{6,10},{8,4},{10,6},{0,2},{2,0},{12,14},{14,12},{5,9},{7,11}... | collective-permute-start | bytes 1966088 | tf_op jit(solution)/shard_map/ppermute | solution.py:129
  7.4 1.5 %collective-permute-start.4 = (bf16[80,4096]{1,0:T(8,128)(2,1)}, bf16[80,4096]{1,0:T(8,128)(2,1)}, u32[]{:S(2)}, u32[]{:S(2)}) collective-permute-start(bf16[80,4096]{1,0:T(8,128)(2,1)} %bitcast.6.mine), channel_id=1, source_target_pairs={{4,6},{6,4},{8,10},{10,8},{5,7},{7,5},{9,11},{11,9},{20,22},{22,20... | collective-permute-start | bytes 1966088 | tf_op jit(solution)/shard_map/ppermute | solution.py:129
  8.9 1.8 %slice.6 = bf16[48,4096]{1,0:T(8,128)(2,1)} slice(bf16[256,4096]{1,0:T(8,128)(2,1)} %own.1), slice={[0:48], [0:4096]} | slice | bytes 786432 | tf_op jit(solution)/shard_map/slice | solution.py:353
  10.7 1.5 %collective-permute-start.2 = (bf16[48,4096]{1,0:T(8,128)(2,1)}, bf16[48,4096]{1,0:T(8,128)(2,1)}, u32[]{:S(2)}, u32[]{:S(2)}) collective-permute-start(bf16[48,4096]{1,0:T(8,128)(2,1)} %slice.6), channel_id=1, source_target_pairs={{0,16},{16,0},{1,17},{17,1},{2,18},{18,2},{3,19},{19,3},{4,20},{20... | collective-permute-start | bytes 1179656 | tf_op jit(solution)/shard_map/ppermute | solution.py:354
  12.2 0.0 copy-done.1
  12.2 0.5 multiply_reduce_fusion
  12.7 0.0 copy-start.4
  12.7 2.5 %psum.7 = f32[256]{0:T(256)S(1)} all-reduce(f32[256]{0:T(256)S(1)} %multiply_reduce_fusion), channel_id=1, replica_groups=mesh['parts'=2,'dp'=8,'tensor'=2] {'tensor'}, use_global_device_ids=true, to_apply=%region_3.4 | all-reduce | flops 256 | bytes 2048 | tf_op jit(solution)/shard_map/psum | solution.py:355
  15.2 0.5 collective-permute-start.3
  15.7 1.3 %slice.7 = bf16[208,4096]{1,0:T(8,128)(2,1)} slice(bf16[256,4096]{1,0:T(8,128)(2,1)S(1)} %copy-done.1), slice={[48:256], [0:4096]} | slice | bytes 3407872 | tf_op jit(solution)/shard_map/slice | solution.py:358
  17.0 4.3 %collective-permute-done.3 = f32[256]{0:T(256)S(1)} collective-permute-done((f32[256]{0:T(256)S(1)}, f32[256]{0:T(256)S(1)}, u32[]{:S(2)}, u32[]{:S(2)}) %collective-permute-start.3) | collective-permute-done | bytes 1056 | tf_op jit(solution)/shard_map/ppermute | solution.py:356
  21.3 0.0 collective-permute-done.2.ahead
  21.3 0.0 collective-permute-done.near
  21.3 1.1 %collective-permute-done.1.cross = bf16[80,4096]{1,0:T(8,128)(2,1)} collective-permute-done((bf16[80,4096]{1,0:T(8,128)(2,1)}, bf16[80,4096]{1,0:T(8,128)(2,1)}, u32[]{:S(2)}, u32[]{:S(2)}) %collective-permute-start.1) | collective-permute-done | bytes 655392 | tf_op jit(solution)/shard_map/ppermute | solution.py:129
  22.4 1.5 %collective-permute-start.6 = (bf16[80,4096]{1,0:T(8,128)(2,1)}, bf16[80,4096]{1,0:T(8,128)(2,1)}, u32[]{:S(2)}, u32[]{:S(2)}) collective-permute-start(bf16[80,4096]{1,0:T(8,128)(2,1)} %collective-permute-done.near), channel_id=1, source_target_pairs={{4,8},{6,10},{8,4},{10,6},{0,2},{2,0},{12,14},{14,12},{5,9},{7,11}... | collective-permute-start | bytes 1966088 | tf_op jit(solution)/shard_map/ppermute | solution.py:129
  23.9 1.7 %collective-permute-start.5 = (bf16[80,4096]{1,0:T(8,128)(2,1)}, bf16[80,4096]{1,0:T(8,128)(2,1)}, u32[]{:S(2)}, u32[]{:S(2)}) collective-permute-start(bf16[80,4096]{1,0:T(8,128)(2,1)} %collective-permute-done.1.cross), channel_id=1, source_target_pairs={{0,4},{2,6},{4,0},{6,2},{8,12},{10,14},{12,8},{14,10},{1,5},{3,7},... | collective-permute-start | bytes 1966088 | tf_op jit(solution)/shard_map/ppermute | solution.py:129
  25.5 1.5 %collective-permute-start.10 = (bf16[208,4096]{1,0:T(8,128)(2,1)}, bf16[208,4096]{1,0:T(8,128)(2,1)}, u32[]{:S(2)}, u32[]{:S(2)}) collective-permute-start(bf16[208,4096]{1,0:T(8,128)(2,1)} %slice.7), channel_id=1, source_target_pairs={{0,16},{16,0},{1,17},{17,1},{2,18},{18,2},{3,19},{19,3},{4,20},{20... | collective-permute-start | bytes 5111816 | tf_op jit(solution)/shard_map/ppermute | solution.py:360
  27.1 0.0 collective-permute-done.4.side
  27.1 0.7 collective-permute-start.7
  27.8 10.2 %collective-permute-done.6.onward = bf16[80,4096]{1,0:T(8,128)(2,1)} collective-permute-done((bf16[80,4096]{1,0:T(8,128)(2,1)}, bf16[80,4096]{1,0:T(8,128)(2,1)}, u32[]{:S(2)}, u32[]{:S(2)}) %collective-permute-start.6) | collective-permute-done | bytes 655392 | tf_op jit(solution)/shard_map/ppermute | solution.py:129
  38.0 1.2 %collective-permute-done.5.second = bf16[80,4096]{1,0:T(8,128)(2,1)} collective-permute-done((bf16[80,4096]{1,0:T(8,128)(2,1)}, bf16[80,4096]{1,0:T(8,128)(2,1)}, u32[]{:S(2)}, u32[]{:S(2)}) %collective-permute-start.5) | collective-permute-done | bytes 655392 | tf_op jit(solution)/shard_map/ppermute | solution.py:129
  39.2 1.3 %collective-permute-start.11 = (bf16[80,4096]{1,0:T(8,128)(2,1)}, bf16[80,4096]{1,0:T(8,128)(2,1)}, u32[]{:S(2)}, u32[]{:S(2)}) collective-permute-start(bf16[80,4096]{1,0:T(8,128)(2,1)} %collective-permute-done.6.onward), channel_id=1, source_target_pairs={{4,0},{6,2},{8,12},{10,14},{5,1},{7,3},{9,13},{11,15},{20,16},{22,... | collective-permute-start | bytes 1966088 | tf_op jit(solution)/shard_map/ppermute | solution.py:129
  40.5 0.0 collective-permute-done.7.cross_over
  40.5 0.0 copy-start.2
  40.5 0.8 copy-done.2
  41.3 1.6 %collective-permute-start.8 = (bf16[80,4096]{1,0:T(8,128)(2,1)}, bf16[80,4096]{1,0:T(8,128)(2,1)}, u32[]{:S(2)}, u32[]{:S(2)}) collective-permute-start(bf16[80,4096]{1,0:T(8,128)(2,1)} %collective-permute-done.6.onward), channel_id=1, source_target_pairs={{4,6},{6,4},{8,10},{10,8},{5,7},{7,5},{9,11},{11,9},{20,22},{22,20... | collective-permute-start | bytes 1966088 | tf_op jit(solution)/shard_map/ppermute | solution.py:129
  42.9 3.3 %collective-permute-start.9 = (bf16[80,4096]{1,0:T(8,128)(2,1)}, bf16[80,4096]{1,0:T(8,128)(2,1)}, u32[]{:S(2)}, u32[]{:S(2)}) collective-permute-start(bf16[80,4096]{1,0:T(8,128)(2,1)} %collective-permute-done.5.second), channel_id=1, source_target_pairs={{0,2},{2,0},{12,14},{14,12},{1,3},{3,1},{13,15},{15,13},{16,18},{1... | collective-permute-start | bytes 1966088 | tf_op jit(solution)/shard_map/ppermute | solution.py:129
  46.2 9.3 %collective-permute-done.11.piece = bf16[80,4096]{1,0:T(8,128)(2,1)} collective-permute-done((bf16[80,4096]{1,0:T(8,128)(2,1)}, bf16[80,4096]{1,0:T(8,128)(2,1)}, u32[]{:S(2)}, u32[]{:S(2)}) %collective-permute-start.11) | collective-permute-done | bytes 655392 | tf_op jit(solution)/shard_map/ppermute | solution.py:129
  55.5 3.6 %collective-permute-start.12 = (bf16[80,4096]{1,0:T(8,128)(2,1)}, bf16[80,4096]{1,0:T(8,128)(2,1)}, u32[]{:S(2)}, u32[]{:S(2)}) collective-permute-start(bf16[80,4096]{1,0:T(8,128)(2,1)} %collective-permute-done.11.piece), channel_id=1, source_target_pairs={{0,2},{2,0},{12,14},{14,12},{1,3},{3,1},{13,15},{15,13},{16,18},{1... | collective-permute-start | bytes 1966088 | tf_op jit(solution)/shard_map/ppermute | solution.py:129
  59.1 0.0 copy-done.7
  59.1 0.2 reduce-window.13
  59.3 0.1 pad_add_fusion.at
  59.4 0.0 collective-permute-done.8.far_over
  59.4 1.9 %collective-permute-done.9.second_over = bf16[80,4096]{1,0:T(8,128)(2,1)} collective-permute-done((bf16[80,4096]{1,0:T(8,128)(2,1)}, bf16[80,4096]{1,0:T(8,128)(2,1)}, u32[]{:S(2)}, u32[]{:S(2)}) %collective-permute-start.9) | collective-permute-done | bytes 655392 | tf_op jit(solution)/shard_map/ppermute | solution.py:129
  61.3 1.8 %collective-permute-done.10.behind = bf16[208,4096]{1,0:T(8,128)(2,1)} collective-permute-done((bf16[208,4096]{1,0:T(8,128)(2,1)}, bf16[208,4096]{1,0:T(8,128)(2,1)}, u32[]{:S(2)}, u32[]{:S(2)}) %collective-permute-start.10) | collective-permute-done | bytes 1703968 | tf_op jit(solution)/shard_map/ppermute | solution.py:360
  63.0 0.0 copy-done.4
  63.0 0.0 copy-start.3
  63.0 1.1 %copy-done.3 = bf16[80,4096]{1,0:T(8,128)(2,1)S(1)} copy-done((bf16[80,4096]{1,0:T(8,128)(2,1)S(1)}, bf16[80,4096]{1,0:T(8,128)(2,1)}, u32[]{:S(2)}) %copy-start.3) | copy-done | bytes 655384
  64.1 8.1 %project_early.1 = (f32[512,384]{1,0:T(8,128)S(1)}, f32[512,384]{1,0:T(8,128)S(1)}, bf16[512,4096]{1,0:T(8,128)(2,1)S(1)}) custom-call(s32[4]{0:T(128)S(1)} %pad_add_fusion.at, bf16[80,4096]{1,0:T(8,128)(2,1)} %bitcast.6.mine, bf16[80,4096]{1,0:T(8,128)(2,1)} %collective-permute-done.near, bf16[80,4096]{1,0:T(8,128)(2,1)} %collective-permute-done.1.cross, ...), custom_call_target="tpu_custom_call" | custom-call | flops 2684354560 | bytes 12582912 | tf_op jit(solution)/shard_map/project_early/pallas_call | solution.py:365
  72.3 1.0 collective-permute-done.12.piece_over
  73.2 0.0 copy-start.6
  73.2 0.0 copy-start.5
  73.2 2.9 %project_late.1 = (f32[512,384]{1,0:T(8,128)S(1)}, f32[512,384]{1,0:T(8,128)S(1)}) custom-call(s32[4]{0:T(128)S(1)} %pad_add_fusion.at, f32[512,384]{1,0:T(8,128)S(1)} %get-tuple-element.25.first_keep, f32[512,384]{1,0:T(8,128)S(1)} %get-tuple-element.26.first_send, ...), custom_call_target="tpu_custom_call", output_to_operand_aliasing={{0}: (1, {}), {1}: (2, {})} | custom-call | flops 1073741824 | bytes 6291456 | tf_op jit(solution)/shard_map/project_late/pallas_call | solution.py:386
  76.2 0.1 collective-permute-start.13
  76.2 0.0 copy-done.6
  76.3 0.1 select_reduce_fusion
  76.4 0.0 copy-done.5
  76.4 0.2 fusion.5
  76.6 0.3 fusion.1
  76.9 1.6 %collective-permute-done.13.other = f32[512,384]{1,0:T(8,128)S(1)} collective-permute-done((f32[512,384]{1,0:T(8,128)S(1)}, f32[512,384]{1,0:T(8,128)S(1)}, u32[]{:S(2)}, u32[]{:S(2)}) %collective-permute-start.13) | collective-permute-done | bytes 786464 | tf_op jit(solution)/shard_map/ppermute | solution.py:406
  78.5 0.8 sum_halves.1
  79.3 5.1 %all-to-all-start = ((bf16[16,32,384]{2,1,0:T(8,128)(2,1)}), bf16[16,32,384]{2,1,0:T(8,128)(2,1)S(1)}, u32[]{:S(2)}, u32[]{:S(2)}) async-start(bf16[16,32,384]{2,1,0:T(8,128)(2,1)} %bitcast.10), calls=%async_computation | async-start | bytes 786432 | tf_op jit(solution)/shard_map/all_to_all | solution.py:407
  84.5 0.1 reduce
  84.6 0.1 pad_maximum_fusion
  84.7 0.1 select_reduce_fusion.2
  84.8 0.1 fusion.pick
  84.9 0.1 and_convert_fusion.allowed
  85.0 12.3 %all-to-all-done = bf16[16,32,384]{2,1,0:T(8,128)(2,1)S(1)} async-done(((bf16[16,32,384]{2,1,0:T(8,128)(2,1)}), bf16[16,32,384]{2,1,0:T(8,128)(2,1)S(1)}, u32[]{:S(2)}, u32[]{:S(2)}) %all-to-all-start) | async-done | bytes 393248 | tf_op jit(solution)/shard_map/all_to_all | solution.py:407
  97.4 2.3 %attend.1 = (bf16[128,128]{1,0:T(8,128)(2,1)}, bf16[128,128]{1,0:T(8,128)(2,1)}, bf16[128,512]{1,0:T(8,128)(2,1)}) custom-call(bf16[128,256]{1,0:T(8,128)(2,1)S(1)} %fusion.pick, bf16[2,256,384]{2,1,0:T(8,128)(2,1)S(1)} %bitcast.25, f32[128,128]{1,0:T(8,128)S(1)} %get-tuple-element.38.cosine, f32[128,128]{1,0:T(8,128)S(1)} %get-tuple-element.39.sine, ...), custom_call_target="tpu_custom_call" | custom-call | tf_op jit(solution)/shard_map/attend/pallas_call | solution.py:321
  (8 shorter events, 0.1 us)
Async XLA Ops:
  0.6 1.3 %copy-start = (bf16[4096,160]{0,1:T(8,128)(2,1)S(1)}, bf16[4096,160]{0,1:T(8,128)(2,1)}, u32[]{:S(2)}) copy-start(bf16[4096,160]{0,1:T(8,128)(2,1)} %param.8) | copy-start | bytes 3932164
  0.6 11.6 %copy-start.1 = (bf16[256,4096]{1,0:T(8,128)(2,1)S(1)}, bf16[256,4096]{1,0:T(8,128)(2,1)}, u32[]{:S(2)}) copy-start(bf16[256,4096]{1,0:T(8,128)(2,1)} %own.1) | copy-start | bytes 6291460
  2.8 18.5 %collective-permute-start = (bf16[80,4096]{1,0:T(8,128)(2,1)}, bf16[80,4096]{1,0:T(8,128)(2,1)}, u32[]{:S(2)}, u32[]{:S(2)}) collective-permute-start(bf16[80,4096]{1,0:T(8,128)(2,1)} %bitcast.6.mine), channel_id=1, source_target_pairs={{0,4},{2,6},{4,0},{6,2},{8,12},{10,14},{12,8},{14,10},{1,5},{3,7},... | collective-permute-start | bytes 1966088 | tf_op jit(solution)/shard_map/ppermute | solution.py:129
  5.9 16.5 %collective-permute-start.1 = (bf16[80,4096]{1,0:T(8,128)(2,1)}, bf16[80,4096]{1,0:T(8,128)(2,1)}, u32[]{:S(2)}, u32[]{:S(2)}) collective-permute-start(bf16[80,4096]{1,0:T(8,128)(2,1)} %bitcast.6.mine), channel_id=1, source_target_pairs={{4,8},{6,10},{8,4},{10,6},{0,2},{2,0},{12,14},{14,12},{5,9},{7,11}... | collective-permute-start | bytes 1966088 | tf_op jit(solution)/shard_map/ppermute | solution.py:129
  7.4 19.7 %collective-permute-start.4 = (bf16[80,4096]{1,0:T(8,128)(2,1)}, bf16[80,4096]{1,0:T(8,128)(2,1)}, u32[]{:S(2)}, u32[]{:S(2)}) collective-permute-start(bf16[80,4096]{1,0:T(8,128)(2,1)} %bitcast.6.mine), channel_id=1, source_target_pairs={{4,6},{6,4},{8,10},{10,8},{5,7},{7,5},{9,11},{11,9},{20,22},{22,20... | collective-permute-start | bytes 1966088 | tf_op jit(solution)/shard_map/ppermute | solution.py:129
  10.7 10.6 %collective-permute-start.2 = (bf16[48,4096]{1,0:T(8,128)(2,1)}, bf16[48,4096]{1,0:T(8,128)(2,1)}, u32[]{:S(2)}, u32[]{:S(2)}) collective-permute-start(bf16[48,4096]{1,0:T(8,128)(2,1)} %slice.6), channel_id=1, source_target_pairs={{0,16},{16,0},{1,17},{17,1},{2,18},{18,2},{3,19},{19,3},{4,20},{20... | collective-permute-start | bytes 1179656 | tf_op jit(solution)/shard_map/ppermute | solution.py:354
  12.7 46.4 %copy-start.7 = (s32[1,8]{1,0:T(1,128)S(1)}, s32[1,8]{1,0:T(1,128)}, u32[]{:S(2)}) copy-start(s32[1,8]{1,0:T(1,128)} %param.10) | copy-start | bytes 100
  12.7 50.3 %copy-start.4 = (f32[4096]{0:T(1024)S(1)}, f32[4096]{0:T(1024)}, u32[]{:S(2)}) copy-start(f32[4096]{0:T(1024)} %param.7) | copy-start | bytes 49156
  15.2 6.1 %collective-permute-start.3 = (f32[256]{0:T(256)S(1)}, f32[256]{0:T(256)S(1)}, u32[]{:S(2)}, u32[]{:S(2)}) collective-permute-start(f32[256]{0:T(256)S(1)} %add_rsqrt_fusion), channel_id=1, source_target_pairs={{0,16},{16,0},{1,17},{17,1},{2,18},{18,2},{3,19},{19,3},{4,20},{20... | collective-permute-start | bytes 3080 | tf_op jit(solution)/shard_map/ppermute | solution.py:356
  22.4 15.6 %collective-permute-start.6 = (bf16[80,4096]{1,0:T(8,128)(2,1)}, bf16[80,4096]{1,0:T(8,128)(2,1)}, u32[]{:S(2)}, u32[]{:S(2)}) collective-permute-start(bf16[80,4096]{1,0:T(8,128)(2,1)} %collective-permute-done.near), channel_id=1, source_target_pairs={{4,8},{6,10},{8,4},{10,6},{0,2},{2,0},{12,14},{14,12},{5,9},{7,11}... | collective-permute-start | bytes 1966088 | tf_op jit(solution)/shard_map/ppermute | solution.py:129
  23.9 15.3 %collective-permute-start.5 = (bf16[80,4096]{1,0:T(8,128)(2,1)}, bf16[80,4096]{1,0:T(8,128)(2,1)}, u32[]{:S(2)}, u32[]{:S(2)}) collective-permute-start(bf16[80,4096]{1,0:T(8,128)(2,1)} %collective-permute-done.1.cross), channel_id=1, source_target_pairs={{0,4},{2,6},{4,0},{6,2},{8,12},{10,14},{12,8},{14,10},{1,5},{3,7},... | collective-permute-start | bytes 1966088 | tf_op jit(solution)/shard_map/ppermute | solution.py:129
  25.5 37.5 %collective-permute-start.10 = (bf16[208,4096]{1,0:T(8,128)(2,1)}, bf16[208,4096]{1,0:T(8,128)(2,1)}, u32[]{:S(2)}, u32[]{:S(2)}) collective-permute-start(bf16[208,4096]{1,0:T(8,128)(2,1)} %slice.7), channel_id=1, source_target_pairs={{0,16},{16,0},{1,17},{17,1},{2,18},{18,2},{3,19},{19,3},{4,20},{20... | collective-permute-start | bytes 5111816 | tf_op jit(solution)/shard_map/ppermute | solution.py:360
  27.1 13.4 %collective-permute-start.7 = (bf16[80,4096]{1,0:T(8,128)(2,1)}, bf16[80,4096]{1,0:T(8,128)(2,1)S(1)}, u32[]{:S(2)}, u32[]{:S(2)}) collective-permute-start(bf16[80,4096]{1,0:T(8,128)(2,1)} %collective-permute-done.1.cross), channel_id=1, source_target_pairs={{4,6},{6,4},{8,10},{10,8},{5,7},{7,5},{9,11},{11,9},{20,22},{22,20... | collective-permute-start | bytes 1966088 | tf_op jit(solution)/shard_map/ppermute | solution.py:129
  39.2 16.3 %collective-permute-start.11 = (bf16[80,4096]{1,0:T(8,128)(2,1)}, bf16[80,4096]{1,0:T(8,128)(2,1)}, u32[]{:S(2)}, u32[]{:S(2)}) collective-permute-start(bf16[80,4096]{1,0:T(8,128)(2,1)} %collective-permute-done.6.onward), channel_id=1, source_target_pairs={{4,0},{6,2},{8,12},{10,14},{5,1},{7,3},{9,13},{11,15},{20,16},{22,... | collective-permute-start | bytes 1966088 | tf_op jit(solution)/shard_map/ppermute | solution.py:129
  40.5 0.8 copy-start.2
  41.3 18.0 %collective-permute-start.8 = (bf16[80,4096]{1,0:T(8,128)(2,1)}, bf16[80,4096]{1,0:T(8,128)(2,1)}, u32[]{:S(2)}, u32[]{:S(2)}) collective-permute-start(bf16[80,4096]{1,0:T(8,128)(2,1)} %collective-permute-done.6.onward), channel_id=1, source_target_pairs={{4,6},{6,4},{8,10},{10,8},{5,7},{7,5},{9,11},{11,9},{20,22},{22,20... | collective-permute-start | bytes 1966088 | tf_op jit(solution)/shard_map/ppermute | solution.py:129
  42.9 18.4 %collective-permute-start.9 = (bf16[80,4096]{1,0:T(8,128)(2,1)}, bf16[80,4096]{1,0:T(8,128)(2,1)}, u32[]{:S(2)}, u32[]{:S(2)}) collective-permute-start(bf16[80,4096]{1,0:T(8,128)(2,1)} %collective-permute-done.5.second), channel_id=1, source_target_pairs={{0,2},{2,0},{12,14},{14,12},{1,3},{3,1},{13,15},{15,13},{16,18},{1... | collective-permute-start | bytes 1966088 | tf_op jit(solution)/shard_map/ppermute | solution.py:129
  55.5 17.7 %collective-permute-start.12 = (bf16[80,4096]{1,0:T(8,128)(2,1)}, bf16[80,4096]{1,0:T(8,128)(2,1)}, u32[]{:S(2)}, u32[]{:S(2)}) collective-permute-start(bf16[80,4096]{1,0:T(8,128)(2,1)} %collective-permute-done.11.piece), channel_id=1, source_target_pairs={{0,2},{2,0},{12,14},{14,12},{1,3},{3,1},{13,15},{15,13},{16,18},{1... | collective-permute-start | bytes 1966088 | tf_op jit(solution)/shard_map/ppermute | solution.py:129
  63.0 1.1 %copy-start.3 = (bf16[80,4096]{1,0:T(8,128)(2,1)S(1)}, bf16[80,4096]{1,0:T(8,128)(2,1)}, u32[]{:S(2)}) copy-start(bf16[80,4096]{1,0:T(8,128)(2,1)} %copy-done.2) | copy-start | bytes 1966084
  73.2 3.0 %copy-start.6 = (s32[1,8]{1,0:T(1,128)S(1)}, s32[1,8]{1,0:T(1,128)}, u32[]{:S(2)}) copy-start(s32[1,8]{1,0:T(1,128)} %param.11) | copy-start | bytes 100
  73.2 3.1 %copy-start.5 = (s32[8,8]{1,0:T(8,128)S(1)}, s32[8,8]{1,0:T(8,128)}, u32[]{:S(2)}) copy-start(s32[8,8]{1,0:T(8,128)} %param.9) | copy-start | bytes 772
  76.2 2.4 %collective-permute-start.13 = (f32[512,384]{1,0:T(8,128)S(1)}, f32[512,384]{1,0:T(8,128)S(1)}, u32[]{:S(2)}, u32[]{:S(2)}) collective-permute-start(f32[512,384]{1,0:T(8,128)S(1)} %get-tuple-element.30), channel_id=1, source_target_pairs={{0,1},{1,0},{2,3},{3,2},{4,5},{5,4},{6,7},{7,6},{8,9},{9,8},{10,11... | collective-permute-start | bytes 2359304 | tf_op jit(solution)/shard_map/ppermute | solution.py:406
  79.3 18.0 %all-to-all-start = ((bf16[16,32,384]{2,1,0:T(8,128)(2,1)}), bf16[16,32,384]{2,1,0:T(8,128)(2,1)S(1)}, u32[]{:S(2)}, u32[]{:S(2)}) async-start(bf16[16,32,384]{2,1,0:T(8,128)(2,1)} %bitcast.10), calls=%async_computation | async-start | bytes 786432 | tf_op jit(solution)/shard_map/all_to_all | solution.py:407

commit v11 on v10

--- a/solution.py
+++ b/solution.py
@@ -138,8 +138,8 @@
     cross_over = send(cross_next, overs(MIDDLE))
     onward_next, _ = lax.optimization_barrier((onward, second))
     last = send(onward_next, alongs(OUTWARD))
-    second_over = send(second, overs(ENDS))
-    onward_next, _ = lax.optimization_barrier((onward, cross_over))
+    second_next, _ = lax.optimization_barrier((second, cross_over))
+    second_over = send(second_next, overs(ENDS))
     far_over = send(onward_next, overs(MIDDLE))
     last_over = send(last, overs(ENDS))
     early = (mine, near, cross, side, second, onward, cross_over, far_over, second_over)
@@ -343,7 +343,7 @@
     count = turned.shape[0] // (2 * BLOCK)
     size = count * BLOCK
     swap = [(0, 1), (1, 0)]
-    cut_at = sent_rows.shape[0] * 3 // 16
+    cut_at = sent_rows.shape[0] * 4 // 16
     whole = pl.BlockSpec(memory_space=pltpu.VMEM)
     anywhere = pl.BlockSpec(memory_space=pl.ANY)
     scalars = pl.BlockSpec(memory_space=pltpu.SMEM)

time: 100 us -> 99.3 us (level)
  waiting for transfers between devices: 44.7 us -> 43.2 us
    ppermute x10, waiting for transfers between devices: 24.6 us -> 22.4 us  [send(): return lax.ppermute(block, 'dp', pairs)]
    ppermute x1, waiting for transfers between devices: 4.31 us -> 5.63 us  [paired(): their_scale = lax.ppermute(scale, 'parts', swap)]
  transfers between devices with their start and end apart: 15 -> 15, of which waited for: 10 -> 8; matrix products, arithmetic and copies ran while one was open for 5% -> 5% of each run, Pallas kernels for 8% -> 8%
where the time goes in v11:
time: 99.3 us; the launch traced here: 98.8 us
  waiting for transfers between devices  43.2 us (44%)
  starting transfers between devices  29 us (29%)
  Pallas kernels  14.2 us (14%)
  local copies, waits for them, and re-layouts  7.47 us (8%)
  blocking collectives  2.47 us (2%)
  other arithmetic  1.7 us (2%)
    ppermute x10, waiting for transfers between devices, send(): return lax.ppermute(block, 'dp', pairs)  22.4 us
    ppermute x10, starting transfers between devices, send(): return lax.ppermute(block, 'dp', pairs)  19.6 us
    all_to_all x1, waiting for transfers between devices, paired(): arrived = lax.all_to_all(ready, ('parts', 'dp'), 0, 0, tiled=True)  12.3 us
    pallas_call x1, Pallas kernels, paired(): pl.pallas_call(early_kernel, out_shape=(half, half, jax.ShapeDtypeStruct(...  8.12 us
    all_to_all x1, starting transfers between devices, paired(): arrived = lax.all_to_all(ready, ('parts', 'dp'), 0, 0, tiled=True)  5.83 us
    ppermute x1, waiting for transfers between devices, paired(): their_scale = lax.ppermute(scale, 'parts', swap)  5.63 us
    unnamed x16, local copies, waits for them, and re-layouts  3.25 us
    pallas_call x1, Pallas kernels, paired(): pl.pallas_call(late_kernel, out_shape=(half, half), in_specs=[scalars] +...  2.93 us
  transfers between devices with their start and end apart: 15, of which 8 were waited for; matrix products, arithmetic and copies ran while one was open for 5% of the time, Pallas kernels for 8%

profile of v11, /device:TPU:0, one launch (start us, length us, event | category | flops | bytes accessed | tf_op | source)
XLA Modules:
  0.0 98.8 jit_solution(13294294240730991922)
XLA Ops:
  0.6 0.0 copy-start
  0.6 0.0 copy-start.1
  0.7 1.3 %copy-done = bf16[4096,160]{0,1:T(8,128)(2,1)S(1)} copy-done((bf16[4096,160]{0,1:T(8,128)(2,1)S(1)}, bf16[4096,160]{0,1:T(8,128)(2,1)}, u32[]{:S(2)}) %copy-start) | copy-done | bytes 1310744
  2.0 0.9 constant_dynamic-slice_fusion
  2.9 3.0 %collective-permute-start = (bf16[80,4096]{1,0:T(8,128)(2,1)}, bf16[80,4096]{1,0:T(8,128)(2,1)}, u32[]{:S(2)}, u32[]{:S(2)}) collective-permute-start(bf16[80,4096]{1,0:T(8,128)(2,1)} %bitcast.6.mine), channel_id=1, source_target_pairs={{0,4},{2,6},{4,0},{6,2},{8,12},{10,14},{12,8},{14,10},{1,5},{3,7},... | collective-permute-start | bytes 1966088 | tf_op jit(solution)/shard_map/ppermute | solution.py:129
  5.9 1.5 %collective-permute-start.1 = (bf16[80,4096]{1,0:T(8,128)(2,1)}, bf16[80,4096]{1,0:T(8,128)(2,1)}, u32[]{:S(2)}, u32[]{:S(2)}) collective-permute-start(bf16[80,4096]{1,0:T(8,128)(2,1)} %bitcast.6.mine), channel_id=1, source_target_pairs={{4,8},{6,10},{8,4},{10,6},{0,2},{2,0},{12,14},{14,12},{5,9},{7,11}... | collective-permute-start | bytes 1966088 | tf_op jit(solution)/shard_map/ppermute | solution.py:129
  7.4 1.9 %slice.6 = bf16[64,4096]{1,0:T(8,128)(2,1)} slice(bf16[256,4096]{1,0:T(8,128)(2,1)} %own.1), slice={[0:64], [0:4096]} | slice | bytes 1048576 | tf_op jit(solution)/shard_map/slice | solution.py:353
  9.2 1.5 %collective-permute-start.2 = (bf16[64,4096]{1,0:T(8,128)(2,1)}, bf16[64,4096]{1,0:T(8,128)(2,1)}, u32[]{:S(2)}, u32[]{:S(2)}) collective-permute-start(bf16[64,4096]{1,0:T(8,128)(2,1)} %slice.6), channel_id=1, source_target_pairs={{0,16},{16,0},{1,17},{17,1},{2,18},{18,2},{3,19},{19,3},{4,20},{20... | collective-permute-start | bytes 1572872 | tf_op jit(solution)/shard_map/ppermute | solution.py:354
  10.8 1.5 %collective-permute-start.4 = (bf16[80,4096]{1,0:T(8,128)(2,1)}, bf16[80,4096]{1,0:T(8,128)(2,1)}, u32[]{:S(2)}, u32[]{:S(2)}) collective-permute-start(bf16[80,4096]{1,0:T(8,128)(2,1)} %bitcast.6.mine), channel_id=1, source_target_pairs={{4,6},{6,4},{8,10},{10,8},{5,7},{7,5},{9,11},{11,9},{20,22},{22,20... | collective-permute-start | bytes 1966088 | tf_op jit(solution)/shard_map/ppermute | solution.py:129
  12.3 0.0 copy-done.1
  12.3 0.5 multiply_reduce_fusion
  12.8 0.0 copy-start.7
  12.8 0.0 copy-start.4
  12.8 2.5 %psum.7 = f32[256]{0:T(256)S(1)} all-reduce(f32[256]{0:T(256)S(1)} %multiply_reduce_fusion), channel_id=1, replica_groups=mesh['parts'=2,'dp'=8,'tensor'=2] {'tensor'}, use_global_device_ids=true, to_apply=%region_3.4 | all-reduce | flops 256 | bytes 2048 | tf_op jit(solution)/shard_map/psum | solution.py:355
  15.3 0.5 collective-permute-start.3
  15.8 1.3 %slice.7 = bf16[192,4096]{1,0:T(8,128)(2,1)} slice(bf16[256,4096]{1,0:T(8,128)(2,1)S(1)} %copy-done.1), slice={[64:256], [0:4096]} | slice | bytes 3145728 | tf_op jit(solution)/shard_map/slice | solution.py:358
  17.0 5.6 %collective-permute-done.3 = f32[256]{0:T(256)S(1)} collective-permute-done((f32[256]{0:T(256)S(1)}, f32[256]{0:T(256)S(1)}, u32[]{:S(2)}, u32[]{:S(2)}) %collective-permute-start.3) | collective-permute-done | bytes 1056 | tf_op jit(solution)/shard_map/ppermute | solution.py:356
  22.7 0.0 collective-permute-done.2.ahead
  22.7 0.0 collective-permute-done.near
  22.7 0.0 collective-permute-done.1.cross
  22.7 1.7 %collective-permute-start.5 = (bf16[80,4096]{1,0:T(8,128)(2,1)}, bf16[80,4096]{1,0:T(8,128)(2,1)}, u32[]{:S(2)}, u32[]{:S(2)}) collective-permute-start(bf16[80,4096]{1,0:T(8,128)(2,1)} %collective-permute-done.1.cross), channel_id=1, source_target_pairs={{0,4},{2,6},{4,0},{6,2},{8,12},{10,14},{12,8},{14,10},{1,5},{3,7},... | collective-permute-start | bytes 1966088 | tf_op jit(solution)/shard_map/ppermute | solution.py:129
  24.4 1.5 %collective-permute-start.6 = (bf16[80,4096]{1,0:T(8,128)(2,1)}, bf16[80,4096]{1,0:T(8,128)(2,1)}, u32[]{:S(2)}, u32[]{:S(2)}) collective-permute-start(bf16[80,4096]{1,0:T(8,128)(2,1)} %collective-permute-done.near), channel_id=1, source_target_pairs={{4,8},{6,10},{8,4},{10,6},{0,2},{2,0},{12,14},{14,12},{5,9},{7,11}... | collective-permute-start | bytes 1966088 | tf_op jit(solution)/shard_map/ppermute | solution.py:129
  25.9 1.5 %collective-permute-start.10 = (bf16[192,4096]{1,0:T(8,128)(2,1)}, bf16[192,4096]{1,0:T(8,128)(2,1)}, u32[]{:S(2)}, u32[]{:S(2)}) collective-permute-start(bf16[192,4096]{1,0:T(8,128)(2,1)} %slice.7), channel_id=1, source_target_pairs={{0,16},{16,0},{1,17},{17,1},{2,18},{18,2},{3,19},{19,3},{4,20},{20... | collective-permute-start | bytes 4718600 | tf_op jit(solution)/shard_map/ppermute | solution.py:360
  27.4 0.0 collective-permute-done.4.side
  27.4 0.7 collective-permute-start.7
  28.1 9.9 %collective-permute-done.5.second = bf16[80,4096]{1,0:T(8,128)(2,1)} collective-permute-done((bf16[80,4096]{1,0:T(8,128)(2,1)}, bf16[80,4096]{1,0:T(8,128)(2,1)}, u32[]{:S(2)}, u32[]{:S(2)}) %collective-permute-start.5) | collective-permute-done | bytes 655392 | tf_op jit(solution)/shard_map/ppermute | solution.py:129
  38.1 1.4 %collective-permute-done.6.onward = bf16[80,4096]{1,0:T(8,128)(2,1)} collective-permute-done((bf16[80,4096]{1,0:T(8,128)(2,1)}, bf16[80,4096]{1,0:T(8,128)(2,1)}, u32[]{:S(2)}, u32[]{:S(2)}) %collective-permute-start.6) | collective-permute-done | bytes 655392 | tf_op jit(solution)/shard_map/ppermute | solution.py:129
  39.5 1.3 %collective-permute-start.11 = (bf16[80,4096]{1,0:T(8,128)(2,1)}, bf16[80,4096]{1,0:T(8,128)(2,1)}, u32[]{:S(2)}, u32[]{:S(2)}) collective-permute-start(bf16[80,4096]{1,0:T(8,128)(2,1)} %collective-permute-done.6.onward), channel_id=1, source_target_pairs={{4,0},{6,2},{8,12},{10,14},{5,1},{7,3},{9,13},{11,15},{20,16},{22,... | collective-permute-start | bytes 1966088 | tf_op jit(solution)/shard_map/ppermute | solution.py:129
  40.8 0.0 collective-permute-done.7.cross_over
  40.8 0.0 copy-start.2
  40.8 0.8 copy-done.2
  41.6 3.4 %collective-permute-start.9 = (bf16[80,4096]{1,0:T(8,128)(2,1)}, bf16[80,4096]{1,0:T(8,128)(2,1)}, u32[]{:S(2)}, u32[]{:S(2)}) collective-permute-start(bf16[80,4096]{1,0:T(8,128)(2,1)} %collective-permute-done.5.second), channel_id=1, source_target_pairs={{0,2},{2,0},{12,14},{14,12},{1,3},{3,1},{13,15},{15,13},{16,18},{1... | collective-permute-start | bytes 1966088 | tf_op jit(solution)/shard_map/ppermute | solution.py:129
  45.0 1.6 %collective-permute-start.8 = (bf16[80,4096]{1,0:T(8,128)(2,1)}, bf16[80,4096]{1,0:T(8,128)(2,1)}, u32[]{:S(2)}, u32[]{:S(2)}) collective-permute-start(bf16[80,4096]{1,0:T(8,128)(2,1)} %collective-permute-done.6.onward), channel_id=1, source_target_pairs={{4,6},{6,4},{8,10},{10,8},{5,7},{7,5},{9,11},{11,9},{20,22},{22,20... | collective-permute-start | bytes 1966088 | tf_op jit(solution)/shard_map/ppermute | solution.py:129
  46.6 8.9 %collective-permute-done.11.piece = bf16[80,4096]{1,0:T(8,128)(2,1)} collective-permute-done((bf16[80,4096]{1,0:T(8,128)(2,1)}, bf16[80,4096]{1,0:T(8,128)(2,1)}, u32[]{:S(2)}, u32[]{:S(2)}) %collective-permute-start.11) | collective-permute-done | bytes 655392 | tf_op jit(solution)/shard_map/ppermute | solution.py:129
  55.5 3.4 %collective-permute-start.12 = (bf16[80,4096]{1,0:T(8,128)(2,1)}, bf16[80,4096]{1,0:T(8,128)(2,1)}, u32[]{:S(2)}, u32[]{:S(2)}) collective-permute-start(bf16[80,4096]{1,0:T(8,128)(2,1)} %collective-permute-done.11.piece), channel_id=1, source_target_pairs={{0,2},{2,0},{12,14},{14,12},{1,3},{3,1},{13,15},{15,13},{16,18},{1... | collective-permute-start | bytes 1966088 | tf_op jit(solution)/shard_map/ppermute | solution.py:129
  58.9 0.0 copy-done.7
  58.9 0.2 reduce-window.13
  59.1 0.1 pad_add_fusion.at
  59.2 0.0 collective-permute-done.9.second_over
  59.2 0.0 collective-permute-done.8.far_over
  59.2 1.2 %collective-permute-done.10.behind = bf16[192,4096]{1,0:T(8,128)(2,1)} collective-permute-done((bf16[192,4096]{1,0:T(8,128)(2,1)}, bf16[192,4096]{1,0:T(8,128)(2,1)}, u32[]{:S(2)}, u32[]{:S(2)}) %collective-permute-start.10) | collective-permute-done | bytes 1572896 | tf_op jit(solution)/shard_map/ppermute | solution.py:360
  60.3 0.0 copy-done.4
  60.3 0.0 copy-start.3
  60.4 1.1 %copy-done.3 = bf16[80,4096]{1,0:T(8,128)(2,1)S(1)} copy-done((bf16[80,4096]{1,0:T(8,128)(2,1)S(1)}, bf16[80,4096]{1,0:T(8,128)(2,1)}, u32[]{:S(2)}) %copy-start.3) | copy-done | bytes 655384
  61.4 8.1 %project_early.1 = (f32[512,384]{1,0:T(8,128)S(1)}, f32[512,384]{1,0:T(8,128)S(1)}, bf16[512,4096]{1,0:T(8,128)(2,1)S(1)}) custom-call(s32[4]{0:T(128)S(1)} %pad_add_fusion.at, bf16[80,4096]{1,0:T(8,128)(2,1)} %bitcast.6.mine, bf16[80,4096]{1,0:T(8,128)(2,1)} %collective-permute-done.near, bf16[80,4096]{1,0:T(8,128)(2,1)} %collective-permute-done.1.cross, ...), custom_call_target="tpu_custom_call" | custom-call | flops 2684354560 | bytes 12582912 | tf_op jit(solution)/shard_map/project_early/pallas_call | solution.py:365
  69.6 2.1 %collective-permute-done.12.piece_over = bf16[80,4096]{1,0:T(8,128)(2,1)} collective-permute-done((bf16[80,4096]{1,0:T(8,128)(2,1)}, bf16[80,4096]{1,0:T(8,128)(2,1)}, u32[]{:S(2)}, u32[]{:S(2)}) %collective-permute-start.12) | collective-permute-done | bytes 655392 | tf_op jit(solution)/shard_map/ppermute | solution.py:129
  71.7 0.0 copy-start.6
  71.7 2.9 %project_late.1 = (f32[512,384]{1,0:T(8,128)S(1)}, f32[512,384]{1,0:T(8,128)S(1)}) custom-call(s32[4]{0:T(128)S(1)} %pad_add_fusion.at, f32[512,384]{1,0:T(8,128)S(1)} %get-tuple-element.26.first_keep, f32[512,384]{1,0:T(8,128)S(1)} %get-tuple-element.27.first_send, ...), custom_call_target="tpu_custom_call", output_to_operand_aliasing={{0}: (1, {}), {1}: (2, {})} | custom-call | flops 1073741824 | bytes 6291456 | tf_op jit(solution)/shard_map/project_late/pallas_call | solution.py:386
  74.6 0.1 collective-permute-start.13
  74.7 0.0 copy-done.6
  74.7 0.1 select_reduce_fusion
  74.8 0.0 copy-done.5
  74.8 0.2 fusion.5
  75.0 0.3 fusion.1
  75.3 1.6 %collective-permute-done.13.other = f32[512,384]{1,0:T(8,128)S(1)} collective-permute-done((f32[512,384]{1,0:T(8,128)S(1)}, f32[512,384]{1,0:T(8,128)S(1)}, u32[]{:S(2)}, u32[]{:S(2)}) %collective-permute-start.13) | collective-permute-done | bytes 786464 | tf_op jit(solution)/shard_map/ppermute | solution.py:406
  77.0 0.8 sum_halves.1
  77.8 5.8 %all-to-all-start = ((bf16[16,32,384]{2,1,0:T(8,128)(2,1)}), bf16[16,32,384]{2,1,0:T(8,128)(2,1)S(1)}, u32[]{:S(2)}, u32[]{:S(2)}) async-start(bf16[16,32,384]{2,1,0:T(8,128)(2,1)} %bitcast.10), calls=%async_computation | async-start | bytes 786432 | tf_op jit(solution)/shard_map/all_to_all | solution.py:407
  83.7 0.1 reduce
  83.8 0.1 pad_maximum_fusion
  83.9 0.1 select_reduce_fusion.2
  84.0 0.1 fusion.pick
  84.1 0.1 and_convert_fusion.allowed
  84.2 12.3 %all-to-all-done = bf16[16,32,384]{2,1,0:T(8,128)(2,1)S(1)} async-done(((bf16[16,32,384]{2,1,0:T(8,128)(2,1)}), bf16[16,32,384]{2,1,0:T(8,128)(2,1)S(1)}, u32[]{:S(2)}, u32[]{:S(2)}) %all-to-all-start) | async-done | bytes 393248 | tf_op jit(solution)/shard_map/all_to_all | solution.py:407
  96.5 2.3 %attend.1 = (bf16[128,128]{1,0:T(8,128)(2,1)}, bf16[128,128]{1,0:T(8,128)(2,1)}, bf16[128,512]{1,0:T(8,128)(2,1)}) custom-call(bf16[128,256]{1,0:T(8,128)(2,1)S(1)} %fusion.pick, bf16[2,256,384]{2,1,0:T(8,128)(2,1)S(1)} %bitcast.25, f32[128,128]{1,0:T(8,128)S(1)} %get-tuple-element.38.cosine, f32[128,128]{1,0:T(8,128)S(1)} %get-tuple-element.39.sine, ...), custom_call_target="tpu_custom_call" | custom-call | tf_op jit(solution)/shard_map/attend/pallas_call | solution.py:321
  (8 shorter events, 0.1 us)
Async XLA Ops:
  0.6 1.3 %copy-start = (bf16[4096,160]{0,1:T(8,128)(2,1)S(1)}, bf16[4096,160]{0,1:T(8,128)(2,1)}, u32[]{:S(2)}) copy-start(bf16[4096,160]{0,1:T(8,128)(2,1)} %param.8) | copy-start | bytes 3932164
  0.6 11.6 %copy-start.1 = (bf16[256,4096]{1,0:T(8,128)(2,1)S(1)}, bf16[256,4096]{1,0:T(8,128)(2,1)}, u32[]{:S(2)}) copy-start(bf16[256,4096]{1,0:T(8,128)(2,1)} %own.1) | copy-start | bytes 6291460
  2.9 19.8 %collective-permute-start = (bf16[80,4096]{1,0:T(8,128)(2,1)}, bf16[80,4096]{1,0:T(8,128)(2,1)}, u32[]{:S(2)}, u32[]{:S(2)}) collective-permute-start(bf16[80,4096]{1,0:T(8,128)(2,1)} %bitcast.6.mine), channel_id=1, source_target_pairs={{0,4},{2,6},{4,0},{6,2},{8,12},{10,14},{12,8},{14,10},{1,5},{3,7},... | collective-permute-start | bytes 1966088 | tf_op jit(solution)/shard_map/ppermute | solution.py:129
  5.9 16.8 %collective-permute-start.1 = (bf16[80,4096]{1,0:T(8,128)(2,1)}, bf16[80,4096]{1,0:T(8,128)(2,1)}, u32[]{:S(2)}, u32[]{:S(2)}) collective-permute-start(bf16[80,4096]{1,0:T(8,128)(2,1)} %bitcast.6.mine), channel_id=1, source_target_pairs={{4,8},{6,10},{8,4},{10,6},{0,2},{2,0},{12,14},{14,12},{5,9},{7,11}... | collective-permute-start | bytes 1966088 | tf_op jit(solution)/shard_map/ppermute | solution.py:129
  9.2 13.4 %collective-permute-start.2 = (bf16[64,4096]{1,0:T(8,128)(2,1)}, bf16[64,4096]{1,0:T(8,128)(2,1)}, u32[]{:S(2)}, u32[]{:S(2)}) collective-permute-start(bf16[64,4096]{1,0:T(8,128)(2,1)} %slice.6), channel_id=1, source_target_pairs={{0,16},{16,0},{1,17},{17,1},{2,18},{18,2},{3,19},{19,3},{4,20},{20... | collective-permute-start | bytes 1572872 | tf_op jit(solution)/shard_map/ppermute | solution.py:354
  10.8 16.7 %collective-permute-start.4 = (bf16[80,4096]{1,0:T(8,128)(2,1)}, bf16[80,4096]{1,0:T(8,128)(2,1)}, u32[]{:S(2)}, u32[]{:S(2)}) collective-permute-start(bf16[80,4096]{1,0:T(8,128)(2,1)} %bitcast.6.mine), channel_id=1, source_target_pairs={{4,6},{6,4},{8,10},{10,8},{5,7},{7,5},{9,11},{11,9},{20,22},{22,20... | collective-permute-start | bytes 1966088 | tf_op jit(solution)/shard_map/ppermute | solution.py:129
  12.8 46.1 %copy-start.7 = (s32[1,8]{1,0:T(1,128)S(1)}, s32[1,8]{1,0:T(1,128)}, u32[]{:S(2)}) copy-start(s32[1,8]{1,0:T(1,128)} %param.10) | copy-start | bytes 100
  12.8 47.6 %copy-start.4 = (f32[4096]{0:T(1024)S(1)}, f32[4096]{0:T(1024)}, u32[]{:S(2)}) copy-start(f32[4096]{0:T(1024)} %param.7) | copy-start | bytes 49156
  15.3 7.4 %collective-permute-start.3 = (f32[256]{0:T(256)S(1)}, f32[256]{0:T(256)S(1)}, u32[]{:S(2)}, u32[]{:S(2)}) collective-permute-start(f32[256]{0:T(256)S(1)} %add_rsqrt_fusion), channel_id=1, source_target_pairs={{0,16},{16,0},{1,17},{17,1},{2,18},{18,2},{3,19},{19,3},{4,20},{20... | collective-permute-start | bytes 3080 | tf_op jit(solution)/shard_map/ppermute | solution.py:356
  22.7 15.4 %collective-permute-start.5 = (bf16[80,4096]{1,0:T(8,128)(2,1)}, bf16[80,4096]{1,0:T(8,128)(2,1)}, u32[]{:S(2)}, u32[]{:S(2)}) collective-permute-start(bf16[80,4096]{1,0:T(8,128)(2,1)} %collective-permute-done.1.cross), channel_id=1, source_target_pairs={{0,4},{2,6},{4,0},{6,2},{8,12},{10,14},{12,8},{14,10},{1,5},{3,7},... | collective-permute-start | bytes 1966088 | tf_op jit(solution)/shard_map/ppermute | solution.py:129
  24.4 15.1 %collective-permute-start.6 = (bf16[80,4096]{1,0:T(8,128)(2,1)}, bf16[80,4096]{1,0:T(8,128)(2,1)}, u32[]{:S(2)}, u32[]{:S(2)}) collective-permute-start(bf16[80,4096]{1,0:T(8,128)(2,1)} %collective-permute-done.near), channel_id=1, source_target_pairs={{4,8},{6,10},{8,4},{10,6},{0,2},{2,0},{12,14},{14,12},{5,9},{7,11}... | collective-permute-start | bytes 1966088 | tf_op jit(solution)/shard_map/ppermute | solution.py:129
  25.9 34.4 %collective-permute-start.10 = (bf16[192,4096]{1,0:T(8,128)(2,1)}, bf16[192,4096]{1,0:T(8,128)(2,1)}, u32[]{:S(2)}, u32[]{:S(2)}) collective-permute-start(bf16[192,4096]{1,0:T(8,128)(2,1)} %slice.7), channel_id=1, source_target_pairs={{0,16},{16,0},{1,17},{17,1},{2,18},{18,2},{3,19},{19,3},{4,20},{20... | collective-permute-start | bytes 4718600 | tf_op jit(solution)/shard_map/ppermute | solution.py:360
  27.4 13.3 %collective-permute-start.7 = (bf16[80,4096]{1,0:T(8,128)(2,1)}, bf16[80,4096]{1,0:T(8,128)(2,1)S(1)}, u32[]{:S(2)}, u32[]{:S(2)}) collective-permute-start(bf16[80,4096]{1,0:T(8,128)(2,1)} %collective-permute-done.1.cross), channel_id=1, source_target_pairs={{4,6},{6,4},{8,10},{10,8},{5,7},{7,5},{9,11},{11,9},{20,22},{22,20... | collective-permute-start | bytes 1966088 | tf_op jit(solution)/shard_map/ppermute | solution.py:129
  39.5 16.0 %collective-permute-start.11 = (bf16[80,4096]{1,0:T(8,128)(2,1)}, bf16[80,4096]{1,0:T(8,128)(2,1)}, u32[]{:S(2)}, u32[]{:S(2)}) collective-permute-start(bf16[80,4096]{1,0:T(8,128)(2,1)} %collective-permute-done.6.onward), channel_id=1, source_target_pairs={{4,0},{6,2},{8,12},{10,14},{5,1},{7,3},{9,13},{11,15},{20,16},{22,... | collective-permute-start | bytes 1966088 | tf_op jit(solution)/shard_map/ppermute | solution.py:129
  40.8 0.8 copy-start.2
  41.6 17.6 %collective-permute-start.9 = (bf16[80,4096]{1,0:T(8,128)(2,1)}, bf16[80,4096]{1,0:T(8,128)(2,1)}, u32[]{:S(2)}, u32[]{:S(2)}) collective-permute-start(bf16[80,4096]{1,0:T(8,128)(2,1)} %collective-permute-done.5.second), channel_id=1, source_target_pairs={{0,2},{2,0},{12,14},{14,12},{1,3},{3,1},{13,15},{15,13},{16,18},{1... | collective-permute-start | bytes 1966088 | tf_op jit(solution)/shard_map/ppermute | solution.py:129
  45.0 14.2 %collective-permute-start.8 = (bf16[80,4096]{1,0:T(8,128)(2,1)}, bf16[80,4096]{1,0:T(8,128)(2,1)}, u32[]{:S(2)}, u32[]{:S(2)}) collective-permute-start(bf16[80,4096]{1,0:T(8,128)(2,1)} %collective-permute-done.6.onward), channel_id=1, source_target_pairs={{4,6},{6,4},{8,10},{10,8},{5,7},{7,5},{9,11},{11,9},{20,22},{22,20... | collective-permute-start | bytes 1966088 | tf_op jit(solution)/shard_map/ppermute | solution.py:129
  55.5 16.2 %collective-permute-start.12 = (bf16[80,4096]{1,0:T(8,128)(2,1)}, bf16[80,4096]{1,0:T(8,128)(2,1)}, u32[]{:S(2)}, u32[]{:S(2)}) collective-permute-start(bf16[80,4096]{1,0:T(8,128)(2,1)} %collective-permute-done.11.piece), channel_id=1, source_target_pairs={{0,2},{2,0},{12,14},{14,12},{1,3},{3,1},{13,15},{15,13},{16,18},{1... | collective-permute-start | bytes 1966088 | tf_op jit(solution)/shard_map/ppermute | solution.py:129
  60.3 1.1 %copy-start.3 = (bf16[80,4096]{1,0:T(8,128)(2,1)S(1)}, bf16[80,4096]{1,0:T(8,128)(2,1)}, u32[]{:S(2)}) copy-start(bf16[80,4096]{1,0:T(8,128)(2,1)} %copy-done.2) | copy-start | bytes 1966084
  71.7 3.0 %copy-start.6 = (s32[1,8]{1,0:T(1,128)S(1)}, s32[1,8]{1,0:T(1,128)}, u32[]{:S(2)}) copy-start(s32[1,8]{1,0:T(1,128)} %param.11) | copy-start | bytes 100
  71.7 3.1 %copy-start.5 = (s32[8,8]{1,0:T(8,128)S(1)}, s32[8,8]{1,0:T(8,128)}, u32[]{:S(2)}) copy-start(s32[8,8]{1,0:T(8,128)} %param.9) | copy-start | bytes 772
  74.6 2.4 %collective-permute-start.13 = (f32[512,384]{1,0:T(8,128)S(1)}, f32[512,384]{1,0:T(8,128)S(1)}, u32[]{:S(2)}, u32[]{:S(2)}) collective-permute-start(f32[512,384]{1,0:T(8,128)S(1)} %get-tuple-element.30), channel_id=1, source_target_pairs={{0,1},{1,0},{2,3},{3,2},{4,5},{5,4},{6,7},{7,6},{8,9},{9,8},{10,11... | collective-permute-start | bytes 2359304 | tf_op jit(solution)/shard_map/ppermute | solution.py:406
  77.8 18.7 %all-to-all-start = ((bf16[16,32,384]{2,1,0:T(8,128)(2,1)}), bf16[16,32,384]{2,1,0:T(8,128)(2,1)S(1)}, u32[]{:S(2)}, u32[]{:S(2)}) async-start(bf16[16,32,384]{2,1,0:T(8,128)(2,1)} %bitcast.10), calls=%async_computation | async-start | bytes 786432 | tf_op jit(solution)/shard_map/all_to_all | solution.py:407

commit v12 on v11

--- a/solution.py
+++ b/solution.py
@@ -99,14 +99,6 @@
     core = lax.axis_index("tensor")
     other = lax.ppermute(cut(partial, width, 1 - core), "tensor", [(0, 1), (1, 0)])
     return (cut(partial, width, core) + other).astype(jnp.bfloat16)
-
-
-def over(block, places):
-    return lax.ppermute(block, "dp", [(2 * z + x, 2 * z + 1 - x) for z in places for x in range(2)])
-
-
-def along(block, moves):
-    return lax.ppermute(block, "dp", [(2 * a + x, 2 * b + x) for a, b in moves for x in range(2)])
 
 
 PAIRS = ((0, 1), (1, 0), (2, 3), (3, 2))
@@ -148,10 +140,19 @@
 
 def early_kernel(
     at, mine, near, cross, side, second, onward, cross_over, far_over, second_over,
-    own, ahead, behind, own_scale, their_scale, gain, keep, send, rows, whole,
+    own, ahead, behind, own_scale, their_scale, gain, keep, send, rows, whole, sem,
 ):
     z, x, part, core = at[0], at[1], at[2], at[3]
     size = mine.shape[0]
+
+    at_end = (z == 0) | (z == 3)
+    middle = jnp.logical_not(at_end)
+    there = pl.multiple_of((2 * (3 - z) + 1 - x) * size, BLOCK)
+    fetch = pltpu.make_async_copy(cross_over, whole.at[pl.ds(there, size)], sem)
+
+    @pl.when(middle)
+    def _():
+        fetch.start()
 
     def place(pairs):
         for where, pieces in pairs:
@@ -177,7 +178,6 @@
                 )
             done += source.shape[0]
 
-    at_end = (z == 0) | (z == 3)
     pair = z + 1 - 2 * (z % 2)
 
     @pl.when(at_end)
@@ -191,16 +191,20 @@
             )
         )
 
-    @pl.when(jnp.logical_not(at_end))
+    @pl.when(middle)
     def _():
         place(
             (
                 (z, (mine, side)),
                 (pair, (near, second)),
                 ((z + 2) % 4, (onward, far_over)),
-                (3 - z, (cross, cross_over)),
+                (3 - z, (cross,)),
             )
         )
+
+    @pl.when(middle)
+    def _():
+        fetch.wait()
 
     share = whole.shape[0] * HQ // (HQ + 2) // 2
     halves = [product(rows[...], whole[c * share : (c + 1) * share, :]) for c in range(2)]
@@ -343,7 +347,7 @@
     count = turned.shape[0] // (2 * BLOCK)
     size = count * BLOCK
     swap = [(0, 1), (1, 0)]
-    cut_at = sent_rows.shape[0] * 4 // 16
+    cut_at = sent_rows.shape[0] * 3 // 16
     whole = pl.BlockSpec(memory_space=pltpu.VMEM)
     anywhere = pl.BlockSpec(memory_space=pl.ANY)
     scalars = pl.BlockSpec(memory_space=pltpu.SMEM)
@@ -365,9 +369,9 @@
     keep, send, rows = pl.pallas_call(
         early_kernel,
         out_shape=(half, half, jax.ShapeDtypeStruct((2 * slots, depth), jnp.bfloat16)),
-        in_specs=[scalars] + [whole] * 15,
+        in_specs=[scalars] + [whole] * 6 + [pl.BlockSpec(memory_space=pltpu.HBM)] + [whole] * 8,
         out_specs=(whole,) * 3,
-        scratch_shapes=[pltpu.VMEM((width, depth), jnp.bfloat16)],
+        scratch_shapes=[pltpu.VMEM((width, depth), jnp.bfloat16), pltpu.SemaphoreType.DMA],
         compiler_params=pltpu.CompilerParams(vmem_limit_bytes=28 << 20),
         cost_estimate=pl.CostEstimate(
             flops=4 * slots * width * depth, bytes_accessed=12 << 20, transcendentals=0

time: 99.3 us -> 99.3 us (level)
    ppermute x1, waiting for transfers between devices: 1.16 us -> 3.39 us  [paired(): behind = lax.ppermute(rest, 'parts', swap)]
    ppermute x1, waiting for transfers between devices: 5.63 us -> 4.31 us  [paired(): their_scale = lax.ppermute(scale, 'parts', swap)]
where the time goes in v12:
time: 99.3 us; the launch traced here: 98.8 us
  waiting for transfers between devices  43.4 us (44%)
  starting transfers between devices  28.8 us (29%)
  Pallas kernels  14.2 us (14%)
  local copies, waits for them, and re-layouts  7.38 us (7%)
  blocking collectives  2.47 us (2%)
  other arithmetic  1.7 us (2%)
    ppermute x10, waiting for transfers between devices, send(): return lax.ppermute(block, 'dp', pairs)  21.7 us
    ppermute x10, starting transfers between devices, send(): return lax.ppermute(block, 'dp', pairs)  20.1 us
    all_to_all x1, waiting for transfers between devices, paired(): arrived = lax.all_to_all(ready, ('parts', 'dp'), 0, 0, tiled=True)  12.3 us
    pallas_call x1, Pallas kernels, paired(): pl.pallas_call(early_kernel, out_shape=(half, half, jax.ShapeDtypeStruct(...  8.15 us
    all_to_all x1, starting transfers between devices, paired(): arrived = lax.all_to_all(ready, ('parts', 'dp'), 0, 0, tiled=True)  5.09 us
    ppermute x1, waiting for transfers between devices, paired(): their_scale = lax.ppermute(scale, 'parts', swap)  4.31 us
    ppermute x1, waiting for transfers between devices, paired(): behind = lax.ppermute(rest, 'parts', swap)  3.39 us
    unnamed x16, local copies, waits for them, and re-layouts  3.24 us
  transfers between devices with their start and end apart: 15, of which 8 were waited for; matrix products, arithmetic and copies ran while one was open for 5% of the time, Pallas kernels for 8%

profile of v12, /device:TPU:0, one launch (start us, length us, event | category | flops | bytes accessed | tf_op | source)
XLA Modules:
  0.0 98.8 jit_solution(1407496758061504627)
XLA Ops:
  0.6 0.0 copy-start
  0.6 0.0 copy-start.1
  0.7 1.3 %copy-done = bf16[4096,160]{0,1:T(8,128)(2,1)S(1)} copy-done((bf16[4096,160]{0,1:T(8,128)(2,1)S(1)}, bf16[4096,160]{0,1:T(8,128)(2,1)}, u32[]{:S(2)}) %copy-start) | copy-done | bytes 1310744
  2.0 0.9 constant_dynamic-slice_fusion
  2.8 3.0 %collective-permute-start = (bf16[80,4096]{1,0:T(8,128)(2,1)}, bf16[80,4096]{1,0:T(8,128)(2,1)}, u32[]{:S(2)}, u32[]{:S(2)}) collective-permute-start(bf16[80,4096]{1,0:T(8,128)(2,1)} %bitcast.6.mine), channel_id=1, source_target_pairs={{0,4},{2,6},{4,0},{6,2},{8,12},{10,14},{12,8},{14,10},{1,5},{3,7},... | collective-permute-start | bytes 1966088 | tf_op jit(solution)/shard_map/ppermute | solution.py:121
  5.9 1.5 %collective-permute-start.1 = (bf16[80,4096]{1,0:T(8,128)(2,1)}, bf16[80,4096]{1,0:T(8,128)(2,1)}, u32[]{:S(2)}, u32[]{:S(2)}) collective-permute-start(bf16[80,4096]{1,0:T(8,128)(2,1)} %bitcast.6.mine), channel_id=1, source_target_pairs={{4,8},{6,10},{8,4},{10,6},{0,2},{2,0},{12,14},{14,12},{5,9},{7,11}... | collective-permute-start | bytes 1966088 | tf_op jit(solution)/shard_map/ppermute | solution.py:121
  7.4 1.5 %collective-permute-start.4 = (bf16[80,4096]{1,0:T(8,128)(2,1)}, bf16[80,4096]{1,0:T(8,128)(2,1)}, u32[]{:S(2)}, u32[]{:S(2)}) collective-permute-start(bf16[80,4096]{1,0:T(8,128)(2,1)} %bitcast.6.mine), channel_id=1, source_target_pairs={{4,6},{6,4},{8,10},{10,8},{5,7},{7,5},{9,11},{11,9},{20,22},{22,20... | collective-permute-start | bytes 1966088 | tf_op jit(solution)/shard_map/ppermute | solution.py:121
  8.9 1.8 %slice.6 = bf16[48,4096]{1,0:T(8,128)(2,1)} slice(bf16[256,4096]{1,0:T(8,128)(2,1)} %own.1), slice={[0:48], [0:4096]} | slice | bytes 786432 | tf_op jit(solution)/shard_map/slice | solution.py:357
  10.7 1.5 %collective-permute-start.2 = (bf16[48,4096]{1,0:T(8,128)(2,1)}, bf16[48,4096]{1,0:T(8,128)(2,1)}, u32[]{:S(2)}, u32[]{:S(2)}) collective-permute-start(bf16[48,4096]{1,0:T(8,128)(2,1)} %slice.6), channel_id=1, source_target_pairs={{0,16},{16,0},{1,17},{17,1},{2,18},{18,2},{3,19},{19,3},{4,20},{20... | collective-permute-start | bytes 1179656 | tf_op jit(solution)/shard_map/ppermute | solution.py:358
  12.2 0.0 copy-done.1
  12.2 0.5 multiply_reduce_fusion
  12.7 0.0 copy-start.4
  12.7 2.5 %psum.7 = f32[256]{0:T(256)S(1)} all-reduce(f32[256]{0:T(256)S(1)} %multiply_reduce_fusion), channel_id=1, replica_groups=mesh['parts'=2,'dp'=8,'tensor'=2] {'tensor'}, use_global_device_ids=true, to_apply=%region_3.4 | all-reduce | flops 256 | bytes 2048 | tf_op jit(solution)/shard_map/psum | solution.py:359
  15.2 0.5 collective-permute-start.3
  15.7 1.3 %slice.7 = bf16[208,4096]{1,0:T(8,128)(2,1)} slice(bf16[256,4096]{1,0:T(8,128)(2,1)S(1)} %copy-done.1), slice={[48:256], [0:4096]} | slice | bytes 3407872 | tf_op jit(solution)/shard_map/slice | solution.py:362
  17.0 4.3 %collective-permute-done.3 = f32[256]{0:T(256)S(1)} collective-permute-done((f32[256]{0:T(256)S(1)}, f32[256]{0:T(256)S(1)}, u32[]{:S(2)}, u32[]{:S(2)}) %collective-permute-start.3) | collective-permute-done | bytes 1056 | tf_op jit(solution)/shard_map/ppermute | solution.py:360
  21.3 0.0 collective-permute-done.2.ahead
  21.3 0.0 collective-permute-done.near
  21.3 1.1 %collective-permute-done.1.cross = bf16[80,4096]{1,0:T(8,128)(2,1)} collective-permute-done((bf16[80,4096]{1,0:T(8,128)(2,1)}, bf16[80,4096]{1,0:T(8,128)(2,1)}, u32[]{:S(2)}, u32[]{:S(2)}) %collective-permute-start.1) | collective-permute-done | bytes 655392 | tf_op jit(solution)/shard_map/ppermute | solution.py:121
  22.4 2.2 %collective-permute-start.5 = (bf16[80,4096]{1,0:T(8,128)(2,1)}, bf16[80,4096]{1,0:T(8,128)(2,1)}, u32[]{:S(2)}, u32[]{:S(2)}) collective-permute-start(bf16[80,4096]{1,0:T(8,128)(2,1)} %collective-permute-done.1.cross), channel_id=1, source_target_pairs={{0,4},{2,6},{4,0},{6,2},{8,12},{10,14},{12,8},{14,10},{1,5},{3,7},... | collective-permute-start | bytes 1966088 | tf_op jit(solution)/shard_map/ppermute | solution.py:121
  24.6 0.7 collective-permute-start.6
  25.3 1.5 %collective-permute-start.10 = (bf16[208,4096]{1,0:T(8,128)(2,1)}, bf16[208,4096]{1,0:T(8,128)(2,1)}, u32[]{:S(2)}, u32[]{:S(2)}) collective-permute-start(bf16[208,4096]{1,0:T(8,128)(2,1)} %slice.7), channel_id=1, source_target_pairs={{0,16},{16,0},{1,17},{17,1},{2,18},{18,2},{3,19},{19,3},{4,20},{20... | collective-permute-start | bytes 5111816 | tf_op jit(solution)/shard_map/ppermute | solution.py:364
  26.8 0.0 collective-permute-done.4.side
  26.8 0.7 collective-permute-start.7
  27.5 10.5 %collective-permute-done.5.second = bf16[80,4096]{1,0:T(8,128)(2,1)} collective-permute-done((bf16[80,4096]{1,0:T(8,128)(2,1)}, bf16[80,4096]{1,0:T(8,128)(2,1)}, u32[]{:S(2)}, u32[]{:S(2)}) %collective-permute-start.5) | collective-permute-done | bytes 655392 | tf_op jit(solution)/shard_map/ppermute | solution.py:121
  38.0 1.5 %collective-permute-done.6.onward = bf16[80,4096]{1,0:T(8,128)(2,1)} collective-permute-done((bf16[80,4096]{1,0:T(8,128)(2,1)}, bf16[80,4096]{1,0:T(8,128)(2,1)}, u32[]{:S(2)}, u32[]{:S(2)}) %collective-permute-start.6) | collective-permute-done | bytes 655392 | tf_op jit(solution)/shard_map/ppermute | solution.py:121
  39.5 1.3 %collective-permute-start.11 = (bf16[80,4096]{1,0:T(8,128)(2,1)}, bf16[80,4096]{1,0:T(8,128)(2,1)}, u32[]{:S(2)}, u32[]{:S(2)}) collective-permute-start(bf16[80,4096]{1,0:T(8,128)(2,1)} %collective-permute-done.6.onward), channel_id=1, source_target_pairs={{4,0},{6,2},{8,12},{10,14},{5,1},{7,3},{9,13},{11,15},{20,16},{22,... | collective-permute-start | bytes 1966088 | tf_op jit(solution)/shard_map/ppermute | solution.py:121
  40.8 0.0 collective-permute-done.7.cross_over
  40.8 0.0 copy-start.2
  40.8 0.8 copy-done.2
  41.6 3.4 %collective-permute-start.9 = (bf16[80,4096]{1,0:T(8,128)(2,1)}, bf16[80,4096]{1,0:T(8,128)(2,1)}, u32[]{:S(2)}, u32[]{:S(2)}) collective-permute-start(bf16[80,4096]{1,0:T(8,128)(2,1)} %collective-permute-done.5.second), channel_id=1, source_target_pairs={{0,2},{2,0},{12,14},{14,12},{1,3},{3,1},{13,15},{15,13},{16,18},{1... | collective-permute-start | bytes 1966088 | tf_op jit(solution)/shard_map/ppermute | solution.py:121
  45.0 1.6 %collective-permute-start.8 = (bf16[80,4096]{1,0:T(8,128)(2,1)}, bf16[80,4096]{1,0:T(8,128)(2,1)}, u32[]{:S(2)}, u32[]{:S(2)}) collective-permute-start(bf16[80,4096]{1,0:T(8,128)(2,1)} %collective-permute-done.6.onward), channel_id=1, source_target_pairs={{4,6},{6,4},{8,10},{10,8},{5,7},{7,5},{9,11},{11,9},{20,22},{22,20... | collective-permute-start | bytes 1966088 | tf_op jit(solution)/shard_map/ppermute | solution.py:121
  46.6 8.7 %collective-permute-done.11.piece = bf16[80,4096]{1,0:T(8,128)(2,1)} collective-permute-done((bf16[80,4096]{1,0:T(8,128)(2,1)}, bf16[80,4096]{1,0:T(8,128)(2,1)}, u32[]{:S(2)}, u32[]{:S(2)}) %collective-permute-start.11) | collective-permute-done | bytes 655392 | tf_op jit(solution)/shard_map/ppermute | solution.py:121
  55.3 4.2 %collective-permute-start.12 = (bf16[80,4096]{1,0:T(8,128)(2,1)}, bf16[80,4096]{1,0:T(8,128)(2,1)}, u32[]{:S(2)}, u32[]{:S(2)}) collective-permute-start(bf16[80,4096]{1,0:T(8,128)(2,1)} %collective-permute-done.11.piece), channel_id=1, source_target_pairs={{0,2},{2,0},{12,14},{14,12},{1,3},{3,1},{13,15},{15,13},{16,18},{1... | collective-permute-start | bytes 1966088 | tf_op jit(solution)/shard_map/ppermute | solution.py:121
  59.5 0.0 copy-done.7
  59.5 0.2 reduce-window.13
  59.7 0.1 pad_add_fusion.at
  59.7 0.0 collective-permute-done.9.second_over
  59.7 0.0 collective-permute-done.8.far_over
  59.7 3.4 %collective-permute-done.10.behind = bf16[208,4096]{1,0:T(8,128)(2,1)} collective-permute-done((bf16[208,4096]{1,0:T(8,128)(2,1)}, bf16[208,4096]{1,0:T(8,128)(2,1)}, u32[]{:S(2)}, u32[]{:S(2)}) %collective-permute-start.10) | collective-permute-done | bytes 1703968 | tf_op jit(solution)/shard_map/ppermute | solution.py:364
  63.1 0.0 copy-done.4
  63.1 0.0 copy-start.3
  63.1 1.1 %copy-done.3 = bf16[80,4096]{1,0:T(8,128)(2,1)S(1)} copy-done((bf16[80,4096]{1,0:T(8,128)(2,1)S(1)}, bf16[80,4096]{1,0:T(8,128)(2,1)}, u32[]{:S(2)}) %copy-start.3) | copy-done | bytes 655384
  64.2 8.1 %project_early.1 = (f32[512,384]{1,0:T(8,128)S(1)}, f32[512,384]{1,0:T(8,128)S(1)}, bf16[512,4096]{1,0:T(8,128)(2,1)S(1)}) custom-call(s32[4]{0:T(128)S(1)} %pad_add_fusion.at, bf16[80,4096]{1,0:T(8,128)(2,1)} %bitcast.6.mine, bf16[80,4096]{1,0:T(8,128)(2,1)} %collective-permute-done.near, bf16[80,4096]{1,0:T(8,128)(2,1)} %collective-permute-done.1.cross, ...), custom_call_target="tpu_custom_call" | custom-call | flops 2684354560 | bytes 12582912 | tf_op jit(solution)/shard_map/project_early/pallas_call | solution.py:369
  72.4 0.0 collective-permute-done.12.piece_over
  72.4 0.0 copy-start.6
  72.4 0.0 copy-start.5
  72.4 2.9 %project_late.1 = (f32[512,384]{1,0:T(8,128)S(1)}, f32[512,384]{1,0:T(8,128)S(1)}) custom-call(s32[4]{0:T(128)S(1)} %pad_add_fusion.at, f32[512,384]{1,0:T(8,128)S(1)} %get-tuple-element.26.first_keep, f32[512,384]{1,0:T(8,128)S(1)} %get-tuple-element.27.first_send, ...), custom_call_target="tpu_custom_call", output_to_operand_aliasing={{0}: (1, {}), {1}: (2, {})} | custom-call | flops 1073741824 | bytes 6291456 | tf_op jit(solution)/shard_map/project_late/pallas_call | solution.py:390
  75.3 0.1 collective-permute-start.13
  75.4 0.0 copy-done.6
  75.4 0.1 select_reduce_fusion
  75.5 0.0 copy-done.5
  75.6 0.2 fusion.5
  75.7 0.3 fusion.1
  76.1 1.6 %collective-permute-done.13.other = f32[512,384]{1,0:T(8,128)S(1)} collective-permute-done((f32[512,384]{1,0:T(8,128)S(1)}, f32[512,384]{1,0:T(8,128)S(1)}, u32[]{:S(2)}, u32[]{:S(2)}) %collective-permute-start.13) | collective-permute-done | bytes 786464 | tf_op jit(solution)/shard_map/ppermute | solution.py:410
  77.7 0.8 sum_halves.1
  78.5 5.1 %all-to-all-start = ((bf16[16,32,384]{2,1,0:T(8,128)(2,1)}), bf16[16,32,384]{2,1,0:T(8,128)(2,1)S(1)}, u32[]{:S(2)}, u32[]{:S(2)}) async-start(bf16[16,32,384]{2,1,0:T(8,128)(2,1)} %bitcast.10), calls=%async_computation | async-start | bytes 786432 | tf_op jit(solution)/shard_map/all_to_all | solution.py:411
  83.6 0.1 reduce
  83.8 0.1 pad_maximum_fusion
  83.9 0.1 select_reduce_fusion.2
  84.0 0.1 fusion.pick
  84.1 0.1 and_convert_fusion.allowed
  84.2 12.3 %all-to-all-done = bf16[16,32,384]{2,1,0:T(8,128)(2,1)S(1)} async-done(((bf16[16,32,384]{2,1,0:T(8,128)(2,1)}), bf16[16,32,384]{2,1,0:T(8,128)(2,1)S(1)}, u32[]{:S(2)}, u32[]{:S(2)}) %all-to-all-start) | async-done | bytes 393248 | tf_op jit(solution)/shard_map/all_to_all | solution.py:411
  96.5 2.3 %attend.1 = (bf16[128,128]{1,0:T(8,128)(2,1)}, bf16[128,128]{1,0:T(8,128)(2,1)}, bf16[128,512]{1,0:T(8,128)(2,1)}) custom-call(bf16[128,256]{1,0:T(8,128)(2,1)S(1)} %fusion.pick, bf16[2,256,384]{2,1,0:T(8,128)(2,1)S(1)} %bitcast.25, f32[128,128]{1,0:T(8,128)S(1)} %get-tuple-element.38.cosine, f32[128,128]{1,0:T(8,128)S(1)} %get-tuple-element.39.sine, ...), custom_call_target="tpu_custom_call" | custom-call | tf_op jit(solution)/shard_map/attend/pallas_call | solution.py:325
  (8 shorter events, 0.1 us)
Async XLA Ops:
  0.6 1.3 %copy-start = (bf16[4096,160]{0,1:T(8,128)(2,1)S(1)}, bf16[4096,160]{0,1:T(8,128)(2,1)}, u32[]{:S(2)}) copy-start(bf16[4096,160]{0,1:T(8,128)(2,1)} %param.8) | copy-start | bytes 3932164
  0.6 11.6 %copy-start.1 = (bf16[256,4096]{1,0:T(8,128)(2,1)S(1)}, bf16[256,4096]{1,0:T(8,128)(2,1)}, u32[]{:S(2)}) copy-start(bf16[256,4096]{1,0:T(8,128)(2,1)} %own.1) | copy-start | bytes 6291460
  2.8 18.5 %collective-permute-start = (bf16[80,4096]{1,0:T(8,128)(2,1)}, bf16[80,4096]{1,0:T(8,128)(2,1)}, u32[]{:S(2)}, u32[]{:S(2)}) collective-permute-start(bf16[80,4096]{1,0:T(8,128)(2,1)} %bitcast.6.mine), channel_id=1, source_target_pairs={{0,4},{2,6},{4,0},{6,2},{8,12},{10,14},{12,8},{14,10},{1,5},{3,7},... | collective-permute-start | bytes 1966088 | tf_op jit(solution)/shard_map/ppermute | solution.py:121
  5.9 16.5 %collective-permute-start.1 = (bf16[80,4096]{1,0:T(8,128)(2,1)}, bf16[80,4096]{1,0:T(8,128)(2,1)}, u32[]{:S(2)}, u32[]{:S(2)}) collective-permute-start(bf16[80,4096]{1,0:T(8,128)(2,1)} %bitcast.6.mine), channel_id=1, source_target_pairs={{4,8},{6,10},{8,4},{10,6},{0,2},{2,0},{12,14},{14,12},{5,9},{7,11}... | collective-permute-start | bytes 1966088 | tf_op jit(solution)/shard_map/ppermute | solution.py:121
  7.4 19.5 %collective-permute-start.4 = (bf16[80,4096]{1,0:T(8,128)(2,1)}, bf16[80,4096]{1,0:T(8,128)(2,1)}, u32[]{:S(2)}, u32[]{:S(2)}) collective-permute-start(bf16[80,4096]{1,0:T(8,128)(2,1)} %bitcast.6.mine), channel_id=1, source_target_pairs={{4,6},{6,4},{8,10},{10,8},{5,7},{7,5},{9,11},{11,9},{20,22},{22,20... | collective-permute-start | bytes 1966088 | tf_op jit(solution)/shard_map/ppermute | solution.py:121
  10.7 10.6 %collective-permute-start.2 = (bf16[48,4096]{1,0:T(8,128)(2,1)}, bf16[48,4096]{1,0:T(8,128)(2,1)}, u32[]{:S(2)}, u32[]{:S(2)}) collective-permute-start(bf16[48,4096]{1,0:T(8,128)(2,1)} %slice.6), channel_id=1, source_target_pairs={{0,16},{16,0},{1,17},{17,1},{2,18},{18,2},{3,19},{19,3},{4,20},{20... | collective-permute-start | bytes 1179656 | tf_op jit(solution)/shard_map/ppermute | solution.py:358
  12.7 46.8 %copy-start.7 = (s32[1,8]{1,0:T(1,128)S(1)}, s32[1,8]{1,0:T(1,128)}, u32[]{:S(2)}) copy-start(s32[1,8]{1,0:T(1,128)} %param.10) | copy-start | bytes 100
  12.7 50.4 %copy-start.4 = (f32[4096]{0:T(1024)S(1)}, f32[4096]{0:T(1024)}, u32[]{:S(2)}) copy-start(f32[4096]{0:T(1024)} %param.7) | copy-start | bytes 49156
  15.2 6.1 %collective-permute-start.3 = (f32[256]{0:T(256)S(1)}, f32[256]{0:T(256)S(1)}, u32[]{:S(2)}, u32[]{:S(2)}) collective-permute-start(f32[256]{0:T(256)S(1)} %add_rsqrt_fusion), channel_id=1, source_target_pairs={{0,16},{16,0},{1,17},{17,1},{2,18},{18,2},{3,19},{19,3},{4,20},{20... | collective-permute-start | bytes 3080 | tf_op jit(solution)/shard_map/ppermute | solution.py:360
  22.4 15.6 %collective-permute-start.5 = (bf16[80,4096]{1,0:T(8,128)(2,1)}, bf16[80,4096]{1,0:T(8,128)(2,1)}, u32[]{:S(2)}, u32[]{:S(2)}) collective-permute-start(bf16[80,4096]{1,0:T(8,128)(2,1)} %collective-permute-done.1.cross), channel_id=1, source_target_pairs={{0,4},{2,6},{4,0},{6,2},{8,12},{10,14},{12,8},{14,10},{1,5},{3,7},... | collective-permute-start | bytes 1966088 | tf_op jit(solution)/shard_map/ppermute | solution.py:121
  24.6 14.8 %collective-permute-start.6 = (bf16[80,4096]{1,0:T(8,128)(2,1)}, bf16[80,4096]{1,0:T(8,128)(2,1)}, u32[]{:S(2)}, u32[]{:S(2)}) collective-permute-start(bf16[80,4096]{1,0:T(8,128)(2,1)} %collective-permute-done.near), channel_id=1, source_target_pairs={{4,8},{6,10},{8,4},{10,6},{0,2},{2,0},{12,14},{14,12},{5,9},{7,11}... | collective-permute-start | bytes 1966088 | tf_op jit(solution)/shard_map/ppermute | solution.py:121
  25.3 37.8 %collective-permute-start.10 = (bf16[208,4096]{1,0:T(8,128)(2,1)}, bf16[208,4096]{1,0:T(8,128)(2,1)}, u32[]{:S(2)}, u32[]{:S(2)}) collective-permute-start(bf16[208,4096]{1,0:T(8,128)(2,1)} %slice.7), channel_id=1, source_target_pairs={{0,16},{16,0},{1,17},{17,1},{2,18},{18,2},{3,19},{19,3},{4,20},{20... | collective-permute-start | bytes 5111816 | tf_op jit(solution)/shard_map/ppermute | solution.py:364
  26.8 13.9 %collective-permute-start.7 = (bf16[80,4096]{1,0:T(8,128)(2,1)}, bf16[80,4096]{1,0:T(8,128)(2,1)S(1)}, u32[]{:S(2)}, u32[]{:S(2)}) collective-permute-start(bf16[80,4096]{1,0:T(8,128)(2,1)} %collective-permute-done.1.cross), channel_id=1, source_target_pairs={{4,6},{6,4},{8,10},{10,8},{5,7},{7,5},{9,11},{11,9},{20,22},{22,20... | collective-permute-start | bytes 1966088 | tf_op jit(solution)/shard_map/ppermute | solution.py:121
  39.5 15.8 %collective-permute-start.11 = (bf16[80,4096]{1,0:T(8,128)(2,1)}, bf16[80,4096]{1,0:T(8,128)(2,1)}, u32[]{:S(2)}, u32[]{:S(2)}) collective-permute-start(bf16[80,4096]{1,0:T(8,128)(2,1)} %collective-permute-done.6.onward), channel_id=1, source_target_pairs={{4,0},{6,2},{8,12},{10,14},{5,1},{7,3},{9,13},{11,15},{20,16},{22,... | collective-permute-start | bytes 1966088 | tf_op jit(solution)/shard_map/ppermute | solution.py:121
  40.8 0.8 copy-start.2
  41.6 18.2 %collective-permute-start.9 = (bf16[80,4096]{1,0:T(8,128)(2,1)}, bf16[80,4096]{1,0:T(8,128)(2,1)}, u32[]{:S(2)}, u32[]{:S(2)}) collective-permute-start(bf16[80,4096]{1,0:T(8,128)(2,1)} %collective-permute-done.5.second), channel_id=1, source_target_pairs={{0,2},{2,0},{12,14},{14,12},{1,3},{3,1},{13,15},{15,13},{16,18},{1... | collective-permute-start | bytes 1966088 | tf_op jit(solution)/shard_map/ppermute | solution.py:121
  45.0 14.8 %collective-permute-start.8 = (bf16[80,4096]{1,0:T(8,128)(2,1)}, bf16[80,4096]{1,0:T(8,128)(2,1)}, u32[]{:S(2)}, u32[]{:S(2)}) collective-permute-start(bf16[80,4096]{1,0:T(8,128)(2,1)} %collective-permute-done.6.onward), channel_id=1, source_target_pairs={{4,6},{6,4},{8,10},{10,8},{5,7},{7,5},{9,11},{11,9},{20,22},{22,20... | collective-permute-start | bytes 1966088 | tf_op jit(solution)/shard_map/ppermute | solution.py:121
  55.3 17.1 %collective-permute-start.12 = (bf16[80,4096]{1,0:T(8,128)(2,1)}, bf16[80,4096]{1,0:T(8,128)(2,1)}, u32[]{:S(2)}, u32[]{:S(2)}) collective-permute-start(bf16[80,4096]{1,0:T(8,128)(2,1)} %collective-permute-done.11.piece), channel_id=1, source_target_pairs={{0,2},{2,0},{12,14},{14,12},{1,3},{3,1},{13,15},{15,13},{16,18},{1... | collective-permute-start | bytes 1966088 | tf_op jit(solution)/shard_map/ppermute | solution.py:121
  63.1 1.1 %copy-start.3 = (bf16[80,4096]{1,0:T(8,128)(2,1)S(1)}, bf16[80,4096]{1,0:T(8,128)(2,1)}, u32[]{:S(2)}) copy-start(bf16[80,4096]{1,0:T(8,128)(2,1)} %copy-done.2) | copy-start | bytes 1966084
  72.4 3.0 %copy-start.6 = (s32[1,8]{1,0:T(1,128)S(1)}, s32[1,8]{1,0:T(1,128)}, u32[]{:S(2)}) copy-start(s32[1,8]{1,0:T(1,128)} %param.11) | copy-start | bytes 100
  72.4 3.1 %copy-start.5 = (s32[8,8]{1,0:T(8,128)S(1)}, s32[8,8]{1,0:T(8,128)}, u32[]{:S(2)}) copy-start(s32[8,8]{1,0:T(8,128)} %param.9) | copy-start | bytes 772
  75.3 2.4 %collective-permute-start.13 = (f32[512,384]{1,0:T(8,128)S(1)}, f32[512,384]{1,0:T(8,128)S(1)}, u32[]{:S(2)}, u32[]{:S(2)}) collective-permute-start(f32[512,384]{1,0:T(8,128)S(1)} %get-tuple-element.30), channel_id=1, source_target_pairs={{0,1},{1,0},{2,3},{3,2},{4,5},{5,4},{6,7},{7,6},{8,9},{9,8},{10,11... | collective-permute-start | bytes 2359304 | tf_op jit(solution)/shard_map/ppermute | solution.py:410
  78.5 18.0 %all-to-all-start = ((bf16[16,32,384]{2,1,0:T(8,128)(2,1)}), bf16[16,32,384]{2,1,0:T(8,128)(2,1)S(1)}, u32[]{:S(2)}, u32[]{:S(2)}) async-start(bf16[16,32,384]{2,1,0:T(8,128)(2,1)} %bitcast.10), calls=%async_computation | async-start | bytes 786432 | tf_op jit(solution)/shard_map/all_to_all | solution.py:411

commit v13 on v12

--- a/solution.py
+++ b/solution.py
@@ -140,19 +140,30 @@
 
 def early_kernel(
     at, mine, near, cross, side, second, onward, cross_over, far_over, second_over,
-    own, ahead, behind, own_scale, their_scale, gain, keep, send, rows, whole, sem,
+    own, ahead, behind, own_scale, their_scale, gain, keep, send, rows, whole, sems,
 ):
     z, x, part, core = at[0], at[1], at[2], at[3]
     size = mine.shape[0]
 
     at_end = (z == 0) | (z == 3)
     middle = jnp.logical_not(at_end)
-    there = pl.multiple_of((2 * (3 - z) + 1 - x) * size, BLOCK)
-    fetch = pltpu.make_async_copy(cross_over, whole.at[pl.ds(there, size)], sem)
-
-    @pl.when(middle)
-    def _():
-        fetch.start()
+
+    def fetch(k, piece, where):
+        start = pl.multiple_of((2 * where + 1 - x) * size, BLOCK)
+        return pltpu.make_async_copy(piece, whole.at[pl.ds(start, size)], sems.at[k])
+
+    at_ends = (fetch(0, second_over, (z + 2) % 4),)
+    in_middle = (
+        fetch(0, far_over, (z + 2) % 4),
+        fetch(1, cross_over, 3 - z),
+        fetch(2, side, z),
+    )
+    for here, copies in ((at_end, at_ends), (middle, in_middle)):
+
+        @pl.when(here)
+        def _():
+            for copy in copies:
+                copy.start()
 
     def place(pairs):
         for where, pieces in pairs:
@@ -186,7 +197,7 @@
             (
                 (z, (mine, cross)),
                 (pair, (near, onward)),
-                ((z + 2) % 4, (second, second_over)),
+                ((z + 2) % 4, (second,)),
                 (3 - z, (mine, cross)),
             )
         )
@@ -195,16 +206,19 @@
     def _():
         place(
             (
-                (z, (mine, side)),
+                (z, (mine,)),
                 (pair, (near, second)),
-                ((z + 2) % 4, (onward, far_over)),
+                ((z + 2) % 4, (onward,)),
                 (3 - z, (cross,)),
             )
         )
 
-    @pl.when(middle)
-    def _():
-        fetch.wait()
+    for here, copies in ((at_end, at_ends), (middle, in_middle)):
+
+        @pl.when(here)
+        def _():
+            for copy in copies:
+                copy.wait()
 
     share = whole.shape[0] * HQ // (HQ + 2) // 2
     halves = [product(rows[...], whole[c * share : (c + 1) * share, :]) for c in range(2)]
@@ -349,7 +363,7 @@
     swap = [(0, 1), (1, 0)]
     cut_at = sent_rows.shape[0] * 3 // 16
     whole = pl.BlockSpec(memory_space=pltpu.VMEM)
-    anywhere = pl.BlockSpec(memory_space=pl.ANY)
+    apart = pl.BlockSpec(memory_space=pltpu.HBM)
     scalars = pl.BlockSpec(memory_space=pltpu.SMEM)
     mine = lax.dynamic_index_in_dim(
         turned.reshape(count, 2, BLOCK, depth), part, 1, False
@@ -369,9 +383,9 @@
     keep, send, rows = pl.pallas_call(
         early_kernel,
         out_shape=(half, half, jax.ShapeDtypeStruct((2 * slots, depth), jnp.bfloat16)),
-        in_specs=[scalars] + [whole] * 6 + [pl.BlockSpec(memory_space=pltpu.HBM)] + [whole] * 8,
+        in_specs=[scalars] + [whole] * 3 + [apart] + [whole] * 2 + [apart] * 3 + [whole] * 6,
         out_specs=(whole,) * 3,
-        scratch_shapes=[pltpu.VMEM((width, depth), jnp.bfloat16), pltpu.SemaphoreType.DMA],
+        scratch_shapes=[pltpu.VMEM((width, depth), jnp.bfloat16), pltpu.SemaphoreType.DMA((3,))],
         compiler_params=pltpu.CompilerParams(vmem_limit_bytes=28 << 20),
         cost_estimate=pl.CostEstimate(
             flops=4 * slots * width * depth, bytes_accessed=12 << 20, transcendentals=0

time: 99.3 us -> 99.3 us (level)
  transfers between devices with their start and end apart: 15 -> 15, of which waited for: 8 -> 9; matrix products, arithmetic and copies ran while one was open for 5% -> 5% of each run, Pallas kernels for 8% -> 8%
where the time goes in v13:
time: 99.3 us; the launch traced here: 98.8 us
  waiting for transfers between devices  43.6 us (44%)
  starting transfers between devices  29.2 us (29%)
  Pallas kernels  13.6 us (14%)
  local copies, waits for them, and re-layouts  7.37 us (7%)
  blocking collectives  2.47 us (2%)
  other arithmetic  1.7 us (2%)
    ppermute x10, waiting for transfers between devices, send(): return lax.ppermute(block, 'dp', pairs)  21.9 us
    ppermute x10, starting transfers between devices, send(): return lax.ppermute(block, 'dp', pairs)  20.1 us
    all_to_all x1, waiting for transfers between devices, paired(): arrived = lax.all_to_all(ready, ('parts', 'dp'), 0, 0, tiled=True)  12.3 us
    pallas_call x1, Pallas kernels, paired(): pl.pallas_call(early_kernel, out_shape=(half, half, jax.ShapeDtypeStruct(...  7.56 us
    all_to_all x1, starting transfers between devices, paired(): arrived = lax.all_to_all(ready, ('parts', 'dp'), 0, 0, tiled=True)  5.49 us
    ppermute x1, waiting for transfers between devices, paired(): their_scale = lax.ppermute(scale, 'parts', swap)  4.31 us
    ppermute x1, waiting for transfers between devices, paired(): behind = lax.ppermute(rest, 'parts', swap)  3.39 us
    unnamed x16, local copies, waits for them, and re-layouts  3.23 us
  transfers between devices with their start and end apart: 15, of which 9 were waited for; matrix products, arithmetic and copies ran while one was open for 5% of the time, Pallas kernels for 8%

profile of v13, /device:TPU:0, one launch (start us, length us, event | category | flops | bytes accessed | tf_op | source)
XLA Modules:
  0.0 98.8 jit_solution(5512325714433380778)
XLA Ops:
  0.6 0.0 copy-start
  0.6 0.0 copy-start.1
  0.7 1.3 %copy-done = bf16[4096,160]{0,1:T(8,128)(2,1)S(1)} copy-done((bf16[4096,160]{0,1:T(8,128)(2,1)S(1)}, bf16[4096,160]{0,1:T(8,128)(2,1)}, u32[]{:S(2)}) %copy-start) | copy-done | bytes 1310744
  2.0 0.9 constant_dynamic-slice_fusion
  2.8 3.0 %collective-permute-start = (bf16[80,4096]{1,0:T(8,128)(2,1)}, bf16[80,4096]{1,0:T(8,128)(2,1)}, u32[]{:S(2)}, u32[]{:S(2)}) collective-permute-start(bf16[80,4096]{1,0:T(8,128)(2,1)} %bitcast.6.mine), channel_id=1, source_target_pairs={{0,4},{2,6},{4,0},{6,2},{8,12},{10,14},{12,8},{14,10},{1,5},{3,7},... | collective-permute-start | bytes 1966088 | tf_op jit(solution)/shard_map/ppermute | solution.py:121
  5.9 1.5 %collective-permute-start.1 = (bf16[80,4096]{1,0:T(8,128)(2,1)}, bf16[80,4096]{1,0:T(8,128)(2,1)}, u32[]{:S(2)}, u32[]{:S(2)}) collective-permute-start(bf16[80,4096]{1,0:T(8,128)(2,1)} %bitcast.6.mine), channel_id=1, source_target_pairs={{4,8},{6,10},{8,4},{10,6},{0,2},{2,0},{12,14},{14,12},{5,9},{7,11}... | collective-permute-start | bytes 1966088 | tf_op jit(solution)/shard_map/ppermute | solution.py:121
  7.4 1.5 %collective-permute-start.4 = (bf16[80,4096]{1,0:T(8,128)(2,1)}, bf16[80,4096]{1,0:T(8,128)(2,1)}, u32[]{:S(2)}, u32[]{:S(2)}) collective-permute-start(bf16[80,4096]{1,0:T(8,128)(2,1)} %bitcast.6.mine), channel_id=1, source_target_pairs={{4,6},{6,4},{8,10},{10,8},{5,7},{7,5},{9,11},{11,9},{20,22},{22,20... | collective-permute-start | bytes 1966088 | tf_op jit(solution)/shard_map/ppermute | solution.py:121
  8.9 1.8 %slice.6 = bf16[48,4096]{1,0:T(8,128)(2,1)} slice(bf16[256,4096]{1,0:T(8,128)(2,1)} %own.1), slice={[0:48], [0:4096]} | slice | bytes 786432 | tf_op jit(solution)/shard_map/slice | solution.py:371
  10.7 1.5 %collective-permute-start.2 = (bf16[48,4096]{1,0:T(8,128)(2,1)}, bf16[48,4096]{1,0:T(8,128)(2,1)}, u32[]{:S(2)}, u32[]{:S(2)}) collective-permute-start(bf16[48,4096]{1,0:T(8,128)(2,1)} %slice.6), channel_id=1, source_target_pairs={{0,16},{16,0},{1,17},{17,1},{2,18},{18,2},{3,19},{19,3},{4,20},{20... | collective-permute-start | bytes 1179656 | tf_op jit(solution)/shard_map/ppermute | solution.py:372
  12.2 0.0 copy-done.1
  12.2 0.5 multiply_reduce_fusion
  12.7 0.0 copy-start.7
  12.7 0.0 copy-start.4
  12.7 2.5 %psum.7 = f32[256]{0:T(256)S(1)} all-reduce(f32[256]{0:T(256)S(1)} %multiply_reduce_fusion), channel_id=1, replica_groups=mesh['parts'=2,'dp'=8,'tensor'=2] {'tensor'}, use_global_device_ids=true, to_apply=%region_3.4 | all-reduce | flops 256 | bytes 2048 | tf_op jit(solution)/shard_map/psum | solution.py:373
  15.2 0.5 collective-permute-start.3
  15.7 1.3 %slice.7 = bf16[208,4096]{1,0:T(8,128)(2,1)} slice(bf16[256,4096]{1,0:T(8,128)(2,1)S(1)} %copy-done.1), slice={[48:256], [0:4096]} | slice | bytes 3407872 | tf_op jit(solution)/shard_map/slice | solution.py:376
  17.0 4.3 %collective-permute-done.3 = f32[256]{0:T(256)S(1)} collective-permute-done((f32[256]{0:T(256)S(1)}, f32[256]{0:T(256)S(1)}, u32[]{:S(2)}, u32[]{:S(2)}) %collective-permute-start.3) | collective-permute-done | bytes 1056 | tf_op jit(solution)/shard_map/ppermute | solution.py:374
  21.3 0.0 collective-permute-done.2.ahead
  21.3 0.0 collective-permute-done.near
  21.3 1.1 %collective-permute-done.1.cross = bf16[80,4096]{1,0:T(8,128)(2,1)} collective-permute-done((bf16[80,4096]{1,0:T(8,128)(2,1)}, bf16[80,4096]{1,0:T(8,128)(2,1)}, u32[]{:S(2)}, u32[]{:S(2)}) %collective-permute-start.1) | collective-permute-done | bytes 655392 | tf_op jit(solution)/shard_map/ppermute | solution.py:121
  22.4 2.2 %collective-permute-start.5 = (bf16[80,4096]{1,0:T(8,128)(2,1)}, bf16[80,4096]{1,0:T(8,128)(2,1)}, u32[]{:S(2)}, u32[]{:S(2)}) collective-permute-start(bf16[80,4096]{1,0:T(8,128)(2,1)} %collective-permute-done.1.cross), channel_id=1, source_target_pairs={{0,4},{2,6},{4,0},{6,2},{8,12},{10,14},{12,8},{14,10},{1,5},{3,7},... | collective-permute-start | bytes 1966088 | tf_op jit(solution)/shard_map/ppermute | solution.py:121
  24.6 0.7 collective-permute-start.6
  25.3 1.5 %collective-permute-start.10 = (bf16[208,4096]{1,0:T(8,128)(2,1)}, bf16[208,4096]{1,0:T(8,128)(2,1)}, u32[]{:S(2)}, u32[]{:S(2)}) collective-permute-start(bf16[208,4096]{1,0:T(8,128)(2,1)} %slice.7), channel_id=1, source_target_pairs={{0,16},{16,0},{1,17},{17,1},{2,18},{18,2},{3,19},{19,3},{4,20},{20... | collective-permute-start | bytes 5111816 | tf_op jit(solution)/shard_map/ppermute | solution.py:378
  26.8 0.0 collective-permute-done.4.side
  26.8 0.7 collective-permute-start.7
  27.5 10.5 %collective-permute-done.5.second = bf16[80,4096]{1,0:T(8,128)(2,1)} collective-permute-done((bf16[80,4096]{1,0:T(8,128)(2,1)}, bf16[80,4096]{1,0:T(8,128)(2,1)}, u32[]{:S(2)}, u32[]{:S(2)}) %collective-permute-start.5) | collective-permute-done | bytes 655392 | tf_op jit(solution)/shard_map/ppermute | solution.py:121
  38.0 1.5 %collective-permute-done.6.onward = bf16[80,4096]{1,0:T(8,128)(2,1)} collective-permute-done((bf16[80,4096]{1,0:T(8,128)(2,1)}, bf16[80,4096]{1,0:T(8,128)(2,1)}, u32[]{:S(2)}, u32[]{:S(2)}) %collective-permute-start.6) | collective-permute-done | bytes 655392 | tf_op jit(solution)/shard_map/ppermute | solution.py:121
  39.5 1.3 %collective-permute-start.11 = (bf16[80,4096]{1,0:T(8,128)(2,1)}, bf16[80,4096]{1,0:T(8,128)(2,1)}, u32[]{:S(2)}, u32[]{:S(2)}) collective-permute-start(bf16[80,4096]{1,0:T(8,128)(2,1)} %collective-permute-done.6.onward), channel_id=1, source_target_pairs={{4,0},{6,2},{8,12},{10,14},{5,1},{7,3},{9,13},{11,15},{20,16},{22,... | collective-permute-start | bytes 1966088 | tf_op jit(solution)/shard_map/ppermute | solution.py:121
  40.8 0.0 collective-permute-done.7.cross_over
  40.8 0.0 copy-start.2
  40.8 0.8 copy-done.2
  41.6 3.4 %collective-permute-start.9 = (bf16[80,4096]{1,0:T(8,128)(2,1)}, bf16[80,4096]{1,0:T(8,128)(2,1)}, u32[]{:S(2)}, u32[]{:S(2)}) collective-permute-start(bf16[80,4096]{1,0:T(8,128)(2,1)} %collective-permute-done.5.second), channel_id=1, source_target_pairs={{0,2},{2,0},{12,14},{14,12},{1,3},{3,1},{13,15},{15,13},{16,18},{1... | collective-permute-start | bytes 1966088 | tf_op jit(solution)/shard_map/ppermute | solution.py:121
  45.0 1.6 %collective-permute-start.8 = (bf16[80,4096]{1,0:T(8,128)(2,1)}, bf16[80,4096]{1,0:T(8,128)(2,1)}, u32[]{:S(2)}, u32[]{:S(2)}) collective-permute-start(bf16[80,4096]{1,0:T(8,128)(2,1)} %collective-permute-done.6.onward), channel_id=1, source_target_pairs={{4,6},{6,4},{8,10},{10,8},{5,7},{7,5},{9,11},{11,9},{20,22},{22,20... | collective-permute-start | bytes 1966088 | tf_op jit(solution)/shard_map/ppermute | solution.py:121
  46.6 8.7 %collective-permute-done.11.piece = bf16[80,4096]{1,0:T(8,128)(2,1)} collective-permute-done((bf16[80,4096]{1,0:T(8,128)(2,1)}, bf16[80,4096]{1,0:T(8,128)(2,1)}, u32[]{:S(2)}, u32[]{:S(2)}) %collective-permute-start.11) | collective-permute-done | bytes 655392 | tf_op jit(solution)/shard_map/ppermute | solution.py:121
  55.3 4.2 %collective-permute-start.12 = (bf16[80,4096]{1,0:T(8,128)(2,1)}, bf16[80,4096]{1,0:T(8,128)(2,1)}, u32[]{:S(2)}, u32[]{:S(2)}) collective-permute-start(bf16[80,4096]{1,0:T(8,128)(2,1)} %collective-permute-done.11.piece), channel_id=1, source_target_pairs={{0,2},{2,0},{12,14},{14,12},{1,3},{3,1},{13,15},{15,13},{16,18},{1... | collective-permute-start | bytes 1966088 | tf_op jit(solution)/shard_map/ppermute | solution.py:121
  59.5 0.0 copy-done.7
  59.5 0.2 reduce-window.13
  59.7 0.1 pad_add_fusion.at
  59.7 0.0 collective-permute-done.9.second_over
  59.7 0.0 collective-permute-done.8.far_over
  59.7 3.4 %collective-permute-done.10.behind = bf16[208,4096]{1,0:T(8,128)(2,1)} collective-permute-done((bf16[208,4096]{1,0:T(8,128)(2,1)}, bf16[208,4096]{1,0:T(8,128)(2,1)}, u32[]{:S(2)}, u32[]{:S(2)}) %collective-permute-start.10) | collective-permute-done | bytes 1703968 | tf_op jit(solution)/shard_map/ppermute | solution.py:378
  63.1 0.0 copy-done.4
  63.1 0.0 copy-start.3
  63.1 1.1 %copy-done.3 = bf16[80,4096]{1,0:T(8,128)(2,1)S(1)} copy-done((bf16[80,4096]{1,0:T(8,128)(2,1)S(1)}, bf16[80,4096]{1,0:T(8,128)(2,1)}, u32[]{:S(2)}) %copy-start.3) | copy-done | bytes 655384
  64.2 7.6 %project_early.1 = (f32[512,384]{1,0:T(8,128)S(1)}, f32[512,384]{1,0:T(8,128)S(1)}, bf16[512,4096]{1,0:T(8,128)(2,1)S(1)}) custom-call(s32[4]{0:T(128)S(1)} %pad_add_fusion.at, bf16[80,4096]{1,0:T(8,128)(2,1)} %bitcast.6.mine, bf16[80,4096]{1,0:T(8,128)(2,1)} %collective-permute-done.near, bf16[80,4096]{1,0:T(8,128)(2,1)} %collective-permute-done.1.cross, ...), custom_call_target="tpu_custom_call" | custom-call | flops 2684354560 | bytes 12582912 | tf_op jit(solution)/shard_map/project_early/pallas_call | solution.py:383
  71.8 0.2 collective-permute-done.12.piece_over
  72.0 0.0 copy-start.5
  72.0 2.9 %project_late.1 = (f32[512,384]{1,0:T(8,128)S(1)}, f32[512,384]{1,0:T(8,128)S(1)}) custom-call(s32[4]{0:T(128)S(1)} %pad_add_fusion.at, f32[512,384]{1,0:T(8,128)S(1)} %get-tuple-element.26.first_keep, f32[512,384]{1,0:T(8,128)S(1)} %get-tuple-element.27.first_send, ...), custom_call_target="tpu_custom_call", output_to_operand_aliasing={{0}: (1, {}), {1}: (2, {})} | custom-call | flops 1073741824 | bytes 6291456 | tf_op jit(solution)/shard_map/project_late/pallas_call | solution.py:404
  74.9 0.1 collective-permute-start.13
  75.0 0.0 copy-done.6
  75.0 0.1 select_reduce_fusion
  75.1 0.0 copy-done.5
  75.1 0.2 fusion.5
  75.3 0.3 fusion.1
  75.6 1.6 %collective-permute-done.13.other = f32[512,384]{1,0:T(8,128)S(1)} collective-permute-done((f32[512,384]{1,0:T(8,128)S(1)}, f32[512,384]{1,0:T(8,128)S(1)}, u32[]{:S(2)}, u32[]{:S(2)}) %collective-permute-start.13) | collective-permute-done | bytes 786464 | tf_op jit(solution)/shard_map/ppermute | solution.py:424
  77.3 0.8 sum_halves.1
  78.1 5.5 %all-to-all-start = ((bf16[16,32,384]{2,1,0:T(8,128)(2,1)}), bf16[16,32,384]{2,1,0:T(8,128)(2,1)S(1)}, u32[]{:S(2)}, u32[]{:S(2)}) async-start(bf16[16,32,384]{2,1,0:T(8,128)(2,1)} %bitcast.10), calls=%async_computation | async-start | bytes 786432 | tf_op jit(solution)/shard_map/all_to_all | solution.py:425
  83.6 0.1 reduce
  83.8 0.1 pad_maximum_fusion
  83.9 0.1 select_reduce_fusion.2
  84.0 0.1 fusion.pick
  84.1 0.1 and_convert_fusion.allowed
  84.2 12.3 %all-to-all-done = bf16[16,32,384]{2,1,0:T(8,128)(2,1)S(1)} async-done(((bf16[16,32,384]{2,1,0:T(8,128)(2,1)}), bf16[16,32,384]{2,1,0:T(8,128)(2,1)S(1)}, u32[]{:S(2)}, u32[]{:S(2)}) %all-to-all-start) | async-done | bytes 393248 | tf_op jit(solution)/shard_map/all_to_all | solution.py:425
  96.5 2.3 %attend.1 = (bf16[128,128]{1,0:T(8,128)(2,1)}, bf16[128,128]{1,0:T(8,128)(2,1)}, bf16[128,512]{1,0:T(8,128)(2,1)}) custom-call(bf16[128,256]{1,0:T(8,128)(2,1)S(1)} %fusion.pick, bf16[2,256,384]{2,1,0:T(8,128)(2,1)S(1)} %bitcast.25, f32[128,128]{1,0:T(8,128)S(1)} %get-tuple-element.38.cosine, f32[128,128]{1,0:T(8,128)S(1)} %get-tuple-element.39.sine, ...), custom_call_target="tpu_custom_call" | custom-call | tf_op jit(solution)/shard_map/attend/pallas_call | solution.py:339
  (8 shorter events, 0.1 us)
Async XLA Ops:
  0.6 1.3 %copy-start = (bf16[4096,160]{0,1:T(8,128)(2,1)S(1)}, bf16[4096,160]{0,1:T(8,128)(2,1)}, u32[]{:S(2)}) copy-start(bf16[4096,160]{0,1:T(8,128)(2,1)} %param.8) | copy-start | bytes 3932164
  0.6 11.6 %copy-start.1 = (bf16[256,4096]{1,0:T(8,128)(2,1)S(1)}, bf16[256,4096]{1,0:T(8,128)(2,1)}, u32[]{:S(2)}) copy-start(bf16[256,4096]{1,0:T(8,128)(2,1)} %own.1) | copy-start | bytes 6291460
  2.8 18.5 %collective-permute-start = (bf16[80,4096]{1,0:T(8,128)(2,1)}, bf16[80,4096]{1,0:T(8,128)(2,1)}, u32[]{:S(2)}, u32[]{:S(2)}) collective-permute-start(bf16[80,4096]{1,0:T(8,128)(2,1)} %bitcast.6.mine), channel_id=1, source_target_pairs={{0,4},{2,6},{4,0},{6,2},{8,12},{10,14},{12,8},{14,10},{1,5},{3,7},... | collective-permute-start | bytes 1966088 | tf_op jit(solution)/shard_map/ppermute | solution.py:121
  5.9 16.5 %collective-permute-start.1 = (bf16[80,4096]{1,0:T(8,128)(2,1)}, bf16[80,4096]{1,0:T(8,128)(2,1)}, u32[]{:S(2)}, u32[]{:S(2)}) collective-permute-start(bf16[80,4096]{1,0:T(8,128)(2,1)} %bitcast.6.mine), channel_id=1, source_target_pairs={{4,8},{6,10},{8,4},{10,6},{0,2},{2,0},{12,14},{14,12},{5,9},{7,11}... | collective-permute-start | bytes 1966088 | tf_op jit(solution)/shard_map/ppermute | solution.py:121
  7.4 19.5 %collective-permute-start.4 = (bf16[80,4096]{1,0:T(8,128)(2,1)}, bf16[80,4096]{1,0:T(8,128)(2,1)}, u32[]{:S(2)}, u32[]{:S(2)}) collective-permute-start(bf16[80,4096]{1,0:T(8,128)(2,1)} %bitcast.6.mine), channel_id=1, source_target_pairs={{4,6},{6,4},{8,10},{10,8},{5,7},{7,5},{9,11},{11,9},{20,22},{22,20... | collective-permute-start | bytes 1966088 | tf_op jit(solution)/shard_map/ppermute | solution.py:121
  10.7 10.6 %collective-permute-start.2 = (bf16[48,4096]{1,0:T(8,128)(2,1)}, bf16[48,4096]{1,0:T(8,128)(2,1)}, u32[]{:S(2)}, u32[]{:S(2)}) collective-permute-start(bf16[48,4096]{1,0:T(8,128)(2,1)} %slice.6), channel_id=1, source_target_pairs={{0,16},{16,0},{1,17},{17,1},{2,18},{18,2},{3,19},{19,3},{4,20},{20... | collective-permute-start | bytes 1179656 | tf_op jit(solution)/shard_map/ppermute | solution.py:372
  12.7 46.8 %copy-start.7 = (s32[1,8]{1,0:T(1,128)S(1)}, s32[1,8]{1,0:T(1,128)}, u32[]{:S(2)}) copy-start(s32[1,8]{1,0:T(1,128)} %param.10) | copy-start | bytes 100
  12.7 50.4 %copy-start.4 = (f32[4096]{0:T(1024)S(1)}, f32[4096]{0:T(1024)}, u32[]{:S(2)}) copy-start(f32[4096]{0:T(1024)} %param.7) | copy-start | bytes 49156
  15.2 6.1 %collective-permute-start.3 = (f32[256]{0:T(256)S(1)}, f32[256]{0:T(256)S(1)}, u32[]{:S(2)}, u32[]{:S(2)}) collective-permute-start(f32[256]{0:T(256)S(1)} %add_rsqrt_fusion), channel_id=1, source_target_pairs={{0,16},{16,0},{1,17},{17,1},{2,18},{18,2},{3,19},{19,3},{4,20},{20... | collective-permute-start | bytes 3080 | tf_op jit(solution)/shard_map/ppermute | solution.py:374
  22.4 15.6 %collective-permute-start.5 = (bf16[80,4096]{1,0:T(8,128)(2,1)}, bf16[80,4096]{1,0:T(8,128)(2,1)}, u32[]{:S(2)}, u32[]{:S(2)}) collective-permute-start(bf16[80,4096]{1,0:T(8,128)(2,1)} %collective-permute-done.1.cross), channel_id=1, source_target_pairs={{0,4},{2,6},{4,0},{6,2},{8,12},{10,14},{12,8},{14,10},{1,5},{3,7},... | collective-permute-start | bytes 1966088 | tf_op jit(solution)/shard_map/ppermute | solution.py:121
  24.6 14.8 %collective-permute-start.6 = (bf16[80,4096]{1,0:T(8,128)(2,1)}, bf16[80,4096]{1,0:T(8,128)(2,1)}, u32[]{:S(2)}, u32[]{:S(2)}) collective-permute-start(bf16[80,4096]{1,0:T(8,128)(2,1)} %collective-permute-done.near), channel_id=1, source_target_pairs={{4,8},{6,10},{8,4},{10,6},{0,2},{2,0},{12,14},{14,12},{5,9},{7,11}... | collective-permute-start | bytes 1966088 | tf_op jit(solution)/shard_map/ppermute | solution.py:121
  25.3 37.8 %collective-permute-start.10 = (bf16[208,4096]{1,0:T(8,128)(2,1)}, bf16[208,4096]{1,0:T(8,128)(2,1)}, u32[]{:S(2)}, u32[]{:S(2)}) collective-permute-start(bf16[208,4096]{1,0:T(8,128)(2,1)} %slice.7), channel_id=1, source_target_pairs={{0,16},{16,0},{1,17},{17,1},{2,18},{18,2},{3,19},{19,3},{4,20},{20... | collective-permute-start | bytes 5111816 | tf_op jit(solution)/shard_map/ppermute | solution.py:378
  26.8 13.9 %collective-permute-start.7 = (bf16[80,4096]{1,0:T(8,128)(2,1)}, bf16[80,4096]{1,0:T(8,128)(2,1)S(1)}, u32[]{:S(2)}, u32[]{:S(2)}) collective-permute-start(bf16[80,4096]{1,0:T(8,128)(2,1)} %collective-permute-done.1.cross), channel_id=1, source_target_pairs={{4,6},{6,4},{8,10},{10,8},{5,7},{7,5},{9,11},{11,9},{20,22},{22,20... | collective-permute-start | bytes 1966088 | tf_op jit(solution)/shard_map/ppermute | solution.py:121
  39.5 15.8 %collective-permute-start.11 = (bf16[80,4096]{1,0:T(8,128)(2,1)}, bf16[80,4096]{1,0:T(8,128)(2,1)}, u32[]{:S(2)}, u32[]{:S(2)}) collective-permute-start(bf16[80,4096]{1,0:T(8,128)(2,1)} %collective-permute-done.6.onward), channel_id=1, source_target_pairs={{4,0},{6,2},{8,12},{10,14},{5,1},{7,3},{9,13},{11,15},{20,16},{22,... | collective-permute-start | bytes 1966088 | tf_op jit(solution)/shard_map/ppermute | solution.py:121
  40.8 0.8 copy-start.2
  41.6 18.2 %collective-permute-start.9 = (bf16[80,4096]{1,0:T(8,128)(2,1)}, bf16[80,4096]{1,0:T(8,128)(2,1)}, u32[]{:S(2)}, u32[]{:S(2)}) collective-permute-start(bf16[80,4096]{1,0:T(8,128)(2,1)} %collective-permute-done.5.second), channel_id=1, source_target_pairs={{0,2},{2,0},{12,14},{14,12},{1,3},{3,1},{13,15},{15,13},{16,18},{1... | collective-permute-start | bytes 1966088 | tf_op jit(solution)/shard_map/ppermute | solution.py:121
  45.0 14.8 %collective-permute-start.8 = (bf16[80,4096]{1,0:T(8,128)(2,1)}, bf16[80,4096]{1,0:T(8,128)(2,1)}, u32[]{:S(2)}, u32[]{:S(2)}) collective-permute-start(bf16[80,4096]{1,0:T(8,128)(2,1)} %collective-permute-done.6.onward), channel_id=1, source_target_pairs={{4,6},{6,4},{8,10},{10,8},{5,7},{7,5},{9,11},{11,9},{20,22},{22,20... | collective-permute-start | bytes 1966088 | tf_op jit(solution)/shard_map/ppermute | solution.py:121
  55.3 16.7 %collective-permute-start.12 = (bf16[80,4096]{1,0:T(8,128)(2,1)}, bf16[80,4096]{1,0:T(8,128)(2,1)}, u32[]{:S(2)}, u32[]{:S(2)}) collective-permute-start(bf16[80,4096]{1,0:T(8,128)(2,1)} %collective-permute-done.11.piece), channel_id=1, source_target_pairs={{0,2},{2,0},{12,14},{14,12},{1,3},{3,1},{13,15},{15,13},{16,18},{1... | collective-permute-start | bytes 1966088 | tf_op jit(solution)/shard_map/ppermute | solution.py:121
  63.1 1.1 %copy-start.3 = (bf16[80,4096]{1,0:T(8,128)(2,1)S(1)}, bf16[80,4096]{1,0:T(8,128)(2,1)}, u32[]{:S(2)}) copy-start(bf16[80,4096]{1,0:T(8,128)(2,1)} %copy-done.2) | copy-start | bytes 1966084
  72.0 3.0 %copy-start.6 = (s32[1,8]{1,0:T(1,128)S(1)}, s32[1,8]{1,0:T(1,128)}, u32[]{:S(2)}) copy-start(s32[1,8]{1,0:T(1,128)} %param.11) | copy-start | bytes 100
  72.0 3.1 %copy-start.5 = (s32[8,8]{1,0:T(8,128)S(1)}, s32[8,8]{1,0:T(8,128)}, u32[]{:S(2)}) copy-start(s32[8,8]{1,0:T(8,128)} %param.9) | copy-start | bytes 772
  74.9 2.4 %collective-permute-start.13 = (f32[512,384]{1,0:T(8,128)S(1)}, f32[512,384]{1,0:T(8,128)S(1)}, u32[]{:S(2)}, u32[]{:S(2)}) collective-permute-start(f32[512,384]{1,0:T(8,128)S(1)} %get-tuple-element.30), channel_id=1, source_target_pairs={{0,1},{1,0},{2,3},{3,2},{4,5},{5,4},{6,7},{7,6},{8,9},{9,8},{10,11... | collective-permute-start | bytes 2359304 | tf_op jit(solution)/shard_map/ppermute | solution.py:424
  78.1 18.4 %all-to-all-start = ((bf16[16,32,384]{2,1,0:T(8,128)(2,1)}), bf16[16,32,384]{2,1,0:T(8,128)(2,1)S(1)}, u32[]{:S(2)}, u32[]{:S(2)}) async-start(bf16[16,32,384]{2,1,0:T(8,128)(2,1)} %bitcast.10), calls=%async_computation | async-start | bytes 786432 | tf_op jit(solution)/shard_map/all_to_all | solution.py:425
